TPU v7x, 32 devices: a whole 2x2x4 slice. The times are simulated.
32 devices in a mesh: dp: 4 (over z), ctx: 8 (over y, x, core).
Axes of the slice: x: 2, y: 2, z: 4, core: 2. Of those that a mesh axis runs over, the one named last changes fastest.
Arguments:
- inputs: bfloat16 [4, 4096, 4096], P('dp', 'ctx'), may hold values from -6 to 6
- qkv_weight: bfloat16 [4096, 768], P('ctx'), may hold values from -0.09375 to 0.09375
- queries: bfloat16 [4, 4096, 512], P('dp', 'ctx'), may hold values from -6 to 6
- keys_values: bfloat16 [4, 4096, 256], P('dp', 'ctx'), may hold values from -6 to 6
- out_grad: bfloat16 [4, 4096, 512], P('dp', 'ctx'), may hold values from -6 to 6
- lengths: int32 [4, 16], P('dp'), may hold values from 1 to 1536, as said below
Outputs:
- grad_queries: bfloat16 [4, 4096, 512], P('dp', 'ctx')
- grad_kv: bfloat16 [4, 4096, 256], P('dp', 'ctx')
- grad_inputs: bfloat16 [4, 4096, 4096], P('dp', 'ctx')
- grad_weight: bfloat16 [4096, 768], P('ctx')
Inputs may be any that keep to these rules, and one draw needn't show every extreme that they name: Each row's lengths sum to 4096; the first is 1, the second exactly 1536, none longer.
All inputs are finite; a program needn't handle non-finite values.
Results may differ from a plain program's by a relative error of at most 0.0074.
Values may be sent and summed in bfloat16 or wider, within the bound.
No kernel may reach another device: no remote copies, remote signals or barrier semaphores. Data moves between devices by JAX's collectives and lax.ppermute only.
A program may use at most 128 MiB of HBM per device.

v0:
```python
import jax
import jax.numpy as jnp
from jax import lax
from jax.sharding import PartitionSpec as P

MOST = 1536


NEG_FILL = -1e30


def shifted(array, axis, by):
    devices = lax.axis_size(axis)
    pairs = [(i, i + by) for i in range(devices) if 0 <= i + by < devices]
    return lax.ppermute(array, axis, pairs)


def passed_along(array, axis, by):
    devices = lax.axis_size(axis)
    return lax.ppermute(array, axis, [(i, (i + by) % devices) for i in range(devices)])


def doc_of(positions, doc_ends):
    return jnp.sum((positions[:, None] >= doc_ends[None, :]).astype(jnp.int32), axis=1)


def per_device(inputs, qkv_weight, queries, keys_values, out_grad, lengths):
    tok_rows = queries.shape[1]
    head_size = keys_values.shape[2] // 2
    head_count = queries.shape[2] // head_size
    ctx_size = lax.axis_size("ctx")
    scaling = head_size ** (-0.5)
    my_index = lax.axis_index("ctx")
    doc_ends = jnp.cumsum(lengths[0])
    q_pos = my_index * tok_rows + jnp.arange(tok_rows, dtype=jnp.int32)
    q_doc = doc_of(q_pos, doc_ends)
    q_heads = queries[0].reshape(tok_rows, head_count, head_size)
    g_heads = out_grad[0].reshape(tok_rows, head_count, head_size)
    local_kv = keys_values[0]
    reach_devs = MOST // tok_rows

    def allowed_of(key_start, key_count):
        k_pos = key_start + jnp.arange(key_count, dtype=jnp.int32)
        k_doc = doc_of(k_pos, doc_ends)
        return (q_doc[:, None] == k_doc[None, :]) & (k_pos[None, :] <= q_pos[:, None])

    def start_of(distance):
        return jnp.mod(my_index - distance, ctx_size) * tok_rows

    def score_terms(key_piece):
        keys_part = key_piece[:, :head_size]
        values_part = key_piece[:, head_size:]
        scores = (
            jnp.einsum("thd,kd->htk", q_heads, keys_part, preferred_element_type=jnp.float32)
            * scaling
        )
        dprobs = jnp.einsum("thd,kd->htk", g_heads, values_part, preferred_element_type=jnp.float32)
        return (scores, dprobs)

    def stats_core(stats, key_piece, allowed):
        run_max, run_sum, run_dot = stats
        scores, dprobs = score_terms(key_piece)
        masked = jnp.where(allowed[None], scores, NEG_FILL)
        new_max = jnp.maximum(run_max, jnp.max(masked, axis=2))
        factor = jnp.exp(run_max - new_max)
        weights = jnp.where(allowed[None], jnp.exp(scores - new_max[:, :, None]), 0.0)
        return (
            new_max,
            run_sum * factor + jnp.sum(weights, axis=2),
            run_dot * factor + jnp.sum(weights * dprobs, axis=2),
        )

    def stats_update(stats, key_piece, key_start):
        allowed = allowed_of(key_start, key_piece.shape[0])
        return stats_core(stats, key_piece, allowed)

    init_stats = (
        jnp.full((head_count, tok_rows), NEG_FILL, jnp.float32),
        jnp.zeros((head_count, tok_rows), jnp.float32),
        jnp.zeros((head_count, tok_rows), jnp.float32),
    )
    first_stats = stats_update(init_stats, local_kv, my_index * tok_rows)

    def visit_stats(turn_index, carried):
        key_piece = shifted(carried[0], "ctx", 1)
        return (key_piece, stats_update(carried[1], key_piece, start_of(turn_index)))

    final_stats = lax.fori_loop(1, reach_devs + 1, visit_stats, (local_kv, first_stats))[1]
    lse = final_stats[0] + jnp.log(final_stats[1])
    delta = final_stats[2] / final_stats[1]

    def grad_core(key_piece, allowed):
        scores, dprobs = score_terms(key_piece)
        probs = jnp.where(allowed[None], jnp.exp(scores - lse[:, :, None]), 0.0)
        dscores = probs * (dprobs - delta[:, :, None])
        probs_low = probs.astype(jnp.bfloat16)
        dscores_low = dscores.astype(jnp.bfloat16)
        dq_add = jnp.einsum(
            "htk,kd->thd", dscores_low, key_piece[:, :head_size], preferred_element_type=jnp.float32
        )
        dk_add = (
            jnp.einsum("htk,thd->kd", dscores_low, q_heads, preferred_element_type=jnp.float32)
            * scaling
        )
        dv_add = jnp.einsum("htk,thd->kd", probs_low, g_heads, preferred_element_type=jnp.float32)
        return (dq_add, jnp.concatenate([dk_add, dv_add], axis=1))

    def grad_update(key_piece, key_start):
        allowed = allowed_of(key_start, key_piece.shape[0])
        return grad_core(key_piece, allowed)

    dq_first, kv_first = grad_update(local_kv, my_index * tok_rows)

    def visit_grads(turn_index, carried):
        key_piece = shifted(carried[0], "ctx", 1)
        travel_grad = passed_along(carried[1], "ctx", 1)
        dq_add, kv_add = grad_update(key_piece, start_of(turn_index))
        return (key_piece, travel_grad + kv_add, carried[2] + dq_add)

    walked = lax.fori_loop(1, reach_devs + 1, visit_grads, (local_kv, kv_first, dq_first))
    dq_acc = walked[2]
    kv_grad = passed_along(walked[1].astype(jnp.bfloat16), "ctx", -reach_devs).astype(jnp.float32)
    grad_queries = (dq_acc * scaling).astype(jnp.bfloat16).reshape(tok_rows, head_count * head_size)
    grad_kv = kv_grad.astype(jnp.bfloat16)
    grad_qkv = jnp.concatenate([grad_queries, grad_kv], axis=1)
    x_local = inputs[0]
    grad_in = lax.dot_general(
        grad_qkv,
        lax.all_gather(qkv_weight, "ctx", axis=0, tiled=True),
        (((1,), (1,)), ((), ())),
        preferred_element_type=jnp.float32,
    ).astype(jnp.bfloat16)
    shard_grad = lax.psum_scatter(
        lax.dot_general(
            x_local, grad_qkv, (((0,), (0,)), ((), ())), preferred_element_type=jnp.float32
        ),
        "ctx",
        scatter_dimension=0,
        tiled=True,
    )
    weight_sum = lax.psum(shard_grad, "dp").astype(jnp.bfloat16)
    return (grad_queries[None], grad_kv[None], grad_in[None], weight_sum)


def solution(mesh):
    placed = (
        P("dp", "ctx", None),
        P("ctx", None),
        P("dp", "ctx", None),
        P("dp", "ctx", None),
        P("dp", "ctx", None),
        P("dp", None),
    )
    return jax.shard_map(
        per_device,
        mesh=mesh,
        in_specs=placed,
        out_specs=(
            P("dp", "ctx", None),
            P("dp", "ctx", None),
            P("dp", "ctx", None),
            P("ctx", None),
        ),
        check_vma=False,
    )
```

profile of v0, /device:TPU:0, one launch (start us, length us, event | category | flops | bytes accessed | tf_op | source)
XLA Modules:
  0.0 297.6 jit_solution(11610561815131491220)
XLA Ops:
  7.2 1.0 copy.106
  8.3 0.8 copy.52
  9.6 1.3 copy.53
  11.1 2.9 fusion.31
  14.5 5.6 %fusion.28 = (f32[4,512]{1,0:T(4,128)S(1)}, f32[4,512]{1,0:T(4,128)S(1)}, f32[512,512,4]{1,0,2:T(8,128)}) fusion(f32[512,512,4]{1,0,2:T(8,128)} %get-tuple-element.720, f32[4,512]{1,0:T(4,128)S(1)} %broadcast_maximum_fusion, pred[512,512]{0,1:T(8,128)(4,1)S(1)} %compare_and_fusion.2, bf16[512,4,128]{0,2,1:T(8,128)(2,1)S(1)} %bitcast.194, ...), kind=kOutput, calls=%fused_computation.50 | convolution fusion | flops 274722816 | bytes 9330688 | tf_op jit(solution)/shard_map/thd,kd->htk/dot_general | solution.py:57
  20.1 38.4 %while.42 = (s32[]{:T(128)}, bf16[512,256]{1,0:T(8,128)(2,1)S(1)}, f32[4,512]{1,0:T(4,128)S(1)}, f32[4,512]{1,0:T(4,128)S(1)}, f32[4,512]{1,0:T(4,128)S(1)}, /*i...) while((s32[]{:T(128)}, bf16[512,256]{1,0:T(8,128)(2,1)S(1)}, ...), condition=%wide.region_10.11_spmd.clone, body=%wide.region_5.10_spmd.clone.sunk | while | flops 550271488 | bytes 16679306 | solution.py:88
  20.3 2.4 collective-permute-start
  23.1 0.7 collective-permute-done
  23.8 0.9 fusion.88
  24.7 0.9 fusion.90
  25.6 1.5 fusion.89
  27.2 10.2 %collective-permute-start = (bf16[512,256]{1,0:T(8,128)(2,1)S(1)}, bf16[512,256]{1,0:T(8,128)(2,1)S(1)}, u32[]{:S(2)}, u32[]{:S(2)}) collective-permute-start(bf16[512,256]{1,0:T(8,128)(2,1)S(1)} %get-tuple-element.891), channel_id=1, source_target_pairs={{0,1},{1,2},{2,3},{3,4},{4,5},{5,6},{6,7},{8,9},{9,10},{10,11},{11... | collective-permute-start | bytes 786440 | tf_op jit(solution)/shard_map/while/body/eval_jaxpr/ppermute | solution.py:15
  37.8 0.7 collective-permute-done
  38.6 0.9 fusion.88
  39.5 0.9 fusion.90
  40.4 1.5 fusion.89
  42.0 12.0 %collective-permute-start = (bf16[512,256]{1,0:T(8,128)(2,1)S(1)}, bf16[512,256]{1,0:T(8,128)(2,1)S(1)}, u32[]{:S(2)}, u32[]{:S(2)}) collective-permute-start(bf16[512,256]{1,0:T(8,128)(2,1)S(1)} %get-tuple-element.891), channel_id=1, source_target_pairs={{0,1},{1,2},{2,3},{3,4},{4,5},{5,6},{6,7},{8,9},{9,10},{10,11},{11... | collective-permute-start | bytes 786440 | tf_op jit(solution)/shard_map/while/body/eval_jaxpr/ppermute | solution.py:15
  54.4 0.7 collective-permute-done
  55.1 0.9 fusion.88
  56.0 0.9 fusion.90
  56.9 1.5 fusion.89
  58.5 4.9 %fusion.30 = bf16[4,512,512]{1,2,0:T(8,128)(2,1)S(1)} fusion(f32[512,512,4]{1,0,2:T(8,128)} %get-tuple-element.721, f32[512,512,4]{1,0,2:T(8,128)} %get-tuple-element.720, f32[4,512]{1,0:T(4,128)S(1)} %get-tuple-element.932, f32[4,512]{1,0:T(4,128)S(1)} %get-tuple-element.930, pred[512,512]{0,1:T(8,128)(4,1)S(1)} %compare_and_fusion.2), kind=kLoop, calls=%fused_computation.52 | loop fusion | flops 6291456 | bytes 10764288 | tf_op jit(solution)/shard_map/convert_element_type | solution.py:97
  63.4 0.8 fusion.44
  64.2 1.1 fusion.41
  65.3 0.8 pad_maximum_fusion.1
  66.2 0.7 convolution_bitcast_fusion.3
  66.9 47.2 %while.43 = (s32[]{:T(128)}, bf16[512,256]{1,0:T(8,128)(2,1)S(1)}, f32[512,256]{0,1:T(8,128)}, f32[512,4,128]{2,0,1:T(8,128)S(1)}, s32[512]{0:T(512)S(1)}, /*ind...) while((s32[]{:T(128)}, bf16[512,256]{1,0:T(8,128)(2,1)S(1)}, ...), condition=%wide.region_13.14_spmd.clone, body=%wide.region_11.13_spmd.clone.sunk | while | flops 1354064384 | bytes 30056888 | solution.py:120
  66.9 8.1 %collective-permute-start.1 = (bf16[512,256]{1,0:T(8,128)(2,1)S(1)}, bf16[512,256]{1,0:T(8,128)(2,1)S(1)}, u32[]{:S(2)}, u32[]{:S(2)}) collective-permute-start(bf16[512,256]{1,0:T(8,128)(2,1)S(1)} %get-tuple-element.940), channel_id=1, source_target_pairs={{0,1},{1,2},{2,3},{3,4},{4,5},{5,6},{6,7},{8,9},{9,10},{10,11},{11... | collective-permute-start | bytes 786440 | tf_op jit(solution)/shard_map/while/body/eval_jaxpr/ppermute | solution.py:15
  75.0 2.5 collective-permute-start.2
  77.9 0.7 fusion.98
  78.6 1.5 fusion.100
  80.1 0.9 fusion.102
  81.0 0.8 fusion.101
  81.9 1.1 fusion.99
  82.9 1.8 collective-permute-done.2
  84.8 0.9 maximum_add_fusion.2
  85.6 3.6 %collective-permute-start.1 = (bf16[512,256]{1,0:T(8,128)(2,1)S(1)}, bf16[512,256]{1,0:T(8,128)(2,1)S(1)}, u32[]{:S(2)}, u32[]{:S(2)}) collective-permute-start(bf16[512,256]{1,0:T(8,128)(2,1)S(1)} %get-tuple-element.940), channel_id=1, source_target_pairs={{0,1},{1,2},{2,3},{3,4},{4,5},{5,6},{6,7},{8,9},{9,10},{10,11},{11... | collective-permute-start | bytes 786440 | tf_op jit(solution)/shard_map/while/body/eval_jaxpr/ppermute | solution.py:15
  89.3 2.4 collective-permute-start.2
  92.1 0.7 fusion.98
  92.8 1.5 fusion.100
  94.3 0.9 fusion.102
  95.2 0.8 fusion.101
  96.0 1.1 fusion.99
  97.1 1.9 collective-permute-done.2
  99.0 0.9 maximum_add_fusion.2
  99.9 3.5 %collective-permute-start.1 = (bf16[512,256]{1,0:T(8,128)(2,1)S(1)}, bf16[512,256]{1,0:T(8,128)(2,1)S(1)}, u32[]{:S(2)}, u32[]{:S(2)}) collective-permute-start(bf16[512,256]{1,0:T(8,128)(2,1)S(1)} %get-tuple-element.940), channel_id=1, source_target_pairs={{0,1},{1,2},{2,3},{3,4},{4,5},{5,6},{6,7},{8,9},{9,10},{10,11},{11... | collective-permute-start | bytes 786440 | tf_op jit(solution)/shard_map/while/body/eval_jaxpr/ppermute | solution.py:15
  103.4 2.4 collective-permute-start.2
  106.3 0.7 fusion.98
  106.9 1.5 fusion.100
  108.5 0.9 fusion.102
  109.4 0.8 fusion.101
  110.2 1.1 fusion.99
  111.3 1.9 collective-permute-done.2
  113.2 0.9 maximum_add_fusion.2
  114.1 1.1 convert_element_type.69
  115.2 3.0 %collective-permute-start.3 = (bf16[512,256]{0,1:T(8,128)(2,1)S(1)}, bf16[512,256]{0,1:T(8,128)(2,1)S(1)}, u32[]{:S(2)}, u32[]{:S(2)}) collective-permute-start(bf16[512,256]{0,1:T(8,128)(2,1)S(1)} %convert_element_type.69), channel_id=1, source_target_pairs={{0,5},{1,6},{2,7},{3,0},{4,1},{5,2},{6,3},{7,4},{8,13},{9,14},{10,... | collective-permute-start | bytes 786440 | tf_op jit(solution)/shard_map/ppermute | solution.py:20
  118.6 6.6 %collective-permute-done.3 = bf16[512,256]{0,1:T(8,128)(2,1)S(1)} collective-permute-done((bf16[512,256]{0,1:T(8,128)(2,1)S(1)}, bf16[512,256]{0,1:T(8,128)(2,1)S(1)}, u32[]{:S(2)}, u32[]{:S(2)}) %collective-permute-start.3) | collective-permute-done | bytes 262176 | tf_op jit(solution)/shard_map/ppermute | solution.py:20
  125.2 8.9 %convolution_bitcast_fusion.2 = f32[4096,768]{0,1:T(8,128)} fusion(bf16[1,512,4096]{2,1,0:T(8,128)(2,1)} %param.10, bf16[512,256]{0,1:T(8,128)(2,1)S(1)} %collective-permute-done.3, bf16[512,512]{0,1:T(8,128)(2,1)S(1)} %bitcast.202), kind=kOutput, calls=%fused_computation.44 | convolution fusion | flops 3222798336 | bytes 17563648 | tf_op jit(solution)/shard_map/dot_general | solution.py:134
  134.2 1.0 copy.63
  135.2 0.8 copy.64
  136.0 7.8 %fusion.26 = bf16[1,512,4096]{2,1,0:T(8,128)(2,1)} fusion(bf16[4096,768]{1,0:T(8,128)(2,1)} %all-gather.2.cloned.1.call-done, bf16[512,256]{0,1:T(8,128)(2,1)S(1)} %collective-permute-done.3, bf16[512,512]{0,1:T(8,128)(2,1)S(1)} %bitcast.204), kind=kOutput, calls=%fused_computation.46 | convolution fusion | flops 3224895488 | bytes 11272192 | tf_op jit(solution)/shard_map/dot_general | solution.py:127
  143.9 85.2 %reduce-scatter.2.cloned.1.call-done = f32[512,768]{0,1:T(8,128)} async-done(((f32[4096,768]{0,1:T(8,128)}), f32[512,768]{0,1:T(8,128)}) %reduce-scatter.2.cloned.1.call-update) | async-done | bytes 1572880 | tf_op jit(solution)/shard_map/reduce_scatter | solution.py:133
  229.1 60.5 %all-reduce.1 = bf16[512,768]{0,1:T(8,128)(2,1)S(1)} all-reduce(f32[512,768]{0,1:T(8,128)} %reduce-scatter.2.cloned.1.call-done), channel_id=1, replica_groups=mesh['dp'=4,'ctx'=8] {'dp'}, use_global_device_ids=true, to_apply=%region_15.16 | all-reduce | flops 393216 | bytes 2359296 | tf_op jit(solution)/shard_map/psum | solution.py:141
  289.6 1.2 copy.65
  (62 shorter events, 4.4 us)
Async XLA Ops:
  7.2 128.9 %all-gather.2.cloned.1.call-start = ((), (), s32[]{:S(2)}) async-start(), calls=%async_computation.1 | async-start | bytes 7077888 | tf_op jit(solution)/shard_map/all_gather | solution.py:129
  8.2 5.8 %copy-start.1 = (bf16[1,512,512]{2,1,0:T(8,128)(2,1)S(1)}, bf16[1,512,512]{2,1,0:T(8,128)(2,1)}, u32[]{:S(2)}) copy-start(bf16[1,512,512]{2,1,0:T(8,128)(2,1)} %param.14) | copy-start | bytes 1572868
  8.2 220.9 %reduce-scatter.2.cloned.1.call-start = ((), (), s32[]{:S(2)}) async-start(), calls=%async_computation.2 | async-start | bytes 14155776 | tf_op jit(solution)/shard_map/reduce_scatter | solution.py:133
  20.3 3.5 %collective-permute-start = (bf16[512,256]{1,0:T(8,128)(2,1)S(1)}, bf16[512,256]{1,0:T(8,128)(2,1)S(1)}, u32[]{:S(2)}, u32[]{:S(2)}) collective-permute-start(bf16[512,256]{1,0:T(8,128)(2,1)S(1)} %get-tuple-element.891), channel_id=1, source_target_pairs={{0,1},{1,2},{2,3},{3,4},{4,5},{5,6},{6,7},{8,9},{9,10},{10,11},{11... | collective-permute-start | bytes 786440 | tf_op jit(solution)/shard_map/while/body/eval_jaxpr/ppermute | solution.py:15
  27.2 11.4 %collective-permute-start = (bf16[512,256]{1,0:T(8,128)(2,1)S(1)}, bf16[512,256]{1,0:T(8,128)(2,1)S(1)}, u32[]{:S(2)}, u32[]{:S(2)}) collective-permute-start(bf16[512,256]{1,0:T(8,128)(2,1)S(1)} %get-tuple-element.891), channel_id=1, source_target_pairs={{0,1},{1,2},{2,3},{3,4},{4,5},{5,6},{6,7},{8,9},{9,10},{10,11},{11... | collective-permute-start | bytes 786440 | tf_op jit(solution)/shard_map/while/body/eval_jaxpr/ppermute | solution.py:15
  42.0 13.2 %collective-permute-start = (bf16[512,256]{1,0:T(8,128)(2,1)S(1)}, bf16[512,256]{1,0:T(8,128)(2,1)S(1)}, u32[]{:S(2)}, u32[]{:S(2)}) collective-permute-start(bf16[512,256]{1,0:T(8,128)(2,1)S(1)} %get-tuple-element.891), channel_id=1, source_target_pairs={{0,1},{1,2},{2,3},{3,4},{4,5},{5,6},{6,7},{8,9},{9,10},{10,11},{11... | collective-permute-start | bytes 786440 | tf_op jit(solution)/shard_map/while/body/eval_jaxpr/ppermute | solution.py:15
  58.5 5.7 %copy-start = (f32[512,512,4]{1,0,2:T(8,128)S(1)}, f32[512,512,4]{1,0,2:T(8,128)}, u32[]{:S(2)}) copy-start(f32[512,512,4]{1,0,2:T(8,128)} %get-tuple-element.720) | copy-start | bytes 12582916
  66.9 11.0 %collective-permute-start.1 = (bf16[512,256]{1,0:T(8,128)(2,1)S(1)}, bf16[512,256]{1,0:T(8,128)(2,1)S(1)}, u32[]{:S(2)}, u32[]{:S(2)}) collective-permute-start(bf16[512,256]{1,0:T(8,128)(2,1)S(1)} %get-tuple-element.940), channel_id=1, source_target_pairs={{0,1},{1,2},{2,3},{3,4},{4,5},{5,6},{6,7},{8,9},{9,10},{10,11},{11... | collective-permute-start | bytes 786440 | tf_op jit(solution)/shard_map/while/body/eval_jaxpr/ppermute | solution.py:15
  75.0 9.8 %collective-permute-start.2 = (f32[512,256]{0,1:T(8,128)}, f32[512,256]{0,1:T(8,128)S(1)}, u32[]{:S(2)}, u32[]{:S(2)}) collective-permute-start(f32[512,256]{0,1:T(8,128)} %get-tuple-element.941), channel_id=1, source_target_pairs={{0,1},{1,2},{2,3},{3,4},{4,5},{5,6},{6,7},{7,0},{8,9},{9,10},{10,1... | collective-permute-start | bytes 1572872 | tf_op jit(solution)/shard_map/while/body/eval_jaxpr/ppermute | solution.py:20
  85.6 6.4 %collective-permute-start.1 = (bf16[512,256]{1,0:T(8,128)(2,1)S(1)}, bf16[512,256]{1,0:T(8,128)(2,1)S(1)}, u32[]{:S(2)}, u32[]{:S(2)}) collective-permute-start(bf16[512,256]{1,0:T(8,128)(2,1)S(1)} %get-tuple-element.940), channel_id=1, source_target_pairs={{0,1},{1,2},{2,3},{3,4},{4,5},{5,6},{6,7},{8,9},{9,10},{10,11},{11... | collective-permute-start | bytes 786440 | tf_op jit(solution)/shard_map/while/body/eval_jaxpr/ppermute | solution.py:15
  89.3 9.8 %collective-permute-start.2 = (f32[512,256]{0,1:T(8,128)}, f32[512,256]{0,1:T(8,128)S(1)}, u32[]{:S(2)}, u32[]{:S(2)}) collective-permute-start(f32[512,256]{0,1:T(8,128)} %get-tuple-element.941), channel_id=1, source_target_pairs={{0,1},{1,2},{2,3},{3,4},{4,5},{5,6},{6,7},{7,0},{8,9},{9,10},{10,1... | collective-permute-start | bytes 1572872 | tf_op jit(solution)/shard_map/while/body/eval_jaxpr/ppermute | solution.py:20
  99.9 6.3 %collective-permute-start.1 = (bf16[512,256]{1,0:T(8,128)(2,1)S(1)}, bf16[512,256]{1,0:T(8,128)(2,1)S(1)}, u32[]{:S(2)}, u32[]{:S(2)}) collective-permute-start(bf16[512,256]{1,0:T(8,128)(2,1)S(1)} %get-tuple-element.940), channel_id=1, source_target_pairs={{0,1},{1,2},{2,3},{3,4},{4,5},{5,6},{6,7},{8,9},{9,10},{10,11},{11... | collective-permute-start | bytes 786440 | tf_op jit(solution)/shard_map/while/body/eval_jaxpr/ppermute | solution.py:15
  103.4 9.8 %collective-permute-start.2 = (f32[512,256]{0,1:T(8,128)}, f32[512,256]{0,1:T(8,128)S(1)}, u32[]{:S(2)}, u32[]{:S(2)}) collective-permute-start(f32[512,256]{0,1:T(8,128)} %get-tuple-element.941), channel_id=1, source_target_pairs={{0,1},{1,2},{2,3},{3,4},{4,5},{5,6},{6,7},{7,0},{8,9},{9,10},{10,1... | collective-permute-start | bytes 1572872 | tf_op jit(solution)/shard_map/while/body/eval_jaxpr/ppermute | solution.py:20
  115.2 10.1 %collective-permute-start.3 = (bf16[512,256]{0,1:T(8,128)(2,1)S(1)}, bf16[512,256]{0,1:T(8,128)(2,1)S(1)}, u32[]{:S(2)}, u32[]{:S(2)}) collective-permute-start(bf16[512,256]{0,1:T(8,128)(2,1)S(1)} %convert_element_type.69), channel_id=1, source_target_pairs={{0,5},{1,6},{2,7},{3,0},{4,1},{5,2},{6,3},{7,4},{8,13},{9,14},{10,... | collective-permute-start | bytes 786440 | tf_op jit(solution)/shard_map/ppermute | solution.py:20
Sparse Core Ops, SparseCore 0:
  9.9 52.2 all-gather.1
  134.3 94.7 reduce-scatter.1
where the time goes:
time: 298 us
  waiting for transfers between devices  99.7 us (33%)
  blocking collectives  60.5 us (20%)
  starting transfers between devices  50.3 us (17%)
  matrix products  49.8 us (17%)
  other arithmetic  15.2 us (5%)
  between operations  14.2 us (5%)
  local copies, waits for them, and re-layouts  7.23 us (2%)
    reduce_scatter x1, waiting for transfers between devices, per_device(): lax.psum_scatter(lax.dot_general(x_local, grad_qkv, (((0,), (0,)), ((), (...  85.2 us
    psum x1, blocking collectives, per_device(): weight_sum = lax.psum(shard_grad, 'dp').astype(jnp.bfloat16)  60.5 us
    ppermute x6, starting transfers between devices, shifted(): return lax.ppermute(array, axis, pairs)  39.9 us
    dot_general x7, matrix products, score_terms(): jnp.einsum('thd,kd->htk', g_heads, values_part, preferred_element_type=jn...  14.6 us
    ppermute x4, waiting for transfers between devices, passed_along(): lax.ppermute(array, axis, [(i, (i + by) % devices) for i in range(devices)])  12.3 us
    ppermute x4, starting transfers between devices, passed_along(): lax.ppermute(array, axis, [(i, (i + by) % devices) for i in range(devices)])  10.3 us
    dot_general x1, matrix products, per_device(): lax.dot_general(x_local, grad_qkv, (((0,), (0,)), ((), ())), preferred_el...  8.91 us
    dot_general x1, matrix products, per_device(): lax.dot_general(grad_qkv, lax.all_gather(qkv_weight, 'ctx', axis=0, tiled...  7.84 us
  transfers between devices with their start and end apart: 12, of which 8 were waited for; matrix products, arithmetic and copies ran while one was open for 24% of the time, Pallas kernels for 0%

commit v1 on v0

v1 whole, which is shorter than its diff:
```python
import functools

import jax
import jax.numpy as jnp
from jax import lax
from jax.experimental import pallas as pl
from jax.experimental.pallas import tpu as pltpu
from jax.sharding import PartitionSpec as P

MOST = 1536
NEG_FILL = -1e30
LOG2E = 1.4426950408889634
KEY_STEP = 256
Q_STEP = 128


def nt_dot(a, b):
    return lax.dot_general(a, b, (((1,), (1,)), ((), ())), preferred_element_type=jnp.float32)


def nn_dot(a, b):
    return lax.dot_general(a, b, (((1,), (0,)), ((), ())), preferred_element_type=jnp.float32)


def attention_kernel(
    idx_ref, len_ref, q_ref, g_ref, own_ref, d2_ref, r_ref, x_ref,
    gq_ref, gqt_ref, own_out, d2_out, r_out, x_out,
    kv_scr, kt_scr, s_scr, dp_scr, acc_scr,
):
    rows = q_ref.shape[0]
    hd = kv_scr.shape[1] // 2
    heads = q_ref.shape[1] // hd
    wide = heads * Q_STEP
    scaling = hd ** (-0.5)
    index = idx_ref[0]
    parity = lax.rem(index, 2)
    base = (index - 3) * rows
    r_off = pl.multiple_of((1 - parity) * 2 * rows, rows)
    x_off = pl.multiple_of(parity * 2 * rows, rows)
    kv_scr[pl.ds(r_off, rows), :] = r_ref[...]
    kv_scr[pl.ds(x_off, rows), :] = x_ref[...]
    kv_scr[rows : 2 * rows, :] = d2_ref[...]
    kv_scr[3 * rows :, :] = own_ref[...]
    for slot in range(4):
        part = slice(slot * rows, (slot + 1) * rows)
        kt_scr[:, part] = kv_scr[part, :hd].T
    acc_scr[...] = jnp.zeros_like(acc_scr)
    ends = []
    total = -base
    for j in range(len_ref.shape[1]):
        ends.append(total)
        total = total + len_ref[0, j]

    for tile in range(rows // Q_STEP):
        q_rows = slice(tile * Q_STEP, (tile + 1) * Q_STEP)
        first = 3 * rows + tile * Q_STEP
        q_pos = first + (lax.broadcasted_iota(jnp.int32, (1, wide), 1) & (Q_STEP - 1))
        doc_start = jnp.full((1, wide), ends[0], jnp.int32)
        least = ends[0]
        for end in ends[1:]:
            doc_start = jnp.where(q_pos >= end, end, doc_start)
            least = jnp.where(first >= end, end, least)
        q_cat = jnp.concatenate([q_ref[q_rows, h * hd : (h + 1) * hd] for h in range(heads)], axis=0)
        g_cat = jnp.concatenate([g_ref[q_rows, h * hd : (h + 1) * hd] for h in range(heads)], axis=0)
        begin = jnp.maximum(least, 0) // KEY_STEP
        stop = -(-(first + Q_STEP) // KEY_STEP)

        def scores_step(c, top):
            at = pl.ds(pl.multiple_of(c * KEY_STEP, KEY_STEP), KEY_STEP)
            s = nt_dot(kv_scr[at, :hd], q_cat)
            k_pos = c * KEY_STEP + lax.broadcasted_iota(jnp.int32, (KEY_STEP, wide), 0)
            s = jnp.where((k_pos >= doc_start) & (k_pos <= q_pos), s, NEG_FILL)
            s_scr[at, :] = s
            dp_scr[at, :] = nt_dot(kv_scr[at, hd:], g_cat)
            return jnp.maximum(top, jnp.max(s, axis=0, keepdims=True))

        top = lax.fori_loop(begin, stop, scores_step, jnp.full((1, wide), NEG_FILL, jnp.float32))

        def sums_step(c, carried):
            at = pl.ds(pl.multiple_of(c * KEY_STEP, KEY_STEP), KEY_STEP)
            e = jnp.exp2((s_scr[at, :] - top) * (scaling * LOG2E))
            s_scr[at, :] = e
            return (
                carried[0] + jnp.sum(e, axis=0, keepdims=True),
                carried[1] + jnp.sum(e * dp_scr[at, :], axis=0, keepdims=True),
            )

        zero = jnp.zeros((1, wide), jnp.float32)
        norm, dot = lax.fori_loop(begin, stop, sums_step, (zero, zero))
        inverse = 1.0 / norm
        delta = dot * inverse

        def grads_step(c, dq):
            at = pl.ds(pl.multiple_of(c * KEY_STEP, KEY_STEP), KEY_STEP)
            p = s_scr[at, :] * inverse
            ds_low = (p * (dp_scr[at, :] - delta)).astype(jnp.bfloat16)
            p_low = p.astype(jnp.bfloat16)
            acc_scr[at, :hd] += nn_dot(ds_low, q_cat)
            acc_scr[at, hd:] += nn_dot(p_low, g_cat)
            return dq + nn_dot(kt_scr[:, at], ds_low)

        dq = lax.fori_loop(begin, stop, grads_step, jnp.zeros((hd, wide), jnp.float32)) * scaling
        for h in range(heads):
            piece = dq[:, h * Q_STEP : (h + 1) * Q_STEP]
            gqt_ref[h * hd : (h + 1) * hd, q_rows] = piece.astype(jnp.bfloat16)
            gq_ref[q_rows, h * hd : (h + 1) * hd] = piece.T.astype(jnp.bfloat16)

    def put(out, at):
        out[:, :hd] = (acc_scr[at, :hd] * scaling).astype(out.dtype)
        out[:, hd:] = acc_scr[at, hd:].astype(out.dtype)

    put(r_out, pl.ds(r_off, rows))
    put(x_out, pl.ds(x_off, rows))
    put(d2_out, slice(rows, 2 * rows))
    put(own_out, slice(3 * rows, 4 * rows))


def attention(index, lengths, q, g, own, d2, r, x):
    rows, width = q.shape
    both = own.shape[1]
    hd = both // 2
    wide = width // hd * Q_STEP
    vmem = pl.BlockSpec(memory_space=pltpu.VMEM)
    smem = pl.BlockSpec(memory_space=pltpu.SMEM)
    return pl.pallas_call(
        attention_kernel,
        name="attention",
        out_shape=(
            jax.ShapeDtypeStruct((rows, width), jnp.bfloat16),
            jax.ShapeDtypeStruct((width, rows), jnp.bfloat16),
            jax.ShapeDtypeStruct((rows, both), jnp.float32),
            jax.ShapeDtypeStruct((rows, both), jnp.float32),
            jax.ShapeDtypeStruct((rows, both), jnp.float32),
            jax.ShapeDtypeStruct((rows, both), jnp.bfloat16),
        ),
        in_specs=[smem, smem] + [vmem] * 6,
        out_specs=[vmem] * 6,
        scratch_shapes=[
            pltpu.VMEM((4 * rows, both), jnp.bfloat16),
            pltpu.VMEM((hd, 4 * rows), jnp.bfloat16),
            pltpu.VMEM((4 * rows, wide), jnp.float32),
            pltpu.VMEM((4 * rows, wide), jnp.float32),
            pltpu.VMEM((4 * rows, both), jnp.float32),
        ],
        compiler_params=pltpu.CompilerParams(vmem_limit_bytes=40 * 2**20),
        cost_estimate=pl.CostEstimate(flops=6 * 10**9, bytes_accessed=6 * 2**20, transcendentals=4 * 2**20),
    )(index, lengths, q, g, own, d2, r, x)


def weight_kernel(places, gt_ref, gt_other, x_ref, x_other, own_out, *outs):
    k = pl.program_id(0)
    total = nn_dot(gt_ref[...], x_ref[...]) + nn_dot(gt_other[...], x_other[...])

    @pl.when(k == 0)
    def _():
        own_out[...] = total

    for turn, out in enumerate(outs):
        @pl.when(k == turn + 1)
        def _(out=out):
            out[...] = total.astype(out.dtype)


def weight_partials(places, gt, gt_other, x, x_other, block):
    cols, rows = gt.shape
    chips = x_other.shape[1] // block
    whole = lambda k, s: (0, 0)
    return pl.pallas_call(
        weight_kernel,
        name="weight_partials",
        out_shape=[jax.ShapeDtypeStruct((cols, block), jnp.float32)]
        + [jax.ShapeDtypeStruct((cols, block), jnp.bfloat16)] * (chips - 1),
        grid_spec=pltpu.PrefetchScalarGridSpec(
            num_scalar_prefetch=1,
            grid=(chips,),
            in_specs=[
                pl.BlockSpec((cols, rows), whole),
                pl.BlockSpec((cols, rows), whole),
                pl.BlockSpec((rows, block), lambda k, s: (0, (s[0] ^ k) * 2 + s[1])),
                pl.BlockSpec((rows, block), lambda k, s: (0, s[0] ^ k)),
            ],
            out_specs=[pl.BlockSpec((cols, block), whole)] * chips,
        ),
        compiler_params=pltpu.CompilerParams(vmem_limit_bytes=40 * 2**20),
        cost_estimate=pl.CostEstimate(
            flops=4 * cols * rows * block * chips, bytes_accessed=8 * 2**20, transcendentals=0
        ),
    )(places, gt, gt_other, x, x_other)


def input_kernel(places, gq_ref, gkv_ref, *refs):
    out_ref = refs[-1]
    k = pl.program_id(0)
    q_cols = gq_ref.shape[1]
    for turn, w_ref in enumerate(refs[:-1]):
        @pl.when(k == turn)
        def _(w_ref=w_ref):
            out_ref[...] = (
                nt_dot(gq_ref[...], w_ref[:, :q_cols]) + nt_dot(gkv_ref[...], w_ref[:, q_cols:])
            ).astype(out_ref.dtype)


def input_grad(places, gq, gkv, blocks):
    rows = gq.shape[0]
    block, cols = blocks[0].shape
    count = len(blocks)
    whole = lambda k, s: (0, 0)
    return pl.pallas_call(
        input_kernel,
        name="input_grad",
        out_shape=jax.ShapeDtypeStruct((rows, block * count), jnp.bfloat16),
        grid_spec=pltpu.PrefetchScalarGridSpec(
            num_scalar_prefetch=1,
            grid=(count,),
            in_specs=[pl.BlockSpec(gq.shape, whole), pl.BlockSpec(gkv.shape, whole)]
            + [pl.BlockSpec((block, cols), whole)] * count,
            out_specs=pl.BlockSpec((rows, block), lambda k, s: (0, (s[0] * 2 + s[1]) ^ k)),
        ),
        compiler_params=pltpu.CompilerParams(vmem_limit_bytes=40 * 2**20),
        cost_estimate=pl.CostEstimate(
            flops=2 * rows * cols * block * count, bytes_accessed=11 * 2**20, transcendentals=0
        ),
    )(places, gq, gkv, *blocks)


def flipped(array, bits):
    size = lax.axis_size("ctx")
    return lax.ppermute(array, "ctx", [(i, i ^ bits) for i in range(size)])


def tree_sum(part):
    z = lax.axis_index("dp")
    first = lax.ppermute(part.astype(jnp.bfloat16), "dp", [(0, 1), (3, 2)])
    half = lax.optimization_barrier((part + first.astype(jnp.float32)).astype(jnp.bfloat16))
    other = lax.ppermute(half, "dp", [(1, 2), (2, 1)])
    full = (half.astype(jnp.float32) + other.astype(jnp.float32)).astype(jnp.bfloat16)
    back = lax.ppermute(full, "dp", [(1, 0), (2, 3)])
    return jnp.where((z == 1) | (z == 2), full, back)


def per_device(inputs, qkv_weight, queries, keys_values, out_grad, lengths):
    f32, bf16 = jnp.float32, jnp.bfloat16
    size = lax.axis_size("ctx")
    planes = lax.axis_size("dp")
    index = lax.axis_index("ctx")
    core = index % 2
    chip = index // 2
    rows = queries.shape[1]
    assert MOST == 3 * rows
    own = keys_values[0]
    by_two = [(i, i + 2) for i in range(size - 2)]
    mixed = [(i, i + 1) for i in range(0, size, 2)] + [(i, i + 3) for i in range(1, size - 3, 2)]
    back = lambda pairs: [(b, a) for a, b in pairs]
    small = size == 8 and planes == 4
    block = qkv_weight.shape[0]

    d2 = lax.ppermute(own, "ctx", by_two)
    x = lax.ppermute(own, "ctx", mixed)
    r = flipped(d2, 1)
    x_local = inputs[0]
    if small:
        x_pairs = x_local.reshape(rows, size // 2, 2, block)
        x_send = lax.dynamic_index_in_dim(x_pairs, 1 - core, 2, keepdims=False).reshape(rows, -1)
        x_other = flipped(x_send, 1)
        w_parts = [qkv_weight] + [flipped(qkv_weight, bits) for bits in (2, 4, 6)]
        w_other = [flipped(w, 1) for w in w_parts]
        w_blocks = [w for pair in zip(w_parts, w_other) for w in pair]
    else:
        w_full = lax.all_gather(qkv_weight, "ctx", axis=0, tiled=True)

    gq, gqt, kv_own, kv_d2, kv_r, kv_x = attention(
        index.reshape(1), lengths, queries[0], out_grad[0], own, d2, r, x
    )
    kv_d2 = (kv_d2 + flipped(kv_r, 1)).astype(bf16)
    from_two = lax.ppermute(kv_d2, "ctx", back(by_two))
    from_x = lax.ppermute(kv_x, "ctx", back(mixed))
    gkv = (kv_own + from_two.astype(f32) + from_x.astype(f32)).astype(bf16)

    if small:
        places = jnp.stack([chip, core])

        def reduced(gt):
            mine, *others = weight_partials(places, gt, flipped(gt, 1), x_local, x_other, block)
            for bits, other in zip((2, 4, 6), others):
                mine = mine + flipped(other, bits).astype(f32)
            return tree_sum(mine)

        weight_q = reduced(gqt)
        weight_kv = reduced(gkv.T)
        weight_sum = jnp.concatenate([weight_q, weight_kv], axis=0).T
        grad_in = input_grad(places, gq, gkv, w_blocks)
    else:
        grad_qkv = jnp.concatenate([gq, gkv], axis=1)
        grad_in = nt_dot(grad_qkv, w_full).astype(bf16)
        partial = lax.dot_general(
            x_local, grad_qkv, (((0,), (0,)), ((), ())), preferred_element_type=f32
        )
        shard = lax.psum_scatter(partial, "ctx", scatter_dimension=0, tiled=True)
        weight_sum = lax.psum(shard, "dp").astype(bf16)
    return (gq[None], gkv[None], grad_in[None], weight_sum)


def solution(mesh):
    placed = (
        P("dp", "ctx", None),
        P("ctx", None),
        P("dp", "ctx", None),
        P("dp", "ctx", None),
        P("dp", "ctx", None),
        P("dp", None),
    )
    return jax.shard_map(
        per_device,
        mesh=mesh,
        in_specs=placed,
        out_specs=(
            P("dp", "ctx", None),
            P("dp", "ctx", None),
            P("dp", "ctx", None),
            P("ctx", None),
        ),
        check_vma=False,
    )
```

time: 298 us -> 188 us (0.63)
  blocking collectives: 60.5 us -> 0 us
  matrix products: 49.8 us -> 0 us
  local copies, waits for them, and re-layouts: 7.23 us -> 42.3 us
  waiting for transfers between devices: 99.7 us -> 69.1 us
  Pallas kernels: 0 us -> 23 us
  between operations: 14.2 us -> 1 us
  other arithmetic: 15.2 us -> 7.63 us
  starting transfers between devices: 50.3 us -> 44.2 us
    reduce_scatter x1 -> x0, waiting for transfers between devices: 85.2 us -> none  [per_device(): lax.psum_scatter(lax.dot_general(x_local, grad_qkv, (((0,), (0,)), ((), (...]
    psum x1 -> x0, blocking collectives: 60.5 us -> none  [per_device(): weight_sum = lax.psum(shard_grad, 'dp').astype(jnp.bfloat16)]
    ppermute x10 -> x28, waiting for transfers between devices: 14.5 us -> 69.1 us  [the longest x18 47.7 us: flipped(): return lax.ppermute(array, 'ctx', [(i, i ^ bits) for i in range(size)])]
    dot_general x28 -> x0, matrix products: 49.8 us -> none  [the longest x7 14.6 us: score_terms(): jnp.einsum('thd,kd->htk', g_heads, values_part, preferred_element_type=jn...]
    pallas_call x0 -> x4, Pallas kernels: none -> 23 us  [the longest x1 9 us: input_grad(): pl.pallas_call(input_kernel, name='input_grad', out_shape=jax.ShapeDtypeS...]
    dynamic_slice x0 -> x1, local copies, waits for them, and re-layouts: none -> 14.6 us  [per_device(): lax.dynamic_index_in_dim(x_pairs, 1 - core, 2, keepdims=False)]
    unnamed x13 -> x47, local copies, waits for them, and re-layouts: 6 us -> 14.9 us
    another operation x1, local copies, waits for them, and re-layouts: 0.78 us -> 7.79 us  [per_device(): x_pairs = x_local.reshape(rows, size // 2, 2, block)]
  transfers between devices with their start and end apart: 12 -> 28, of which waited for: 8 -> 9; matrix products, arithmetic and copies ran while one was open for 24% -> 20% of each run, Pallas kernels for 0% -> 12%
where the time goes in v1:
time: 188 us; the launch traced here: 187 us
  waiting for transfers between devices  69.1 us (37%)
  starting transfers between devices  44.2 us (24%)
  local copies, waits for them, and re-layouts  42.3 us (22%)
  Pallas kernels  23 us (12%)
  other arithmetic  7.63 us (4%)
    ppermute x18, waiting for transfers between devices, flipped(): return lax.ppermute(array, 'ctx', [(i, i ^ bits) for i in range(size)])  47.7 us
    ppermute x18, starting transfers between devices, flipped(): return lax.ppermute(array, 'ctx', [(i, i ^ bits) for i in range(size)])  23.3 us
    unnamed x47, local copies, waits for them, and re-layouts  14.9 us
    dynamic_slice x1, local copies, waits for them, and re-layouts, per_device(): lax.dynamic_index_in_dim(x_pairs, 1 - core, 2, keepdims=False)  14.6 us
    ppermute x1, waiting for transfers between devices, per_device(): from_two = lax.ppermute(kv_d2, 'ctx', back(by_two))  10.7 us
    pallas_call x1, Pallas kernels, input_grad(): pl.pallas_call(input_kernel, name='input_grad', out_shape=jax.ShapeDtypeS...  9 us
    another operation x1, local copies, waits for them, and re-layouts, per_device(): x_pairs = x_local.reshape(rows, size // 2, 2, block)  7.79 us
    ppermute x2, starting transfers between devices, tree_sum(): first = lax.ppermute(part.astype(jnp.bfloat16), 'dp', [(0, 1), (3, 2)])  7.31 us
  transfers between devices with their start and end apart: 28, of which 9 were waited for; matrix products, arithmetic and copies ran while one was open for 20% of the time, Pallas kernels for 12%

profile of v1, /device:TPU:0, one launch (start us, length us, event | category | flops | bytes accessed | tf_op | source)
XLA Modules:
  0.0 187.2 jit_solution(12792193820055776581)
XLA Ops:
  0.6 4.9 %collective-permute-start = (bf16[512,256]{1,0:T(8,128)(2,1)}, bf16[512,256]{1,0:T(8,128)(2,1)S(1)}, u32[]{:S(2)}, u32[]{:S(2)}) collective-permute-start(bf16[512,256]{1,0:T(8,128)(2,1)} %bitcast.22), channel_id=1, source_target_pairs={{0,2},{1,3},{2,4},{3,5},{4,6},{5,7},{8,10},{9,11},{10,12},{11,13},... | collective-permute-start | bytes 786440 | tf_op jit(solution)/shard_map/ppermute | solution.py:257
  5.5 1.5 collective-permute-start.2
  7.0 7.8 %reshape_squeeze.3 = bf16[512,4,2,512]{3,2,1,0:T(2,128)(2,1)} reshape(bf16[1,512,4096]{2,1,0:T(8,128)(2,1)} %param.6) | data formatting | bytes 8388608 | tf_op jit(solution)/shard_map/reshape;squeeze | solution.py:262
  14.8 2.1 %collective-permute-start.1 = (bf16[512,256]{1,0:T(8,128)(2,1)S(1)}, bf16[512,256]{1,0:T(8,128)(2,1)S(1)}, u32[]{:S(2)}, u32[]{:S(2)}) collective-permute-start(bf16[512,256]{1,0:T(8,128)(2,1)S(1)} %collective-permute-done.d2_ref), channel_id=1, source_target_pairs={{0,1},{1,0},{2,3},{3,2},{4,5},{5,4},{6,7},{7,6},{8,9},{9,8},{10,11... | collective-permute-start | bytes 786440 | tf_op jit(solution)/shard_map/ppermute | solution.py:228
  16.9 14.6 %dynamic-slice_reduce_fusion = bf16[512,4,512]{2,1,0:T(4,128)(2,1)S(1)} fusion(bf16[512,4,2,512]{3,2,1,0:T(2,128)(2,1)} %reshape_squeeze.3, s32[]{:T(128)S(6)} %select_n.34), kind=kLoop, calls=%fused_computation | loop fusion | bytes 4194308 | tf_op jit(solution)/shard_map/jit(dynamic_index_in_dim)/dynamic_slice | solution.py:263
  31.5 2.0 %copy.19 = bf16[64,8,4,512]{3,1,2,0:T(8,128)(2,1)} copy(bf16[64,8,4,512]{3,2,1,0:T(4,128)(2,1)S(1)} %bitcast.26) | data formatting | bytes 4194304
  33.5 0.7 copy-done.16
  34.2 0.9 copy-done.17
  35.2 7.1 %attention.1 = (bf16[512,512]{1,0:T(8,128)(2,1)}, bf16[512,512]{1,0:T(8,128)(2,1)S(1)}, f32[512,256]{1,0:T(8,128)S(1)}, f32[512,256]{1,0:T(8,128)S(1)}, f32[512,...) custom-call(s32[1]{0:T(128)} %bitcast.idx_ref, s32[1,16]{1,0:T(1,128)S(1)} %copy-done.18, bf16[512,512]{1,0:T(8,128)(2,1)S(1)} %bitcast.20, ...), custom_call_target="tpu_custom_call" | custom-call | flops 6000000000 | bytes 6291456 | tf_op jit(solution)/shard_map/attention/pallas_call | solution.py:125
  42.3 0.8 copy-done.1
  43.1 0.7 copy-done.2
  43.8 0.8 copy-done.11
  44.6 2.1 %copy.10 = f32[512,256]{0,1:T(8,128)} copy(f32[512,256]{1,0:T(8,128)} %copy-done.1) | data formatting | bytes 1048576 | tf_op jit(solution)/shard_map/attention/pallas_call | solution.py:125
  46.7 7.0 %collective-permute-start.3 = (f32[512,256]{0,1:T(8,128)}, f32[512,256]{0,1:T(8,128)}, u32[]{:S(2)}, u32[]{:S(2)}) collective-permute-start(f32[512,256]{0,1:T(8,128)} %copy.10), channel_id=1, source_target_pairs={{0,1},{1,0},{2,3},{3,2},{4,5},{5,4},{6,7},{7,6},{8,9},{9,8},{10,11... | collective-permute-start | bytes 1572872 | tf_op jit(solution)/shard_map/ppermute | solution.py:228
  53.7 1.0 copy.11
  54.7 0.8 copy.13
  55.5 1.3 collective-permute-start.5
  56.8 2.0 %add_convert_fusion.5 = bf16[512,256]{0,1:T(8,128)(2,1)} fusion(f32[512,256]{0,1:T(8,128)} %copy.11, f32[512,256]{0,1:T(8,128)} %collective-permute-done.3), kind=kLoop, calls=%fused_computation.9 | loop fusion | flops 262144 | bytes 1310720 | tf_op jit(solution)/shard_map/convert_element_type | solution.py:274
  58.8 1.3 collective-permute-start.4
  60.1 1.2 collective-permute-start.13
  61.2 1.0 copy.12
  62.2 0.7 copy-done.21
  63.0 10.7 %collective-permute-done.4 = bf16[512,256]{0,1:T(8,128)(2,1)} collective-permute-done((bf16[512,256]{0,1:T(8,128)(2,1)}, bf16[512,256]{0,1:T(8,128)(2,1)}, u32[]{:S(2)}, u32[]{:S(2)}) %collective-permute-start.4) | collective-permute-done | bytes 262176 | tf_op jit(solution)/shard_map/ppermute | solution.py:275
  73.7 1.3 add_convert_fusion.4
  75.0 0.3 collective-permute-start.21
  75.3 1.3 collective-permute-done.21.gt_other
  76.6 2.2 %copy-done = bf16[1,512,4096]{2,1,0:T(8,128)(2,1)S(1)} copy-done((bf16[1,512,4096]{2,1,0:T(8,128)(2,1)S(1)}, bf16[1,512,4096]{2,1,0:T(8,128)(2,1)}, u32[]{:S(2)}) %copy-start) | copy-done | bytes 4194328
  78.8 2.8 %weight_partials.3 = (f32[256,512]{1,0:T(8,128)S(1)}, bf16[256,512]{1,0:T(8,128)(2,1)S(1)}, bf16[256,512]{1,0:T(8,128)(2,1)S(1)}, bf16[256,512]{1,0:T(8,128)(2,1)S(1)}) custom-call(s32[2]{0:T(128)S(1)} %pad_add_fusion.places, bf16[256,512]{1,0:T(8,128)(2,1)S(1)} %bitcast.18, bf16[256,512]{1,0:T(8,128)(2,1)S(1)} %collective-permute-done.21.gt_other, ...), custom_call_target="tpu_custom_call" | custom-call | flops 1073741824 | bytes 8388608 | tf_op jit(solution)/shard_map/weight_partials/pallas_call | solution.py:168
  81.6 3.2 %collective-permute-start.22 = (bf16[256,512]{1,0:T(8,128)(2,1)S(1)}, bf16[256,512]{1,0:T(8,128)(2,1)S(1)}, u32[]{:S(2)}, u32[]{:S(2)}) collective-permute-start(bf16[256,512]{1,0:T(8,128)(2,1)S(1)} %get-tuple-element.29), channel_id=1, source_target_pairs={{0,2},{1,3},{2,0},{3,1},{4,6},{5,7},{6,4},{7,5},{8,10},{9,11},{10,... | collective-permute-start | bytes 786440 | tf_op jit(solution)/shard_map/ppermute | solution.py:228
  84.8 1.5 collective-permute-start.24
  86.3 4.0 %weight_partials.2 = (f32[512,512]{1,0:T(8,128)S(1)}, bf16[512,512]{1,0:T(8,128)(2,1)S(1)}, bf16[512,512]{1,0:T(8,128)(2,1)S(1)}, bf16[512,512]{1,0:T(8,128)(2,1)S(1)}) custom-call(s32[2]{0:T(128)S(1)} %pad_add_fusion.places, bf16[512,512]{1,0:T(8,128)(2,1)S(1)} %copy-done.12, bf16[512,512]{1,0:T(8,128)(2,1)S(1)} %collective-permute-done.13.gt_other, ...), custom_call_target="tpu_custom_call" | custom-call | flops 2147483648 | bytes 8388608 | tf_op jit(solution)/shard_map/weight_partials/pallas_call | solution.py:168
  90.3 2.0 %collective-permute-start.15 = (bf16[512,512]{1,0:T(8,128)(2,1)S(1)}, bf16[512,512]{1,0:T(8,128)(2,1)S(1)}, u32[]{:S(2)}, u32[]{:S(2)}) collective-permute-start(bf16[512,512]{1,0:T(8,128)(2,1)S(1)} %get-tuple-element.25), channel_id=1, source_target_pairs={{0,2},{1,3},{2,0},{3,1},{4,6},{5,7},{6,4},{7,5},{8,10},{9,11},{10,... | collective-permute-start | bytes 1572872 | tf_op jit(solution)/shard_map/ppermute | solution.py:228
  92.4 1.5 collective-permute-start.17
  93.9 5.7 %collective-permute-done.23 = bf16[256,512]{1,0:T(8,128)(2,1)S(1)} collective-permute-done((bf16[256,512]{1,0:T(8,128)(2,1)S(1)}, bf16[256,512]{1,0:T(8,128)(2,1)S(1)}, u32[]{:S(2)}, u32[]{:S(2)}) %collective-permute-start.23) | collective-permute-done | bytes 262176 | tf_op jit(solution)/shard_map/ppermute | solution.py:228
  99.6 0.1 fusion.1
  99.7 3.6 %collective-permute-start.25 = (bf16[256,512]{1,0:T(8,128)(2,1)S(1)}, bf16[256,512]{1,0:T(8,128)(2,1)S(1)}, u32[]{:S(2)}, u32[]{:S(2)}) collective-permute-start(bf16[256,512]{1,0:T(8,128)(2,1)S(1)} %fusion.1), channel_id=1, source_target_pairs={{0,8},{24,16},{1,9},{25,17},{2,10},{26,18},{3,11},{27,19},{4,12},{... | collective-permute-start | bytes 786440 | tf_op jit(solution)/shard_map/ppermute | solution.py:233
  103.4 5.4 %collective-permute-done.15 = bf16[512,512]{1,0:T(8,128)(2,1)S(1)} collective-permute-done((bf16[512,512]{1,0:T(8,128)(2,1)S(1)}, bf16[512,512]{1,0:T(8,128)(2,1)S(1)}, u32[]{:S(2)}, u32[]{:S(2)}) %collective-permute-start.15) | collective-permute-done | bytes 524320 | tf_op jit(solution)/shard_map/ppermute | solution.py:228
  108.8 12.2 %collective-permute-done.16 = bf16[512,512]{1,0:T(8,128)(2,1)S(1)} collective-permute-done((bf16[512,512]{1,0:T(8,128)(2,1)S(1)}, bf16[512,512]{1,0:T(8,128)(2,1)S(1)}, u32[]{:S(2)}, u32[]{:S(2)}) %collective-permute-start.16) | collective-permute-done | bytes 524320 | tf_op jit(solution)/shard_map/ppermute | solution.py:228
  120.9 0.3 fusion
  121.2 3.7 %collective-permute-start.18 = (bf16[512,512]{1,0:T(8,128)(2,1)S(1)}, bf16[512,512]{1,0:T(8,128)(2,1)S(1)}, u32[]{:S(2)}, u32[]{:S(2)}) collective-permute-start(bf16[512,512]{1,0:T(8,128)(2,1)S(1)} %fusion), channel_id=1, source_target_pairs={{0,8},{24,16},{1,9},{25,17},{2,10},{26,18},{3,11},{27,19},{4,12},{... | collective-permute-start | bytes 1572872 | tf_op jit(solution)/shard_map/ppermute | solution.py:233
  124.9 0.3 collective-permute-start.9
  125.3 1.5 collective-permute-start.11
  126.8 1.7 collective-permute-start.7
  128.5 0.2 add_convert_fusion.3
  128.7 0.7 collective-permute-start.26
  129.4 5.7 %collective-permute-done.18 = bf16[512,512]{1,0:T(8,128)(2,1)S(1)} collective-permute-done((bf16[512,512]{1,0:T(8,128)(2,1)S(1)}, bf16[512,512]{1,0:T(8,128)(2,1)S(1)}, u32[]{:S(2)}, u32[]{:S(2)}) %collective-permute-start.18) | collective-permute-done | bytes 524320 | tf_op jit(solution)/shard_map/ppermute | solution.py:233
  135.0 1.2 add_convert_fusion.1
  136.2 1.5 collective-permute-start.19
  137.7 22.3 %collective-permute-done.9.refs_4_ = bf16[512,768]{1,0:T(8,128)(2,1)S(1)} collective-permute-done((bf16[512,768]{1,0:T(8,128)(2,1)S(1)}, bf16[512,768]{1,0:T(8,128)(2,1)S(1)}, u32[]{:S(2)}, u32[]{:S(2)}) %collective-permute-start.9) | collective-permute-done | bytes 786464 | tf_op jit(solution)/shard_map/ppermute | solution.py:228
  160.0 0.5 collective-permute-start.10
  160.5 0.8 collective-permute-done.7.refs_2_
  161.3 0.7 copy-done.20
  162.1 0.5 collective-permute-start.8
  162.7 0.8 copy.16
  163.5 1.0 add_convert_fusion.2
  164.6 1.3 collective-permute-start.27
  165.9 1.3 add_convert_fusion
  167.2 1.3 collective-permute-start.20
  168.6 1.1 copy-done.6
  169.7 1.1 copy-done.8
  170.9 1.0 copy-done.19
  171.9 9.0 %input_grad.1 = bf16[512,4096]{1,0:T(8,128)(2,1)} custom-call(s32[2]{0:T(128)S(1)} %pad_add_fusion.places, bf16[512,512]{1,0:T(8,128)(2,1)S(1)} %copy-done.19, bf16[512,256]{1,0:T(8,128)(2,1)S(1)} %copy.14.gkv_ref, bf16[512,768]{1,0:T(8,128)(2,1)S(1)} %copy-done.4, bf16[512,768]{1,0:T(8,128)(2,1)} %collective-permute-done.6.refs_1_, ...), custom_call_target="tpu_custom_call" | custom-call | flops 3221225472 | bytes 11534336 | tf_op jit(solution)/shard_map/input_grad/pallas_call | solution.py:208
  180.9 5.0 %collective-permute-done.20 = bf16[512,512]{1,0:T(8,128)(2,1)S(1)} collective-permute-done((bf16[512,512]{1,0:T(8,128)(2,1)S(1)}, bf16[512,512]{1,0:T(8,128)(2,1)S(1)}, u32[]{:S(2)}, u32[]{:S(2)}) %collective-permute-start.20) | collective-permute-done | bytes 524320 | tf_op jit(solution)/shard_map/ppermute | solution.py:237
  186.0 1.2 copy.17
  (62 shorter events, 0.5 us)
Async XLA Ops:
  0.6 14.2 %collective-permute-start = (bf16[512,256]{1,0:T(8,128)(2,1)}, bf16[512,256]{1,0:T(8,128)(2,1)S(1)}, u32[]{:S(2)}, u32[]{:S(2)}) collective-permute-start(bf16[512,256]{1,0:T(8,128)(2,1)} %bitcast.22), channel_id=1, source_target_pairs={{0,2},{1,3},{2,4},{3,5},{4,6},{5,7},{8,10},{9,11},{10,12},{11,13},... | collective-permute-start | bytes 786440 | tf_op jit(solution)/shard_map/ppermute | solution.py:257
  5.5 28.0 %collective-permute-start.2 = (bf16[512,256]{1,0:T(8,128)(2,1)}, bf16[512,256]{1,0:T(8,128)(2,1)S(1)}, u32[]{:S(2)}, u32[]{:S(2)}) collective-permute-start(bf16[512,256]{1,0:T(8,128)(2,1)} %bitcast.23), channel_id=1, source_target_pairs={{0,1},{2,3},{4,5},{6,7},{1,4},{3,6},{8,9},{10,11},{12,13},{14,15},... | collective-permute-start | bytes 786440 | tf_op jit(solution)/shard_map/ppermute | solution.py:258
  14.8 16.6 %copy-start.14 = (bf16[512,256]{1,0:T(8,128)(2,1)}, bf16[512,256]{1,0:T(8,128)(2,1)S(1)}, u32[]{:S(2)}) copy-start(bf16[512,256]{1,0:T(8,128)(2,1)S(1)} %collective-permute-done.d2_ref) | copy-start | bytes 786436
  14.8 19.4 %collective-permute-start.1 = (bf16[512,256]{1,0:T(8,128)(2,1)S(1)}, bf16[512,256]{1,0:T(8,128)(2,1)S(1)}, u32[]{:S(2)}, u32[]{:S(2)}) collective-permute-start(bf16[512,256]{1,0:T(8,128)(2,1)S(1)} %collective-permute-done.d2_ref), channel_id=1, source_target_pairs={{0,1},{1,0},{2,3},{3,2},{4,5},{5,4},{6,7},{7,6},{8,9},{9,8},{10,11... | collective-permute-start | bytes 786440 | tf_op jit(solution)/shard_map/ppermute | solution.py:228
  31.4 2.7 %copy-start.9 = (bf16[1,512,512]{2,1,0:T(8,128)(2,1)S(1)}, bf16[1,512,512]{2,1,0:T(8,128)(2,1)}, u32[]{:S(2)}) copy-start(bf16[1,512,512]{2,1,0:T(8,128)(2,1)} %param.8) | copy-start | bytes 1572868
  31.5 2.7 %copy-start.10 = (bf16[1,512,512]{2,1,0:T(8,128)(2,1)S(1)}, bf16[1,512,512]{2,1,0:T(8,128)(2,1)}, u32[]{:S(2)}) copy-start(bf16[1,512,512]{2,1,0:T(8,128)(2,1)} %param.10) | copy-start | bytes 1572868
  31.5 2.7 %copy-start.13 = (bf16[1,512,256]{2,1,0:T(8,128)(2,1)S(1)}, bf16[1,512,256]{2,1,0:T(8,128)(2,1)}, u32[]{:S(2)}) copy-start(bf16[1,512,256]{2,1,0:T(8,128)(2,1)} %param.9) | copy-start | bytes 786436
  31.5 2.7 %copy-start.15 = (bf16[512,256]{1,0:T(8,128)(2,1)S(1)}, bf16[512,256]{1,0:T(8,128)(2,1)}, u32[]{:S(2)}) copy-start(bf16[512,256]{1,0:T(8,128)(2,1)} %copy-done.14) | copy-start | bytes 786436
  31.5 2.7 %copy-start.18 = (s32[1,16]{1,0:T(1,128)S(1)}, s32[1,16]{1,0:T(1,128)}, u32[]{:S(2)}) copy-start(s32[1,16]{1,0:T(1,128)} %len_ref.1) | copy-start | bytes 196
  33.5 43.1 %collective-permute-start.14 = (bf16[512,2048]{1,0:T(8,128)(2,1)}, bf16[512,2048]{1,0:T(8,128)(2,1)S(1)}, u32[]{:S(2)}, u32[]{:S(2)}) collective-permute-start(bf16[512,2048]{1,0:T(8,128)(2,1)} %bitcast.13), channel_id=1, source_target_pairs={{0,1},{1,0},{2,3},{3,2},{4,5},{5,4},{6,7},{7,6},{8,9},{9,8},{10,11... | collective-permute-start | bytes 6291464 | tf_op jit(solution)/shard_map/ppermute | solution.py:228
  33.5 0.7 copy-start.16
  34.2 1.0 copy-start.17
  42.3 0.8 copy-start.1
  43.1 0.7 copy-start.2
  43.8 0.8 copy-start.11
  44.6 10.1 %copy-start.3 = (bf16[512,256]{1,0:T(8,128)(2,1)S(1)}, bf16[512,256]{1,0:T(8,128)(2,1)}, u32[]{:S(2)}) copy-start(bf16[512,256]{1,0:T(8,128)(2,1)} %copy-done.2) | copy-start | bytes 786436
  46.7 10.1 %collective-permute-start.3 = (f32[512,256]{0,1:T(8,128)}, f32[512,256]{0,1:T(8,128)}, u32[]{:S(2)}, u32[]{:S(2)}) collective-permute-start(f32[512,256]{0,1:T(8,128)} %copy.10), channel_id=1, source_target_pairs={{0,1},{1,0},{2,3},{3,2},{4,5},{5,4},{6,7},{7,6},{8,9},{9,8},{10,11... | collective-permute-start | bytes 1572872 | tf_op jit(solution)/shard_map/ppermute | solution.py:228
  55.5 6.7 %collective-permute-start.5 = (bf16[512,256]{0,1:T(8,128)(2,1)}, bf16[512,256]{0,1:T(8,128)(2,1)S(1)}, u32[]{:S(2)}, u32[]{:S(2)}) collective-permute-start(bf16[512,256]{0,1:T(8,128)(2,1)} %copy.13), channel_id=1, source_target_pairs={{1,0},{3,2},{5,4},{7,6},{4,1},{6,3},{9,8},{11,10},{13,12},{15,14},... | collective-permute-start | bytes 786440 | tf_op jit(solution)/shard_map/ppermute | solution.py:276
  58.8 14.9 %collective-permute-start.4 = (bf16[512,256]{0,1:T(8,128)(2,1)}, bf16[512,256]{0,1:T(8,128)(2,1)}, u32[]{:S(2)}, u32[]{:S(2)}) collective-permute-start(bf16[512,256]{0,1:T(8,128)(2,1)} %add_convert_fusion.5), channel_id=1, source_target_pairs={{2,0},{3,1},{4,2},{5,3},{6,4},{7,5},{10,8},{11,9},{12,10},{13,11},... | collective-permute-start | bytes 786440 | tf_op jit(solution)/shard_map/ppermute | solution.py:275
  60.1 26.3 %collective-permute-start.13 = (bf16[512,512]{1,0:T(8,128)(2,1)}, bf16[512,512]{1,0:T(8,128)(2,1)S(1)}, u32[]{:S(2)}, u32[]{:S(2)}) collective-permute-start(bf16[512,512]{1,0:T(8,128)(2,1)} %copy-done.11), channel_id=1, source_target_pairs={{0,1},{1,0},{2,3},{3,2},{4,5},{5,4},{6,7},{7,6},{8,9},{9,8},{10,11... | collective-permute-start | bytes 1572872 | tf_op jit(solution)/shard_map/ppermute | solution.py:228
  62.2 0.7 copy-start.21
  75.0 1.6 collective-permute-start.21
  76.6 2.2 %copy-start = (bf16[1,512,4096]{2,1,0:T(8,128)(2,1)S(1)}, bf16[1,512,4096]{2,1,0:T(8,128)(2,1)}, u32[]{:S(2)}) copy-start(bf16[1,512,4096]{2,1,0:T(8,128)(2,1)} %param.6) | copy-start | bytes 12582916
  78.8 7.6 %copy-start.12 = (bf16[512,512]{1,0:T(8,128)(2,1)S(1)}, bf16[512,512]{1,0:T(8,128)(2,1)}, u32[]{:S(2)}) copy-start(bf16[512,512]{1,0:T(8,128)(2,1)} %copy-done.11) | copy-start | bytes 1572868
  81.6 10.8 %collective-permute-start.22 = (bf16[256,512]{1,0:T(8,128)(2,1)S(1)}, bf16[256,512]{1,0:T(8,128)(2,1)S(1)}, u32[]{:S(2)}, u32[]{:S(2)}) collective-permute-start(bf16[256,512]{1,0:T(8,128)(2,1)S(1)} %get-tuple-element.29), channel_id=1, source_target_pairs={{0,2},{1,3},{2,0},{3,1},{4,6},{5,7},{6,4},{7,5},{8,10},{9,11},{10,... | collective-permute-start | bytes 786440 | tf_op jit(solution)/shard_map/ppermute | solution.py:228
  84.8 14.8 %collective-permute-start.23 = (bf16[256,512]{1,0:T(8,128)(2,1)S(1)}, bf16[256,512]{1,0:T(8,128)(2,1)S(1)}, u32[]{:S(2)}, u32[]{:S(2)}) collective-permute-start(bf16[256,512]{1,0:T(8,128)(2,1)S(1)} %get-tuple-element.30), channel_id=1, source_target_pairs={{0,4},{1,5},{2,6},{3,7},{4,0},{5,1},{6,2},{7,3},{8,12},{9,13},{10,... | collective-permute-start | bytes 786440 | tf_op jit(solution)/shard_map/ppermute | solution.py:228
  84.8 14.8 %collective-permute-start.24 = (bf16[256,512]{1,0:T(8,128)(2,1)S(1)}, bf16[256,512]{1,0:T(8,128)(2,1)S(1)}, u32[]{:S(2)}, u32[]{:S(2)}) collective-permute-start(bf16[256,512]{1,0:T(8,128)(2,1)S(1)} %get-tuple-element.31), channel_id=1, source_target_pairs={{0,6},{1,7},{2,4},{3,5},{4,2},{5,3},{6,0},{7,1},{8,14},{9,15},{10,... | collective-permute-start | bytes 786440 | tf_op jit(solution)/shard_map/ppermute | solution.py:228
  90.3 18.4 %collective-permute-start.15 = (bf16[512,512]{1,0:T(8,128)(2,1)S(1)}, bf16[512,512]{1,0:T(8,128)(2,1)S(1)}, u32[]{:S(2)}, u32[]{:S(2)}) collective-permute-start(bf16[512,512]{1,0:T(8,128)(2,1)S(1)} %get-tuple-element.25), channel_id=1, source_target_pairs={{0,2},{1,3},{2,0},{3,1},{4,6},{5,7},{6,4},{7,5},{8,10},{9,11},{10,... | collective-permute-start | bytes 1572872 | tf_op jit(solution)/shard_map/ppermute | solution.py:228
  92.4 28.6 %collective-permute-start.16 = (bf16[512,512]{1,0:T(8,128)(2,1)S(1)}, bf16[512,512]{1,0:T(8,128)(2,1)S(1)}, u32[]{:S(2)}, u32[]{:S(2)}) collective-permute-start(bf16[512,512]{1,0:T(8,128)(2,1)S(1)} %get-tuple-element.26), channel_id=1, source_target_pairs={{0,4},{1,5},{2,6},{3,7},{4,0},{5,1},{6,2},{7,3},{8,12},{9,13},{10,... | collective-permute-start | bytes 1572872 | tf_op jit(solution)/shard_map/ppermute | solution.py:228
  92.4 28.6 %collective-permute-start.17 = (bf16[512,512]{1,0:T(8,128)(2,1)S(1)}, bf16[512,512]{1,0:T(8,128)(2,1)S(1)}, u32[]{:S(2)}, u32[]{:S(2)}) collective-permute-start(bf16[512,512]{1,0:T(8,128)(2,1)S(1)} %get-tuple-element.27), channel_id=1, source_target_pairs={{0,6},{1,7},{2,4},{3,5},{4,2},{5,3},{6,0},{7,1},{8,14},{9,15},{10,... | collective-permute-start | bytes 1572872 | tf_op jit(solution)/shard_map/ppermute | solution.py:228
  99.6 25.3 %copy-start.4 = (bf16[512,768]{1,0:T(8,128)(2,1)S(1)}, bf16[512,768]{1,0:T(8,128)(2,1)}, u32[]{:S(2)}) copy-start(bf16[512,768]{1,0:T(8,128)(2,1)} %refs_0_.1) | copy-start | bytes 2359300
  99.7 28.8 %collective-permute-start.25 = (bf16[256,512]{1,0:T(8,128)(2,1)S(1)}, bf16[256,512]{1,0:T(8,128)(2,1)S(1)}, u32[]{:S(2)}, u32[]{:S(2)}) collective-permute-start(bf16[256,512]{1,0:T(8,128)(2,1)S(1)} %fusion.1), channel_id=1, source_target_pairs={{0,8},{24,16},{1,9},{25,17},{2,10},{26,18},{3,11},{27,19},{4,12},{... | collective-permute-start | bytes 786440 | tf_op jit(solution)/shard_map/ppermute | solution.py:233
  121.2 13.8 %collective-permute-start.18 = (bf16[512,512]{1,0:T(8,128)(2,1)S(1)}, bf16[512,512]{1,0:T(8,128)(2,1)S(1)}, u32[]{:S(2)}, u32[]{:S(2)}) collective-permute-start(bf16[512,512]{1,0:T(8,128)(2,1)S(1)} %fusion), channel_id=1, source_target_pairs={{0,8},{24,16},{1,9},{25,17},{2,10},{26,18},{3,11},{27,19},{4,12},{... | collective-permute-start | bytes 1572872 | tf_op jit(solution)/shard_map/ppermute | solution.py:233
  124.9 35.1 %collective-permute-start.9 = (bf16[512,768]{1,0:T(8,128)(2,1)S(1)}, bf16[512,768]{1,0:T(8,128)(2,1)S(1)}, u32[]{:S(2)}, u32[]{:S(2)}) collective-permute-start(bf16[512,768]{1,0:T(8,128)(2,1)S(1)} %copy-done.4), channel_id=1, source_target_pairs={{0,4},{1,5},{2,6},{3,7},{4,0},{5,1},{6,2},{7,3},{8,12},{9,13},{10,... | collective-permute-start | bytes 2359304 | tf_op jit(solution)/shard_map/ppermute | solution.py:228
  125.3 34.7 %collective-permute-start.11 = (bf16[512,768]{1,0:T(8,128)(2,1)S(1)}, bf16[512,768]{1,0:T(8,128)(2,1)S(1)}, u32[]{:S(2)}, u32[]{:S(2)}) collective-permute-start(bf16[512,768]{1,0:T(8,128)(2,1)S(1)} %copy-done.4), channel_id=1, source_target_pairs={{0,6},{1,7},{2,4},{3,5},{4,2},{5,3},{6,0},{7,1},{8,14},{9,15},{10,... | collective-permute-start | bytes 2359304 | tf_op jit(solution)/shard_map/ppermute | solution.py:228
  126.8 34.5 %collective-permute-start.7 = (bf16[512,768]{1,0:T(8,128)(2,1)S(1)}, bf16[512,768]{1,0:T(8,128)(2,1)}, u32[]{:S(2)}, u32[]{:S(2)}) collective-permute-start(bf16[512,768]{1,0:T(8,128)(2,1)S(1)} %copy-done.4), channel_id=1, source_target_pairs={{0,2},{1,3},{2,0},{3,1},{4,6},{5,7},{6,4},{7,5},{8,10},{9,11},{10,... | collective-permute-start | bytes 2359304 | tf_op jit(solution)/shard_map/ppermute | solution.py:228
  128.7 32.7 %collective-permute-start.26 = (bf16[256,512]{1,0:T(8,128)(2,1)S(1)}, bf16[256,512]{1,0:T(8,128)(2,1)S(1)}, u32[]{:S(2)}, u32[]{:S(2)}) collective-permute-start(bf16[256,512]{1,0:T(8,128)(2,1)S(1)} %add_convert_fusion.3), channel_id=1, source_target_pairs={{8,16},{16,8},{9,17},{17,9},{10,18},{18,10},{11,19},{19,11},{12,20... | collective-permute-start | bytes 786440 | tf_op jit(solution)/shard_map/ppermute | solution.py:235
  136.2 28.4 %collective-permute-start.19 = (bf16[512,512]{1,0:T(8,128)(2,1)}, bf16[512,512]{1,0:T(8,128)(2,1)}, u32[]{:S(2)}, u32[]{:S(2)}) collective-permute-start(bf16[512,512]{1,0:T(8,128)(2,1)} %add_convert_fusion.1), channel_id=1, source_target_pairs={{8,16},{16,8},{9,17},{17,9},{10,18},{18,10},{11,19},{19,11},{12,20... | collective-permute-start | bytes 1572872 | tf_op jit(solution)/shard_map/ppermute | solution.py:235
  160.0 7.2 %copy-start.5 = (bf16[512,768]{1,0:T(8,128)(2,1)}, bf16[512,768]{1,0:T(8,128)(2,1)S(1)}, u32[]{:S(2)}) copy-start(bf16[512,768]{1,0:T(8,128)(2,1)S(1)} %collective-permute-done.9.refs_4_) | copy-start | bytes 2359300
  160.0 7.2 %collective-permute-start.6 = (bf16[512,768]{1,0:T(8,128)(2,1)S(1)}, bf16[512,768]{1,0:T(8,128)(2,1)}, u32[]{:S(2)}, u32[]{:S(2)}) collective-permute-start(bf16[512,768]{1,0:T(8,128)(2,1)S(1)} %copy-done.4), channel_id=1, source_target_pairs={{0,1},{1,0},{2,3},{3,2},{4,5},{5,4},{6,7},{7,6},{8,9},{9,8},{10,11... | collective-permute-start | bytes 2359304 | tf_op jit(solution)/shard_map/ppermute | solution.py:228
  160.0 8.6 %copy-start.7 = (bf16[512,768]{1,0:T(8,128)(2,1)}, bf16[512,768]{1,0:T(8,128)(2,1)S(1)}, u32[]{:S(2)}) copy-start(bf16[512,768]{1,0:T(8,128)(2,1)S(1)} %collective-permute-done.11.refs_6_) | copy-start | bytes 2359300
  160.0 8.5 %collective-permute-start.10 = (bf16[512,768]{1,0:T(8,128)(2,1)S(1)}, bf16[512,768]{1,0:T(8,128)(2,1)}, u32[]{:S(2)}, u32[]{:S(2)}) collective-permute-start(bf16[512,768]{1,0:T(8,128)(2,1)S(1)} %collective-permute-done.9.refs_4_), channel_id=1, source_target_pairs={{0,1},{1,0},{2,3},{3,2},{4,5},{5,4},{6,7},{7,6},{8,9},{9,8},{10,11... | collective-permute-start | bytes 2359304 | tf_op jit(solution)/shard_map/ppermute | solution.py:228
  161.3 7.2 %collective-permute-start.12 = (bf16[512,768]{1,0:T(8,128)(2,1)S(1)}, bf16[512,768]{1,0:T(8,128)(2,1)}, u32[]{:S(2)}, u32[]{:S(2)}) collective-permute-start(bf16[512,768]{1,0:T(8,128)(2,1)S(1)} %collective-permute-done.11.refs_6_), channel_id=1, source_target_pairs={{0,1},{1,0},{2,3},{3,2},{4,5},{5,4},{6,7},{7,6},{8,9},{9,8},{10,11... | collective-permute-start | bytes 2359304 | tf_op jit(solution)/shard_map/ppermute | solution.py:228
  161.3 0.7 copy-start.20
  162.1 6.5 %collective-permute-start.8 = (bf16[512,768]{1,0:T(8,128)(2,1)}, bf16[512,768]{1,0:T(8,128)(2,1)}, u32[]{:S(2)}, u32[]{:S(2)}) collective-permute-start(bf16[512,768]{1,0:T(8,128)(2,1)} %collective-permute-done.7.refs_2_), channel_id=1, source_target_pairs={{0,1},{1,0},{2,3},{3,2},{4,5},{5,4},{6,7},{7,6},{8,9},{9,8},{10,11... | collective-permute-start | bytes 2359304 | tf_op jit(solution)/shard_map/ppermute | solution.py:228
  164.6 16.3 %collective-permute-start.27 = (bf16[256,512]{1,0:T(8,128)(2,1)S(1)}, bf16[256,512]{1,0:T(8,128)(2,1)S(1)}, u32[]{:S(2)}, u32[]{:S(2)}) collective-permute-start(bf16[256,512]{1,0:T(8,128)(2,1)S(1)} %add_convert_fusion.2), channel_id=1, source_target_pairs={{8,0},{16,24},{9,1},{17,25},{10,2},{18,26},{11,3},{19,27},{12,4},{... | collective-permute-start | bytes 786440 | tf_op jit(solution)/shard_map/ppermute | solution.py:237
  167.2 18.7 %collective-permute-start.20 = (bf16[512,512]{1,0:T(8,128)(2,1)S(1)}, bf16[512,512]{1,0:T(8,128)(2,1)S(1)}, u32[]{:S(2)}, u32[]{:S(2)}) collective-permute-start(bf16[512,512]{1,0:T(8,128)(2,1)S(1)} %add_convert_fusion), channel_id=1, source_target_pairs={{8,0},{16,24},{9,1},{17,25},{10,2},{18,26},{11,3},{19,27},{12,4},{... | collective-permute-start | bytes 1572872 | tf_op jit(solution)/shard_map/ppermute | solution.py:237
  168.6 1.1 copy-start.6
  169.7 1.1 copy-start.8
  170.9 1.0 copy-start.19

commit v2 on v1

--- a/solution.py
+++ b/solution.py
@@ -142,8 +142,8 @@
             pltpu.VMEM((4 * rows, wide), jnp.float32),
             pltpu.VMEM((4 * rows, both), jnp.float32),
         ],
-        compiler_params=pltpu.CompilerParams(vmem_limit_bytes=40 * 2**20),
-        cost_estimate=pl.CostEstimate(flops=6 * 10**9, bytes_accessed=6 * 2**20, transcendentals=4 * 2**20),
+        compiler_params=pltpu.CompilerParams(vmem_limit_bytes=28 * 2**20),
+        cost_estimate=pl.CostEstimate(flops=12 * 10**9, bytes_accessed=6 * 2**20, transcendentals=4 * 2**20),
     )(index, lengths, q, g, own, d2, r, x)
 
 
@@ -163,7 +163,7 @@
 
 def weight_partials(places, gt, gt_other, x, x_other, block):
     cols, rows = gt.shape
-    chips = x_other.shape[1] // block
+    chips = x_other.shape[1] // block // 2
     whole = lambda k, s: (0, 0)
     return pl.pallas_call(
         weight_kernel,
@@ -177,7 +177,7 @@
                 pl.BlockSpec((cols, rows), whole),
                 pl.BlockSpec((cols, rows), whole),
                 pl.BlockSpec((rows, block), lambda k, s: (0, (s[0] ^ k) * 2 + s[1])),
-                pl.BlockSpec((rows, block), lambda k, s: (0, s[0] ^ k)),
+                pl.BlockSpec((rows, block), lambda k, s: (0, (s[0] ^ k) * 2 + s[1])),
             ],
             out_specs=[pl.BlockSpec((cols, block), whole)] * chips,
         ),
@@ -223,19 +223,89 @@
     )(places, gq, gkv, *blocks)
 
 
-def flipped(array, bits):
-    size = lax.axis_size("ctx")
-    return lax.ppermute(array, "ctx", [(i, i ^ bits) for i in range(size)])
-
-
-def tree_sum(part):
-    z = lax.axis_index("dp")
-    first = lax.ppermute(part.astype(jnp.bfloat16), "dp", [(0, 1), (3, 2)])
-    half = lax.optimization_barrier((part + first.astype(jnp.float32)).astype(jnp.bfloat16))
-    other = lax.ppermute(half, "dp", [(1, 2), (2, 1)])
-    full = (half.astype(jnp.float32) + other.astype(jnp.float32)).astype(jnp.bfloat16)
-    back = lax.ppermute(full, "dp", [(1, 0), (2, 3)])
-    return jnp.where((z == 1) | (z == 2), full, back)
+def finish_kernel(own_ref, two_ref, x_ref, out_ref, out_t_ref):
+    total = own_ref[...] + two_ref[...].astype(jnp.float32) + x_ref[...].astype(jnp.float32)
+    out_ref[...] = total.astype(out_ref.dtype)
+    out_t_ref[...] = total.T.astype(out_t_ref.dtype)
+
+
+def finish_kv(own, from_two, from_x):
+    rows, cols = own.shape
+    return pl.pallas_call(
+        finish_kernel,
+        name="finish_kv",
+        out_shape=(
+            jax.ShapeDtypeStruct((rows, cols), jnp.bfloat16),
+            jax.ShapeDtypeStruct((cols, rows), jnp.bfloat16),
+        ),
+        cost_estimate=pl.CostEstimate(flops=4 * rows * cols, bytes_accessed=2**21, transcendentals=0),
+    )(own, from_two, from_x)
+
+
+def quarters_kernel(z_ref, own_ref, a_ref, b_ref, c_ref, mine_out, *outs):
+    z = z_ref[0]
+    quarter = mine_out.shape[0]
+    for k, out in enumerate((mine_out, *outs)):
+        at = pl.ds(pl.multiple_of((z ^ k) * quarter, quarter), quarter)
+        total = own_ref[at, :]
+        for ref in (a_ref, b_ref, c_ref):
+            total = total + ref[at, :].astype(jnp.float32)
+        out[...] = total.astype(out.dtype)
+
+
+def quarters_of(z, own, others):
+    rows, cols = own.shape
+    piece = (rows // 4, cols)
+    vmem = pl.BlockSpec(own.shape, lambda i: (0, 0))
+    out = pl.BlockSpec(piece, lambda i: (0, 0))
+    return pl.pallas_call(
+        quarters_kernel,
+        name="quarters",
+        out_shape=[jax.ShapeDtypeStruct(piece, jnp.float32)] + [jax.ShapeDtypeStruct(piece, jnp.bfloat16)] * 3,
+        grid=(1,),
+        in_specs=[pl.BlockSpec(memory_space=pltpu.SMEM)] + [vmem] * 4,
+        out_specs=[out] * 4,
+        cost_estimate=pl.CostEstimate(flops=4 * rows * cols, bytes_accessed=2**21, transcendentals=0),
+    )(z, own, *others)
+
+
+def joined_kernel(z_ref, *refs):
+    z = z_ref[0]
+    count = (len(refs) - 2) // 4
+    out_ref, scr = refs[-2:]
+    start = 0
+    for part in range(count):
+        pieces = refs[4 * part : 4 * part + 4]
+        quarter = pieces[0].shape[0]
+        for k, piece in enumerate(pieces):
+            scr[pl.ds(pl.multiple_of(start + (z ^ k) * quarter, quarter), quarter), :] = piece[...]
+        start += 4 * quarter
+    out_ref[...] = scr[...].T
+
+
+def joined(z, parts):
+    pieces = [piece for part in parts for piece in part]
+    cols = pieces[0].shape[1]
+    rows = sum(piece.shape[0] for piece in pieces)
+    return pl.pallas_call(
+        joined_kernel,
+        name="joined",
+        out_shape=jax.ShapeDtypeStruct((cols, rows), jnp.bfloat16),
+        grid=(1,),
+        in_specs=[pl.BlockSpec(memory_space=pltpu.SMEM)]
+        + [pl.BlockSpec(piece.shape, lambda i: (0, 0)) for piece in pieces],
+        out_specs=pl.BlockSpec((cols, rows), lambda i: (0, 0)),
+        scratch_shapes=[pltpu.VMEM((rows, cols), jnp.bfloat16)],
+        cost_estimate=pl.CostEstimate(flops=rows * cols, bytes_accessed=2**21, transcendentals=0),
+    )(z, *pieces)
+
+
+def flipped(array, bits, axis="ctx"):
+    return lax.ppermute(array, axis, [(i, i ^ bits) for i in range(lax.axis_size(axis))])
+
+
+def tied(array, *after):
+    return lax.optimization_barrier((array, *after))[0]
 
 
 def per_device(inputs, qkv_weight, queries, keys_values, out_grad, lengths):
@@ -243,8 +313,6 @@
     size = lax.axis_size("ctx")
     planes = lax.axis_size("dp")
     index = lax.axis_index("ctx")
-    core = index % 2
-    chip = index // 2
     rows = queries.shape[1]
     assert MOST == 3 * rows
     own = keys_values[0]
@@ -253,18 +321,15 @@
     back = lambda pairs: [(b, a) for a, b in pairs]
     small = size == 8 and planes == 4
     block = qkv_weight.shape[0]
+    x_local = inputs[0]
 
     d2 = lax.ppermute(own, "ctx", by_two)
     x = lax.ppermute(own, "ctx", mixed)
     r = flipped(d2, 1)
-    x_local = inputs[0]
     if small:
-        x_pairs = x_local.reshape(rows, size // 2, 2, block)
-        x_send = lax.dynamic_index_in_dim(x_pairs, 1 - core, 2, keepdims=False).reshape(rows, -1)
-        x_other = flipped(x_send, 1)
-        w_parts = [qkv_weight] + [flipped(qkv_weight, bits) for bits in (2, 4, 6)]
-        w_other = [flipped(w, 1) for w in w_parts]
-        w_blocks = [w for pair in zip(w_parts, w_other) for w in pair]
+        w_own = tied(qkv_weight, d2, x)
+        w_parts = [w_own] + [flipped(w_own, bits) for bits in (2, 4, 6)]
+        x_other = flipped(tied(x_local, r), 1)
     else:
         w_full = lax.all_gather(qkv_weight, "ctx", axis=0, tiled=True)
 
@@ -274,20 +339,25 @@
     kv_d2 = (kv_d2 + flipped(kv_r, 1)).astype(bf16)
     from_two = lax.ppermute(kv_d2, "ctx", back(by_two))
     from_x = lax.ppermute(kv_x, "ctx", back(mixed))
-    gkv = (kv_own + from_two.astype(f32) + from_x.astype(f32)).astype(bf16)
+    gkv, gkvt = finish_kv(kv_own, from_two, from_x)
 
     if small:
-        places = jnp.stack([chip, core])
-
-        def reduced(gt):
-            mine, *others = weight_partials(places, gt, flipped(gt, 1), x_local, x_other, block)
-            for bits, other in zip((2, 4, 6), others):
-                mine = mine + flipped(other, bits).astype(f32)
-            return tree_sum(mine)
-
-        weight_q = reduced(gqt)
-        weight_kv = reduced(gkv.T)
-        weight_sum = jnp.concatenate([weight_q, weight_kv], axis=0).T
+        places = jnp.stack([index // 2, index % 2])
+        z = lax.axis_index("dp").reshape(1)
+
+        def reduced(gt, *after):
+            gt_other = tied(flipped(gt, 1), *after)
+            mine, *others = weight_partials(places, gt, gt_other, x_local, x_other, block)
+            others = [flipped(other, bits) for bits, other in zip((2, 4, 6), others)]
+            mine, *pieces = quarters_of(z, mine, others)
+            for k, piece in enumerate(pieces):
+                mine = mine + flipped(piece, k + 1, "dp").astype(f32)
+            mine = mine.astype(bf16)
+            return [mine] + [flipped(mine, k, "dp") for k in (1, 2, 3)]
+
+        parts = [reduced(gqt, *w_parts), reduced(gkvt)]
+        weight_sum = joined(z, parts)
+        w_blocks = [w for part in w_parts for w in (part, flipped(part, 1))]
         grad_in = input_grad(places, gq, gkv, w_blocks)
     else:
         grad_qkv = jnp.concatenate([gq, gkv], axis=1)

time: 188 us -> 209 us (1.11)
  local copies, waits for them, and re-layouts: 42.3 us -> 12.5 us
  waiting for transfers between devices: 69.1 us -> 98.7 us
  Pallas kernels: 23 us -> 36.6 us
  starting transfers between devices: 44.2 us -> 57.7 us
  other arithmetic: 7.63 us -> 2.1 us
    ppermute x24 -> x30, waiting for transfers between devices: 58.3 us -> 83.7 us  [flipped(): lax.ppermute(array, axis, [(i, i ^ bits) for i in range(lax.axis_size(axi...]
    dynamic_slice x1 -> x0, local copies, waits for them, and re-layouts: 14.6 us -> none  [per_device(): lax.dynamic_index_in_dim(x_pairs, 1 - core, 2, keepdims=False)]
    ppermute x24 -> x30, starting transfers between devices: 35.4 us -> 48 us  [flipped(): lax.ppermute(array, axis, [(i, i ^ bits) for i in range(lax.axis_size(axi...]
    pallas_call x0 -> x4, Pallas kernels: none -> 9.11 us  [the longest x2 4.66 us: quarters_of(): pl.pallas_call(quarters_kernel, name='quarters', out_shape=[jax.ShapeDtyp...]
    another operation x1 -> x0, local copies, waits for them, and re-layouts: 7.79 us -> none  [per_device(): x_pairs = x_local.reshape(rows, size // 2, 2, block)]
    ppermute x1, waiting for transfers between devices: 10.7 us -> 4.13 us  [per_device(): from_two = lax.ppermute(kv_d2, 'ctx', back(by_two))]
    ppermute x1, waiting for transfers between devices: 0.01 us -> 5.85 us  [per_device(): d2 = lax.ppermute(own, 'ctx', by_two)]
    ppermute x1, waiting for transfers between devices: 0.01 us -> 5.08 us  [per_device(): x = lax.ppermute(own, 'ctx', mixed)]
  transfers between devices with their start and end apart: 28 -> 34, of which waited for: 9 -> 13; matrix products, arithmetic and copies ran while one was open for 20% -> 1% of each run, Pallas kernels for 12% -> 14%
where the time goes in v2:
time: 209 us; the launch traced here: 208 us
  waiting for transfers between devices  98.7 us (47%)
  starting transfers between devices  57.7 us (28%)
  Pallas kernels  36.6 us (18%)
  local copies, waits for them, and re-layouts  12.5 us (6%)
  other arithmetic  2.1 us (1%)
    ppermute x30, waiting for transfers between devices, flipped(): lax.ppermute(array, axis, [(i, i ^ bits) for i in range(lax.axis_size(axi...  83.7 us
    ppermute x30, starting transfers between devices, flipped(): lax.ppermute(array, axis, [(i, i ^ bits) for i in range(lax.axis_size(axi...  48 us
    unnamed x52, local copies, waits for them, and re-layouts  12.5 us
    pallas_call x2, Pallas kernels, weight_partials(): pl.pallas_call(weight_kernel, name='weight_partials', out_shape=[jax.Shap...  11.5 us
    pallas_call x1, Pallas kernels, input_grad(): pl.pallas_call(input_kernel, name='input_grad', out_shape=jax.ShapeDtypeS...  9 us
    pallas_call x1, Pallas kernels, attention(): pl.pallas_call(attention_kernel, name='attention', out_shape=(jax.ShapeDt...  6.99 us
    ppermute x1, waiting for transfers between devices, per_device(): d2 = lax.ppermute(own, 'ctx', by_two)  5.85 us
    ppermute x1, waiting for transfers between devices, per_device(): x = lax.ppermute(own, 'ctx', mixed)  5.08 us
  transfers between devices with their start and end apart: 34, of which 13 were waited for; matrix products, arithmetic and copies ran while one was open for 1% of the time, Pallas kernels for 14%

profile of v2, /device:TPU:0, one launch (start us, length us, event | category | flops | bytes accessed | tf_op | source)
XLA Modules:
  0.0 208.5 jit_solution(16512909154206365835)
XLA Ops:
  0.6 4.9 %collective-permute-start = (bf16[512,256]{1,0:T(8,128)(2,1)}, bf16[512,256]{1,0:T(8,128)(2,1)S(1)}, u32[]{:S(2)}, u32[]{:S(2)}) collective-permute-start(bf16[512,256]{1,0:T(8,128)(2,1)} %bitcast.16), channel_id=1, source_target_pairs={{0,2},{1,3},{2,4},{3,5},{4,6},{5,7},{8,10},{9,11},{10,12},{11,13},... | collective-permute-start | bytes 786440 | tf_op jit(solution)/shard_map/ppermute | solution.py:326
  5.5 5.8 %collective-permute-done.d2_ref = bf16[512,256]{1,0:T(8,128)(2,1)S(1)} collective-permute-done((bf16[512,256]{1,0:T(8,128)(2,1)}, bf16[512,256]{1,0:T(8,128)(2,1)S(1)}, u32[]{:S(2)}, u32[]{:S(2)}) %collective-permute-start) | collective-permute-done | bytes 262176 | tf_op jit(solution)/shard_map/ppermute | solution.py:326
  11.3 1.5 collective-permute-done.1.r_ref
  12.9 0.1 collective-permute-start.14
  13.0 2.3 %collective-permute-start.2 = (bf16[512,256]{1,0:T(8,128)(2,1)}, bf16[512,256]{1,0:T(8,128)(2,1)S(1)}, u32[]{:S(2)}, u32[]{:S(2)}) collective-permute-start(bf16[512,256]{1,0:T(8,128)(2,1)} %bitcast.17), channel_id=1, source_target_pairs={{0,1},{2,3},{4,5},{6,7},{1,4},{3,6},{8,9},{10,11},{12,13},{14,15},... | collective-permute-start | bytes 786440 | tf_op jit(solution)/shard_map/ppermute | solution.py:327
  15.3 5.1 %collective-permute-done.2.x_ref = bf16[512,256]{1,0:T(8,128)(2,1)S(1)} collective-permute-done((bf16[512,256]{1,0:T(8,128)(2,1)}, bf16[512,256]{1,0:T(8,128)(2,1)S(1)}, u32[]{:S(2)}, u32[]{:S(2)}) %collective-permute-start.2) | collective-permute-done | bytes 262176 | tf_op jit(solution)/shard_map/ppermute | solution.py:327
  20.4 1.0 copy-done.7
  21.4 1.0 copy-done.8
  22.5 0.9 copy-done.9
  23.4 0.7 copy-done.11
  24.1 7.0 %attention.1 = (bf16[512,512]{1,0:T(8,128)(2,1)}, bf16[512,512]{1,0:T(8,128)(2,1)S(1)}, f32[512,256]{1,0:T(8,128)S(1)}, f32[512,256]{1,0:T(8,128)S(1)}, f32[512,...) custom-call(s32[1]{0:T(128)} %bitcast.idx_ref, s32[1,16]{1,0:T(1,128)S(1)} %copy-done.11, bf16[512,512]{1,0:T(8,128)(2,1)S(1)} %bitcast.14, ...), custom_call_target="tpu_custom_call" | custom-call | flops 12000000000 | bytes 6291456 | tf_op jit(solution)/shard_map/attention/pallas_call | solution.py:125
  31.1 7.8 %collective-permute-start.3 = (f32[512,256]{1,0:T(8,128)S(1)}, f32[512,256]{1,0:T(8,128)S(1)}, u32[]{:S(2)}, u32[]{:S(2)}) collective-permute-start(f32[512,256]{1,0:T(8,128)S(1)} %get-tuple-element.34), channel_id=1, source_target_pairs={{0,1},{1,0},{2,3},{3,2},{4,5},{5,4},{6,7},{7,6},{8,9},{9,8},{10,11... | collective-permute-start | bytes 1572872 | tf_op jit(solution)/shard_map/ppermute | solution.py:304
  38.9 1.3 collective-permute-start.5
  40.2 0.2 collective-permute-done.3
  40.5 0.1 add_convert_fusion
  40.5 1.3 collective-permute-start.4
  41.9 9.1 %collective-permute-start.11 = (bf16[512,768]{1,0:T(8,128)(2,1)S(1)}, bf16[512,768]{1,0:T(8,128)(2,1)S(1)}, u32[]{:S(2)}, u32[]{:S(2)}) collective-permute-start(bf16[512,768]{1,0:T(8,128)(2,1)S(1)} %copy-done.6), channel_id=1, source_target_pairs={{0,6},{1,7},{2,4},{3,5},{4,2},{5,3},{6,0},{7,1},{8,14},{9,15},{10,... | collective-permute-start | bytes 2359304 | tf_op jit(solution)/shard_map/ppermute | solution.py:304
  51.0 1.9 collective-permute-start.7
  52.9 4.1 %collective-permute-done.4.two_ref = bf16[512,256]{1,0:T(8,128)(2,1)S(1)} collective-permute-done((bf16[512,256]{1,0:T(8,128)(2,1)S(1)}, bf16[512,256]{1,0:T(8,128)(2,1)S(1)}, u32[]{:S(2)}, u32[]{:S(2)}) %collective-permute-start.4) | collective-permute-done | bytes 262176 | tf_op jit(solution)/shard_map/ppermute | solution.py:340
  57.1 0.7 copy-done.19
  57.8 2.1 %finish_kv.1 = (bf16[512,256]{1,0:T(8,128)(2,1)}, bf16[256,512]{1,0:T(8,128)(2,1)}) custom-call(f32[512,256]{1,0:T(8,128)} %copy-done.4, bf16[512,256]{1,0:T(8,128)(2,1)} %copy-done.19, bf16[512,256]{1,0:T(8,128)(2,1)} %copy-done.18), custom_call_target="tpu_custom_call" | custom-call | flops 524288 | bytes 2097152 | tf_op jit(solution)/shard_map/finish_kv/pallas_call | solution.py:234
  59.9 0.1 pad_add_fusion.places
  60.0 14.6 %collective-permute-done.11.refs_6_ = bf16[512,768]{1,0:T(8,128)(2,1)S(1)} collective-permute-done((bf16[512,768]{1,0:T(8,128)(2,1)S(1)}, bf16[512,768]{1,0:T(8,128)(2,1)S(1)}, u32[]{:S(2)}, u32[]{:S(2)}) %collective-permute-start.11) | collective-permute-done | bytes 786464 | tf_op jit(solution)/shard_map/ppermute | solution.py:304
  74.5 16.2 %collective-permute-done.7.refs_2_ = bf16[512,768]{1,0:T(8,128)(2,1)} collective-permute-done((bf16[512,768]{1,0:T(8,128)(2,1)S(1)}, bf16[512,768]{1,0:T(8,128)(2,1)}, u32[]{:S(2)}, u32[]{:S(2)}) %collective-permute-start.7) | collective-permute-done | bytes 786464 | tf_op jit(solution)/shard_map/ppermute | solution.py:304
  90.8 2.2 %copy-done = bf16[1,512,4096]{2,1,0:T(8,128)(2,1)S(1)} copy-done((bf16[1,512,4096]{2,1,0:T(8,128)(2,1)S(1)}, bf16[1,512,4096]{2,1,0:T(8,128)(2,1)}, u32[]{:S(2)}) %copy-start) | copy-done | bytes 4194328
  93.0 0.9 copy-done.5
  93.9 5.3 %weight_partials.3 = (f32[256,512]{1,0:T(8,128)S(1)}, bf16[256,512]{1,0:T(8,128)(2,1)S(1)}, bf16[256,512]{1,0:T(8,128)(2,1)}, bf16[256,512]{1,0:T(8,128)(2,1)}) custom-call(s32[2]{0:T(128)S(1)} %pad_add_fusion.places, bf16[256,512]{1,0:T(8,128)(2,1)S(1)} %copy-done.5, bf16[256,512]{1,0:T(8,128)(2,1)S(1)} %collective-permute-done.24.gt_other, ...), custom_call_target="tpu_custom_call" | custom-call | flops 1073741824 | bytes 8388608 | tf_op jit(solution)/shard_map/weight_partials/pallas_call | solution.py:168
  99.3 0.8 copy-done.3
  100.1 3.4 %collective-permute-start.25 = (bf16[256,512]{1,0:T(8,128)(2,1)S(1)}, bf16[256,512]{1,0:T(8,128)(2,1)S(1)}, u32[]{:S(2)}, u32[]{:S(2)}) collective-permute-start(bf16[256,512]{1,0:T(8,128)(2,1)S(1)} %get-tuple-element.51), channel_id=1, source_target_pairs={{0,2},{1,3},{2,0},{3,1},{4,6},{5,7},{6,4},{7,5},{8,10},{9,11},{10,... | collective-permute-start | bytes 786440 | tf_op jit(solution)/shard_map/ppermute | solution.py:304
  103.5 6.1 %weight_partials.2 = (f32[512,512]{1,0:T(8,128)S(1)}, bf16[512,512]{1,0:T(8,128)(2,1)}, bf16[512,512]{1,0:T(8,128)(2,1)}, bf16[512,512]{1,0:T(8,128)(2,1)S(1)}) custom-call(s32[2]{0:T(128)S(1)} %pad_add_fusion.places, bf16[512,512]{1,0:T(8,128)(2,1)S(1)} %get-tuple-element.38.gt_ref, bf16[512,512]{1,0:T(8,128)(2,1)S(1)} %collective-permute-done.13.gt_other, ...), custom_call_target="tpu_custom_call" | custom-call | flops 2147483648 | bytes 8388608 | tf_op jit(solution)/shard_map/weight_partials/pallas_call | solution.py:168
  109.6 1.0 copy-done.2
  110.5 2.6 %collective-permute-start.16 = (bf16[512,512]{1,0:T(8,128)(2,1)}, bf16[512,512]{1,0:T(8,128)(2,1)}, u32[]{:S(2)}, u32[]{:S(2)}) collective-permute-start(bf16[512,512]{1,0:T(8,128)(2,1)} %get-tuple-element.43), channel_id=1, source_target_pairs={{0,4},{1,5},{2,6},{3,7},{4,0},{5,1},{6,2},{7,3},{8,12},{9,13},{10,... | collective-permute-start | bytes 1572872 | tf_op jit(solution)/shard_map/ppermute | solution.py:304
  113.1 1.5 collective-permute-start.17
  114.6 2.0 collective-permute-start.26
  116.6 31.1 %collective-permute-done.26.b_ref = bf16[256,512]{1,0:T(8,128)(2,1)S(1)} collective-permute-done((bf16[256,512]{1,0:T(8,128)(2,1)}, bf16[256,512]{1,0:T(8,128)(2,1)S(1)}, u32[]{:S(2)}, u32[]{:S(2)}) %collective-permute-start.26) | collective-permute-done | bytes 262176 | tf_op jit(solution)/shard_map/ppermute | solution.py:304
  147.7 0.7 copy-done.15
  148.5 0.1 copy-done.16
  148.5 2.1 quarters.3
  150.6 1.6 collective-permute-start.28
  152.2 2.6 %collective-permute-start.29 = (bf16[64,512]{1,0:T(8,128)(2,1)}, bf16[64,512]{1,0:T(8,128)(2,1)S(1)}, u32[]{:S(2)}, u32[]{:S(2)}) collective-permute-start(bf16[64,512]{1,0:T(8,128)(2,1)} %get-tuple-element.56), channel_id=1, source_target_pairs={{0,16},{8,24},{16,0},{24,8},{1,17},{9,25},{17,1},{25,9},{2,18},{10... | collective-permute-start | bytes 196616 | tf_op jit(solution)/shard_map/ppermute | solution.py:304
  154.8 0.9 collective-permute-done.28
  155.7 3.0 %collective-permute-start.30 = (bf16[64,512]{1,0:T(8,128)(2,1)}, bf16[64,512]{1,0:T(8,128)(2,1)S(1)}, u32[]{:S(2)}, u32[]{:S(2)}) collective-permute-start(bf16[64,512]{1,0:T(8,128)(2,1)} %get-tuple-element.57), channel_id=1, source_target_pairs={{0,24},{8,16},{16,8},{24,0},{1,25},{9,17},{17,9},{25,1},{2,26},{10... | collective-permute-start | bytes 196616 | tf_op jit(solution)/shard_map/ppermute | solution.py:304
  158.8 0.7 collective-permute-done.29
  159.5 0.5 collective-permute-start.10
  160.0 0.1 collective-permute-start.12
  160.1 0.4 collective-permute-start.8
  160.5 2.6 %quarters.2 = (f32[128,512]{1,0:T(8,128)}, bf16[128,512]{1,0:T(8,128)(2,1)}, bf16[128,512]{1,0:T(8,128)(2,1)}, bf16[128,512]{1,0:T(8,128)(2,1)}) custom-call(s32[1]{0:T(128)} %bitcast.9.z_ref, f32[512,512]{1,0:T(8,128)} %copy-done.2, bf16[512,512]{1,0:T(8,128)(2,1)} %collective-permute-done.15.a_ref, bf16[512,512]{1,0:T(8,128)(2,1)} %collective-permute-done.16.b_ref, ...), custom_call_target="tpu_custom_call" | custom-call | flops 1048576 | bytes 2097152 | tf_op jit(solution)/shard_map/quarters/pallas_call | solution.py:261
  163.1 5.7 %collective-permute-done.18 = bf16[128,512]{1,0:T(8,128)(2,1)S(1)} collective-permute-done((bf16[128,512]{1,0:T(8,128)(2,1)}, bf16[128,512]{1,0:T(8,128)(2,1)S(1)}, u32[]{:S(2)}, u32[]{:S(2)}) %collective-permute-start.18) | collective-permute-done | bytes 131104 | tf_op jit(solution)/shard_map/ppermute | solution.py:304
  168.8 0.8 collective-permute-start.19
  169.6 7.8 %collective-permute-done.19 = bf16[128,512]{1,0:T(8,128)(2,1)S(1)} collective-permute-done((bf16[128,512]{1,0:T(8,128)(2,1)}, bf16[128,512]{1,0:T(8,128)(2,1)S(1)}, u32[]{:S(2)}, u32[]{:S(2)}) %collective-permute-start.19) | collective-permute-done | bytes 131104 | tf_op jit(solution)/shard_map/ppermute | solution.py:304
  177.3 1.6 collective-permute-start.20
  179.0 0.9 add_convert_fusion.2.refs_4_
  179.9 4.8 %collective-permute-done.20 = bf16[128,512]{1,0:T(8,128)(2,1)S(1)} collective-permute-done((bf16[128,512]{1,0:T(8,128)(2,1)}, bf16[128,512]{1,0:T(8,128)(2,1)S(1)}, u32[]{:S(2)}, u32[]{:S(2)}) %collective-permute-start.20) | collective-permute-done | bytes 131104 | tf_op jit(solution)/shard_map/ppermute | solution.py:304
  184.7 1.0 add_convert_fusion.1.refs_0_
  185.8 2.0 collective-permute-start.32
  187.8 2.4 %collective-permute-start.33 = (bf16[64,512]{1,0:T(8,128)(2,1)S(1)}, bf16[64,512]{1,0:T(8,128)(2,1)S(1)}, u32[]{:S(2)}, u32[]{:S(2)}) collective-permute-start(bf16[64,512]{1,0:T(8,128)(2,1)S(1)} %add_convert_fusion.2.refs_4_), channel_id=1, source_target_pairs={{0,24},{8,16},{16,8},{24,0},{1,25},{9,17},{17,9},{25,1},{2,26},{10... | collective-permute-start | bytes 196616 | tf_op jit(solution)/shard_map/ppermute | solution.py:304
  190.2 2.0 collective-permute-start.22
  192.2 2.4 %collective-permute-start.23 = (bf16[128,512]{1,0:T(8,128)(2,1)S(1)}, bf16[128,512]{1,0:T(8,128)(2,1)S(1)}, u32[]{:S(2)}, u32[]{:S(2)}) collective-permute-start(bf16[128,512]{1,0:T(8,128)(2,1)S(1)} %add_convert_fusion.1.refs_0_), channel_id=1, source_target_pairs={{0,24},{8,16},{16,8},{24,0},{1,25},{9,17},{17,9},{25,1},{2,26},{10... | collective-permute-start | bytes 393224 | tf_op jit(solution)/shard_map/ppermute | solution.py:304
  194.6 1.0 copy-done.12
  195.7 9.0 %input_grad.1 = bf16[512,4096]{1,0:T(8,128)(2,1)} custom-call(s32[2]{0:T(128)S(1)} %pad_add_fusion.places, bf16[512,512]{1,0:T(8,128)(2,1)S(1)} %copy-done.12, bf16[512,256]{1,0:T(8,128)(2,1)S(1)} %copy-done.10, bf16[512,768]{1,0:T(8,128)(2,1)S(1)} %copy-done.6, bf16[512,768]{1,0:T(8,128)(2,1)S(1)} %collective-permute-done.6.refs_1_, ...), custom_call_target="tpu_custom_call" | custom-call | flops 3221225472 | bytes 11534336 | tf_op jit(solution)/shard_map/input_grad/pallas_call | solution.py:208
  204.8 0.5 copy-done.24
  205.4 0.1 copy-done.21
  205.5 0.6 copy-done.22
  206.1 2.4 %joined.1 = bf16[512,768]{1,0:T(8,128)(2,1)} custom-call(s32[1]{0:T(128)} %bitcast.9.z_ref, bf16[128,512]{1,0:T(8,128)(2,1)} %copy-done.13, bf16[128,512]{1,0:T(8,128)(2,1)} %copy-done.20, bf16[128,512]{1,0:T(8,128)(2,1)} %copy-done.21, bf16[128,512]{1,0:T(8,128)(2,1)} %copy-done.22, bf16[64,512]{1,0:T(8,128)(2,1)} %copy-done.17, ...), custom_call_target="tpu_custom_call" | custom-call | flops 393216 | bytes 2097152 | tf_op jit(solution)/shard_map/joined/pallas_call | solution.py:290
  (68 shorter events, 0.2 us)
Async XLA Ops:
  0.6 10.7 %collective-permute-start = (bf16[512,256]{1,0:T(8,128)(2,1)}, bf16[512,256]{1,0:T(8,128)(2,1)S(1)}, u32[]{:S(2)}, u32[]{:S(2)}) collective-permute-start(bf16[512,256]{1,0:T(8,128)(2,1)} %bitcast.16), channel_id=1, source_target_pairs={{0,2},{1,3},{2,4},{3,5},{4,6},{5,7},{8,10},{9,11},{10,12},{11,13},... | collective-permute-start | bytes 786440 | tf_op jit(solution)/shard_map/ppermute | solution.py:326
  11.3 1.5 collective-permute-start.1
  12.9 77.9 %collective-permute-start.14 = (bf16[512,4096]{1,0:T(8,128)(2,1)}, bf16[512,4096]{1,0:T(8,128)(2,1)}, u32[]{:S(2)}, u32[]{:S(2)}) collective-permute-start(bf16[512,4096]{1,0:T(8,128)(2,1)} %bitcast.11), channel_id=1, source_target_pairs={{0,1},{1,0},{2,3},{3,2},{4,5},{5,4},{6,7},{7,6},{8,9},{9,8},{10,11... | collective-permute-start | bytes 12582920 | tf_op jit(solution)/shard_map/ppermute | solution.py:304
  13.0 7.4 %collective-permute-start.2 = (bf16[512,256]{1,0:T(8,128)(2,1)}, bf16[512,256]{1,0:T(8,128)(2,1)S(1)}, u32[]{:S(2)}, u32[]{:S(2)}) collective-permute-start(bf16[512,256]{1,0:T(8,128)(2,1)} %bitcast.17), channel_id=1, source_target_pairs={{0,1},{2,3},{4,5},{6,7},{1,4},{3,6},{8,9},{10,11},{12,13},{14,15},... | collective-permute-start | bytes 786440 | tf_op jit(solution)/shard_map/ppermute | solution.py:327
  20.4 1.0 copy-start.7
  21.4 1.0 copy-start.8
  22.5 0.9 copy-start.9
  23.4 0.7 copy-start.11
  24.1 17.8 %copy-start.6 = (bf16[512,768]{1,0:T(8,128)(2,1)S(1)}, bf16[512,768]{1,0:T(8,128)(2,1)}, u32[]{:S(2)}) copy-start(bf16[512,768]{1,0:T(8,128)(2,1)} %refs_0_) | copy-start | bytes 2359300
  31.1 26.0 %copy-start.4 = (f32[512,256]{1,0:T(8,128)}, f32[512,256]{1,0:T(8,128)S(1)}, u32[]{:S(2)}) copy-start(f32[512,256]{1,0:T(8,128)S(1)} %get-tuple-element.32.own_ref) | copy-start | bytes 1572868
  31.1 9.4 %collective-permute-start.3 = (f32[512,256]{1,0:T(8,128)S(1)}, f32[512,256]{1,0:T(8,128)S(1)}, u32[]{:S(2)}, u32[]{:S(2)}) collective-permute-start(f32[512,256]{1,0:T(8,128)S(1)} %get-tuple-element.34), channel_id=1, source_target_pairs={{0,1},{1,0},{2,3},{3,2},{4,5},{5,4},{6,7},{7,6},{8,9},{9,8},{10,11... | collective-permute-start | bytes 1572872 | tf_op jit(solution)/shard_map/ppermute | solution.py:304
  38.9 14.0 %collective-permute-start.5 = (bf16[512,256]{1,0:T(8,128)(2,1)S(1)}, bf16[512,256]{1,0:T(8,128)(2,1)S(1)}, u32[]{:S(2)}, u32[]{:S(2)}) collective-permute-start(bf16[512,256]{1,0:T(8,128)(2,1)S(1)} %get-tuple-element.35), channel_id=1, source_target_pairs={{1,0},{3,2},{5,4},{7,6},{4,1},{6,3},{9,8},{11,10},{13,12},{15,14},... | collective-permute-start | bytes 786440 | tf_op jit(solution)/shard_map/ppermute | solution.py:341
  40.5 16.5 %collective-permute-start.4 = (bf16[512,256]{1,0:T(8,128)(2,1)S(1)}, bf16[512,256]{1,0:T(8,128)(2,1)S(1)}, u32[]{:S(2)}, u32[]{:S(2)}) collective-permute-start(bf16[512,256]{1,0:T(8,128)(2,1)S(1)} %add_convert_fusion), channel_id=1, source_target_pairs={{2,0},{3,1},{4,2},{5,3},{6,4},{7,5},{10,8},{11,9},{12,10},{13,11},... | collective-permute-start | bytes 786440 | tf_op jit(solution)/shard_map/ppermute | solution.py:340
  41.9 32.7 %collective-permute-start.11 = (bf16[512,768]{1,0:T(8,128)(2,1)S(1)}, bf16[512,768]{1,0:T(8,128)(2,1)S(1)}, u32[]{:S(2)}, u32[]{:S(2)}) collective-permute-start(bf16[512,768]{1,0:T(8,128)(2,1)S(1)} %copy-done.6), channel_id=1, source_target_pairs={{0,6},{1,7},{2,4},{3,5},{4,2},{5,3},{6,0},{7,1},{8,14},{9,15},{10,... | collective-permute-start | bytes 2359304 | tf_op jit(solution)/shard_map/ppermute | solution.py:304
  51.0 39.8 %collective-permute-start.7 = (bf16[512,768]{1,0:T(8,128)(2,1)S(1)}, bf16[512,768]{1,0:T(8,128)(2,1)}, u32[]{:S(2)}, u32[]{:S(2)}) collective-permute-start(bf16[512,768]{1,0:T(8,128)(2,1)S(1)} %copy-done.6), channel_id=1, source_target_pairs={{0,2},{1,3},{2,0},{3,1},{4,6},{5,7},{6,4},{7,5},{8,10},{9,11},{10,... | collective-permute-start | bytes 2359304 | tf_op jit(solution)/shard_map/ppermute | solution.py:304
  52.9 4.2 %copy-start.18 = (bf16[512,256]{1,0:T(8,128)(2,1)}, bf16[512,256]{1,0:T(8,128)(2,1)S(1)}, u32[]{:S(2)}) copy-start(bf16[512,256]{1,0:T(8,128)(2,1)S(1)} %collective-permute-done.5.x_ref) | copy-start | bytes 786436
  52.9 37.8 %collective-permute-start.9 = (bf16[512,768]{1,0:T(8,128)(2,1)S(1)}, bf16[512,768]{1,0:T(8,128)(2,1)}, u32[]{:S(2)}, u32[]{:S(2)}) collective-permute-start(bf16[512,768]{1,0:T(8,128)(2,1)S(1)} %copy-done.6), channel_id=1, source_target_pairs={{0,4},{1,5},{2,6},{3,7},{4,0},{5,1},{6,2},{7,3},{8,12},{9,13},{10,... | collective-permute-start | bytes 2359304 | tf_op jit(solution)/shard_map/ppermute | solution.py:304
  57.1 0.7 copy-start.19
  57.1 2.8 %collective-permute-start.13 = (bf16[512,512]{1,0:T(8,128)(2,1)S(1)}, bf16[512,512]{1,0:T(8,128)(2,1)S(1)}, u32[]{:S(2)}, u32[]{:S(2)}) collective-permute-start(bf16[512,512]{1,0:T(8,128)(2,1)S(1)} %get-tuple-element.38.gt_ref), channel_id=1, source_target_pairs={{0,1},{1,0},{2,3},{3,2},{4,5},{5,4},{6,7},{7,6},{8,9},{9,8},{10,11... | collective-permute-start | bytes 1572872 | tf_op jit(solution)/shard_map/ppermute | solution.py:304
  59.9 30.9 %collective-permute-start.24 = (bf16[256,512]{1,0:T(8,128)(2,1)}, bf16[256,512]{1,0:T(8,128)(2,1)S(1)}, u32[]{:S(2)}, u32[]{:S(2)}) collective-permute-start(bf16[256,512]{1,0:T(8,128)(2,1)} %get-tuple-element.49.gt_ref), channel_id=1, source_target_pairs={{0,1},{1,0},{2,3},{3,2},{4,5},{5,4},{6,7},{7,6},{8,9},{9,8},{10,11... | collective-permute-start | bytes 786440 | tf_op jit(solution)/shard_map/ppermute | solution.py:304
  90.8 2.2 %copy-start = (bf16[1,512,4096]{2,1,0:T(8,128)(2,1)S(1)}, bf16[1,512,4096]{2,1,0:T(8,128)(2,1)}, u32[]{:S(2)}) copy-start(bf16[1,512,4096]{2,1,0:T(8,128)(2,1)} %param.6) | copy-start | bytes 12582916
  93.0 0.9 copy-start.5
  93.9 9.5 %copy-start.1 = (bf16[1,512,4096]{2,1,0:T(8,128)(2,1)S(1)}, bf16[1,512,4096]{2,1,0:T(8,128)(2,1)}, u32[]{:S(2)}) copy-start(bf16[1,512,4096]{2,1,0:T(8,128)(2,1)} %param.6) | copy-start | bytes 12582916
  99.3 0.8 copy-start.3
  100.1 16.6 %collective-permute-start.25 = (bf16[256,512]{1,0:T(8,128)(2,1)S(1)}, bf16[256,512]{1,0:T(8,128)(2,1)S(1)}, u32[]{:S(2)}, u32[]{:S(2)}) collective-permute-start(bf16[256,512]{1,0:T(8,128)(2,1)S(1)} %get-tuple-element.51), channel_id=1, source_target_pairs={{0,2},{1,3},{2,0},{3,1},{4,6},{5,7},{6,4},{7,5},{8,10},{9,11},{10,... | collective-permute-start | bytes 786440 | tf_op jit(solution)/shard_map/ppermute | solution.py:304
  109.6 1.0 copy-start.2
  110.5 84.1 %copy-start.10 = (bf16[512,256]{1,0:T(8,128)(2,1)S(1)}, bf16[512,256]{1,0:T(8,128)(2,1)}, u32[]{:S(2)}) copy-start(bf16[512,256]{1,0:T(8,128)(2,1)} %get-tuple-element.36.gkv_ref) | copy-start | bytes 786436
  110.5 48.9 %collective-permute-start.15 = (bf16[512,512]{1,0:T(8,128)(2,1)}, bf16[512,512]{1,0:T(8,128)(2,1)}, u32[]{:S(2)}, u32[]{:S(2)}) collective-permute-start(bf16[512,512]{1,0:T(8,128)(2,1)} %get-tuple-element.42), channel_id=1, source_target_pairs={{0,2},{1,3},{2,0},{3,1},{4,6},{5,7},{6,4},{7,5},{8,10},{9,11},{10,... | collective-permute-start | bytes 1572872 | tf_op jit(solution)/shard_map/ppermute | solution.py:304
  110.5 49.5 %collective-permute-start.16 = (bf16[512,512]{1,0:T(8,128)(2,1)}, bf16[512,512]{1,0:T(8,128)(2,1)}, u32[]{:S(2)}, u32[]{:S(2)}) collective-permute-start(bf16[512,512]{1,0:T(8,128)(2,1)} %get-tuple-element.43), channel_id=1, source_target_pairs={{0,4},{1,5},{2,6},{3,7},{4,0},{5,1},{6,2},{7,3},{8,12},{9,13},{10,... | collective-permute-start | bytes 1572872 | tf_op jit(solution)/shard_map/ppermute | solution.py:304
  113.1 46.9 %collective-permute-start.17 = (bf16[512,512]{1,0:T(8,128)(2,1)S(1)}, bf16[512,512]{1,0:T(8,128)(2,1)}, u32[]{:S(2)}, u32[]{:S(2)}) collective-permute-start(bf16[512,512]{1,0:T(8,128)(2,1)S(1)} %get-tuple-element.44), channel_id=1, source_target_pairs={{0,6},{1,7},{2,4},{3,5},{4,2},{5,3},{6,0},{7,1},{8,14},{9,15},{10,... | collective-permute-start | bytes 1572872 | tf_op jit(solution)/shard_map/ppermute | solution.py:304
  114.6 33.1 %collective-permute-start.26 = (bf16[256,512]{1,0:T(8,128)(2,1)}, bf16[256,512]{1,0:T(8,128)(2,1)S(1)}, u32[]{:S(2)}, u32[]{:S(2)}) collective-permute-start(bf16[256,512]{1,0:T(8,128)(2,1)} %get-tuple-element.52), channel_id=1, source_target_pairs={{0,4},{1,5},{2,6},{3,7},{4,0},{5,1},{6,2},{7,3},{8,12},{9,13},{10,... | collective-permute-start | bytes 786440 | tf_op jit(solution)/shard_map/ppermute | solution.py:304
  116.6 31.1 %copy-start.14 = (bf16[256,512]{1,0:T(8,128)(2,1)}, bf16[256,512]{1,0:T(8,128)(2,1)S(1)}, u32[]{:S(2)}) copy-start(bf16[256,512]{1,0:T(8,128)(2,1)S(1)} %collective-permute-done.25.a_ref) | copy-start | bytes 786436
  116.6 31.1 %collective-permute-start.27 = (bf16[256,512]{1,0:T(8,128)(2,1)}, bf16[256,512]{1,0:T(8,128)(2,1)S(1)}, u32[]{:S(2)}, u32[]{:S(2)}) collective-permute-start(bf16[256,512]{1,0:T(8,128)(2,1)} %get-tuple-element.53), channel_id=1, source_target_pairs={{0,6},{1,7},{2,4},{3,5},{4,2},{5,3},{6,0},{7,1},{8,14},{9,15},{10,... | collective-permute-start | bytes 786440 | tf_op jit(solution)/shard_map/ppermute | solution.py:304
  147.7 0.7 copy-start.15
  147.7 0.8 copy-start.16
  150.6 5.1 %collective-permute-start.28 = (bf16[64,512]{1,0:T(8,128)(2,1)}, bf16[64,512]{1,0:T(8,128)(2,1)S(1)}, u32[]{:S(2)}, u32[]{:S(2)}) collective-permute-start(bf16[64,512]{1,0:T(8,128)(2,1)} %get-tuple-element.55), channel_id=1, source_target_pairs={{0,8},{8,0},{16,24},{24,16},{1,9},{9,1},{17,25},{25,17},{2,10},{10... | collective-permute-start | bytes 196616 | tf_op jit(solution)/shard_map/ppermute | solution.py:304
  152.2 7.3 %collective-permute-start.29 = (bf16[64,512]{1,0:T(8,128)(2,1)}, bf16[64,512]{1,0:T(8,128)(2,1)S(1)}, u32[]{:S(2)}, u32[]{:S(2)}) collective-permute-start(bf16[64,512]{1,0:T(8,128)(2,1)} %get-tuple-element.56), channel_id=1, source_target_pairs={{0,16},{8,24},{16,0},{24,8},{1,17},{9,25},{17,1},{25,9},{2,18},{10... | collective-permute-start | bytes 196616 | tf_op jit(solution)/shard_map/ppermute | solution.py:304
  155.7 7.4 %collective-permute-start.30 = (bf16[64,512]{1,0:T(8,128)(2,1)}, bf16[64,512]{1,0:T(8,128)(2,1)S(1)}, u32[]{:S(2)}, u32[]{:S(2)}) collective-permute-start(bf16[64,512]{1,0:T(8,128)(2,1)} %get-tuple-element.57), channel_id=1, source_target_pairs={{0,24},{8,16},{16,8},{24,0},{1,25},{9,17},{17,9},{25,1},{2,26},{10... | collective-permute-start | bytes 196616 | tf_op jit(solution)/shard_map/ppermute | solution.py:304
  159.5 26.3 %collective-permute-start.6 = (bf16[512,768]{1,0:T(8,128)(2,1)S(1)}, bf16[512,768]{1,0:T(8,128)(2,1)S(1)}, u32[]{:S(2)}, u32[]{:S(2)}) collective-permute-start(bf16[512,768]{1,0:T(8,128)(2,1)S(1)} %copy-done.6), channel_id=1, source_target_pairs={{0,1},{1,0},{2,3},{3,2},{4,5},{5,4},{6,7},{7,6},{8,9},{9,8},{10,11... | collective-permute-start | bytes 2359304 | tf_op jit(solution)/shard_map/ppermute | solution.py:304
  159.5 28.3 %collective-permute-start.10 = (bf16[512,768]{1,0:T(8,128)(2,1)}, bf16[512,768]{1,0:T(8,128)(2,1)}, u32[]{:S(2)}, u32[]{:S(2)}) collective-permute-start(bf16[512,768]{1,0:T(8,128)(2,1)} %collective-permute-done.9.refs_4_), channel_id=1, source_target_pairs={{0,1},{1,0},{2,3},{3,2},{4,5},{5,4},{6,7},{7,6},{8,9},{9,8},{10,11... | collective-permute-start | bytes 2359304 | tf_op jit(solution)/shard_map/ppermute | solution.py:304
  160.0 30.2 %collective-permute-start.12 = (bf16[512,768]{1,0:T(8,128)(2,1)S(1)}, bf16[512,768]{1,0:T(8,128)(2,1)}, u32[]{:S(2)}, u32[]{:S(2)}) collective-permute-start(bf16[512,768]{1,0:T(8,128)(2,1)S(1)} %collective-permute-done.11.refs_6_), channel_id=1, source_target_pairs={{0,1},{1,0},{2,3},{3,2},{4,5},{5,4},{6,7},{7,6},{8,9},{9,8},{10,11... | collective-permute-start | bytes 2359304 | tf_op jit(solution)/shard_map/ppermute | solution.py:304
  160.1 30.2 %collective-permute-start.8 = (bf16[512,768]{1,0:T(8,128)(2,1)}, bf16[512,768]{1,0:T(8,128)(2,1)}, u32[]{:S(2)}, u32[]{:S(2)}) collective-permute-start(bf16[512,768]{1,0:T(8,128)(2,1)} %collective-permute-done.7.refs_2_), channel_id=1, source_target_pairs={{0,1},{1,0},{2,3},{3,2},{4,5},{5,4},{6,7},{7,6},{8,9},{9,8},{10,11... | collective-permute-start | bytes 2359304 | tf_op jit(solution)/shard_map/ppermute | solution.py:304
  163.1 5.7 %collective-permute-start.18 = (bf16[128,512]{1,0:T(8,128)(2,1)}, bf16[128,512]{1,0:T(8,128)(2,1)S(1)}, u32[]{:S(2)}, u32[]{:S(2)}) collective-permute-start(bf16[128,512]{1,0:T(8,128)(2,1)} %get-tuple-element.46), channel_id=1, source_target_pairs={{0,8},{8,0},{16,24},{24,16},{1,9},{9,1},{17,25},{25,17},{2,10},{10... | collective-permute-start | bytes 393224 | tf_op jit(solution)/shard_map/ppermute | solution.py:304
  168.8 8.5 %collective-permute-start.19 = (bf16[128,512]{1,0:T(8,128)(2,1)}, bf16[128,512]{1,0:T(8,128)(2,1)S(1)}, u32[]{:S(2)}, u32[]{:S(2)}) collective-permute-start(bf16[128,512]{1,0:T(8,128)(2,1)} %get-tuple-element.47), channel_id=1, source_target_pairs={{0,16},{8,24},{16,0},{24,8},{1,17},{9,25},{17,1},{25,9},{2,18},{10... | collective-permute-start | bytes 393224 | tf_op jit(solution)/shard_map/ppermute | solution.py:304
  177.3 7.4 %collective-permute-start.20 = (bf16[128,512]{1,0:T(8,128)(2,1)}, bf16[128,512]{1,0:T(8,128)(2,1)S(1)}, u32[]{:S(2)}, u32[]{:S(2)}) collective-permute-start(bf16[128,512]{1,0:T(8,128)(2,1)} %get-tuple-element.48), channel_id=1, source_target_pairs={{0,24},{8,16},{16,8},{24,0},{1,25},{9,17},{17,9},{25,1},{2,26},{10... | collective-permute-start | bytes 393224 | tf_op jit(solution)/shard_map/ppermute | solution.py:304
  179.9 24.8 %copy-start.17 = (bf16[64,512]{1,0:T(8,128)(2,1)}, bf16[64,512]{1,0:T(8,128)(2,1)S(1)}, u32[]{:S(2)}) copy-start(bf16[64,512]{1,0:T(8,128)(2,1)S(1)} %add_convert_fusion.2.refs_4_) | copy-start | bytes 196612
  184.7 7.5 %collective-permute-start.31 = (bf16[64,512]{1,0:T(8,128)(2,1)S(1)}, bf16[64,512]{1,0:T(8,128)(2,1)S(1)}, u32[]{:S(2)}, u32[]{:S(2)}) collective-permute-start(bf16[64,512]{1,0:T(8,128)(2,1)S(1)} %add_convert_fusion.2.refs_4_), channel_id=1, source_target_pairs={{0,8},{8,0},{16,24},{24,16},{1,9},{9,1},{17,25},{25,17},{2,10},{10... | collective-permute-start | bytes 196616 | tf_op jit(solution)/shard_map/ppermute | solution.py:304
  185.8 18.9 %copy-start.13 = (bf16[128,512]{1,0:T(8,128)(2,1)}, bf16[128,512]{1,0:T(8,128)(2,1)S(1)}, u32[]{:S(2)}) copy-start(bf16[128,512]{1,0:T(8,128)(2,1)S(1)} %add_convert_fusion.1.refs_0_) | copy-start | bytes 393220
  185.8 18.9 %collective-permute-start.32 = (bf16[64,512]{1,0:T(8,128)(2,1)S(1)}, bf16[64,512]{1,0:T(8,128)(2,1)S(1)}, u32[]{:S(2)}, u32[]{:S(2)}) collective-permute-start(bf16[64,512]{1,0:T(8,128)(2,1)S(1)} %add_convert_fusion.2.refs_4_), channel_id=1, source_target_pairs={{0,16},{8,24},{16,0},{24,8},{1,17},{9,25},{17,1},{25,9},{2,18},{10... | collective-permute-start | bytes 196616 | tf_op jit(solution)/shard_map/ppermute | solution.py:304
  187.8 16.9 %collective-permute-start.33 = (bf16[64,512]{1,0:T(8,128)(2,1)S(1)}, bf16[64,512]{1,0:T(8,128)(2,1)S(1)}, u32[]{:S(2)}, u32[]{:S(2)}) collective-permute-start(bf16[64,512]{1,0:T(8,128)(2,1)S(1)} %add_convert_fusion.2.refs_4_), channel_id=1, source_target_pairs={{0,24},{8,16},{16,8},{24,0},{1,25},{9,17},{17,9},{25,1},{2,26},{10... | collective-permute-start | bytes 196616 | tf_op jit(solution)/shard_map/ppermute | solution.py:304
  190.2 14.5 %collective-permute-start.21 = (bf16[128,512]{1,0:T(8,128)(2,1)S(1)}, bf16[128,512]{1,0:T(8,128)(2,1)S(1)}, u32[]{:S(2)}, u32[]{:S(2)}) collective-permute-start(bf16[128,512]{1,0:T(8,128)(2,1)S(1)} %add_convert_fusion.1.refs_0_), channel_id=1, source_target_pairs={{0,8},{8,0},{16,24},{24,16},{1,9},{9,1},{17,25},{25,17},{2,10},{10... | collective-permute-start | bytes 393224 | tf_op jit(solution)/shard_map/ppermute | solution.py:304
  190.2 14.5 %collective-permute-start.22 = (bf16[128,512]{1,0:T(8,128)(2,1)S(1)}, bf16[128,512]{1,0:T(8,128)(2,1)S(1)}, u32[]{:S(2)}, u32[]{:S(2)}) collective-permute-start(bf16[128,512]{1,0:T(8,128)(2,1)S(1)} %add_convert_fusion.1.refs_0_), channel_id=1, source_target_pairs={{0,16},{8,24},{16,0},{24,8},{1,17},{9,25},{17,1},{25,9},{2,18},{10... | collective-permute-start | bytes 393224 | tf_op jit(solution)/shard_map/ppermute | solution.py:304
  192.2 12.5 %copy-start.23 = (bf16[64,512]{1,0:T(8,128)(2,1)}, bf16[64,512]{1,0:T(8,128)(2,1)S(1)}, u32[]{:S(2)}) copy-start(bf16[64,512]{1,0:T(8,128)(2,1)S(1)} %collective-permute-done.31.refs_5_) | copy-start | bytes 196612
  192.2 12.6 %collective-permute-start.23 = (bf16[128,512]{1,0:T(8,128)(2,1)S(1)}, bf16[128,512]{1,0:T(8,128)(2,1)S(1)}, u32[]{:S(2)}, u32[]{:S(2)}) collective-permute-start(bf16[128,512]{1,0:T(8,128)(2,1)S(1)} %add_convert_fusion.1.refs_0_), channel_id=1, source_target_pairs={{0,24},{8,16},{16,8},{24,0},{1,25},{9,17},{17,9},{25,1},{2,26},{10... | collective-permute-start | bytes 393224 | tf_op jit(solution)/shard_map/ppermute | solution.py:304
  194.6 1.0 copy-start.12
  204.7 0.6 copy-start.24
  204.7 0.6 copy-start.25
  204.7 0.7 copy-start.20
  204.8 0.7 copy-start.21
  205.5 0.7 copy-start.22

commit v3 on v2

--- a/solution.py
+++ b/solution.py
@@ -120,7 +120,7 @@
     both = own.shape[1]
     hd = both // 2
     wide = width // hd * Q_STEP
-    vmem = pl.BlockSpec(memory_space=pltpu.VMEM)
+    whole = lambda shape: pl.BlockSpec(shape, lambda i: (0, 0))
     smem = pl.BlockSpec(memory_space=pltpu.SMEM)
     return pl.pallas_call(
         attention_kernel,
@@ -133,8 +133,9 @@
             jax.ShapeDtypeStruct((rows, both), jnp.float32),
             jax.ShapeDtypeStruct((rows, both), jnp.bfloat16),
         ),
-        in_specs=[smem, smem] + [vmem] * 6,
-        out_specs=[vmem] * 6,
+        grid=(1,),
+        in_specs=[smem, smem] + [whole((rows, width))] * 2 + [whole((rows, both))] * 4,
+        out_specs=[whole((rows, width)), whole((width, rows))] + [whole((rows, both))] * 4,
         scratch_shapes=[
             pltpu.VMEM((4 * rows, both), jnp.bfloat16),
             pltpu.VMEM((hd, 4 * rows), jnp.bfloat16),
@@ -142,7 +143,7 @@
             pltpu.VMEM((4 * rows, wide), jnp.float32),
             pltpu.VMEM((4 * rows, both), jnp.float32),
         ],
-        compiler_params=pltpu.CompilerParams(vmem_limit_bytes=28 * 2**20),
+        compiler_params=pltpu.CompilerParams(vmem_limit_bytes=58 * 2**20),
         cost_estimate=pl.CostEstimate(flops=12 * 10**9, bytes_accessed=6 * 2**20, transcendentals=4 * 2**20),
     )(index, lengths, q, g, own, d2, r, x)
 
@@ -181,18 +182,18 @@
             ],
             out_specs=[pl.BlockSpec((cols, block), whole)] * chips,
         ),
-        compiler_params=pltpu.CompilerParams(vmem_limit_bytes=40 * 2**20),
+        compiler_params=pltpu.CompilerParams(vmem_limit_bytes=58 * 2**20),
         cost_estimate=pl.CostEstimate(
             flops=4 * cols * rows * block * chips, bytes_accessed=8 * 2**20, transcendentals=0
         ),
     )(places, gt, gt_other, x, x_other)
 
 
-def input_kernel(places, gq_ref, gkv_ref, *refs):
+def input_kernel(places, gq_ref, gkv_ref, *refs, count):
     out_ref = refs[-1]
     k = pl.program_id(0)
     q_cols = gq_ref.shape[1]
-    for turn, w_ref in enumerate(refs[:-1]):
+    for turn, w_ref in enumerate(refs[:count]):
         @pl.when(k == turn)
         def _(w_ref=w_ref):
             out_ref[...] = (
@@ -200,27 +201,31 @@
             ).astype(out_ref.dtype)
 
 
-def input_grad(places, gq, gkv, blocks):
+def input_grad(places, gq, gkv, blocks, start, earlier=None):
     rows = gq.shape[0]
     block, cols = blocks[0].shape
     count = len(blocks)
+    total = lax.axis_size("ctx") * block
     whole = lambda k, s: (0, 0)
-    return pl.pallas_call(
-        input_kernel,
+    before = [] if earlier is None else [earlier]
+    return pl.pallas_call(
+        functools.partial(input_kernel, count=count),
         name="input_grad",
-        out_shape=jax.ShapeDtypeStruct((rows, block * count), jnp.bfloat16),
+        out_shape=jax.ShapeDtypeStruct((rows, total), jnp.bfloat16),
         grid_spec=pltpu.PrefetchScalarGridSpec(
             num_scalar_prefetch=1,
             grid=(count,),
             in_specs=[pl.BlockSpec(gq.shape, whole), pl.BlockSpec(gkv.shape, whole)]
-            + [pl.BlockSpec((block, cols), whole)] * count,
-            out_specs=pl.BlockSpec((rows, block), lambda k, s: (0, (s[0] * 2 + s[1]) ^ k)),
-        ),
-        compiler_params=pltpu.CompilerParams(vmem_limit_bytes=40 * 2**20),
+            + [pl.BlockSpec((block, cols), whole)] * count
+            + [pl.BlockSpec(memory_space=pl.ANY)] * len(before),
+            out_specs=pl.BlockSpec((rows, block), lambda k, s: (0, (s[0] * 2 + s[1]) ^ (start + k))),
+        ),
+        input_output_aliases={3 + count: 0} if before else {},
+        compiler_params=pltpu.CompilerParams(vmem_limit_bytes=58 * 2**20),
         cost_estimate=pl.CostEstimate(
             flops=2 * rows * cols * block * count, bytes_accessed=11 * 2**20, transcendentals=0
         ),
-    )(places, gq, gkv, *blocks)
+    )(places, gq, gkv, *blocks, *before)
 
 
 def finish_kernel(own_ref, two_ref, x_ref, out_ref, out_t_ref):
@@ -304,8 +309,8 @@
     return lax.ppermute(array, axis, [(i, i ^ bits) for i in range(lax.axis_size(axis))])
 
 
-def tied(array, *after):
-    return lax.optimization_barrier((array, *after))[0]
+def together(*arrays):
+    return lax.optimization_barrier(arrays)
 
 
 def per_device(inputs, qkv_weight, queries, keys_values, out_grad, lengths):
@@ -325,41 +330,66 @@
 
     d2 = lax.ppermute(own, "ctx", by_two)
     x = lax.ppermute(own, "ctx", mixed)
+    d2, x = lax.optimization_barrier((d2, x))
     r = flipped(d2, 1)
     if small:
-        w_own = tied(qkv_weight, d2, x)
-        w_parts = [w_own] + [flipped(w_own, bits) for bits in (2, 4, 6)]
-        x_other = flipped(tied(x_local, r), 1)
+        w_own, x_in, r = lax.optimization_barrier((qkv_weight, x_local, r))
+        w_x, w_y = flipped(w_own, 2), flipped(w_own, 4)
+        x_other = flipped(x_in, 1)
     else:
         w_full = lax.all_gather(qkv_weight, "ctx", axis=0, tiled=True)
 
-    gq, gqt, kv_own, kv_d2, kv_r, kv_x = attention(
-        index.reshape(1), lengths, queries[0], out_grad[0], own, d2, r, x
-    )
+    grads = attention(index.reshape(1), lengths, queries[0], out_grad[0], own, d2, r, x)
+    if small:
+        *grads, w_x, w_y, x_other = lax.optimization_barrier((*grads, w_x, w_y, x_other))
+    gq, gqt, kv_own, kv_d2, kv_r, kv_x = grads
     kv_d2 = (kv_d2 + flipped(kv_r, 1)).astype(bf16)
     from_two = lax.ppermute(kv_d2, "ctx", back(by_two))
     from_x = lax.ppermute(kv_x, "ctx", back(mixed))
-    gkv, gkvt = finish_kv(kv_own, from_two, from_x)
 
     if small:
         places = jnp.stack([index // 2, index % 2])
         z = lax.axis_index("dp").reshape(1)
 
-        def reduced(gt, *after):
-            gt_other = tied(flipped(gt, 1), *after)
-            mine, *others = weight_partials(places, gt, gt_other, x_local, x_other, block)
-            others = [flipped(other, bits) for bits, other in zip((2, 4, 6), others)]
-            mine, *pieces = quarters_of(z, mine, others)
-            for k, piece in enumerate(pieces):
-                mine = mine + flipped(piece, k + 1, "dp").astype(f32)
-            mine = mine.astype(bf16)
-            return [mine] + [flipped(mine, k, "dp") for k in (1, 2, 3)]
-
-        parts = [reduced(gqt, *w_parts), reduced(gkvt)]
-        weight_sum = joined(z, parts)
-        w_blocks = [w for part in w_parts for w in (part, flipped(part, 1))]
-        grad_in = input_grad(places, gq, gkv, w_blocks)
+        def partials(gt):
+            return weight_partials(places, gt, flipped(gt, 1), x_local, x_other, block)
+
+        def sent(others):
+            return [flipped(other, bits) for bits, other in zip((2, 4, 6), others)]
+
+        def crossed(pieces):
+            return [flipped(piece, k + 1, "dp") for k, piece in enumerate(pieces)]
+
+        def added(mine, pieces):
+            for piece in pieces:
+                mine = mine + piece.astype(f32)
+            return mine.astype(bf16)
+
+        q_own, *q_others = partials(gqt)
+        kv_own, q_own, w_own, w_x, w_y = together(kv_own, q_own, w_own, w_x, w_y)
+        gkv, gkvt = finish_kv(kv_own, from_two, from_x)
+        q_others = sent(q_others)
+        kv_part, *kv_others = partials(gkvt)
+        w_blocks = [w for part in (w_own, w_x, w_y) for w in (part, flipped(part, 1))]
+        kv_others = sent(kv_others)
+        grad_in = input_grad(places, gq, gkv, w_blocks, 0)
+        *q_others, grad_in = together(*q_others, grad_in)
+        q_own, *q_pieces = quarters_of(z, q_own, q_others)
+        q_pieces = crossed(q_pieces)
+        *q_pieces, a, b, c, w_own = together(*q_pieces, *kv_others, w_own)
+        kv_part, *kv_pieces = quarters_of(z, kv_part, (a, b, c))
+        w_d = flipped(w_own, 6)
+        q_mine = added(q_own, q_pieces)
+        q_all = crossed([q_mine] * 3)
+        kv_pieces = crossed(kv_pieces)
+        *kv_pieces, a, b, c, w_d = together(*kv_pieces, *q_all, w_d)
+        kv_mine = added(kv_part, kv_pieces)
+        kv_all = crossed([kv_mine] * 3)
+        grad_in = input_grad(places, gq, gkv, (w_d, flipped(w_d, 1)), 6, grad_in)
+        *kv_all, grad_in = together(*kv_all, grad_in)
+        weight_sum = joined(z, [(q_mine, a, b, c), (kv_mine, *kv_all)])
     else:
+        gkv, _ = finish_kv(kv_own, from_two, from_x)
         grad_qkv = jnp.concatenate([gq, gkv], axis=1)
         grad_in = nt_dot(grad_qkv, w_full).astype(bf16)
         partial = lax.dot_general(

time: 209 us -> 156 us (0.75)
  waiting for transfers between devices: 98.7 us -> 55.9 us
  starting transfers between devices: 57.7 us -> 47.6 us
  local copies, waits for them, and re-layouts: 12.5 us -> 3.9 us
  Pallas kernels: 36.6 us -> 43.6 us
    ppermute x30, waiting for transfers between devices: 83.7 us -> 49.7 us  [flipped(): lax.ppermute(array, axis, [(i, i ^ bits) for i in range(lax.axis_size(axi...]
    ppermute x30, starting transfers between devices: 48 us -> 38.3 us  [flipped(): lax.ppermute(array, axis, [(i, i ^ bits) for i in range(lax.axis_size(axi...]
    unnamed x52 -> x48, local copies, waits for them, and re-layouts: 12.5 us -> 3.9 us
    ppermute x1, waiting for transfers between devices: 5.08 us -> 0.01 us  [per_device(): x = lax.ppermute(own, 'ctx', mixed)]
    ppermute x1, waiting for transfers between devices: 4.13 us -> 0.01 us  [per_device(): from_two = lax.ppermute(kv_d2, 'ctx', back(by_two))]
    pallas_call x1 -> x2, Pallas kernels: 9 us -> 12.6 us  [input_grad(): pl.pallas_call(functools.partial(input_kernel, count=count), name='input_...]
  transfers between devices with their start and end apart: 34 -> 34, of which waited for: 13 -> 11; matrix products, arithmetic and copies ran while one was open for 1% -> 2% of each run, Pallas kernels for 14% -> 27%
where the time goes in v3:
time: 156 us
  waiting for transfers between devices  55.9 us (36%)
  starting transfers between devices  47.6 us (31%)
  Pallas kernels  43.6 us (28%)
  local copies, waits for them, and re-layouts  3.9 us (2%)
  other arithmetic  3.85 us (2%)
    ppermute x30, waiting for transfers between devices, flipped(): lax.ppermute(array, axis, [(i, i ^ bits) for i in range(lax.axis_size(axi...  49.7 us
    ppermute x30, starting transfers between devices, flipped(): lax.ppermute(array, axis, [(i, i ^ bits) for i in range(lax.axis_size(axi...  38.3 us
    pallas_call x2, Pallas kernels, weight_partials(): pl.pallas_call(weight_kernel, name='weight_partials', out_shape=[jax.Shap...  13.2 us
    pallas_call x2, Pallas kernels, input_grad(): pl.pallas_call(functools.partial(input_kernel, count=count), name='input_...  12.6 us
    pallas_call x1, Pallas kernels, attention(): pl.pallas_call(attention_kernel, name='attention', out_shape=(jax.ShapeDt...  8.66 us
    ppermute x1, waiting for transfers between devices, per_device(): d2 = lax.ppermute(own, 'ctx', by_two)  6.17 us
    pallas_call x2, Pallas kernels, quarters_of(): pl.pallas_call(quarters_kernel, name='quarters', out_shape=[jax.ShapeDtyp...  4.67 us
    ppermute x1, starting transfers between devices, per_device(): d2 = lax.ppermute(own, 'ctx', by_two)  4.24 us
  transfers between devices with their start and end apart: 34, of which 11 were waited for; matrix products, arithmetic and copies ran while one was open for 2% of the time, Pallas kernels for 27%

profile of v3, /device:TPU:0, one launch (start us, length us, event | category | flops | bytes accessed | tf_op | source)
XLA Modules:
  0.0 155.8 jit_solution(5733532138542320900)
XLA Ops:
  0.6 2.4 %collective-permute-start.1 = (bf16[512,256]{1,0:T(8,128)(2,1)}, bf16[512,256]{1,0:T(8,128)(2,1)S(1)}, u32[]{:S(2)}, u32[]{:S(2)}) collective-permute-start(bf16[512,256]{1,0:T(8,128)(2,1)} %bitcast.19), channel_id=1, source_target_pairs={{0,1},{2,3},{4,5},{6,7},{1,4},{3,6},{8,9},{10,11},{12,13},{14,15},... | collective-permute-start | bytes 786440 | tf_op jit(solution)/shard_map/ppermute | solution.py:332
  3.0 4.2 %collective-permute-start = (bf16[512,256]{1,0:T(8,128)(2,1)}, bf16[512,256]{1,0:T(8,128)(2,1)S(1)}, u32[]{:S(2)}, u32[]{:S(2)}) collective-permute-start(bf16[512,256]{1,0:T(8,128)(2,1)} %bitcast.20), channel_id=1, source_target_pairs={{0,2},{1,3},{2,4},{3,5},{4,6},{5,7},{8,10},{9,11},{10,12},{11,13},... | collective-permute-start | bytes 786440 | tf_op jit(solution)/shard_map/ppermute | solution.py:331
  7.3 6.2 %collective-permute-done.d2_ref = bf16[512,256]{1,0:T(8,128)(2,1)S(1)} collective-permute-done((bf16[512,256]{1,0:T(8,128)(2,1)}, bf16[512,256]{1,0:T(8,128)(2,1)S(1)}, u32[]{:S(2)}, u32[]{:S(2)}) %collective-permute-start) | collective-permute-done | bytes 262176 | tf_op jit(solution)/shard_map/ppermute | solution.py:331
  13.4 0.9 collective-permute-start.2
  14.4 1.2 collective-permute-done.2.r_ref
  15.5 0.4 collective-permute-start.5
  15.9 3.0 %collective-permute-start.4 = (bf16[512,768]{1,0:T(8,128)(2,1)}, bf16[512,768]{1,0:T(8,128)(2,1)S(1)}, u32[]{:S(2)}, u32[]{:S(2)}) collective-permute-start(bf16[512,768]{1,0:T(8,128)(2,1)} %refs_0_), channel_id=1, source_target_pairs={{0,4},{1,5},{2,6},{3,7},{4,0},{5,1},{6,2},{7,3},{8,12},{9,13},{10,... | collective-permute-start | bytes 2359304 | tf_op jit(solution)/shard_map/ppermute | solution.py:309
  18.9 0.0 collective-permute-start.3
  18.9 8.7 %attention.1 = (bf16[512,512]{1,0:T(8,128)(2,1)}, bf16[512,512]{1,0:T(8,128)(2,1)}, f32[512,256]{1,0:T(8,128)}, f32[512,256]{1,0:T(8,128)}, f32[512,256]{1,0:T(8,128)}, /*index=5*/bf16[512,256]{1,0:T(8,128)(2,1)}) custom-call(s32[1]{0:T(128)} %bitcast.idx_ref, s32[1,16]{1,0:T(1,128)} %len_ref.1, bf16[512,512]{1,0:T(8,128)(2,1)} %bitcast.17, ...), custom_call_target="tpu_custom_call" | custom-call | flops 12000000000 | bytes 6291456 | tf_op jit(solution)/shard_map/attention/pallas_call | solution.py:125
  27.5 9.6 %collective-permute-done.4.refs_4_ = bf16[512,768]{1,0:T(8,128)(2,1)S(1)} collective-permute-done((bf16[512,768]{1,0:T(8,128)(2,1)}, bf16[512,768]{1,0:T(8,128)(2,1)S(1)}, u32[]{:S(2)}, u32[]{:S(2)}) %collective-permute-start.4) | collective-permute-done | bytes 786464 | tf_op jit(solution)/shard_map/ppermute | solution.py:309
  37.1 1.5 collective-permute-done.3.refs_2_
  38.6 0.5 collective-permute-start.6
  39.1 0.7 pad_add_fusion.places
  39.8 1.3 collective-permute-start.9
  41.1 1.1 add_convert_fusion
  42.2 0.0 copy-start
  42.2 1.4 collective-permute-start.8
  43.6 0.8 copy-done.7
  44.4 7.4 %weight_partials.2 = (f32[512,512]{1,0:T(8,128)}, bf16[512,512]{1,0:T(8,128)(2,1)}, bf16[512,512]{1,0:T(8,128)(2,1)}, bf16[512,512]{1,0:T(8,128)(2,1)}) custom-call(s32[2]{0:T(128)} %pad_add_fusion.places, bf16[512,512]{1,0:T(8,128)(2,1)} %get-tuple-element.82.gt_ref, bf16[512,512]{1,0:T(8,128)(2,1)} %copy-done.7, bf16[512,4096]{1,0:T(8,128)(2,1)} %bitcast.12, ...), custom_call_target="tpu_custom_call" | custom-call | flops 2147483648 | bytes 8388608 | tf_op jit(solution)/shard_map/weight_partials/pallas_call | solution.py:169
  51.8 4.3 %collective-permute-start.11 = (bf16[512,512]{1,0:T(8,128)(2,1)}, bf16[512,512]{1,0:T(8,128)(2,1)}, u32[]{:S(2)}, u32[]{:S(2)}) collective-permute-start(bf16[512,512]{1,0:T(8,128)(2,1)} %get-tuple-element.95), channel_id=1, source_target_pairs={{0,2},{1,3},{2,0},{3,1},{4,6},{5,7},{6,4},{7,5},{8,10},{9,11},{10,... | collective-permute-start | bytes 1572872 | tf_op jit(solution)/shard_map/ppermute | solution.py:309
  56.1 0.9 collective-permute-start.15
  57.0 0.1 collective-permute-start.16
  57.1 0.5 collective-permute-start.14
  57.6 0.2 copy-done.14
  57.8 2.1 %finish_kv.1 = (bf16[512,256]{1,0:T(8,128)(2,1)}, bf16[256,512]{1,0:T(8,128)(2,1)}) custom-call(f32[512,256]{1,0:T(8,128)} %get-tuple-element.87.own_ref, bf16[512,256]{1,0:T(8,128)(2,1)} %collective-permute-done.8.two_ref, bf16[512,256]{1,0:T(8,128)(2,1)} %copy-done.14), custom_call_target="tpu_custom_call" | custom-call | flops 524288 | bytes 2097152 | tf_op jit(solution)/shard_map/finish_kv/pallas_call | solution.py:239
  59.9 0.4 collective-permute-start.10
  60.3 8.5 %collective-permute-done.11.a_ref = bf16[512,512]{1,0:T(8,128)(2,1)} collective-permute-done((bf16[512,512]{1,0:T(8,128)(2,1)}, bf16[512,512]{1,0:T(8,128)(2,1)}, u32[]{:S(2)}, u32[]{:S(2)}) %collective-permute-start.11) | collective-permute-done | bytes 524320 | tf_op jit(solution)/shard_map/ppermute | solution.py:309
  68.8 3.8 %collective-permute-start.12 = (bf16[512,512]{1,0:T(8,128)(2,1)}, bf16[512,512]{1,0:T(8,128)(2,1)}, u32[]{:S(2)}, u32[]{:S(2)}) collective-permute-start(bf16[512,512]{1,0:T(8,128)(2,1)} %get-tuple-element.96), channel_id=1, source_target_pairs={{0,4},{1,5},{2,6},{3,7},{4,0},{5,1},{6,2},{7,3},{8,12},{9,13},{10,... | collective-permute-start | bytes 1572872 | tf_op jit(solution)/shard_map/ppermute | solution.py:309
  72.6 0.7 copy-done.12
  73.3 5.9 %weight_partials.3 = (f32[256,512]{1,0:T(8,128)}, bf16[256,512]{1,0:T(8,128)(2,1)}, bf16[256,512]{1,0:T(8,128)(2,1)}, bf16[256,512]{1,0:T(8,128)(2,1)}) custom-call(s32[2]{0:T(128)} %pad_add_fusion.places, bf16[256,512]{1,0:T(8,128)(2,1)} %get-tuple-element.92.gt_ref, bf16[256,512]{1,0:T(8,128)(2,1)} %copy-done.12, bf16[512,4096]{1,0:T(8,128)(2,1)} %bitcast.13, ...), custom_call_target="tpu_custom_call" | custom-call | flops 1073741824 | bytes 8388608 | tf_op jit(solution)/shard_map/weight_partials/pallas_call | solution.py:169
  79.1 0.9 collective-permute-start.20
  80.1 2.0 %collective-permute-start.21 = (bf16[256,512]{1,0:T(8,128)(2,1)}, bf16[256,512]{1,0:T(8,128)(2,1)S(1)}, u32[]{:S(2)}, u32[]{:S(2)}) collective-permute-start(bf16[256,512]{1,0:T(8,128)(2,1)} %get-tuple-element.108), channel_id=1, source_target_pairs={{0,4},{1,5},{2,6},{3,7},{4,0},{5,1},{6,2},{7,3},{8,12},{9,13},{10,... | collective-permute-start | bytes 786440 | tf_op jit(solution)/shard_map/ppermute | solution.py:309
  82.0 0.7 collective-permute-start.22
  82.7 8.3 %input_grad.2.refs_2_ = bf16[512,4096]{1,0:T(8,128)(2,1)} custom-call(s32[2]{0:T(128)} %pad_add_fusion.places, bf16[512,512]{1,0:T(8,128)(2,1)} %get-tuple-element.80.gq_ref, bf16[512,256]{1,0:T(8,128)(2,1)} %get-tuple-element.91.gkv_ref, bf16[512,768]{1,0:T(8,128)(2,1)} %refs_0_, bf16[512,768]{1,0:T(8,128)(2,1)} %collective-permute-done.14.refs_1_, ...), custom_call_target="tpu_custom_call" | custom-call | flops 2415919104 | bytes 11534336 | tf_op jit(solution)/shard_map/input_grad/pallas_call | solution.py:211
  91.0 11.4 %collective-permute-done.12.b_ref = bf16[512,512]{1,0:T(8,128)(2,1)} collective-permute-done((bf16[512,512]{1,0:T(8,128)(2,1)}, bf16[512,512]{1,0:T(8,128)(2,1)}, u32[]{:S(2)}, u32[]{:S(2)}) %collective-permute-start.12) | collective-permute-done | bytes 524320 | tf_op jit(solution)/shard_map/ppermute | solution.py:309
  102.5 2.6 %quarters.2 = (f32[128,512]{1,0:T(8,128)}, bf16[128,512]{1,0:T(8,128)(2,1)}, bf16[128,512]{1,0:T(8,128)(2,1)}, bf16[128,512]{1,0:T(8,128)(2,1)}) custom-call(s32[1]{0:T(128)} %bitcast.9.z_ref, f32[512,512]{1,0:T(8,128)} %get-tuple-element.94.own_ref, bf16[512,512]{1,0:T(8,128)(2,1)} %collective-permute-done.11.a_ref, ...), custom_call_target="tpu_custom_call" | custom-call | flops 1048576 | bytes 2097152 | tf_op jit(solution)/shard_map/quarters/pallas_call | solution.py:266
  105.1 1.6 %collective-permute-start.17 = (bf16[128,512]{1,0:T(8,128)(2,1)}, bf16[128,512]{1,0:T(8,128)(2,1)S(1)}, u32[]{:S(2)}, u32[]{:S(2)}) collective-permute-start(bf16[128,512]{1,0:T(8,128)(2,1)} %get-tuple-element.104), channel_id=1, source_target_pairs={{0,8},{8,0},{16,24},{24,16},{1,9},{9,1},{17,25},{25,17},{2,10},{10... | collective-permute-start | bytes 393224 | tf_op jit(solution)/shard_map/ppermute | solution.py:309
  106.6 2.6 %collective-permute-start.18 = (bf16[128,512]{1,0:T(8,128)(2,1)}, bf16[128,512]{1,0:T(8,128)(2,1)S(1)}, u32[]{:S(2)}, u32[]{:S(2)}) collective-permute-start(bf16[128,512]{1,0:T(8,128)(2,1)} %get-tuple-element.105), channel_id=1, source_target_pairs={{0,16},{8,24},{16,0},{24,8},{1,17},{9,25},{17,1},{25,9},{2,18},{10... | collective-permute-start | bytes 393224 | tf_op jit(solution)/shard_map/ppermute | solution.py:309
  109.2 0.2 collective-permute-start.19
  109.5 2.2 %collective-permute-done.17 = bf16[128,512]{1,0:T(8,128)(2,1)S(1)} collective-permute-done((bf16[128,512]{1,0:T(8,128)(2,1)}, bf16[128,512]{1,0:T(8,128)(2,1)S(1)}, u32[]{:S(2)}, u32[]{:S(2)}) %collective-permute-start.17) | collective-permute-done | bytes 131104 | tf_op jit(solution)/shard_map/ppermute | solution.py:309
  111.7 7.0 %collective-permute-done.18 = bf16[128,512]{1,0:T(8,128)(2,1)S(1)} collective-permute-done((bf16[128,512]{1,0:T(8,128)(2,1)}, bf16[128,512]{1,0:T(8,128)(2,1)S(1)}, u32[]{:S(2)}, u32[]{:S(2)}) %collective-permute-start.18) | collective-permute-done | bytes 131104 | tf_op jit(solution)/shard_map/ppermute | solution.py:309
  118.8 2.1 %quarters.3 = (f32[64,512]{1,0:T(8,128)}, bf16[64,512]{1,0:T(8,128)(2,1)}, bf16[64,512]{1,0:T(8,128)(2,1)}, bf16[64,512]{1,0:T(8,128)(2,1)}) custom-call(s32[1]{0:T(128)} %bitcast.9.z_ref, f32[256,512]{1,0:T(8,128)} %get-tuple-element.93.own_ref, bf16[256,512]{1,0:T(8,128)(2,1)} %copy-done.9, bf16[256,512]{1,0:T(8,128)(2,1)} %copy-done.10, ...), custom_call_target="tpu_custom_call" | custom-call | flops 524288 | bytes 2097152 | tf_op jit(solution)/shard_map/quarters/pallas_call | solution.py:266
  120.9 2.0 %collective-permute-start.23 = (bf16[64,512]{1,0:T(8,128)(2,1)}, bf16[64,512]{1,0:T(8,128)(2,1)S(1)}, u32[]{:S(2)}, u32[]{:S(2)}) collective-permute-start(bf16[64,512]{1,0:T(8,128)(2,1)} %get-tuple-element.114), channel_id=1, source_target_pairs={{0,8},{8,0},{16,24},{24,16},{1,9},{9,1},{17,25},{25,17},{2,10},{10... | collective-permute-start | bytes 196616 | tf_op jit(solution)/shard_map/ppermute | solution.py:309
  122.8 1.1 collective-permute-start.24
  123.9 1.0 add_convert_fusion.1.refs_0_
  124.9 1.5 collective-permute-start.28
  126.4 2.0 %collective-permute-start.27 = (bf16[128,512]{1,0:T(8,128)(2,1)S(1)}, bf16[128,512]{1,0:T(8,128)(2,1)S(1)}, u32[]{:S(2)}, u32[]{:S(2)}) collective-permute-start(bf16[128,512]{1,0:T(8,128)(2,1)S(1)} %add_convert_fusion.1.refs_0_), channel_id=1, source_target_pairs={{0,16},{8,24},{16,0},{24,8},{1,17},{9,25},{17,1},{25,9},{2,18},{10... | collective-permute-start | bytes 393224 | tf_op jit(solution)/shard_map/ppermute | solution.py:309
  128.4 1.0 collective-permute-start.26
  129.4 4.6 %collective-permute-done.24 = bf16[64,512]{1,0:T(8,128)(2,1)S(1)} collective-permute-done((bf16[64,512]{1,0:T(8,128)(2,1)}, bf16[64,512]{1,0:T(8,128)(2,1)S(1)}, u32[]{:S(2)}, u32[]{:S(2)}) %collective-permute-start.24) | collective-permute-done | bytes 65568 | tf_op jit(solution)/shard_map/ppermute | solution.py:309
  134.0 3.6 %collective-permute-start.25 = (bf16[64,512]{1,0:T(8,128)(2,1)}, bf16[64,512]{1,0:T(8,128)(2,1)S(1)}, u32[]{:S(2)}, u32[]{:S(2)}) collective-permute-start(bf16[64,512]{1,0:T(8,128)(2,1)} %get-tuple-element.116), channel_id=1, source_target_pairs={{0,24},{8,16},{16,8},{24,0},{1,25},{9,17},{17,9},{25,1},{2,26},{10... | collective-permute-start | bytes 196616 | tf_op jit(solution)/shard_map/ppermute | solution.py:309
  137.6 2.8 %collective-permute-done.25 = bf16[64,512]{1,0:T(8,128)(2,1)S(1)} collective-permute-done((bf16[64,512]{1,0:T(8,128)(2,1)}, bf16[64,512]{1,0:T(8,128)(2,1)S(1)}, u32[]{:S(2)}, u32[]{:S(2)}) %collective-permute-start.25) | collective-permute-done | bytes 65568 | tf_op jit(solution)/shard_map/ppermute | solution.py:309
  140.4 0.8 collective-permute-done.27.refs_2_
  141.2 0.0 copy-start.5
  141.2 0.1 collective-permute-start.33
  141.3 1.1 add_convert_fusion.2.refs_4_
  142.4 2.8 %collective-permute-start.32 = (bf16[64,512]{1,0:T(8,128)(2,1)S(1)}, bf16[64,512]{1,0:T(8,128)(2,1)S(1)}, u32[]{:S(2)}, u32[]{:S(2)}) collective-permute-start(bf16[64,512]{1,0:T(8,128)(2,1)S(1)} %add_convert_fusion.2.refs_4_), channel_id=1, source_target_pairs={{0,24},{8,16},{16,8},{24,0},{1,25},{9,17},{17,9},{25,1},{2,26},{10... | collective-permute-start | bytes 196616 | tf_op jit(solution)/shard_map/ppermute | solution.py:309
  145.2 0.0 collective-permute-start.31
  145.3 1.6 %collective-permute-start.30 = (bf16[64,512]{1,0:T(8,128)(2,1)S(1)}, bf16[64,512]{1,0:T(8,128)(2,1)S(1)}, u32[]{:S(2)}, u32[]{:S(2)}) collective-permute-start(bf16[64,512]{1,0:T(8,128)(2,1)S(1)} %add_convert_fusion.2.refs_4_), channel_id=1, source_target_pairs={{0,8},{8,0},{16,24},{24,16},{1,9},{9,1},{17,25},{25,17},{2,10},{10... | collective-permute-start | bytes 196616 | tf_op jit(solution)/shard_map/ppermute | solution.py:309
  146.9 0.9 copy-done.6
  147.8 4.3 %input_grad.3 = bf16[512,4096]{1,0:T(8,128)(2,1)} custom-call(s32[2]{0:T(128)} %pad_add_fusion.places, bf16[512,512]{1,0:T(8,128)(2,1)} %get-tuple-element.80.gq_ref, bf16[512,256]{1,0:T(8,128)(2,1)} %get-tuple-element.91.gkv_ref, bf16[512,768]{1,0:T(8,128)(2,1)} %copy-done.5, bf16[512,768]{1,0:T(8,128)(2,1)} %copy-done.6, ...), custom_call_target="tpu_custom_call", output_to_operand_aliasing={{}: (5, {})} | custom-call | flops 805306368 | bytes 11534336 | tf_op jit(solution)/shard_map/input_grad/pallas_call | solution.py:211
  152.2 0.6 copy-done.18
  152.8 0.0 copy-done.19
  152.8 0.6 copy-done.20
  153.4 2.4 %joined.1 = bf16[512,768]{1,0:T(8,128)(2,1)} custom-call(s32[1]{0:T(128)} %bitcast.9.z_ref, bf16[128,512]{1,0:T(8,128)(2,1)} %copy-done.8, bf16[128,512]{1,0:T(8,128)(2,1)} %copy-done.17, bf16[128,512]{1,0:T(8,128)(2,1)} %copy-done.16, bf16[128,512]{1,0:T(8,128)(2,1)} %copy-done.15, bf16[64,512]{1,0:T(8,128)(2,1)} %copy-done.13, bf16[64,512]{1,0:T(8,128)(2,1)} %copy-done.20, ...), custom_call_target="tpu_custom_call" | custom-call | flops 393216 | bytes 2097152 | tf_op jit(solution)/shard_map/joined/pallas_call | solution.py:295
  (65 shorter events, 0.1 us)
Async XLA Ops:
  0.6 6.6 %collective-permute-start.1 = (bf16[512,256]{1,0:T(8,128)(2,1)}, bf16[512,256]{1,0:T(8,128)(2,1)S(1)}, u32[]{:S(2)}, u32[]{:S(2)}) collective-permute-start(bf16[512,256]{1,0:T(8,128)(2,1)} %bitcast.19), channel_id=1, source_target_pairs={{0,1},{2,3},{4,5},{6,7},{1,4},{3,6},{8,9},{10,11},{12,13},{14,15},... | collective-permute-start | bytes 786440 | tf_op jit(solution)/shard_map/ppermute | solution.py:332
  3.0 10.4 %collective-permute-start = (bf16[512,256]{1,0:T(8,128)(2,1)}, bf16[512,256]{1,0:T(8,128)(2,1)S(1)}, u32[]{:S(2)}, u32[]{:S(2)}) collective-permute-start(bf16[512,256]{1,0:T(8,128)(2,1)} %bitcast.20), channel_id=1, source_target_pairs={{0,2},{1,3},{2,4},{3,5},{4,6},{5,7},{8,10},{9,11},{10,12},{11,13},... | collective-permute-start | bytes 786440 | tf_op jit(solution)/shard_map/ppermute | solution.py:331
  7.3 11.6 %copy-start.21 = (bf16[512,256]{1,0:T(8,128)(2,1)}, bf16[512,256]{1,0:T(8,128)(2,1)S(1)}, u32[]{:S(2)}) copy-start(bf16[512,256]{1,0:T(8,128)(2,1)S(1)} %collective-permute-done.1.x_ref) | copy-start | bytes 786436
  13.4 5.4 %copy-start.22 = (bf16[512,256]{1,0:T(8,128)(2,1)}, bf16[512,256]{1,0:T(8,128)(2,1)S(1)}, u32[]{:S(2)}) copy-start(bf16[512,256]{1,0:T(8,128)(2,1)S(1)} %collective-permute-done.d2_ref) | copy-start | bytes 786436
  13.4 2.1 %collective-permute-start.2 = (bf16[512,256]{1,0:T(8,128)(2,1)S(1)}, bf16[512,256]{1,0:T(8,128)(2,1)S(1)}, u32[]{:S(2)}, u32[]{:S(2)}) collective-permute-start(bf16[512,256]{1,0:T(8,128)(2,1)S(1)} %collective-permute-done.d2_ref), channel_id=1, source_target_pairs={{0,1},{1,0},{2,3},{3,2},{4,5},{5,4},{6,7},{7,6},{8,9},{9,8},{10,11... | collective-permute-start | bytes 786440 | tf_op jit(solution)/shard_map/ppermute | solution.py:309
  15.5 3.3 %copy-start.23 = (bf16[512,256]{1,0:T(8,128)(2,1)}, bf16[512,256]{1,0:T(8,128)(2,1)S(1)}, u32[]{:S(2)}) copy-start(bf16[512,256]{1,0:T(8,128)(2,1)S(1)} %collective-permute-done.2.r_ref) | copy-start | bytes 786436
  15.5 23.1 %collective-permute-start.5 = (bf16[512,4096]{1,0:T(8,128)(2,1)}, bf16[512,4096]{1,0:T(8,128)(2,1)}, u32[]{:S(2)}, u32[]{:S(2)}) collective-permute-start(bf16[512,4096]{1,0:T(8,128)(2,1)} %bitcast.11), channel_id=1, source_target_pairs={{0,1},{1,0},{2,3},{3,2},{4,5},{5,4},{6,7},{7,6},{8,9},{9,8},{10,11... | collective-permute-start | bytes 12582920 | tf_op jit(solution)/shard_map/ppermute | solution.py:309
  15.9 21.2 %collective-permute-start.4 = (bf16[512,768]{1,0:T(8,128)(2,1)}, bf16[512,768]{1,0:T(8,128)(2,1)S(1)}, u32[]{:S(2)}, u32[]{:S(2)}) collective-permute-start(bf16[512,768]{1,0:T(8,128)(2,1)} %refs_0_), channel_id=1, source_target_pairs={{0,4},{1,5},{2,6},{3,7},{4,0},{5,1},{6,2},{7,3},{8,12},{9,13},{10,... | collective-permute-start | bytes 2359304 | tf_op jit(solution)/shard_map/ppermute | solution.py:309
  18.9 19.7 %collective-permute-start.3 = (bf16[512,768]{1,0:T(8,128)(2,1)}, bf16[512,768]{1,0:T(8,128)(2,1)S(1)}, u32[]{:S(2)}, u32[]{:S(2)}) collective-permute-start(bf16[512,768]{1,0:T(8,128)(2,1)} %refs_0_), channel_id=1, source_target_pairs={{0,2},{1,3},{2,0},{3,1},{4,6},{5,7},{6,4},{7,5},{8,10},{9,11},{10,... | collective-permute-start | bytes 2359304 | tf_op jit(solution)/shard_map/ppermute | solution.py:309
  37.1 19.9 %copy-start.2 = (bf16[512,768]{1,0:T(8,128)(2,1)}, bf16[512,768]{1,0:T(8,128)(2,1)S(1)}, u32[]{:S(2)}) copy-start(bf16[512,768]{1,0:T(8,128)(2,1)S(1)} %collective-permute-done.4.refs_4_) | copy-start | bytes 2359300
  38.6 17.5 %copy-start.3 = (bf16[512,768]{1,0:T(8,128)(2,1)}, bf16[512,768]{1,0:T(8,128)(2,1)S(1)}, u32[]{:S(2)}) copy-start(bf16[512,768]{1,0:T(8,128)(2,1)S(1)} %collective-permute-done.3.refs_2_) | copy-start | bytes 2359300
  38.6 2.5 %collective-permute-start.7 = (f32[512,256]{1,0:T(8,128)}, f32[512,256]{1,0:T(8,128)S(1)}, u32[]{:S(2)}, u32[]{:S(2)}) collective-permute-start(f32[512,256]{1,0:T(8,128)} %get-tuple-element.89), channel_id=1, source_target_pairs={{0,1},{1,0},{2,3},{3,2},{4,5},{5,4},{6,7},{7,6},{8,9},{9,8},{10,11... | collective-permute-start | bytes 1572872 | tf_op jit(solution)/shard_map/ppermute | solution.py:309
  38.6 5.0 %collective-permute-start.6 = (bf16[512,512]{1,0:T(8,128)(2,1)}, bf16[512,512]{1,0:T(8,128)(2,1)S(1)}, u32[]{:S(2)}, u32[]{:S(2)}) collective-permute-start(bf16[512,512]{1,0:T(8,128)(2,1)} %get-tuple-element.82.gt_ref), channel_id=1, source_target_pairs={{0,1},{1,0},{2,3},{3,2},{4,5},{5,4},{6,7},{7,6},{8,9},{9,8},{10,11... | collective-permute-start | bytes 1572872 | tf_op jit(solution)/shard_map/ppermute | solution.py:309
  39.8 17.3 %collective-permute-start.9 = (bf16[512,256]{1,0:T(8,128)(2,1)}, bf16[512,256]{1,0:T(8,128)(2,1)S(1)}, u32[]{:S(2)}, u32[]{:S(2)}) collective-permute-start(bf16[512,256]{1,0:T(8,128)(2,1)} %get-tuple-element.90), channel_id=1, source_target_pairs={{1,0},{3,2},{5,4},{7,6},{4,1},{6,3},{9,8},{11,10},{13,12},{15,14},... | collective-permute-start | bytes 786440 | tf_op jit(solution)/shard_map/ppermute | solution.py:348
  42.2 14.9 %copy-start = (bf16[512,768]{1,0:T(8,128)(2,1)S(1)}, bf16[512,768]{1,0:T(8,128)(2,1)}, u32[]{:S(2)}) copy-start(bf16[512,768]{1,0:T(8,128)(2,1)} %refs_0_) | copy-start | bytes 2359300
  42.2 15.4 %collective-permute-start.8 = (bf16[512,256]{1,0:T(8,128)(2,1)S(1)}, bf16[512,256]{1,0:T(8,128)(2,1)}, u32[]{:S(2)}, u32[]{:S(2)}) collective-permute-start(bf16[512,256]{1,0:T(8,128)(2,1)S(1)} %add_convert_fusion), channel_id=1, source_target_pairs={{2,0},{3,1},{4,2},{5,3},{6,4},{7,5},{10,8},{11,9},{12,10},{13,11},... | collective-permute-start | bytes 786440 | tf_op jit(solution)/shard_map/ppermute | solution.py:347
  43.6 0.8 copy-start.7
  51.8 17.0 %collective-permute-start.11 = (bf16[512,512]{1,0:T(8,128)(2,1)}, bf16[512,512]{1,0:T(8,128)(2,1)}, u32[]{:S(2)}, u32[]{:S(2)}) collective-permute-start(bf16[512,512]{1,0:T(8,128)(2,1)} %get-tuple-element.95), channel_id=1, source_target_pairs={{0,2},{1,3},{2,0},{3,1},{4,6},{5,7},{6,4},{7,5},{8,10},{9,11},{10,... | collective-permute-start | bytes 1572872 | tf_op jit(solution)/shard_map/ppermute | solution.py:309
  56.1 23.0 %collective-permute-start.15 = (bf16[512,768]{1,0:T(8,128)(2,1)S(1)}, bf16[512,768]{1,0:T(8,128)(2,1)S(1)}, u32[]{:S(2)}, u32[]{:S(2)}) collective-permute-start(bf16[512,768]{1,0:T(8,128)(2,1)S(1)} %collective-permute-done.3.refs_2_), channel_id=1, source_target_pairs={{0,1},{1,0},{2,3},{3,2},{4,5},{5,4},{6,7},{7,6},{8,9},{9,8},{10,11... | collective-permute-start | bytes 2359304 | tf_op jit(solution)/shard_map/ppermute | solution.py:309
  57.0 23.0 %collective-permute-start.16 = (bf16[512,768]{1,0:T(8,128)(2,1)S(1)}, bf16[512,768]{1,0:T(8,128)(2,1)}, u32[]{:S(2)}, u32[]{:S(2)}) collective-permute-start(bf16[512,768]{1,0:T(8,128)(2,1)S(1)} %collective-permute-done.4.refs_4_), channel_id=1, source_target_pairs={{0,1},{1,0},{2,3},{3,2},{4,5},{5,4},{6,7},{7,6},{8,9},{9,8},{10,11... | collective-permute-start | bytes 2359304 | tf_op jit(solution)/shard_map/ppermute | solution.py:309
  57.1 0.7 copy-start.14
  57.1 24.9 %collective-permute-start.14 = (bf16[512,768]{1,0:T(8,128)(2,1)S(1)}, bf16[512,768]{1,0:T(8,128)(2,1)}, u32[]{:S(2)}, u32[]{:S(2)}) collective-permute-start(bf16[512,768]{1,0:T(8,128)(2,1)S(1)} %copy-done), channel_id=1, source_target_pairs={{0,1},{1,0},{2,3},{3,2},{4,5},{5,4},{6,7},{7,6},{8,9},{9,8},{10,11... | collective-permute-start | bytes 2359304 | tf_op jit(solution)/shard_map/ppermute | solution.py:309
  59.9 12.7 %collective-permute-start.10 = (bf16[256,512]{1,0:T(8,128)(2,1)}, bf16[256,512]{1,0:T(8,128)(2,1)S(1)}, u32[]{:S(2)}, u32[]{:S(2)}) collective-permute-start(bf16[256,512]{1,0:T(8,128)(2,1)} %get-tuple-element.92.gt_ref), channel_id=1, source_target_pairs={{0,1},{1,0},{2,3},{3,2},{4,5},{5,4},{6,7},{7,6},{8,9},{9,8},{10,11... | collective-permute-start | bytes 786440 | tf_op jit(solution)/shard_map/ppermute | solution.py:309
  68.8 33.7 %collective-permute-start.12 = (bf16[512,512]{1,0:T(8,128)(2,1)}, bf16[512,512]{1,0:T(8,128)(2,1)}, u32[]{:S(2)}, u32[]{:S(2)}) collective-permute-start(bf16[512,512]{1,0:T(8,128)(2,1)} %get-tuple-element.96), channel_id=1, source_target_pairs={{0,4},{1,5},{2,6},{3,7},{4,0},{5,1},{6,2},{7,3},{8,12},{9,13},{10,... | collective-permute-start | bytes 1572872 | tf_op jit(solution)/shard_map/ppermute | solution.py:309
  72.6 0.7 copy-start.12
  72.6 29.9 %collective-permute-start.13 = (bf16[512,512]{1,0:T(8,128)(2,1)}, bf16[512,512]{1,0:T(8,128)(2,1)}, u32[]{:S(2)}, u32[]{:S(2)}) collective-permute-start(bf16[512,512]{1,0:T(8,128)(2,1)} %get-tuple-element.97), channel_id=1, source_target_pairs={{0,6},{1,7},{2,4},{3,5},{4,2},{5,3},{6,0},{7,1},{8,14},{9,15},{10,... | collective-permute-start | bytes 1572872 | tf_op jit(solution)/shard_map/ppermute | solution.py:309
  79.1 3.6 %copy-start.4 = (bf16[512,768]{1,0:T(8,128)(2,1)}, bf16[512,768]{1,0:T(8,128)(2,1)S(1)}, u32[]{:S(2)}) copy-start(bf16[512,768]{1,0:T(8,128)(2,1)S(1)} %collective-permute-done.15.refs_3_) | copy-start | bytes 2359300
  79.1 30.1 %collective-permute-start.20 = (bf16[256,512]{1,0:T(8,128)(2,1)}, bf16[256,512]{1,0:T(8,128)(2,1)S(1)}, u32[]{:S(2)}, u32[]{:S(2)}) collective-permute-start(bf16[256,512]{1,0:T(8,128)(2,1)} %get-tuple-element.107), channel_id=1, source_target_pairs={{0,2},{1,3},{2,0},{3,1},{4,6},{5,7},{6,4},{7,5},{8,10},{9,11},{10,... | collective-permute-start | bytes 786440 | tf_op jit(solution)/shard_map/ppermute | solution.py:309
  80.1 29.4 %collective-permute-start.21 = (bf16[256,512]{1,0:T(8,128)(2,1)}, bf16[256,512]{1,0:T(8,128)(2,1)S(1)}, u32[]{:S(2)}, u32[]{:S(2)}) collective-permute-start(bf16[256,512]{1,0:T(8,128)(2,1)} %get-tuple-element.108), channel_id=1, source_target_pairs={{0,4},{1,5},{2,6},{3,7},{4,0},{5,1},{6,2},{7,3},{8,12},{9,13},{10,... | collective-permute-start | bytes 786440 | tf_op jit(solution)/shard_map/ppermute | solution.py:309
  82.0 27.5 %collective-permute-start.22 = (bf16[256,512]{1,0:T(8,128)(2,1)}, bf16[256,512]{1,0:T(8,128)(2,1)S(1)}, u32[]{:S(2)}, u32[]{:S(2)}) collective-permute-start(bf16[256,512]{1,0:T(8,128)(2,1)} %get-tuple-element.109), channel_id=1, source_target_pairs={{0,6},{1,7},{2,4},{3,5},{4,2},{5,3},{6,0},{7,1},{8,14},{9,15},{10,... | collective-permute-start | bytes 786440 | tf_op jit(solution)/shard_map/ppermute | solution.py:309
  82.7 36.0 %copy-start.1 = (bf16[512,768]{1,0:T(8,128)(2,1)S(1)}, bf16[512,768]{1,0:T(8,128)(2,1)}, u32[]{:S(2)}) copy-start(bf16[512,768]{1,0:T(8,128)(2,1)} %refs_0_) | copy-start | bytes 2359300
  105.1 6.6 %collective-permute-start.17 = (bf16[128,512]{1,0:T(8,128)(2,1)}, bf16[128,512]{1,0:T(8,128)(2,1)S(1)}, u32[]{:S(2)}, u32[]{:S(2)}) collective-permute-start(bf16[128,512]{1,0:T(8,128)(2,1)} %get-tuple-element.104), channel_id=1, source_target_pairs={{0,8},{8,0},{16,24},{24,16},{1,9},{9,1},{17,25},{25,17},{2,10},{10... | collective-permute-start | bytes 393224 | tf_op jit(solution)/shard_map/ppermute | solution.py:309
  106.6 12.1 %collective-permute-start.18 = (bf16[128,512]{1,0:T(8,128)(2,1)}, bf16[128,512]{1,0:T(8,128)(2,1)S(1)}, u32[]{:S(2)}, u32[]{:S(2)}) collective-permute-start(bf16[128,512]{1,0:T(8,128)(2,1)} %get-tuple-element.105), channel_id=1, source_target_pairs={{0,16},{8,24},{16,0},{24,8},{1,17},{9,25},{17,1},{25,9},{2,18},{10... | collective-permute-start | bytes 393224 | tf_op jit(solution)/shard_map/ppermute | solution.py:309
  109.2 9.5 %copy-start.9 = (bf16[256,512]{1,0:T(8,128)(2,1)}, bf16[256,512]{1,0:T(8,128)(2,1)S(1)}, u32[]{:S(2)}) copy-start(bf16[256,512]{1,0:T(8,128)(2,1)S(1)} %collective-permute-done.20.a_ref) | copy-start | bytes 786436
  109.2 9.5 %collective-permute-start.19 = (bf16[128,512]{1,0:T(8,128)(2,1)}, bf16[128,512]{1,0:T(8,128)(2,1)S(1)}, u32[]{:S(2)}, u32[]{:S(2)}) collective-permute-start(bf16[128,512]{1,0:T(8,128)(2,1)} %get-tuple-element.106), channel_id=1, source_target_pairs={{0,24},{8,16},{16,8},{24,0},{1,25},{9,17},{17,9},{25,1},{2,26},{10... | collective-permute-start | bytes 393224 | tf_op jit(solution)/shard_map/ppermute | solution.py:309
  109.5 9.3 %copy-start.10 = (bf16[256,512]{1,0:T(8,128)(2,1)}, bf16[256,512]{1,0:T(8,128)(2,1)S(1)}, u32[]{:S(2)}) copy-start(bf16[256,512]{1,0:T(8,128)(2,1)S(1)} %collective-permute-done.21.b_ref) | copy-start | bytes 786436
  109.5 9.3 %copy-start.11 = (bf16[256,512]{1,0:T(8,128)(2,1)}, bf16[256,512]{1,0:T(8,128)(2,1)S(1)}, u32[]{:S(2)}) copy-start(bf16[256,512]{1,0:T(8,128)(2,1)S(1)} %collective-permute-done.22.c_ref) | copy-start | bytes 786436
  118.8 22.5 %collective-permute-start.29 = (bf16[512,768]{1,0:T(8,128)(2,1)S(1)}, bf16[512,768]{1,0:T(8,128)(2,1)S(1)}, u32[]{:S(2)}, u32[]{:S(2)}) collective-permute-start(bf16[512,768]{1,0:T(8,128)(2,1)S(1)} %copy-done.1), channel_id=1, source_target_pairs={{0,6},{1,7},{2,4},{3,5},{4,2},{5,3},{6,0},{7,1},{8,14},{9,15},{10,... | collective-permute-start | bytes 2359304 | tf_op jit(solution)/shard_map/ppermute | solution.py:309
  120.9 7.5 %collective-permute-start.23 = (bf16[64,512]{1,0:T(8,128)(2,1)}, bf16[64,512]{1,0:T(8,128)(2,1)S(1)}, u32[]{:S(2)}, u32[]{:S(2)}) collective-permute-start(bf16[64,512]{1,0:T(8,128)(2,1)} %get-tuple-element.114), channel_id=1, source_target_pairs={{0,8},{8,0},{16,24},{24,16},{1,9},{9,1},{17,25},{25,17},{2,10},{10... | collective-permute-start | bytes 196616 | tf_op jit(solution)/shard_map/ppermute | solution.py:309
  122.8 11.2 %collective-permute-start.24 = (bf16[64,512]{1,0:T(8,128)(2,1)}, bf16[64,512]{1,0:T(8,128)(2,1)S(1)}, u32[]{:S(2)}, u32[]{:S(2)}) collective-permute-start(bf16[64,512]{1,0:T(8,128)(2,1)} %get-tuple-element.115), channel_id=1, source_target_pairs={{0,16},{8,24},{16,0},{24,8},{1,17},{9,25},{17,1},{25,9},{2,18},{10... | collective-permute-start | bytes 196616 | tf_op jit(solution)/shard_map/ppermute | solution.py:309
  124.9 27.2 %copy-start.8 = (bf16[128,512]{1,0:T(8,128)(2,1)}, bf16[128,512]{1,0:T(8,128)(2,1)S(1)}, u32[]{:S(2)}) copy-start(bf16[128,512]{1,0:T(8,128)(2,1)S(1)} %add_convert_fusion.1.refs_0_) | copy-start | bytes 393220
  124.9 15.5 %collective-permute-start.28 = (bf16[128,512]{1,0:T(8,128)(2,1)S(1)}, bf16[128,512]{1,0:T(8,128)(2,1)S(1)}, u32[]{:S(2)}, u32[]{:S(2)}) collective-permute-start(bf16[128,512]{1,0:T(8,128)(2,1)S(1)} %add_convert_fusion.1.refs_0_), channel_id=1, source_target_pairs={{0,24},{8,16},{16,8},{24,0},{1,25},{9,17},{17,9},{25,1},{2,26},{10... | collective-permute-start | bytes 393224 | tf_op jit(solution)/shard_map/ppermute | solution.py:309
  126.4 14.8 %collective-permute-start.27 = (bf16[128,512]{1,0:T(8,128)(2,1)S(1)}, bf16[128,512]{1,0:T(8,128)(2,1)S(1)}, u32[]{:S(2)}, u32[]{:S(2)}) collective-permute-start(bf16[128,512]{1,0:T(8,128)(2,1)S(1)} %add_convert_fusion.1.refs_0_), channel_id=1, source_target_pairs={{0,16},{8,24},{16,0},{24,8},{1,17},{9,25},{17,1},{25,9},{2,18},{10... | collective-permute-start | bytes 393224 | tf_op jit(solution)/shard_map/ppermute | solution.py:309
  128.4 12.8 %collective-permute-start.26 = (bf16[128,512]{1,0:T(8,128)(2,1)S(1)}, bf16[128,512]{1,0:T(8,128)(2,1)S(1)}, u32[]{:S(2)}, u32[]{:S(2)}) collective-permute-start(bf16[128,512]{1,0:T(8,128)(2,1)S(1)} %add_convert_fusion.1.refs_0_), channel_id=1, source_target_pairs={{0,8},{8,0},{16,24},{24,16},{1,9},{9,1},{17,25},{25,17},{2,10},{10... | collective-permute-start | bytes 393224 | tf_op jit(solution)/shard_map/ppermute | solution.py:309
  134.0 6.4 %collective-permute-start.25 = (bf16[64,512]{1,0:T(8,128)(2,1)}, bf16[64,512]{1,0:T(8,128)(2,1)S(1)}, u32[]{:S(2)}, u32[]{:S(2)}) collective-permute-start(bf16[64,512]{1,0:T(8,128)(2,1)} %get-tuple-element.116), channel_id=1, source_target_pairs={{0,24},{8,16},{16,8},{24,0},{1,25},{9,17},{17,9},{25,1},{2,26},{10... | collective-permute-start | bytes 196616 | tf_op jit(solution)/shard_map/ppermute | solution.py:309
  140.4 11.8 %copy-start.15 = (bf16[128,512]{1,0:T(8,128)(2,1)}, bf16[128,512]{1,0:T(8,128)(2,1)S(1)}, u32[]{:S(2)}) copy-start(bf16[128,512]{1,0:T(8,128)(2,1)S(1)} %collective-permute-done.28.refs_3_) | copy-start | bytes 393220
  141.2 10.9 %copy-start.16 = (bf16[128,512]{1,0:T(8,128)(2,1)}, bf16[128,512]{1,0:T(8,128)(2,1)S(1)}, u32[]{:S(2)}) copy-start(bf16[128,512]{1,0:T(8,128)(2,1)S(1)} %collective-permute-done.27.refs_2_) | copy-start | bytes 393220
  141.2 11.0 %copy-start.17 = (bf16[128,512]{1,0:T(8,128)(2,1)}, bf16[128,512]{1,0:T(8,128)(2,1)S(1)}, u32[]{:S(2)}) copy-start(bf16[128,512]{1,0:T(8,128)(2,1)S(1)} %collective-permute-done.26.refs_1_) | copy-start | bytes 393220
  141.2 5.6 %copy-start.5 = (bf16[512,768]{1,0:T(8,128)(2,1)}, bf16[512,768]{1,0:T(8,128)(2,1)S(1)}, u32[]{:S(2)}) copy-start(bf16[512,768]{1,0:T(8,128)(2,1)S(1)} %collective-permute-done.29.refs_0_) | copy-start | bytes 2359300
  141.2 5.6 %collective-permute-start.33 = (bf16[512,768]{1,0:T(8,128)(2,1)S(1)}, bf16[512,768]{1,0:T(8,128)(2,1)S(1)}, u32[]{:S(2)}, u32[]{:S(2)}) collective-permute-start(bf16[512,768]{1,0:T(8,128)(2,1)S(1)} %collective-permute-done.29.refs_0_), channel_id=1, source_target_pairs={{0,1},{1,0},{2,3},{3,2},{4,5},{5,4},{6,7},{7,6},{8,9},{9,8},{10,11... | collective-permute-start | bytes 2359304 | tf_op jit(solution)/shard_map/ppermute | solution.py:309
  142.4 9.8 %copy-start.13 = (bf16[64,512]{1,0:T(8,128)(2,1)}, bf16[64,512]{1,0:T(8,128)(2,1)S(1)}, u32[]{:S(2)}) copy-start(bf16[64,512]{1,0:T(8,128)(2,1)S(1)} %add_convert_fusion.2.refs_4_) | copy-start | bytes 196612
  142.4 9.7 %collective-permute-start.32 = (bf16[64,512]{1,0:T(8,128)(2,1)S(1)}, bf16[64,512]{1,0:T(8,128)(2,1)S(1)}, u32[]{:S(2)}, u32[]{:S(2)}) collective-permute-start(bf16[64,512]{1,0:T(8,128)(2,1)S(1)} %add_convert_fusion.2.refs_4_), channel_id=1, source_target_pairs={{0,24},{8,16},{16,8},{24,0},{1,25},{9,17},{17,9},{25,1},{2,26},{10... | collective-permute-start | bytes 196616 | tf_op jit(solution)/shard_map/ppermute | solution.py:309
  145.2 7.0 %collective-permute-start.31 = (bf16[64,512]{1,0:T(8,128)(2,1)S(1)}, bf16[64,512]{1,0:T(8,128)(2,1)S(1)}, u32[]{:S(2)}, u32[]{:S(2)}) collective-permute-start(bf16[64,512]{1,0:T(8,128)(2,1)S(1)} %add_convert_fusion.2.refs_4_), channel_id=1, source_target_pairs={{0,16},{8,24},{16,0},{24,8},{1,17},{9,25},{17,1},{25,9},{2,18},{10... | collective-permute-start | bytes 196616 | tf_op jit(solution)/shard_map/ppermute | solution.py:309
  145.3 6.9 %collective-permute-start.30 = (bf16[64,512]{1,0:T(8,128)(2,1)S(1)}, bf16[64,512]{1,0:T(8,128)(2,1)S(1)}, u32[]{:S(2)}, u32[]{:S(2)}) collective-permute-start(bf16[64,512]{1,0:T(8,128)(2,1)S(1)} %add_convert_fusion.2.refs_4_), channel_id=1, source_target_pairs={{0,8},{8,0},{16,24},{24,16},{1,9},{9,1},{17,25},{25,17},{2,10},{10... | collective-permute-start | bytes 196616 | tf_op jit(solution)/shard_map/ppermute | solution.py:309
  146.9 0.9 copy-start.6
  152.2 0.6 copy-start.18
  152.2 0.6 copy-start.19
  152.8 0.6 copy-start.20

commit v4 on v3

--- a/solution.py
+++ b/solution.py
@@ -10,8 +10,8 @@
 MOST = 1536
 NEG_FILL = -1e30
 LOG2E = 1.4426950408889634
-KEY_STEP = 256
-Q_STEP = 128
+KEY_STEP = 512
+Q_STEP = 256
 
 
 def nt_dot(a, b):
@@ -65,34 +65,36 @@
         begin = jnp.maximum(least, 0) // KEY_STEP
         stop = -(-(first + Q_STEP) // KEY_STEP)
 
-        def scores_step(c, top):
+        def scores_step(c, carried):
+            top, norm, dot = carried
             at = pl.ds(pl.multiple_of(c * KEY_STEP, KEY_STEP), KEY_STEP)
-            s = nt_dot(kv_scr[at, :hd], q_cat)
+            s = nt_dot(kv_scr[at, :hd], q_cat) * (scaling * LOG2E)
             k_pos = c * KEY_STEP + lax.broadcasted_iota(jnp.int32, (KEY_STEP, wide), 0)
             s = jnp.where((k_pos >= doc_start) & (k_pos <= q_pos), s, NEG_FILL)
             s_scr[at, :] = s
-            dp_scr[at, :] = nt_dot(kv_scr[at, hd:], g_cat)
-            return jnp.maximum(top, jnp.max(s, axis=0, keepdims=True))
-
-        top = lax.fori_loop(begin, stop, scores_step, jnp.full((1, wide), NEG_FILL, jnp.float32))
-
-        def sums_step(c, carried):
-            at = pl.ds(pl.multiple_of(c * KEY_STEP, KEY_STEP), KEY_STEP)
-            e = jnp.exp2((s_scr[at, :] - top) * (scaling * LOG2E))
-            s_scr[at, :] = e
-            return (
-                carried[0] + jnp.sum(e, axis=0, keepdims=True),
-                carried[1] + jnp.sum(e * dp_scr[at, :], axis=0, keepdims=True),
-            )
-
-        zero = jnp.zeros((1, wide), jnp.float32)
-        norm, dot = lax.fori_loop(begin, stop, sums_step, (zero, zero))
-        inverse = 1.0 / norm
-        delta = dot * inverse
+            dp = nt_dot(kv_scr[at, hd:], g_cat)
+            dp_scr[at, :] = dp
+            s = s.reshape(KEY_STEP // 8, 8, wide)
+            above = jnp.maximum(top, jnp.max(s, axis=0))
+            shrink = jnp.exp2(top - above)
+            e = jnp.exp2(s - above[None])
+            norm = norm * shrink + jnp.sum(e, axis=0)
+            dot = dot * shrink + jnp.sum(e * dp.reshape(KEY_STEP // 8, 8, wide), axis=0)
+            return above, norm, dot
+
+        zero = jnp.zeros((8, wide), jnp.float32)
+        tops, norms, dots = lax.fori_loop(
+            begin, stop, scores_step, (jnp.full((8, wide), NEG_FILL, jnp.float32), zero, zero)
+        )
+        top = jnp.max(tops, axis=0, keepdims=True)
+        shrink = jnp.exp2(tops - top)
+        norm = jnp.sum(norms * shrink, axis=0, keepdims=True)
+        delta = jnp.sum(dots * shrink, axis=0, keepdims=True) / norm
+        lse = top + jnp.log2(norm)
 
         def grads_step(c, dq):
             at = pl.ds(pl.multiple_of(c * KEY_STEP, KEY_STEP), KEY_STEP)
-            p = s_scr[at, :] * inverse
+            p = jnp.exp2(s_scr[at, :] - lse)
             ds_low = (p * (dp_scr[at, :] - delta)).astype(jnp.bfloat16)
             p_low = p.astype(jnp.bfloat16)
             acc_scr[at, :hd] += nn_dot(ds_low, q_cat)
@@ -148,45 +150,75 @@
     )(index, lengths, q, g, own, d2, r, x)
 
 
-def weight_kernel(places, gt_ref, gt_other, x_ref, x_other, own_out, *outs):
+def weight_kernel(places, gt_ref, gt_other, x_ref, x_other, own_out, keep_out, to_x, to_y):
     k = pl.program_id(0)
+    half = gt_ref.shape[0] // 2
+    upper, lower = slice(0, half), slice(half, 2 * half)
     total = nn_dot(gt_ref[...], x_ref[...]) + nn_dot(gt_other[...], x_other[...])
+    low = total.astype(jnp.bfloat16)
+
+    @pl.when(k == 3)
+    def _():
+        own_out[...] = total
+
+    @pl.when(k == 1)
+    def _():
+        to_x[upper, :] = low[upper, :]
+        keep_out[lower, :] = low[lower, :]
+
+    @pl.when(k == 2)
+    def _():
+        keep_out[upper, :] = low[upper, :]
+        to_y[upper, :] = low[lower, :]
 
     @pl.when(k == 0)
     def _():
-        own_out[...] = total
-
-    for turn, out in enumerate(outs):
-        @pl.when(k == turn + 1)
-        def _(out=out):
-            out[...] = total.astype(out.dtype)
+        to_x[lower, :] = low[upper, :]
+        to_y[lower, :] = low[lower, :]
 
 
 def weight_partials(places, gt, gt_other, x, x_other, block):
     cols, rows = gt.shape
     chips = x_other.shape[1] // block // 2
     whole = lambda k, s: (0, 0)
+    strip = pl.BlockSpec((rows, block), lambda k, s: (0, (s[0] ^ s[2 + k]) * 2 + s[1]))
     return pl.pallas_call(
         weight_kernel,
         name="weight_partials",
         out_shape=[jax.ShapeDtypeStruct((cols, block), jnp.float32)]
-        + [jax.ShapeDtypeStruct((cols, block), jnp.bfloat16)] * (chips - 1),
+        + [jax.ShapeDtypeStruct((cols, block), jnp.bfloat16)] * 3,
         grid_spec=pltpu.PrefetchScalarGridSpec(
             num_scalar_prefetch=1,
             grid=(chips,),
-            in_specs=[
-                pl.BlockSpec((cols, rows), whole),
-                pl.BlockSpec((cols, rows), whole),
-                pl.BlockSpec((rows, block), lambda k, s: (0, (s[0] ^ k) * 2 + s[1])),
-                pl.BlockSpec((rows, block), lambda k, s: (0, (s[0] ^ k) * 2 + s[1])),
-            ],
-            out_specs=[pl.BlockSpec((cols, block), whole)] * chips,
+            in_specs=[pl.BlockSpec((cols, rows), whole)] * 2 + [strip] * 2,
+            out_specs=[pl.BlockSpec((cols, block), whole)] * 4,
         ),
         compiler_params=pltpu.CompilerParams(vmem_limit_bytes=58 * 2**20),
         cost_estimate=pl.CostEstimate(
             flops=4 * cols * rows * block * chips, bytes_accessed=8 * 2**20, transcendentals=0
         ),
     )(places, gt, gt_other, x, x_other)
+
+
+def middle_kernel(own_ref, keep_ref, from_x, from_y, own_out, next_x, next_y):
+    f32 = jnp.float32
+    half = own_ref.shape[0] // 2
+    upper, lower = slice(0, half), slice(half, 2 * half)
+    own_out[upper, :] = own_ref[upper, :] + from_x[upper, :].astype(f32)
+    own_out[lower, :] = own_ref[lower, :] + from_y[upper, :].astype(f32)
+    next_y[...] = (keep_ref[upper, :].astype(f32) + from_x[lower, :].astype(f32)).astype(next_y.dtype)
+    next_x[...] = (keep_ref[lower, :].astype(f32) + from_y[lower, :].astype(f32)).astype(next_x.dtype)
+
+
+def middle(own, keep, from_x, from_y):
+    rows, cols = own.shape
+    half = jax.ShapeDtypeStruct((rows // 2, cols), jnp.bfloat16)
+    return pl.pallas_call(
+        middle_kernel,
+        name="middle",
+        out_shape=[jax.ShapeDtypeStruct(own.shape, jnp.float32), half, half],
+        cost_estimate=pl.CostEstimate(flops=4 * rows * cols, bytes_accessed=2**21, transcendentals=0),
+    )(own, keep, from_x, from_y)
 
 
 def input_kernel(places, gq_ref, gkv_ref, *refs, count):
@@ -247,60 +279,78 @@
     )(own, from_two, from_x)
 
 
-def quarters_kernel(z_ref, own_ref, a_ref, b_ref, c_ref, mine_out, *outs):
+def quarters_kernel(z_ref, own_ref, x_ref, y_ref, mine_out, *outs):
     z = z_ref[0]
     quarter = mine_out.shape[0]
     for k, out in enumerate((mine_out, *outs)):
-        at = pl.ds(pl.multiple_of((z ^ k) * quarter, quarter), quarter)
-        total = own_ref[at, :]
-        for ref in (a_ref, b_ref, c_ref):
-            total = total + ref[at, :].astype(jnp.float32)
-        out[...] = total.astype(out.dtype)
-
-
-def quarters_of(z, own, others):
+        place = z ^ k
+        at = pl.ds(pl.multiple_of(place * quarter, quarter), quarter)
+        half = pl.ds(pl.multiple_of(lax.rem(place, 2) * quarter, quarter), quarter)
+        add = jnp.where(place < 2, y_ref[half, :].astype(jnp.float32), x_ref[half, :].astype(jnp.float32))
+        out[...] = (own_ref[at, :] + add).astype(out.dtype)
+
+
+def quarters_of(z, own, from_x, from_y):
     rows, cols = own.shape
     piece = (rows // 4, cols)
-    vmem = pl.BlockSpec(own.shape, lambda i: (0, 0))
-    out = pl.BlockSpec(piece, lambda i: (0, 0))
+    whole = lambda i: (0, 0)
+    out = pl.BlockSpec(piece, whole)
     return pl.pallas_call(
         quarters_kernel,
         name="quarters",
         out_shape=[jax.ShapeDtypeStruct(piece, jnp.float32)] + [jax.ShapeDtypeStruct(piece, jnp.bfloat16)] * 3,
         grid=(1,),
-        in_specs=[pl.BlockSpec(memory_space=pltpu.SMEM)] + [vmem] * 4,
+        in_specs=[pl.BlockSpec(memory_space=pltpu.SMEM)]
+        + [pl.BlockSpec(a.shape, whole) for a in (own, from_x, from_y)],
         out_specs=[out] * 4,
         cost_estimate=pl.CostEstimate(flops=4 * rows * cols, bytes_accessed=2**21, transcendentals=0),
-    )(z, own, *others)
-
-
-def joined_kernel(z_ref, *refs):
+    )(z, own, from_x, from_y)
+
+
+def added_kernel(*refs):
+    out_ref = refs[-1]
+    start = 0
+    for part in range(0, len(refs) - 1, 4):
+        total = refs[part][...]
+        for ref in refs[part + 1 : part + 4]:
+            total = total + ref[...].astype(jnp.float32)
+        out_ref[start : start + total.shape[0], :] = total.astype(out_ref.dtype)
+        start += total.shape[0]
+
+
+def added(parts):
+    pieces = [piece for part in parts for piece in part]
+    rows, cols = sum(part[0].shape[0] for part in parts), pieces[0].shape[1]
+    return pl.pallas_call(
+        added_kernel,
+        name="added",
+        out_shape=jax.ShapeDtypeStruct((rows, cols), jnp.bfloat16),
+        cost_estimate=pl.CostEstimate(flops=4 * rows * cols, bytes_accessed=2**20, transcendentals=0),
+    )(*pieces)
+
+
+def joined_kernel(z_ref, *refs, split):
     z = z_ref[0]
-    count = (len(refs) - 2) // 4
-    out_ref, scr = refs[-2:]
-    start = 0
-    for part in range(count):
-        pieces = refs[4 * part : 4 * part + 4]
-        quarter = pieces[0].shape[0]
-        for k, piece in enumerate(pieces):
-            scr[pl.ds(pl.multiple_of(start + (z ^ k) * quarter, quarter), quarter), :] = piece[...]
-        start += 4 * quarter
+    *pieces, out_ref, scr = refs
+    rest = pieces[0].shape[0] - split
+    for k, piece in enumerate(pieces):
+        place = z ^ k
+        scr[pl.ds(pl.multiple_of(place * split, split), split), :] = piece[:split, :]
+        scr[pl.ds(pl.multiple_of(4 * split + place * rest, rest), rest), :] = piece[split:, :]
     out_ref[...] = scr[...].T
 
 
-def joined(z, parts):
-    pieces = [piece for part in parts for piece in part]
-    cols = pieces[0].shape[1]
-    rows = sum(piece.shape[0] for piece in pieces)
-    return pl.pallas_call(
-        joined_kernel,
+def joined(z, pieces, split):
+    rows, cols = pieces[0].shape
+    whole = lambda i: (0, 0)
+    return pl.pallas_call(
+        functools.partial(joined_kernel, split=split),
         name="joined",
-        out_shape=jax.ShapeDtypeStruct((cols, rows), jnp.bfloat16),
+        out_shape=jax.ShapeDtypeStruct((cols, 4 * rows), jnp.bfloat16),
         grid=(1,),
-        in_specs=[pl.BlockSpec(memory_space=pltpu.SMEM)]
-        + [pl.BlockSpec(piece.shape, lambda i: (0, 0)) for piece in pieces],
-        out_specs=pl.BlockSpec((cols, rows), lambda i: (0, 0)),
-        scratch_shapes=[pltpu.VMEM((rows, cols), jnp.bfloat16)],
+        in_specs=[pl.BlockSpec(memory_space=pltpu.SMEM)] + [pl.BlockSpec((rows, cols), whole)] * 4,
+        out_specs=pl.BlockSpec((cols, 4 * rows), whole),
+        scratch_shapes=[pltpu.VMEM((4 * rows, cols), jnp.bfloat16)],
         cost_estimate=pl.CostEstimate(flops=rows * cols, bytes_accessed=2**21, transcendentals=0),
     )(z, *pieces)
 
@@ -330,7 +380,9 @@
 
     d2 = lax.ppermute(own, "ctx", by_two)
     x = lax.ppermute(own, "ctx", mixed)
-    d2, x = lax.optimization_barrier((d2, x))
+    w_swapped = flipped(qkv_weight, 1)
+    places = jnp.stack([index // 2, index % 2, *map(jnp.int32, (3, 1, 2, 0))])
+    d2, x, w_swapped, places = together(d2, x, w_swapped, places)
     r = flipped(d2, 1)
     if small:
         w_own, x_in, r = lax.optimization_barrier((qkv_weight, x_local, r))
@@ -344,51 +396,49 @@
         *grads, w_x, w_y, x_other = lax.optimization_barrier((*grads, w_x, w_y, x_other))
     gq, gqt, kv_own, kv_d2, kv_r, kv_x = grads
     kv_d2 = (kv_d2 + flipped(kv_r, 1)).astype(bf16)
-    from_two = lax.ppermute(kv_d2, "ctx", back(by_two))
     from_x = lax.ppermute(kv_x, "ctx", back(mixed))
 
     if small:
-        places = jnp.stack([index // 2, index % 2])
         z = lax.axis_index("dp").reshape(1)
-
-        def partials(gt):
-            return weight_partials(places, gt, flipped(gt, 1), x_local, x_other, block)
-
-        def sent(others):
-            return [flipped(other, bits) for bits, other in zip((2, 4, 6), others)]
 
         def crossed(pieces):
             return [flipped(piece, k + 1, "dp") for k, piece in enumerate(pieces)]
 
-        def added(mine, pieces):
-            for piece in pieces:
-                mine = mine + piece.astype(f32)
-            return mine.astype(bf16)
-
-        q_own, *q_others = partials(gqt)
-        kv_own, q_own, w_own, w_x, w_y = together(kv_own, q_own, w_own, w_x, w_y)
+        gqt_other, kv_d2 = together(flipped(gqt, 1), kv_d2)
+        from_two = lax.ppermute(kv_d2, "ctx", back(by_two))
+        q_parts = weight_partials(places, gqt, gqt_other, x_local, x_other, block)
+        from_two, from_x, w_x, w_y, *q_parts = together(from_two, from_x, w_x, w_y, *q_parts)
+        q_own, q_keep, q_x, q_y = q_parts
+        q_x, q_y = flipped(q_x, 2), flipped(q_y, 4)
         gkv, gkvt = finish_kv(kv_own, from_two, from_x)
-        q_others = sent(q_others)
-        kv_part, *kv_others = partials(gkvt)
-        w_blocks = [w for part in (w_own, w_x, w_y) for w in (part, flipped(part, 1))]
-        kv_others = sent(kv_others)
+        kv_parts = weight_partials(places, gkvt, flipped(gkvt, 1), x_local, x_other, block)
+        w_blocks = (w_own, w_swapped, w_x, flipped(w_x, 1), w_y, flipped(w_y, 1))
+        q_x, q_y, *rest = together(q_x, q_y, *kv_parts, *w_blocks)
+        (kv_own, kv_keep, kv_x, kv_y), w_blocks = rest[:4], rest[4:]
+        q_own, q_x, q_y = middle(q_own, q_keep, q_x, q_y)
+        q_x, q_y = flipped(q_x, 2), flipped(q_y, 4)
+        kv_x, kv_y = flipped(kv_x, 2), flipped(kv_y, 4)
+        q_own, *q_pieces = quarters_of(z, q_own, q_x, q_y)
+        q_pieces = crossed(q_pieces)
+        kv_own, q_own = together(kv_own, q_own)
+        kv_own, kv_x, kv_y = middle(kv_own, kv_keep, kv_x, kv_y)
+        kv_x, kv_y = flipped(kv_x, 2), flipped(kv_y, 4)
+        kv_x, kv_y, *q_pieces = together(kv_x, kv_y, *q_pieces)
+        kv_own, *kv_pieces = quarters_of(z, kv_own, kv_x, kv_y)
+        kv_own, w_x, w_y, *kv_pieces = together(kv_own, w_x, w_y, *kv_pieces)
+        kv_pieces = crossed(kv_pieces)
+        half = block // 2
+        w_top, w_bottom = flipped(w_x[:half], 4), flipped(w_y[half:], 2)
         grad_in = input_grad(places, gq, gkv, w_blocks, 0)
-        *q_others, grad_in = together(*q_others, grad_in)
-        q_own, *q_pieces = quarters_of(z, q_own, q_others)
-        q_pieces = crossed(q_pieces)
-        *q_pieces, a, b, c, w_own = together(*q_pieces, *kv_others, w_own)
-        kv_part, *kv_pieces = quarters_of(z, kv_part, (a, b, c))
-        w_d = flipped(w_own, 6)
-        q_mine = added(q_own, q_pieces)
-        q_all = crossed([q_mine] * 3)
-        kv_pieces = crossed(kv_pieces)
-        *kv_pieces, a, b, c, w_d = together(*kv_pieces, *q_all, w_d)
-        kv_mine = added(kv_part, kv_pieces)
-        kv_all = crossed([kv_mine] * 3)
+        *kv_pieces, grad_in, w_top, w_bottom = together(*kv_pieces, grad_in, w_top, w_bottom)
+        w_d = jnp.concatenate([w_top, w_bottom])
+        mine = added([(q_own, *q_pieces), (kv_own, *kv_pieces)])
+        pieces = crossed([mine] * 3)
         grad_in = input_grad(places, gq, gkv, (w_d, flipped(w_d, 1)), 6, grad_in)
-        *kv_all, grad_in = together(*kv_all, grad_in)
-        weight_sum = joined(z, [(q_mine, a, b, c), (kv_mine, *kv_all)])
+        *pieces, grad_in = together(*pieces, grad_in)
+        weight_sum = joined(z, (mine, *pieces), q_own.shape[0])
     else:
+        from_two = lax.ppermute(kv_d2, "ctx", back(by_two))
         gkv, _ = finish_kv(kv_own, from_two, from_x)
         grad_qkv = jnp.concatenate([gq, gkv], axis=1)
         grad_in = nt_dot(grad_qkv, w_full).astype(bf16)

time: 156 us -> 143 us (0.917)
  waiting for transfers between devices: 55.9 us -> 44.8 us
  starting transfers between devices: 47.6 us -> 39.8 us
  Pallas kernels: 43.6 us -> 50.1 us
  other arithmetic: 3.85 us -> 1.1 us
  local copies, waits for them, and re-layouts: 3.9 us -> 5.92 us
    ppermute x30, waiting for transfers between devices: 49.7 us -> 36.5 us  [flipped(): lax.ppermute(array, axis, [(i, i ^ bits) for i in range(lax.axis_size(axi...]
    ppermute x30, starting transfers between devices: 38.3 us -> 30.2 us  [flipped(): lax.ppermute(array, axis, [(i, i ^ bits) for i in range(lax.axis_size(axi...]
    pallas_call x1 -> x4, Pallas kernels: 2.35 us -> 9.96 us  [the longest x2 5.6 us: middle(): pl.pallas_call(middle_kernel, name='middle', out_shape=[jax.ShapeDtypeStr...]
    ppermute x1, waiting for transfers between devices: 0.01 us -> 2.1 us  [per_device(): from_two = lax.ppermute(kv_d2, 'ctx', back(by_two))]
    convert_element_type x2 -> x0, other arithmetic: 2.09 us -> none  [added(): return mine.astype(bf16)]
    unnamed x48 -> x45, local copies, waits for them, and re-layouts: 3.9 us -> 5.22 us
  transfers between devices with their start and end apart: 34 -> 34, of which waited for: 11 -> 16; matrix products, arithmetic and copies ran while one was open for 2% -> 1% of each run, Pallas kernels for 27% -> 30%
where the time goes in v4:
time: 143 us
  Pallas kernels  50.1 us (35%)
  waiting for transfers between devices  44.8 us (31%)
  starting transfers between devices  39.8 us (28%)
  local copies, waits for them, and re-layouts  5.92 us (4%)
    ppermute x30, waiting for transfers between devices, flipped(): lax.ppermute(array, axis, [(i, i ^ bits) for i in range(lax.axis_size(axi...  36.5 us
    ppermute x30, starting transfers between devices, flipped(): lax.ppermute(array, axis, [(i, i ^ bits) for i in range(lax.axis_size(axi...  30.2 us
    pallas_call x2, Pallas kernels, weight_partials(): pl.pallas_call(weight_kernel, name='weight_partials', out_shape=[jax.Shap...  13.3 us
    pallas_call x2, Pallas kernels, input_grad(): pl.pallas_call(functools.partial(input_kernel, count=count), name='input_...  12.5 us
    pallas_call x1, Pallas kernels, attention(): pl.pallas_call(attention_kernel, name='attention', out_shape=(jax.ShapeDt...  8.05 us
    ppermute x1, waiting for transfers between devices, per_device(): d2 = lax.ppermute(own, 'ctx', by_two)  6.16 us
    pallas_call x2, Pallas kernels, middle(): pl.pallas_call(middle_kernel, name='middle', out_shape=[jax.ShapeDtypeStr...  5.6 us
    unnamed x45, local copies, waits for them, and re-layouts  5.22 us
  transfers between devices with their start and end apart: 34, of which 16 were waited for; matrix products, arithmetic and copies ran while one was open for 1% of the time, Pallas kernels for 30%

profile of v4, /device:TPU:0, one launch (start us, length us, event | category | flops | bytes accessed | tf_op | source)
XLA Modules:
  0.0 142.6 jit_solution(16191043626881742985)
XLA Ops:
  0.6 0.5 collective-permute-start.2
  1.1 2.0 %collective-permute-start.1 = (bf16[512,256]{1,0:T(8,128)(2,1)}, bf16[512,256]{1,0:T(8,128)(2,1)S(1)}, u32[]{:S(2)}, u32[]{:S(2)}) collective-permute-start(bf16[512,256]{1,0:T(8,128)(2,1)} %bitcast.19), channel_id=1, source_target_pairs={{0,1},{2,3},{4,5},{6,7},{1,4},{3,6},{8,9},{10,11},{12,13},{14,15},... | collective-permute-start | bytes 786440 | tf_op jit(solution)/shard_map/ppermute | solution.py:382
  3.1 4.9 %collective-permute-start = (bf16[512,256]{1,0:T(8,128)(2,1)}, bf16[512,256]{1,0:T(8,128)(2,1)S(1)}, u32[]{:S(2)}, u32[]{:S(2)}) collective-permute-start(bf16[512,256]{1,0:T(8,128)(2,1)} %bitcast.20), channel_id=1, source_target_pairs={{0,2},{1,3},{2,4},{3,5},{4,6},{5,7},{8,10},{9,11},{10,12},{11,13},... | collective-permute-start | bytes 786440 | tf_op jit(solution)/shard_map/ppermute | solution.py:381
  8.0 0.6 stack.11.places
  8.6 6.2 %collective-permute-done.d2_ref = bf16[512,256]{1,0:T(8,128)(2,1)S(1)} collective-permute-done((bf16[512,256]{1,0:T(8,128)(2,1)}, bf16[512,256]{1,0:T(8,128)(2,1)S(1)}, u32[]{:S(2)}, u32[]{:S(2)}) %collective-permute-start) | collective-permute-done | bytes 262176 | tf_op jit(solution)/shard_map/ppermute | solution.py:381
  14.8 0.3 collective-permute-start.3
  15.1 1.2 collective-permute-done.3.r_ref
  16.3 0.3 collective-permute-start.6
  16.6 0.4 copy-done.21
  17.0 2.5 %collective-permute-start.5 = (bf16[512,768]{1,0:T(8,128)(2,1)}, bf16[512,768]{1,0:T(8,128)(2,1)S(1)}, u32[]{:S(2)}, u32[]{:S(2)}) collective-permute-start(bf16[512,768]{1,0:T(8,128)(2,1)} %refs_0_), channel_id=1, source_target_pairs={{0,4},{1,5},{2,6},{3,7},{4,0},{5,1},{6,2},{7,3},{8,12},{9,13},{10,... | collective-permute-start | bytes 2359304 | tf_op jit(solution)/shard_map/ppermute | solution.py:359
  19.6 8.0 %attention.1 = (bf16[512,512]{1,0:T(8,128)(2,1)}, bf16[512,512]{1,0:T(8,128)(2,1)}, f32[512,256]{1,0:T(8,128)}, f32[512,256]{1,0:T(8,128)}, f32[512,256]{1,0:T(8,128)}, /*index=5*/bf16[512,256]{1,0:T(8,128)(2,1)}) custom-call(s32[1]{0:T(128)} %bitcast.idx_ref, s32[1,16]{1,0:T(1,128)} %len_ref.1, bf16[512,512]{1,0:T(8,128)(2,1)} %bitcast.17, ...), custom_call_target="tpu_custom_call" | custom-call | flops 12000000000 | bytes 6291456 | tf_op jit(solution)/shard_map/attention/pallas_call | solution.py:127
  27.6 10.0 %collective-permute-done.5.refs_4_ = bf16[512,768]{1,0:T(8,128)(2,1)S(1)} collective-permute-done((bf16[512,768]{1,0:T(8,128)(2,1)}, bf16[512,768]{1,0:T(8,128)(2,1)S(1)}, u32[]{:S(2)}, u32[]{:S(2)}) %collective-permute-start.5) | collective-permute-done | bytes 786464 | tf_op jit(solution)/shard_map/ppermute | solution.py:359
  37.6 1.5 %collective-permute-done.4.refs_2_ = bf16[512,768]{1,0:T(8,128)(2,1)S(1)} collective-permute-done((bf16[512,768]{1,0:T(8,128)(2,1)}, bf16[512,768]{1,0:T(8,128)(2,1)S(1)}, u32[]{:S(2)}, u32[]{:S(2)}) %collective-permute-start.4) | collective-permute-done | bytes 786464 | tf_op jit(solution)/shard_map/ppermute | solution.py:359
  39.2 0.5 collective-permute-start.7
  39.6 1.3 collective-permute-start.10
  40.9 0.3 collective-permute-done.8
  41.3 1.1 add_convert_fusion
  42.4 1.5 %collective-permute-start.9 = (bf16[512,256]{1,0:T(8,128)(2,1)S(1)}, bf16[512,256]{1,0:T(8,128)(2,1)}, u32[]{:S(2)}, u32[]{:S(2)}) collective-permute-start(bf16[512,256]{1,0:T(8,128)(2,1)S(1)} %add_convert_fusion), channel_id=1, source_target_pairs={{2,0},{3,1},{4,2},{5,3},{6,4},{7,5},{10,8},{11,9},{12,10},{13,11},... | collective-permute-start | bytes 786440 | tf_op jit(solution)/shard_map/ppermute | solution.py:408
  43.9 7.4 %weight_partials.2 = (f32[512,512]{1,0:T(8,128)}, bf16[512,512]{1,0:T(8,128)(2,1)}, bf16[512,512]{1,0:T(8,128)(2,1)}, bf16[512,512]{1,0:T(8,128)(2,1)}) custom-call(s32[6]{0:T(128)} %stack.11.places, bf16[512,512]{1,0:T(8,128)(2,1)} %get-tuple-element.108.gt_ref, bf16[512,512]{1,0:T(8,128)(2,1)} %collective-permute-done.7.gt_other, ...), custom_call_target="tpu_custom_call" | custom-call | flops 2147483648 | bytes 8388608 | tf_op jit(solution)/shard_map/weight_partials/pallas_call | solution.py:185
  51.3 2.1 %collective-permute-done.9.two_ref = bf16[512,256]{1,0:T(8,128)(2,1)} collective-permute-done((bf16[512,256]{1,0:T(8,128)(2,1)S(1)}, bf16[512,256]{1,0:T(8,128)(2,1)}, u32[]{:S(2)}, u32[]{:S(2)}) %collective-permute-start.9) | collective-permute-done | bytes 262176 | tf_op jit(solution)/shard_map/ppermute | solution.py:408
  53.4 0.5 collective-permute-start.15
  53.9 1.2 collective-permute-start.11
  55.1 1.9 %collective-permute-start.12 = (bf16[512,512]{1,0:T(8,128)(2,1)}, bf16[512,512]{1,0:T(8,128)(2,1)}, u32[]{:S(2)}, u32[]{:S(2)}) collective-permute-start(bf16[512,512]{1,0:T(8,128)(2,1)} %get-tuple-element.126), channel_id=1, source_target_pairs={{0,4},{1,5},{2,6},{3,7},{4,0},{5,1},{6,2},{7,3},{8,12},{9,13},{10,... | collective-permute-start | bytes 1572872 | tf_op jit(solution)/shard_map/ppermute | solution.py:359
  57.0 2.1 %finish_kv.1 = (bf16[512,256]{1,0:T(8,128)(2,1)}, bf16[256,512]{1,0:T(8,128)(2,1)}) custom-call(f32[512,256]{1,0:T(8,128)} %get-tuple-element.107.own_ref, bf16[512,256]{1,0:T(8,128)(2,1)} %collective-permute-done.9.two_ref, bf16[512,256]{1,0:T(8,128)(2,1)} %collective-permute-done.10.x_ref), custom_call_target="tpu_custom_call" | custom-call | flops 524288 | bytes 2097152 | tf_op jit(solution)/shard_map/finish_kv/pallas_call | solution.py:271
  59.1 1.7 %collective-permute-done.13.gt_other = bf16[256,512]{1,0:T(8,128)(2,1)S(1)} collective-permute-done((bf16[256,512]{1,0:T(8,128)(2,1)}, bf16[256,512]{1,0:T(8,128)(2,1)S(1)}, u32[]{:S(2)}, u32[]{:S(2)}) %collective-permute-start.13) | collective-permute-done | bytes 262176 | tf_op jit(solution)/shard_map/ppermute | solution.py:359
  60.9 0.7 copy-done.9
  61.6 5.9 %weight_partials.3 = (f32[256,512]{1,0:T(8,128)}, bf16[256,512]{1,0:T(8,128)(2,1)}, bf16[256,512]{1,0:T(8,128)(2,1)}, bf16[256,512]{1,0:T(8,128)(2,1)}) custom-call(s32[6]{0:T(128)} %stack.11.places, bf16[256,512]{1,0:T(8,128)(2,1)} %get-tuple-element.127.gt_ref, bf16[256,512]{1,0:T(8,128)(2,1)} %copy-done.9, bf16[512,4096]{1,0:T(8,128)(2,1)} %bitcast.13, ...), custom_call_target="tpu_custom_call" | custom-call | flops 1073741824 | bytes 8388608 | tf_op jit(solution)/shard_map/weight_partials/pallas_call | solution.py:185
  67.4 0.6 collective-permute-done.11.from_x
  68.1 1.2 collective-permute-done.12.from_y
  69.3 3.4 %middle.2 = (f32[512,512]{1,0:T(8,128)}, bf16[256,512]{1,0:T(8,128)(2,1)}, bf16[256,512]{1,0:T(8,128)(2,1)}) custom-call(f32[512,512]{1,0:T(8,128)} %get-tuple-element.136.own_ref, bf16[512,512]{1,0:T(8,128)(2,1)} %get-tuple-element.137.keep_ref, bf16[512,512]{1,0:T(8,128)(2,1)} %collective-permute-done.11.from_x, ...), custom_call_target="tpu_custom_call" | custom-call | flops 1048576 | bytes 2097152 | tf_op jit(solution)/shard_map/middle/pallas_call | solution.py:216
  72.7 0.6 collective-permute-start.16
  73.3 1.5 %collective-permute-start.17 = (bf16[256,512]{1,0:T(8,128)(2,1)}, bf16[256,512]{1,0:T(8,128)(2,1)}, u32[]{:S(2)}, u32[]{:S(2)}) collective-permute-start(bf16[256,512]{1,0:T(8,128)(2,1)} %get-tuple-element.142), channel_id=1, source_target_pairs={{0,4},{1,5},{2,6},{3,7},{4,0},{5,1},{6,2},{7,3},{8,12},{9,13},{10,... | collective-permute-start | bytes 786440 | tf_op jit(solution)/shard_map/ppermute | solution.py:359
  74.7 1.7 %collective-permute-start.18 = (bf16[256,512]{1,0:T(8,128)(2,1)}, bf16[256,512]{1,0:T(8,128)(2,1)S(1)}, u32[]{:S(2)}, u32[]{:S(2)}) collective-permute-start(bf16[256,512]{1,0:T(8,128)(2,1)} %get-tuple-element.147), channel_id=1, source_target_pairs={{0,2},{1,3},{2,0},{3,1},{4,6},{5,7},{6,4},{7,5},{8,10},{9,11},{10,... | collective-permute-start | bytes 786440 | tf_op jit(solution)/shard_map/ppermute | solution.py:359
  76.5 0.3 collective-permute-start.19
  76.8 5.5 %collective-permute-done.16.x_ref = bf16[256,512]{1,0:T(8,128)(2,1)} collective-permute-done((bf16[256,512]{1,0:T(8,128)(2,1)}, bf16[256,512]{1,0:T(8,128)(2,1)}, u32[]{:S(2)}, u32[]{:S(2)}) %collective-permute-start.16) | collective-permute-done | bytes 262176 | tf_op jit(solution)/shard_map/ppermute | solution.py:359
  82.3 0.6 collective-permute-done.17.y_ref
  82.8 2.3 %quarters.2 = (f32[128,512]{1,0:T(8,128)}, bf16[128,512]{1,0:T(8,128)(2,1)}, bf16[128,512]{1,0:T(8,128)(2,1)}, bf16[128,512]{1,0:T(8,128)(2,1)}) custom-call(s32[1]{0:T(128)} %bitcast.9.z_ref, f32[512,512]{1,0:T(8,128)} %get-tuple-element.140.own_ref, bf16[256,512]{1,0:T(8,128)(2,1)} %collective-permute-done.16.x_ref, ...), custom_call_target="tpu_custom_call" | custom-call | flops 1048576 | bytes 2097152 | tf_op jit(solution)/shard_map/quarters/pallas_call | solution.py:298
  85.1 1.6 %collective-permute-start.22 = (bf16[128,512]{1,0:T(8,128)(2,1)}, bf16[128,512]{1,0:T(8,128)(2,1)S(1)}, u32[]{:S(2)}, u32[]{:S(2)}) collective-permute-start(bf16[128,512]{1,0:T(8,128)(2,1)} %get-tuple-element.151), channel_id=1, source_target_pairs={{0,8},{8,0},{16,24},{24,16},{1,9},{9,1},{17,25},{25,17},{2,10},{10... | collective-permute-start | bytes 393224 | tf_op jit(solution)/shard_map/ppermute | solution.py:359
  86.7 2.6 %collective-permute-start.23 = (bf16[128,512]{1,0:T(8,128)(2,1)}, bf16[128,512]{1,0:T(8,128)(2,1)}, u32[]{:S(2)}, u32[]{:S(2)}) collective-permute-start(bf16[128,512]{1,0:T(8,128)(2,1)} %get-tuple-element.152), channel_id=1, source_target_pairs={{0,16},{8,24},{16,0},{24,8},{1,17},{9,25},{17,1},{25,9},{2,18},{10... | collective-permute-start | bytes 393224 | tf_op jit(solution)/shard_map/ppermute | solution.py:359
  89.3 0.2 collective-permute-start.24
  89.5 0.7 copy-done.8
  90.2 2.2 %middle.3 = (f32[256,512]{1,0:T(8,128)}, bf16[128,512]{1,0:T(8,128)(2,1)}, bf16[128,512]{1,0:T(8,128)(2,1)}) custom-call(f32[256,512]{1,0:T(8,128)} %get-tuple-element.145.own_ref, bf16[256,512]{1,0:T(8,128)(2,1)} %get-tuple-element.146.keep_ref, bf16[256,512]{1,0:T(8,128)(2,1)} %copy-done.8, bf16[256,512]{1,0:T(8,128)(2,1)} %collective-permute-done.19.from_y), custom_call_target="tpu_custom_call" | custom-call | flops 524288 | bytes 2097152 | tf_op jit(solution)/shard_map/middle/pallas_call | solution.py:216
  92.4 1.5 %collective-permute-start.20 = (bf16[128,512]{1,0:T(8,128)(2,1)}, bf16[128,512]{1,0:T(8,128)(2,1)S(1)}, u32[]{:S(2)}, u32[]{:S(2)}) collective-permute-start(bf16[128,512]{1,0:T(8,128)(2,1)} %get-tuple-element.149), channel_id=1, source_target_pairs={{0,2},{1,3},{2,0},{3,1},{4,6},{5,7},{6,4},{7,5},{8,10},{9,11},{10,... | collective-permute-start | bytes 393224 | tf_op jit(solution)/shard_map/ppermute | solution.py:359
  93.8 1.7 %collective-permute-start.21 = (bf16[128,512]{1,0:T(8,128)(2,1)}, bf16[128,512]{1,0:T(8,128)(2,1)S(1)}, u32[]{:S(2)}, u32[]{:S(2)}) collective-permute-start(bf16[128,512]{1,0:T(8,128)(2,1)} %get-tuple-element.150), channel_id=1, source_target_pairs={{0,4},{1,5},{2,6},{3,7},{4,0},{5,1},{6,2},{7,3},{8,12},{9,13},{10,... | collective-permute-start | bytes 393224 | tf_op jit(solution)/shard_map/ppermute | solution.py:359
  95.6 0.9 collective-permute-done.24.refs_3_
  96.5 1.1 collective-permute-done.20.x_ref
  97.6 2.0 %collective-permute-done.21.y_ref = bf16[128,512]{1,0:T(8,128)(2,1)S(1)} collective-permute-done((bf16[128,512]{1,0:T(8,128)(2,1)}, bf16[128,512]{1,0:T(8,128)(2,1)S(1)}, u32[]{:S(2)}, u32[]{:S(2)}) %collective-permute-start.21) | collective-permute-done | bytes 131104 | tf_op jit(solution)/shard_map/ppermute | solution.py:359
  99.5 0.6 copy-done.15
  100.2 1.9 %quarters.3 = (f32[64,512]{1,0:T(8,128)}, bf16[64,512]{1,0:T(8,128)(2,1)}, bf16[64,512]{1,0:T(8,128)(2,1)}, bf16[64,512]{1,0:T(8,128)(2,1)}) custom-call(s32[1]{0:T(128)} %bitcast.9.z_ref, f32[256,512]{1,0:T(8,128)} %get-tuple-element.157.own_ref, bf16[128,512]{1,0:T(8,128)(2,1)} %copy-done.14, bf16[128,512]{1,0:T(8,128)(2,1)} %copy-done.15), custom_call_target="tpu_custom_call" | custom-call | flops 524288 | bytes 2097152 | tf_op jit(solution)/shard_map/quarters/pallas_call | solution.py:298
  102.3 1.8 %collective-permute-start.28 = (bf16[256,768]{1,0:T(8,128)(2,1)S(1)}, bf16[256,768]{1,0:T(8,128)(2,1)S(1)}, u32[]{:S(2)}, u32[]{:S(2)}) collective-permute-start(bf16[256,768]{1,0:T(8,128)(2,1)S(1)} %slice.6), channel_id=1, source_target_pairs={{0,4},{1,5},{2,6},{3,7},{4,0},{5,1},{6,2},{7,3},{8,12},{9,13},{10,... | collective-permute-start | bytes 1179656 | tf_op jit(solution)/shard_map/ppermute | solution.py:359
  104.1 0.9 collective-permute-start.25
  104.9 3.4 %collective-permute-start.26 = (bf16[64,512]{1,0:T(8,128)(2,1)}, bf16[64,512]{1,0:T(8,128)(2,1)S(1)}, u32[]{:S(2)}, u32[]{:S(2)}) collective-permute-start(bf16[64,512]{1,0:T(8,128)(2,1)} %get-tuple-element.166), channel_id=1, source_target_pairs={{0,16},{8,24},{16,0},{24,8},{1,17},{9,25},{17,1},{25,9},{2,18},{10... | collective-permute-start | bytes 196616 | tf_op jit(solution)/shard_map/ppermute | solution.py:359
  108.5 8.2 %input_grad.2.refs_2_ = bf16[512,4096]{1,0:T(8,128)(2,1)} custom-call(s32[6]{0:T(128)} %stack.11.places, bf16[512,512]{1,0:T(8,128)(2,1)} %get-tuple-element.106.gq_ref, bf16[512,256]{1,0:T(8,128)(2,1)} %get-tuple-element.124.gkv_ref, bf16[512,768]{1,0:T(8,128)(2,1)} %refs_0_, bf16[512,768]{1,0:T(8,128)(2,1)} %copy-done.4, bf16[512,768]{1,0:T(8,128)(2,1)} %copy-done.2, ...), custom_call_target="tpu_custom_call" | custom-call | flops 2415919104 | bytes 11534336 | tf_op jit(solution)/shard_map/input_grad/pallas_call | solution.py:243
  116.9 0.4 copy-done.16
  117.3 2.0 %added.1.refs_0_ = bf16[192,512]{1,0:T(8,128)(2,1)} custom-call(f32[128,512]{1,0:T(8,128)} %get-tuple-element.144.refs_0_, bf16[128,512]{1,0:T(8,128)(2,1)} %copy-done.13, bf16[128,512]{1,0:T(8,128)(2,1)} %collective-permute-done.23.refs_2_, bf16[128,512]{1,0:T(8,128)(2,1)} %collective-permute-done.24.refs_3_, f32[64,512]{1,0:T(8,128)} %get-tuple-element.164.refs_4_, ...), custom_call_target="tpu_custom_call" | custom-call | flops 393216 | bytes 1048576 | tf_op jit(solution)/shard_map/added/pallas_call | solution.py:324
  119.3 3.7 %collective-permute-start.32 = (bf16[192,512]{1,0:T(8,128)(2,1)}, bf16[192,512]{1,0:T(8,128)(2,1)S(1)}, u32[]{:S(2)}, u32[]{:S(2)}) collective-permute-start(bf16[192,512]{1,0:T(8,128)(2,1)} %added.1.refs_0_), channel_id=1, source_target_pairs={{0,24},{8,16},{16,8},{24,0},{1,25},{9,17},{17,9},{25,1},{2,26},{10... | collective-permute-start | bytes 589832 | tf_op jit(solution)/shard_map/ppermute | solution.py:359
  123.0 0.7 collective-permute-start.30
  123.7 0.9 copy-done.7
  124.6 4.4 %input_grad.3 = bf16[512,4096]{1,0:T(8,128)(2,1)} custom-call(s32[6]{0:T(128)} %stack.11.places, bf16[512,512]{1,0:T(8,128)(2,1)} %get-tuple-element.106.gq_ref, bf16[512,256]{1,0:T(8,128)(2,1)} %get-tuple-element.124.gkv_ref, bf16[512,768]{1,0:T(8,128)(2,1)} %copy-done.3, bf16[512,768]{1,0:T(8,128)(2,1)} %copy-done.7, ...), custom_call_target="tpu_custom_call", output_to_operand_aliasing={{}: (5, {})} | custom-call | flops 805306368 | bytes 11534336 | tf_op jit(solution)/shard_map/input_grad/pallas_call | solution.py:243
  129.0 0.2 collective-permute-done.32.refs_3_
  129.2 9.7 %collective-permute-done.31.refs_2_ = bf16[192,512]{1,0:T(8,128)(2,1)S(1)} collective-permute-done((bf16[192,512]{1,0:T(8,128)(2,1)}, bf16[192,512]{1,0:T(8,128)(2,1)S(1)}, u32[]{:S(2)}, u32[]{:S(2)}) %collective-permute-start.31) | collective-permute-done | bytes 196640 | tf_op jit(solution)/shard_map/ppermute | solution.py:359
  138.9 0.7 copy-done.11
  139.6 0.7 copy-done.12
  140.2 2.4 %joined.1 = bf16[512,768]{1,0:T(8,128)(2,1)} custom-call(s32[1]{0:T(128)} %bitcast.9.z_ref, bf16[192,512]{1,0:T(8,128)(2,1)} %added.1.refs_0_, bf16[192,512]{1,0:T(8,128)(2,1)} %copy-done.12, bf16[192,512]{1,0:T(8,128)(2,1)} %copy-done.11, bf16[192,512]{1,0:T(8,128)(2,1)} %copy-done.10), custom_call_target="tpu_custom_call" | custom-call | flops 98304 | bytes 2097152 | tf_op jit(solution)/shard_map/joined/pallas_call | solution.py:346
  (66 shorter events, 0.7 us)
Async XLA Ops:
  0.6 14.2 %collective-permute-start.2 = (bf16[512,768]{1,0:T(8,128)(2,1)}, bf16[512,768]{1,0:T(8,128)(2,1)S(1)}, u32[]{:S(2)}, u32[]{:S(2)}) collective-permute-start(bf16[512,768]{1,0:T(8,128)(2,1)} %refs_0_), channel_id=1, source_target_pairs={{0,1},{1,0},{2,3},{3,2},{4,5},{5,4},{6,7},{7,6},{8,9},{9,8},{10,11... | collective-permute-start | bytes 2359304 | tf_op jit(solution)/shard_map/ppermute | solution.py:359
  1.1 7.5 %collective-permute-start.1 = (bf16[512,256]{1,0:T(8,128)(2,1)}, bf16[512,256]{1,0:T(8,128)(2,1)S(1)}, u32[]{:S(2)}, u32[]{:S(2)}) collective-permute-start(bf16[512,256]{1,0:T(8,128)(2,1)} %bitcast.19), channel_id=1, source_target_pairs={{0,1},{2,3},{4,5},{6,7},{1,4},{3,6},{8,9},{10,11},{12,13},{14,15},... | collective-permute-start | bytes 786440 | tf_op jit(solution)/shard_map/ppermute | solution.py:382
  3.1 11.7 %collective-permute-start = (bf16[512,256]{1,0:T(8,128)(2,1)}, bf16[512,256]{1,0:T(8,128)(2,1)S(1)}, u32[]{:S(2)}, u32[]{:S(2)}) collective-permute-start(bf16[512,256]{1,0:T(8,128)(2,1)} %bitcast.20), channel_id=1, source_target_pairs={{0,2},{1,3},{2,4},{3,5},{4,6},{5,7},{8,10},{9,11},{10,12},{11,13},... | collective-permute-start | bytes 786440 | tf_op jit(solution)/shard_map/ppermute | solution.py:381
  8.6 10.9 %copy-start.19 = (bf16[512,256]{1,0:T(8,128)(2,1)}, bf16[512,256]{1,0:T(8,128)(2,1)S(1)}, u32[]{:S(2)}) copy-start(bf16[512,256]{1,0:T(8,128)(2,1)S(1)} %collective-permute-done.1.x_ref) | copy-start | bytes 786436
  14.8 1.8 %copy-start.20 = (bf16[512,256]{1,0:T(8,128)(2,1)}, bf16[512,256]{1,0:T(8,128)(2,1)S(1)}, u32[]{:S(2)}) copy-start(bf16[512,256]{1,0:T(8,128)(2,1)S(1)} %collective-permute-done.d2_ref) | copy-start | bytes 786436
  14.8 1.5 %copy-start.4 = (bf16[512,768]{1,0:T(8,128)(2,1)}, bf16[512,768]{1,0:T(8,128)(2,1)S(1)}, u32[]{:S(2)}) copy-start(bf16[512,768]{1,0:T(8,128)(2,1)S(1)} %collective-permute-done.2.refs_1_) | copy-start | bytes 2359300
  14.8 1.5 %collective-permute-start.3 = (bf16[512,256]{1,0:T(8,128)(2,1)S(1)}, bf16[512,256]{1,0:T(8,128)(2,1)S(1)}, u32[]{:S(2)}, u32[]{:S(2)}) collective-permute-start(bf16[512,256]{1,0:T(8,128)(2,1)S(1)} %collective-permute-done.d2_ref), channel_id=1, source_target_pairs={{0,1},{1,0},{2,3},{3,2},{4,5},{5,4},{6,7},{7,6},{8,9},{9,8},{10,11... | collective-permute-start | bytes 786440 | tf_op jit(solution)/shard_map/ppermute | solution.py:359
  16.3 0.7 copy-start.21
  16.3 22.7 %collective-permute-start.6 = (bf16[512,4096]{1,0:T(8,128)(2,1)}, bf16[512,4096]{1,0:T(8,128)(2,1)S(1)}, u32[]{:S(2)}, u32[]{:S(2)}) collective-permute-start(bf16[512,4096]{1,0:T(8,128)(2,1)} %bitcast.11), channel_id=1, source_target_pairs={{0,1},{1,0},{2,3},{3,2},{4,5},{5,4},{6,7},{7,6},{8,9},{9,8},{10,11... | collective-permute-start | bytes 12582920 | tf_op jit(solution)/shard_map/ppermute | solution.py:359
  17.0 20.6 %collective-permute-start.5 = (bf16[512,768]{1,0:T(8,128)(2,1)}, bf16[512,768]{1,0:T(8,128)(2,1)S(1)}, u32[]{:S(2)}, u32[]{:S(2)}) collective-permute-start(bf16[512,768]{1,0:T(8,128)(2,1)} %refs_0_), channel_id=1, source_target_pairs={{0,4},{1,5},{2,6},{3,7},{4,0},{5,1},{6,2},{7,3},{8,12},{9,13},{10,... | collective-permute-start | bytes 2359304 | tf_op jit(solution)/shard_map/ppermute | solution.py:359
  19.6 19.5 %collective-permute-start.4 = (bf16[512,768]{1,0:T(8,128)(2,1)}, bf16[512,768]{1,0:T(8,128)(2,1)S(1)}, u32[]{:S(2)}, u32[]{:S(2)}) collective-permute-start(bf16[512,768]{1,0:T(8,128)(2,1)} %refs_0_), channel_id=1, source_target_pairs={{0,2},{1,3},{2,0},{3,1},{4,6},{5,7},{6,4},{7,5},{8,10},{9,11},{10,... | collective-permute-start | bytes 2359304 | tf_op jit(solution)/shard_map/ppermute | solution.py:359
  37.6 64.5 %copy-start.1 = (bf16[512,768]{1,0:T(8,128)(2,1)}, bf16[512,768]{1,0:T(8,128)(2,1)S(1)}, u32[]{:S(2)}) copy-start(bf16[512,768]{1,0:T(8,128)(2,1)S(1)} %collective-permute-done.5.refs_4_) | copy-start | bytes 2359300
  39.1 63.0 %copy-start.2 = (bf16[512,768]{1,0:T(8,128)(2,1)}, bf16[512,768]{1,0:T(8,128)(2,1)S(1)}, u32[]{:S(2)}) copy-start(bf16[512,768]{1,0:T(8,128)(2,1)S(1)} %collective-permute-done.4.refs_2_) | copy-start | bytes 2359300
  39.1 4.8 %copy-start = (bf16[512,4096]{1,0:T(8,128)(2,1)}, bf16[512,4096]{1,0:T(8,128)(2,1)S(1)}, u32[]{:S(2)}) copy-start(bf16[512,4096]{1,0:T(8,128)(2,1)S(1)} %collective-permute-done.6.x_other) | copy-start | bytes 12582916
  39.1 2.2 %collective-permute-start.8 = (f32[512,256]{1,0:T(8,128)}, f32[512,256]{1,0:T(8,128)S(1)}, u32[]{:S(2)}, u32[]{:S(2)}) collective-permute-start(f32[512,256]{1,0:T(8,128)} %get-tuple-element.110), channel_id=1, source_target_pairs={{0,1},{1,0},{2,3},{3,2},{4,5},{5,4},{6,7},{7,6},{8,9},{9,8},{10,11... | collective-permute-start | bytes 1572872 | tf_op jit(solution)/shard_map/ppermute | solution.py:359
  39.2 3.2 %collective-permute-start.7 = (bf16[512,512]{1,0:T(8,128)(2,1)}, bf16[512,512]{1,0:T(8,128)(2,1)}, u32[]{:S(2)}, u32[]{:S(2)}) collective-permute-start(bf16[512,512]{1,0:T(8,128)(2,1)} %get-tuple-element.108.gt_ref), channel_id=1, source_target_pairs={{0,1},{1,0},{2,3},{3,2},{4,5},{5,4},{6,7},{7,6},{8,9},{9,8},{10,11... | collective-permute-start | bytes 1572872 | tf_op jit(solution)/shard_map/ppermute | solution.py:359
  39.6 11.7 %collective-permute-start.10 = (bf16[512,256]{1,0:T(8,128)(2,1)}, bf16[512,256]{1,0:T(8,128)(2,1)}, u32[]{:S(2)}, u32[]{:S(2)}) collective-permute-start(bf16[512,256]{1,0:T(8,128)(2,1)} %get-tuple-element.112), channel_id=1, source_target_pairs={{1,0},{3,2},{5,4},{7,6},{4,1},{6,3},{9,8},{11,10},{13,12},{15,14},... | collective-permute-start | bytes 786440 | tf_op jit(solution)/shard_map/ppermute | solution.py:399
  42.4 11.0 %collective-permute-start.9 = (bf16[512,256]{1,0:T(8,128)(2,1)S(1)}, bf16[512,256]{1,0:T(8,128)(2,1)}, u32[]{:S(2)}, u32[]{:S(2)}) collective-permute-start(bf16[512,256]{1,0:T(8,128)(2,1)S(1)} %add_convert_fusion), channel_id=1, source_target_pairs={{2,0},{3,1},{4,2},{5,3},{6,4},{7,5},{10,8},{11,9},{12,10},{13,11},... | collective-permute-start | bytes 786440 | tf_op jit(solution)/shard_map/ppermute | solution.py:408
  53.4 15.8 %collective-permute-start.14 = (bf16[512,768]{1,0:T(8,128)(2,1)S(1)}, bf16[512,768]{1,0:T(8,128)(2,1)S(1)}, u32[]{:S(2)}, u32[]{:S(2)}) collective-permute-start(bf16[512,768]{1,0:T(8,128)(2,1)S(1)} %collective-permute-done.4.refs_2_), channel_id=1, source_target_pairs={{0,1},{1,0},{2,3},{3,2},{4,5},{5,4},{6,7},{7,6},{8,9},{9,8},{10,11... | collective-permute-start | bytes 2359304 | tf_op jit(solution)/shard_map/ppermute | solution.py:359
  53.4 15.8 %collective-permute-start.15 = (bf16[512,768]{1,0:T(8,128)(2,1)S(1)}, bf16[512,768]{1,0:T(8,128)(2,1)S(1)}, u32[]{:S(2)}, u32[]{:S(2)}) collective-permute-start(bf16[512,768]{1,0:T(8,128)(2,1)S(1)} %collective-permute-done.5.refs_4_), channel_id=1, source_target_pairs={{0,1},{1,0},{2,3},{3,2},{4,5},{5,4},{6,7},{7,6},{8,9},{9,8},{10,11... | collective-permute-start | bytes 2359304 | tf_op jit(solution)/shard_map/ppermute | solution.py:359
  53.9 14.1 %collective-permute-start.11 = (bf16[512,512]{1,0:T(8,128)(2,1)}, bf16[512,512]{1,0:T(8,128)(2,1)}, u32[]{:S(2)}, u32[]{:S(2)}) collective-permute-start(bf16[512,512]{1,0:T(8,128)(2,1)} %get-tuple-element.125), channel_id=1, source_target_pairs={{0,2},{1,3},{2,0},{3,1},{4,6},{5,7},{6,4},{7,5},{8,10},{9,11},{10,... | collective-permute-start | bytes 1572872 | tf_op jit(solution)/shard_map/ppermute | solution.py:359
  55.1 14.1 %collective-permute-start.12 = (bf16[512,512]{1,0:T(8,128)(2,1)}, bf16[512,512]{1,0:T(8,128)(2,1)}, u32[]{:S(2)}, u32[]{:S(2)}) collective-permute-start(bf16[512,512]{1,0:T(8,128)(2,1)} %get-tuple-element.126), channel_id=1, source_target_pairs={{0,4},{1,5},{2,6},{3,7},{4,0},{5,1},{6,2},{7,3},{8,12},{9,13},{10,... | collective-permute-start | bytes 1572872 | tf_op jit(solution)/shard_map/ppermute | solution.py:359
  59.1 1.7 %collective-permute-start.13 = (bf16[256,512]{1,0:T(8,128)(2,1)}, bf16[256,512]{1,0:T(8,128)(2,1)S(1)}, u32[]{:S(2)}, u32[]{:S(2)}) collective-permute-start(bf16[256,512]{1,0:T(8,128)(2,1)} %get-tuple-element.127.gt_ref), channel_id=1, source_target_pairs={{0,1},{1,0},{2,3},{3,2},{4,5},{5,4},{6,7},{7,6},{8,9},{9,8},{10,11... | collective-permute-start | bytes 786440 | tf_op jit(solution)/shard_map/ppermute | solution.py:359
  60.9 0.7 copy-start.9
  69.2 39.2 %copy-start.5 = (bf16[512,768]{1,0:T(8,128)(2,1)}, bf16[512,768]{1,0:T(8,128)(2,1)S(1)}, u32[]{:S(2)}) copy-start(bf16[512,768]{1,0:T(8,128)(2,1)S(1)} %collective-permute-done.14.refs_3_) | copy-start | bytes 2359300
  69.2 39.2 %copy-start.6 = (bf16[512,768]{1,0:T(8,128)(2,1)}, bf16[512,768]{1,0:T(8,128)(2,1)S(1)}, u32[]{:S(2)}) copy-start(bf16[512,768]{1,0:T(8,128)(2,1)S(1)} %collective-permute-done.15.refs_5_) | copy-start | bytes 2359300
  72.7 9.6 %collective-permute-start.16 = (bf16[256,512]{1,0:T(8,128)(2,1)}, bf16[256,512]{1,0:T(8,128)(2,1)}, u32[]{:S(2)}, u32[]{:S(2)}) collective-permute-start(bf16[256,512]{1,0:T(8,128)(2,1)} %get-tuple-element.141), channel_id=1, source_target_pairs={{0,2},{1,3},{2,0},{3,1},{4,6},{5,7},{6,4},{7,5},{8,10},{9,11},{10,... | collective-permute-start | bytes 786440 | tf_op jit(solution)/shard_map/ppermute | solution.py:359
  73.3 9.6 %collective-permute-start.17 = (bf16[256,512]{1,0:T(8,128)(2,1)}, bf16[256,512]{1,0:T(8,128)(2,1)}, u32[]{:S(2)}, u32[]{:S(2)}) collective-permute-start(bf16[256,512]{1,0:T(8,128)(2,1)} %get-tuple-element.142), channel_id=1, source_target_pairs={{0,4},{1,5},{2,6},{3,7},{4,0},{5,1},{6,2},{7,3},{8,12},{9,13},{10,... | collective-permute-start | bytes 786440 | tf_op jit(solution)/shard_map/ppermute | solution.py:359
  74.7 14.8 %collective-permute-start.18 = (bf16[256,512]{1,0:T(8,128)(2,1)}, bf16[256,512]{1,0:T(8,128)(2,1)S(1)}, u32[]{:S(2)}, u32[]{:S(2)}) collective-permute-start(bf16[256,512]{1,0:T(8,128)(2,1)} %get-tuple-element.147), channel_id=1, source_target_pairs={{0,2},{1,3},{2,0},{3,1},{4,6},{5,7},{6,4},{7,5},{8,10},{9,11},{10,... | collective-permute-start | bytes 786440 | tf_op jit(solution)/shard_map/ppermute | solution.py:359
  76.5 13.0 %collective-permute-start.19 = (bf16[256,512]{1,0:T(8,128)(2,1)}, bf16[256,512]{1,0:T(8,128)(2,1)}, u32[]{:S(2)}, u32[]{:S(2)}) collective-permute-start(bf16[256,512]{1,0:T(8,128)(2,1)} %get-tuple-element.148), channel_id=1, source_target_pairs={{0,4},{1,5},{2,6},{3,7},{4,0},{5,1},{6,2},{7,3},{8,12},{9,13},{10,... | collective-permute-start | bytes 786440 | tf_op jit(solution)/shard_map/ppermute | solution.py:359
  85.1 10.4 %collective-permute-start.22 = (bf16[128,512]{1,0:T(8,128)(2,1)}, bf16[128,512]{1,0:T(8,128)(2,1)S(1)}, u32[]{:S(2)}, u32[]{:S(2)}) collective-permute-start(bf16[128,512]{1,0:T(8,128)(2,1)} %get-tuple-element.151), channel_id=1, source_target_pairs={{0,8},{8,0},{16,24},{24,16},{1,9},{9,1},{17,25},{25,17},{2,10},{10... | collective-permute-start | bytes 393224 | tf_op jit(solution)/shard_map/ppermute | solution.py:359
  86.7 8.9 %collective-permute-start.23 = (bf16[128,512]{1,0:T(8,128)(2,1)}, bf16[128,512]{1,0:T(8,128)(2,1)}, u32[]{:S(2)}, u32[]{:S(2)}) collective-permute-start(bf16[128,512]{1,0:T(8,128)(2,1)} %get-tuple-element.152), channel_id=1, source_target_pairs={{0,16},{8,24},{16,0},{24,8},{1,17},{9,25},{17,1},{25,9},{2,18},{10... | collective-permute-start | bytes 393224 | tf_op jit(solution)/shard_map/ppermute | solution.py:359
  89.3 7.2 %collective-permute-start.24 = (bf16[128,512]{1,0:T(8,128)(2,1)}, bf16[128,512]{1,0:T(8,128)(2,1)}, u32[]{:S(2)}, u32[]{:S(2)}) collective-permute-start(bf16[128,512]{1,0:T(8,128)(2,1)} %get-tuple-element.153), channel_id=1, source_target_pairs={{0,24},{8,16},{16,8},{24,0},{1,25},{9,17},{17,9},{25,1},{2,26},{10... | collective-permute-start | bytes 393224 | tf_op jit(solution)/shard_map/ppermute | solution.py:359
  89.5 0.7 copy-start.8
  92.4 5.2 %collective-permute-start.20 = (bf16[128,512]{1,0:T(8,128)(2,1)}, bf16[128,512]{1,0:T(8,128)(2,1)S(1)}, u32[]{:S(2)}, u32[]{:S(2)}) collective-permute-start(bf16[128,512]{1,0:T(8,128)(2,1)} %get-tuple-element.149), channel_id=1, source_target_pairs={{0,2},{1,3},{2,0},{3,1},{4,6},{5,7},{6,4},{7,5},{8,10},{9,11},{10,... | collective-permute-start | bytes 393224 | tf_op jit(solution)/shard_map/ppermute | solution.py:359
  93.8 5.7 %collective-permute-start.21 = (bf16[128,512]{1,0:T(8,128)(2,1)}, bf16[128,512]{1,0:T(8,128)(2,1)S(1)}, u32[]{:S(2)}, u32[]{:S(2)}) collective-permute-start(bf16[128,512]{1,0:T(8,128)(2,1)} %get-tuple-element.150), channel_id=1, source_target_pairs={{0,4},{1,5},{2,6},{3,7},{4,0},{5,1},{6,2},{7,3},{8,12},{9,13},{10,... | collective-permute-start | bytes 393224 | tf_op jit(solution)/shard_map/ppermute | solution.py:359
  95.6 21.1 %copy-start.13 = (bf16[128,512]{1,0:T(8,128)(2,1)}, bf16[128,512]{1,0:T(8,128)(2,1)S(1)}, u32[]{:S(2)}) copy-start(bf16[128,512]{1,0:T(8,128)(2,1)S(1)} %collective-permute-done.22.refs_1_) | copy-start | bytes 393220
  97.6 2.0 %copy-start.14 = (bf16[128,512]{1,0:T(8,128)(2,1)}, bf16[128,512]{1,0:T(8,128)(2,1)S(1)}, u32[]{:S(2)}) copy-start(bf16[128,512]{1,0:T(8,128)(2,1)S(1)} %collective-permute-done.20.x_ref) | copy-start | bytes 393220
  99.5 0.6 copy-start.15
  102.2 14.5 %collective-permute-start.29 = (bf16[256,768]{1,0:T(8,128)(2,1)S(1)}, bf16[256,768]{1,0:T(8,128)(2,1)S(1)}, u32[]{:S(2)}, u32[]{:S(2)}) collective-permute-start(bf16[256,768]{1,0:T(8,128)(2,1)S(1)} %slice.7), channel_id=1, source_target_pairs={{0,2},{1,3},{2,0},{3,1},{4,6},{5,7},{6,4},{7,5},{8,10},{9,11},{10,... | collective-permute-start | bytes 1179656 | tf_op jit(solution)/shard_map/ppermute | solution.py:359
  102.3 14.4 %collective-permute-start.28 = (bf16[256,768]{1,0:T(8,128)(2,1)S(1)}, bf16[256,768]{1,0:T(8,128)(2,1)S(1)}, u32[]{:S(2)}, u32[]{:S(2)}) collective-permute-start(bf16[256,768]{1,0:T(8,128)(2,1)S(1)} %slice.6), channel_id=1, source_target_pairs={{0,4},{1,5},{2,6},{3,7},{4,0},{5,1},{6,2},{7,3},{8,12},{9,13},{10,... | collective-permute-start | bytes 1179656 | tf_op jit(solution)/shard_map/ppermute | solution.py:359
  104.1 12.6 %collective-permute-start.25 = (bf16[64,512]{1,0:T(8,128)(2,1)}, bf16[64,512]{1,0:T(8,128)(2,1)S(1)}, u32[]{:S(2)}, u32[]{:S(2)}) collective-permute-start(bf16[64,512]{1,0:T(8,128)(2,1)} %get-tuple-element.165), channel_id=1, source_target_pairs={{0,8},{8,0},{16,24},{24,16},{1,9},{9,1},{17,25},{25,17},{2,10},{10... | collective-permute-start | bytes 196616 | tf_op jit(solution)/shard_map/ppermute | solution.py:359
  104.9 11.7 %collective-permute-start.26 = (bf16[64,512]{1,0:T(8,128)(2,1)}, bf16[64,512]{1,0:T(8,128)(2,1)S(1)}, u32[]{:S(2)}, u32[]{:S(2)}) collective-permute-start(bf16[64,512]{1,0:T(8,128)(2,1)} %get-tuple-element.166), channel_id=1, source_target_pairs={{0,16},{8,24},{16,0},{24,8},{1,17},{9,25},{17,1},{25,9},{2,18},{10... | collective-permute-start | bytes 196616 | tf_op jit(solution)/shard_map/ppermute | solution.py:359
  108.3 8.4 %collective-permute-start.27 = (bf16[64,512]{1,0:T(8,128)(2,1)}, bf16[64,512]{1,0:T(8,128)(2,1)S(1)}, u32[]{:S(2)}, u32[]{:S(2)}) collective-permute-start(bf16[64,512]{1,0:T(8,128)(2,1)} %get-tuple-element.167), channel_id=1, source_target_pairs={{0,24},{8,16},{16,8},{24,0},{1,25},{9,17},{17,9},{25,1},{2,26},{10... | collective-permute-start | bytes 196616 | tf_op jit(solution)/shard_map/ppermute | solution.py:359
  116.7 0.6 copy-start.16
  116.7 0.6 copy-start.17
  116.7 0.6 copy-start.18
  116.8 6.9 %copy-start.3 = (bf16[512,768]{1,0:T(8,128)(2,1)}, bf16[512,768]{1,0:T(8,128)(2,1)S(1)}, u32[]{:S(2)}) copy-start(bf16[512,768]{1,0:T(8,128)(2,1)S(1)} %constant_dynamic-update-slice_fusion.refs_0_) | copy-start | bytes 2359300
  116.8 6.9 %collective-permute-start.33 = (bf16[512,768]{1,0:T(8,128)(2,1)S(1)}, bf16[512,768]{1,0:T(8,128)(2,1)S(1)}, u32[]{:S(2)}, u32[]{:S(2)}) collective-permute-start(bf16[512,768]{1,0:T(8,128)(2,1)S(1)} %constant_dynamic-update-slice_fusion.refs_0_), channel_id=1, source_target_pairs={{0,1},{1,0},{2,3},{3,2},{4,5},{5,4},{6,7},{7,6},{8,9},{9,8},{10,11... | collective-permute-start | bytes 2359304 | tf_op jit(solution)/shard_map/ppermute | solution.py:359
  119.3 9.9 %collective-permute-start.32 = (bf16[192,512]{1,0:T(8,128)(2,1)}, bf16[192,512]{1,0:T(8,128)(2,1)S(1)}, u32[]{:S(2)}, u32[]{:S(2)}) collective-permute-start(bf16[192,512]{1,0:T(8,128)(2,1)} %added.1.refs_0_), channel_id=1, source_target_pairs={{0,24},{8,16},{16,8},{24,0},{1,25},{9,17},{17,9},{25,1},{2,26},{10... | collective-permute-start | bytes 589832 | tf_op jit(solution)/shard_map/ppermute | solution.py:359
  123.0 15.9 %collective-permute-start.31 = (bf16[192,512]{1,0:T(8,128)(2,1)}, bf16[192,512]{1,0:T(8,128)(2,1)S(1)}, u32[]{:S(2)}, u32[]{:S(2)}) collective-permute-start(bf16[192,512]{1,0:T(8,128)(2,1)} %added.1.refs_0_), channel_id=1, source_target_pairs={{0,16},{8,24},{16,0},{24,8},{1,17},{9,25},{17,1},{25,9},{2,18},{10... | collective-permute-start | bytes 589832 | tf_op jit(solution)/shard_map/ppermute | solution.py:359
  123.0 15.9 %collective-permute-start.30 = (bf16[192,512]{1,0:T(8,128)(2,1)}, bf16[192,512]{1,0:T(8,128)(2,1)S(1)}, u32[]{:S(2)}, u32[]{:S(2)}) collective-permute-start(bf16[192,512]{1,0:T(8,128)(2,1)} %added.1.refs_0_), channel_id=1, source_target_pairs={{0,8},{8,0},{16,24},{24,16},{1,9},{9,1},{17,25},{25,17},{2,10},{10... | collective-permute-start | bytes 589832 | tf_op jit(solution)/shard_map/ppermute | solution.py:359
  123.7 0.9 copy-start.7
  129.2 9.7 %copy-start.10 = (bf16[192,512]{1,0:T(8,128)(2,1)}, bf16[192,512]{1,0:T(8,128)(2,1)S(1)}, u32[]{:S(2)}) copy-start(bf16[192,512]{1,0:T(8,128)(2,1)S(1)} %collective-permute-done.32.refs_3_) | copy-start | bytes 589828
  138.9 0.7 copy-start.11
  139.5 0.7 copy-start.12

commit v5 on v4

--- a/solution.py
+++ b/solution.py
@@ -12,6 +12,10 @@
 LOG2E = 1.4426950408889634
 KEY_STEP = 512
 Q_STEP = 256
+
+
+SMALL_VMEM = 4 * 2**20
+VMEM = pl.BlockSpec(memory_space=pltpu.VMEM)
 
 
 def nt_dot(a, b):
@@ -136,8 +140,8 @@
             jax.ShapeDtypeStruct((rows, both), jnp.bfloat16),
         ),
         grid=(1,),
-        in_specs=[smem, smem] + [whole((rows, width))] * 2 + [whole((rows, both))] * 4,
-        out_specs=[whole((rows, width)), whole((width, rows))] + [whole((rows, both))] * 4,
+        in_specs=[smem, smem] + [whole((rows, width))] * 2 + [whole((rows, both))] + [VMEM] * 3,
+        out_specs=[VMEM] * 6,
         scratch_shapes=[
             pltpu.VMEM((4 * rows, both), jnp.bfloat16),
             pltpu.VMEM((hd, 4 * rows), jnp.bfloat16),
@@ -145,7 +149,7 @@
             pltpu.VMEM((4 * rows, wide), jnp.float32),
             pltpu.VMEM((4 * rows, both), jnp.float32),
         ],
-        compiler_params=pltpu.CompilerParams(vmem_limit_bytes=58 * 2**20),
+        compiler_params=pltpu.CompilerParams(vmem_limit_bytes=30 * 2**20),
         cost_estimate=pl.CostEstimate(flops=12 * 10**9, bytes_accessed=6 * 2**20, transcendentals=4 * 2**20),
     )(index, lengths, q, g, own, d2, r, x)
 
@@ -180,7 +184,6 @@
 def weight_partials(places, gt, gt_other, x, x_other, block):
     cols, rows = gt.shape
     chips = x_other.shape[1] // block // 2
-    whole = lambda k, s: (0, 0)
     strip = pl.BlockSpec((rows, block), lambda k, s: (0, (s[0] ^ s[2 + k]) * 2 + s[1]))
     return pl.pallas_call(
         weight_kernel,
@@ -190,24 +193,37 @@
         grid_spec=pltpu.PrefetchScalarGridSpec(
             num_scalar_prefetch=1,
             grid=(chips,),
-            in_specs=[pl.BlockSpec((cols, rows), whole)] * 2 + [strip] * 2,
-            out_specs=[pl.BlockSpec((cols, block), whole)] * 4,
-        ),
-        compiler_params=pltpu.CompilerParams(vmem_limit_bytes=58 * 2**20),
+            in_specs=[VMEM] * 2 + [strip] * 2,
+            out_specs=[VMEM] * 4,
+        ),
+        compiler_params=pltpu.CompilerParams(vmem_limit_bytes=12 * 2**20),
         cost_estimate=pl.CostEstimate(
             flops=4 * cols * rows * block * chips, bytes_accessed=8 * 2**20, transcendentals=0
         ),
     )(places, gt, gt_other, x, x_other)
+
+
+def row_loop(rows, step, body):
+    def turn(i, carried):
+        body(pl.multiple_of(i * step, step))
+        return carried
+
+    lax.fori_loop(0, rows // step, turn, 0)
 
 
 def middle_kernel(own_ref, keep_ref, from_x, from_y, own_out, next_x, next_y):
     f32 = jnp.float32
     half = own_ref.shape[0] // 2
-    upper, lower = slice(0, half), slice(half, 2 * half)
-    own_out[upper, :] = own_ref[upper, :] + from_x[upper, :].astype(f32)
-    own_out[lower, :] = own_ref[lower, :] + from_y[upper, :].astype(f32)
-    next_y[...] = (keep_ref[upper, :].astype(f32) + from_x[lower, :].astype(f32)).astype(next_y.dtype)
-    next_x[...] = (keep_ref[lower, :].astype(f32) + from_y[lower, :].astype(f32)).astype(next_x.dtype)
+    step = 32
+
+    def body(at):
+        top, low = pl.ds(at, step), pl.ds(half + at, step)
+        own_out[top, :] = own_ref[top, :] + from_x[top, :].astype(f32)
+        own_out[low, :] = own_ref[low, :] + from_y[top, :].astype(f32)
+        next_y[top, :] = (keep_ref[top, :].astype(f32) + from_x[low, :].astype(f32)).astype(next_y.dtype)
+        next_x[top, :] = (keep_ref[low, :].astype(f32) + from_y[low, :].astype(f32)).astype(next_x.dtype)
+
+    row_loop(half, step, body)
 
 
 def middle(own, keep, from_x, from_y):
@@ -217,6 +233,9 @@
         middle_kernel,
         name="middle",
         out_shape=[jax.ShapeDtypeStruct(own.shape, jnp.float32), half, half],
+        in_specs=[VMEM] * 4,
+        out_specs=[VMEM] * 3,
+        compiler_params=pltpu.CompilerParams(vmem_limit_bytes=SMALL_VMEM),
         cost_estimate=pl.CostEstimate(flops=4 * rows * cols, bytes_accessed=2**21, transcendentals=0),
     )(own, keep, from_x, from_y)
 
@@ -253,7 +272,7 @@
             out_specs=pl.BlockSpec((rows, block), lambda k, s: (0, (s[0] * 2 + s[1]) ^ (start + k))),
         ),
         input_output_aliases={3 + count: 0} if before else {},
-        compiler_params=pltpu.CompilerParams(vmem_limit_bytes=58 * 2**20),
+        compiler_params=pltpu.CompilerParams(vmem_limit_bytes=20 * 2**20),
         cost_estimate=pl.CostEstimate(
             flops=2 * rows * cols * block * count, bytes_accessed=11 * 2**20, transcendentals=0
         ),
@@ -261,9 +280,15 @@
 
 
 def finish_kernel(own_ref, two_ref, x_ref, out_ref, out_t_ref):
-    total = own_ref[...] + two_ref[...].astype(jnp.float32) + x_ref[...].astype(jnp.float32)
-    out_ref[...] = total.astype(out_ref.dtype)
-    out_t_ref[...] = total.T.astype(out_t_ref.dtype)
+    step = 128
+
+    def body(start):
+        at = pl.ds(start, step)
+        total = own_ref[at, :] + two_ref[at, :].astype(jnp.float32) + x_ref[at, :].astype(jnp.float32)
+        out_ref[at, :] = total.astype(out_ref.dtype)
+        out_t_ref[:, at] = total.T.astype(out_t_ref.dtype)
+
+    row_loop(own_ref.shape[0], step, body)
 
 
 def finish_kv(own, from_two, from_x):
@@ -275,6 +300,9 @@
             jax.ShapeDtypeStruct((rows, cols), jnp.bfloat16),
             jax.ShapeDtypeStruct((cols, rows), jnp.bfloat16),
         ),
+        in_specs=[VMEM] * 3,
+        out_specs=[VMEM] * 2,
+        compiler_params=pltpu.CompilerParams(vmem_limit_bytes=SMALL_VMEM),
         cost_estimate=pl.CostEstimate(flops=4 * rows * cols, bytes_accessed=2**21, transcendentals=0),
     )(own, from_two, from_x)
 
@@ -282,40 +310,49 @@
 def quarters_kernel(z_ref, own_ref, x_ref, y_ref, mine_out, *outs):
     z = z_ref[0]
     quarter = mine_out.shape[0]
+    step = 32
     for k, out in enumerate((mine_out, *outs)):
         place = z ^ k
-        at = pl.ds(pl.multiple_of(place * quarter, quarter), quarter)
-        half = pl.ds(pl.multiple_of(lax.rem(place, 2) * quarter, quarter), quarter)
-        add = jnp.where(place < 2, y_ref[half, :].astype(jnp.float32), x_ref[half, :].astype(jnp.float32))
-        out[...] = (own_ref[at, :] + add).astype(out.dtype)
+
+        def body(start, place=place, out=out):
+            at = pl.ds(pl.multiple_of(place * quarter + start, step), step)
+            half = pl.ds(pl.multiple_of(lax.rem(place, 2) * quarter + start, step), step)
+            add = jnp.where(place < 2, y_ref[half, :].astype(jnp.float32), x_ref[half, :].astype(jnp.float32))
+            out[pl.ds(start, step), :] = (own_ref[at, :] + add).astype(out.dtype)
+
+        row_loop(quarter, step, body)
 
 
 def quarters_of(z, own, from_x, from_y):
     rows, cols = own.shape
     piece = (rows // 4, cols)
-    whole = lambda i: (0, 0)
-    out = pl.BlockSpec(piece, whole)
     return pl.pallas_call(
         quarters_kernel,
         name="quarters",
         out_shape=[jax.ShapeDtypeStruct(piece, jnp.float32)] + [jax.ShapeDtypeStruct(piece, jnp.bfloat16)] * 3,
-        grid=(1,),
-        in_specs=[pl.BlockSpec(memory_space=pltpu.SMEM)]
-        + [pl.BlockSpec(a.shape, whole) for a in (own, from_x, from_y)],
-        out_specs=[out] * 4,
+        in_specs=[pl.BlockSpec(memory_space=pltpu.SMEM)] + [VMEM] * 3,
+        out_specs=[VMEM] * 4,
+        compiler_params=pltpu.CompilerParams(vmem_limit_bytes=SMALL_VMEM),
         cost_estimate=pl.CostEstimate(flops=4 * rows * cols, bytes_accessed=2**21, transcendentals=0),
     )(z, own, from_x, from_y)
 
 
 def added_kernel(*refs):
     out_ref = refs[-1]
-    start = 0
+    first = 0
+    step = 32
     for part in range(0, len(refs) - 1, 4):
-        total = refs[part][...]
-        for ref in refs[part + 1 : part + 4]:
-            total = total + ref[...].astype(jnp.float32)
-        out_ref[start : start + total.shape[0], :] = total.astype(out_ref.dtype)
-        start += total.shape[0]
+        own = refs[part]
+
+        def body(start, part=part, first=first):
+            at = pl.ds(start, step)
+            total = refs[part][at, :]
+            for ref in refs[part + 1 : part + 4]:
+                total = total + ref[at, :].astype(jnp.float32)
+            out_ref[pl.ds(pl.multiple_of(first + start, step), step), :] = total.astype(out_ref.dtype)
+
+        row_loop(own.shape[0], step, body)
+        first += own.shape[0]
 
 
 def added(parts):
@@ -325,6 +362,9 @@
         added_kernel,
         name="added",
         out_shape=jax.ShapeDtypeStruct((rows, cols), jnp.bfloat16),
+        in_specs=[VMEM] * len(pieces),
+        out_specs=VMEM,
+        compiler_params=pltpu.CompilerParams(vmem_limit_bytes=SMALL_VMEM),
         cost_estimate=pl.CostEstimate(flops=4 * rows * cols, bytes_accessed=2**20, transcendentals=0),
     )(*pieces)
 
@@ -337,20 +377,24 @@
         place = z ^ k
         scr[pl.ds(pl.multiple_of(place * split, split), split), :] = piece[:split, :]
         scr[pl.ds(pl.multiple_of(4 * split + place * rest, rest), rest), :] = piece[split:, :]
-    out_ref[...] = scr[...].T
+
+    def body(start):
+        at = pl.ds(start, 128)
+        out_ref[:, at] = scr[at, :].T
+
+    row_loop(scr.shape[0], 128, body)
 
 
 def joined(z, pieces, split):
     rows, cols = pieces[0].shape
-    whole = lambda i: (0, 0)
     return pl.pallas_call(
         functools.partial(joined_kernel, split=split),
         name="joined",
         out_shape=jax.ShapeDtypeStruct((cols, 4 * rows), jnp.bfloat16),
-        grid=(1,),
-        in_specs=[pl.BlockSpec(memory_space=pltpu.SMEM)] + [pl.BlockSpec((rows, cols), whole)] * 4,
-        out_specs=pl.BlockSpec((cols, 4 * rows), whole),
+        in_specs=[pl.BlockSpec(memory_space=pltpu.SMEM)] + [VMEM] * 4,
+        out_specs=VMEM,
         scratch_shapes=[pltpu.VMEM((4 * rows, cols), jnp.bfloat16)],
+        compiler_params=pltpu.CompilerParams(vmem_limit_bytes=SMALL_VMEM),
         cost_estimate=pl.CostEstimate(flops=rows * cols, bytes_accessed=2**21, transcendentals=0),
     )(z, *pieces)
 

time: 143 us -> 130 us (0.909)
  Pallas kernels: 50.1 us -> 28.8 us
  waiting for transfers between devices: 44.8 us -> 56.9 us
  starting transfers between devices: 39.8 us -> 35.7 us
    ppermute x30, waiting for transfers between devices: 36.5 us -> 45.3 us  [flipped(): lax.ppermute(array, axis, [(i, i ^ bits) for i in range(lax.axis_size(axi...]
    pallas_call x2, Pallas kernels: 13.3 us -> 7.79 us  [weight_partials(): pl.pallas_call(weight_kernel, name='weight_partials', out_shape=[jax.Shap...]
    pallas_call x2, Pallas kernels: 12.5 us -> 8.06 us  [input_grad(): pl.pallas_call(functools.partial(input_kernel, count=count), name='input_...]
    ppermute x30, starting transfers between devices: 30.2 us -> 26.1 us  [flipped(): lax.ppermute(array, axis, [(i, i ^ bits) for i in range(lax.axis_size(axi...]
    pallas_call x2, Pallas kernels: 5.6 us -> 2.39 us  [middle(): pl.pallas_call(middle_kernel, name='middle', out_shape=[jax.ShapeDtypeStr...]
    ppermute x1, waiting for transfers between devices: 2.1 us -> 4.87 us  [per_device(): from_two = lax.ppermute(kv_d2, 'ctx', back(by_two))]
    pallas_call x2, Pallas kernels: 4.21 us -> 1.47 us  [quarters_of(): pl.pallas_call(quarters_kernel, name='quarters', out_shape=[jax.ShapeDtyp...]
    pallas_call x1, Pallas kernels: 1.95 us -> 0.13 us  [added(): pl.pallas_call(added_kernel, name='added', out_shape=jax.ShapeDtypeStruct...]
  transfers between devices with their start and end apart: 34 -> 34, of which waited for: 16 -> 18; matrix products, arithmetic and copies ran while one was open for 1% -> 0% of each run, Pallas kernels for 30% -> 20%
where the time goes in v5:
time: 130 us; the launch traced here: 129 us
  waiting for transfers between devices  56.9 us (44%)
  starting transfers between devices  35.7 us (27%)
  Pallas kernels  28.8 us (22%)
  local copies, waits for them, and re-layouts  6.86 us (5%)
    ppermute x30, waiting for transfers between devices, flipped(): lax.ppermute(array, axis, [(i, i ^ bits) for i in range(lax.axis_size(axi...  45.3 us
    ppermute x30, starting transfers between devices, flipped(): lax.ppermute(array, axis, [(i, i ^ bits) for i in range(lax.axis_size(axi...  26.1 us
    pallas_call x2, Pallas kernels, input_grad(): pl.pallas_call(functools.partial(input_kernel, count=count), name='input_...  8.06 us
    pallas_call x2, Pallas kernels, weight_partials(): pl.pallas_call(weight_kernel, name='weight_partials', out_shape=[jax.Shap...  7.79 us
    ppermute x1, waiting for transfers between devices, per_device(): d2 = lax.ppermute(own, 'ctx', by_two)  6.7 us
    unnamed x37, local copies, waits for them, and re-layouts  6.7 us
    pallas_call x1, Pallas kernels, attention(): pl.pallas_call(attention_kernel, name='attention', out_shape=(jax.ShapeDt...  6.4 us
    ppermute x1, waiting for transfers between devices, per_device(): from_two = lax.ppermute(kv_d2, 'ctx', back(by_two))  4.87 us
  transfers between devices with their start and end apart: 34, of which 18 were waited for; matrix products, arithmetic and copies ran while one was open for 0% of the time, Pallas kernels for 20%

profile of v5, /device:TPU:0, one launch (start us, length us, event | category | flops | bytes accessed | tf_op | source)
XLA Modules:
  0.0 129.1 jit_solution(17463710804434495269)
XLA Ops:
  0.6 0.5 collective-permute-start.2
  1.1 2.0 %collective-permute-start.1 = (bf16[512,256]{1,0:T(8,128)(2,1)}, bf16[512,256]{1,0:T(8,128)(2,1)S(1)}, u32[]{:S(2)}, u32[]{:S(2)}) collective-permute-start(bf16[512,256]{1,0:T(8,128)(2,1)} %bitcast.18), channel_id=1, source_target_pairs={{0,1},{2,3},{4,5},{6,7},{1,4},{3,6},{8,9},{10,11},{12,13},{14,15},... | collective-permute-start | bytes 786440 | tf_op jit(solution)/shard_map/ppermute | solution.py:426
  3.1 4.9 %collective-permute-start = (bf16[512,256]{1,0:T(8,128)(2,1)}, bf16[512,256]{1,0:T(8,128)(2,1)S(1)}, u32[]{:S(2)}, u32[]{:S(2)}) collective-permute-start(bf16[512,256]{1,0:T(8,128)(2,1)} %bitcast.19), channel_id=1, source_target_pairs={{0,2},{1,3},{2,4},{3,5},{4,6},{5,7},{8,10},{9,11},{10,12},{11,13},... | collective-permute-start | bytes 786440 | tf_op jit(solution)/shard_map/ppermute | solution.py:425
  8.1 6.7 %collective-permute-done.d2_ref = bf16[512,256]{1,0:T(8,128)(2,1)S(1)} collective-permute-done((bf16[512,256]{1,0:T(8,128)(2,1)}, bf16[512,256]{1,0:T(8,128)(2,1)S(1)}, u32[]{:S(2)}, u32[]{:S(2)}) %collective-permute-start) | collective-permute-done | bytes 262176 | tf_op jit(solution)/shard_map/ppermute | solution.py:425
  14.8 0.9 copy-done.4
  15.7 0.3 collective-permute-start.3
  16.0 1.2 collective-permute-done.3.r_ref
  17.2 0.3 collective-permute-start.6
  17.5 2.3 %collective-permute-start.5 = (bf16[512,768]{1,0:T(8,128)(2,1)}, bf16[512,768]{1,0:T(8,128)(2,1)S(1)}, u32[]{:S(2)}, u32[]{:S(2)}) collective-permute-start(bf16[512,768]{1,0:T(8,128)(2,1)} %refs_0_), channel_id=1, source_target_pairs={{0,4},{1,5},{2,6},{3,7},{4,0},{5,1},{6,2},{7,3},{8,12},{9,13},{10,... | collective-permute-start | bytes 2359304 | tf_op jit(solution)/shard_map/ppermute | solution.py:403
  19.8 1.0 copy-done.14
  20.9 1.0 copy-done.15
  21.9 0.9 copy-done.16
  22.9 0.7 copy-done.17
  23.5 6.4 %attention.1 = (bf16[512,512]{1,0:T(8,128)(2,1)}, bf16[512,512]{1,0:T(8,128)(2,1)S(1)}, f32[512,256]{1,0:T(8,128)S(1)}, f32[512,256]{1,0:T(8,128)S(1)}, f32[512,...) custom-call(s32[1]{0:T(128)} %bitcast.idx_ref, s32[1,16]{1,0:T(1,128)S(1)} %copy-done.17, bf16[512,512]{1,0:T(8,128)(2,1)S(1)} %bitcast.16, ...), custom_call_target="tpu_custom_call" | custom-call | flops 12000000000 | bytes 6291456 | tf_op jit(solution)/shard_map/attention/pallas_call | solution.py:131
  29.9 8.2 %collective-permute-done.5.refs_4_ = bf16[512,768]{1,0:T(8,128)(2,1)S(1)} collective-permute-done((bf16[512,768]{1,0:T(8,128)(2,1)}, bf16[512,768]{1,0:T(8,128)(2,1)S(1)}, u32[]{:S(2)}, u32[]{:S(2)}) %collective-permute-start.5) | collective-permute-done | bytes 786464 | tf_op jit(solution)/shard_map/ppermute | solution.py:403
  38.1 1.5 %collective-permute-done.4.refs_2_ = bf16[512,768]{1,0:T(8,128)(2,1)S(1)} collective-permute-done((bf16[512,768]{1,0:T(8,128)(2,1)}, bf16[512,768]{1,0:T(8,128)(2,1)S(1)}, u32[]{:S(2)}, u32[]{:S(2)}) %collective-permute-start.4) | collective-permute-done | bytes 786464 | tf_op jit(solution)/shard_map/ppermute | solution.py:403
  39.6 0.5 collective-permute-start.7
  40.1 1.3 collective-permute-start.10
  41.4 0.1 collective-permute-done.8
  41.5 0.7 collective-permute-done.7.gt_other
  42.2 1.5 %collective-permute-start.9 = (bf16[512,256]{1,0:T(8,128)(2,1)S(1)}, bf16[512,256]{1,0:T(8,128)(2,1)S(1)}, u32[]{:S(2)}, u32[]{:S(2)}) collective-permute-start(bf16[512,256]{1,0:T(8,128)(2,1)S(1)} %add_convert_fusion), channel_id=1, source_target_pairs={{2,0},{3,1},{4,2},{5,3},{6,4},{7,5},{10,8},{11,9},{12,10},{13,11},... | collective-permute-start | bytes 786440 | tf_op jit(solution)/shard_map/ppermute | solution.py:452
  43.7 4.1 %weight_partials.2 = (f32[512,512]{1,0:T(8,128)S(1)}, bf16[512,512]{1,0:T(8,128)(2,1)S(1)}, bf16[512,512]{1,0:T(8,128)(2,1)S(1)}, bf16[512,512]{1,0:T(8,128)(2,1)S(1)}) custom-call(s32[6]{0:T(128)S(1)} %stack.11.places, bf16[512,512]{1,0:T(8,128)(2,1)S(1)} %get-tuple-element.108.gt_ref, bf16[512,512]{1,0:T(8,128)(2,1)S(1)} %collective-permute-done.7.gt_other, ...), custom_call_target="tpu_custom_call" | custom-call | flops 2147483648 | bytes 8388608 | tf_op jit(solution)/shard_map/weight_partials/pallas_call | solution.py:188
  47.8 4.9 %collective-permute-done.9.two_ref = bf16[512,256]{1,0:T(8,128)(2,1)S(1)} collective-permute-done((bf16[512,256]{1,0:T(8,128)(2,1)S(1)}, bf16[512,256]{1,0:T(8,128)(2,1)S(1)}, u32[]{:S(2)}, u32[]{:S(2)}) %collective-permute-start.9) | collective-permute-done | bytes 262176 | tf_op jit(solution)/shard_map/ppermute | solution.py:452
  52.7 0.5 collective-permute-start.15
  53.2 1.6 %collective-permute-start.11 = (bf16[512,512]{1,0:T(8,128)(2,1)S(1)}, bf16[512,512]{1,0:T(8,128)(2,1)S(1)}, u32[]{:S(2)}, u32[]{:S(2)}) collective-permute-start(bf16[512,512]{1,0:T(8,128)(2,1)S(1)} %get-tuple-element.125), channel_id=1, source_target_pairs={{0,2},{1,3},{2,0},{3,1},{4,6},{5,7},{6,4},{7,5},{8,10},{9,11},{10,... | collective-permute-start | bytes 1572872 | tf_op jit(solution)/shard_map/ppermute | solution.py:403
  54.8 1.1 finish_kv.1
  55.8 1.5 %collective-permute-done.13.gt_other = bf16[256,512]{1,0:T(8,128)(2,1)S(1)} collective-permute-done((bf16[256,512]{1,0:T(8,128)(2,1)S(1)}, bf16[256,512]{1,0:T(8,128)(2,1)S(1)}, u32[]{:S(2)}, u32[]{:S(2)}) %collective-permute-start.13) | collective-permute-done | bytes 262176 | tf_op jit(solution)/shard_map/ppermute | solution.py:403
  57.4 3.7 %weight_partials.3 = (f32[256,512]{1,0:T(8,128)S(1)}, bf16[256,512]{1,0:T(8,128)(2,1)S(1)}, bf16[256,512]{1,0:T(8,128)(2,1)}, bf16[256,512]{1,0:T(8,128)(2,1)}) custom-call(s32[6]{0:T(128)S(1)} %stack.11.places, bf16[256,512]{1,0:T(8,128)(2,1)S(1)} %get-tuple-element.127.gt_ref, bf16[256,512]{1,0:T(8,128)(2,1)S(1)} %collective-permute-done.13.gt_other, ...), custom_call_target="tpu_custom_call" | custom-call | flops 1073741824 | bytes 8388608 | tf_op jit(solution)/shard_map/weight_partials/pallas_call | solution.py:188
  61.1 6.0 %collective-permute-done.11.from_x = bf16[512,512]{1,0:T(8,128)(2,1)S(1)} collective-permute-done((bf16[512,512]{1,0:T(8,128)(2,1)S(1)}, bf16[512,512]{1,0:T(8,128)(2,1)S(1)}, u32[]{:S(2)}, u32[]{:S(2)}) %collective-permute-start.11) | collective-permute-done | bytes 524320 | tf_op jit(solution)/shard_map/ppermute | solution.py:403
  67.0 1.3 collective-permute-done.12.from_y
  68.3 1.2 middle.2
  69.7 0.5 collective-permute-start.16
  70.1 0.3 collective-permute-start.17
  70.4 1.5 %collective-permute-start.18 = (bf16[256,512]{1,0:T(8,128)(2,1)}, bf16[256,512]{1,0:T(8,128)(2,1)}, u32[]{:S(2)}, u32[]{:S(2)}) collective-permute-start(bf16[256,512]{1,0:T(8,128)(2,1)} %get-tuple-element.147), channel_id=1, source_target_pairs={{0,2},{1,3},{2,0},{3,1},{4,6},{5,7},{6,4},{7,5},{8,10},{9,11},{10,... | collective-permute-start | bytes 786440 | tf_op jit(solution)/shard_map/ppermute | solution.py:403
  72.0 1.7 %collective-permute-start.19 = (bf16[256,512]{1,0:T(8,128)(2,1)}, bf16[256,512]{1,0:T(8,128)(2,1)}, u32[]{:S(2)}, u32[]{:S(2)}) collective-permute-start(bf16[256,512]{1,0:T(8,128)(2,1)} %get-tuple-element.148), channel_id=1, source_target_pairs={{0,4},{1,5},{2,6},{3,7},{4,0},{5,1},{6,2},{7,3},{8,12},{9,13},{10,... | collective-permute-start | bytes 786440 | tf_op jit(solution)/shard_map/ppermute | solution.py:403
  73.7 5.5 %collective-permute-done.16.x_ref = bf16[256,512]{1,0:T(8,128)(2,1)} collective-permute-done((bf16[256,512]{1,0:T(8,128)(2,1)}, bf16[256,512]{1,0:T(8,128)(2,1)}, u32[]{:S(2)}, u32[]{:S(2)}) %collective-permute-start.16) | collective-permute-done | bytes 262176 | tf_op jit(solution)/shard_map/ppermute | solution.py:403
  79.2 0.5 collective-permute-done.17.y_ref
  79.7 1.3 %quarters.2 = (f32[128,512]{1,0:T(8,128)S(1)}, bf16[128,512]{1,0:T(8,128)(2,1)S(1)}, bf16[128,512]{1,0:T(8,128)(2,1)S(1)}, bf16[128,512]{1,0:T(8,128)(2,1)S(1)}) custom-call(s32[1]{0:T(128)} %bitcast.9.z_ref, f32[512,512]{1,0:T(8,128)S(1)} %get-tuple-element.140.own_ref, bf16[256,512]{1,0:T(8,128)(2,1)} %collective-permute-done.16.x_ref, ...), custom_call_target="tpu_custom_call" | custom-call | flops 1048576 | bytes 2097152 | tf_op jit(solution)/shard_map/quarters/pallas_call | solution.py:329
  81.0 1.6 %collective-permute-start.22 = (bf16[128,512]{1,0:T(8,128)(2,1)S(1)}, bf16[128,512]{1,0:T(8,128)(2,1)S(1)}, u32[]{:S(2)}, u32[]{:S(2)}) collective-permute-start(bf16[128,512]{1,0:T(8,128)(2,1)S(1)} %get-tuple-element.151), channel_id=1, source_target_pairs={{0,8},{8,0},{16,24},{24,16},{1,9},{9,1},{17,25},{25,17},{2,10},{10... | collective-permute-start | bytes 393224 | tf_op jit(solution)/shard_map/ppermute | solution.py:403
  82.7 2.6 %collective-permute-start.23 = (bf16[128,512]{1,0:T(8,128)(2,1)S(1)}, bf16[128,512]{1,0:T(8,128)(2,1)S(1)}, u32[]{:S(2)}, u32[]{:S(2)}) collective-permute-start(bf16[128,512]{1,0:T(8,128)(2,1)S(1)} %get-tuple-element.152), channel_id=1, source_target_pairs={{0,16},{8,24},{16,0},{24,8},{1,17},{9,25},{17,1},{25,9},{2,18},{10... | collective-permute-start | bytes 393224 | tf_op jit(solution)/shard_map/ppermute | solution.py:403
  85.3 0.2 collective-permute-start.24
  85.5 1.0 copy-done.11
  86.5 0.9 copy-done.13
  87.5 1.1 middle.3
  88.6 1.6 %collective-permute-start.20 = (bf16[128,512]{1,0:T(8,128)(2,1)S(1)}, bf16[128,512]{1,0:T(8,128)(2,1)S(1)}, u32[]{:S(2)}, u32[]{:S(2)}) collective-permute-start(bf16[128,512]{1,0:T(8,128)(2,1)S(1)} %get-tuple-element.149), channel_id=1, source_target_pairs={{0,2},{1,3},{2,0},{3,1},{4,6},{5,7},{6,4},{7,5},{8,10},{9,11},{10,... | collective-permute-start | bytes 393224 | tf_op jit(solution)/shard_map/ppermute | solution.py:403
  90.3 0.3 collective-permute-start.21
  90.5 1.6 %collective-permute-done.24.refs_3_ = bf16[128,512]{1,0:T(8,128)(2,1)S(1)} collective-permute-done((bf16[128,512]{1,0:T(8,128)(2,1)S(1)}, bf16[128,512]{1,0:T(8,128)(2,1)S(1)}, u32[]{:S(2)}, u32[]{:S(2)}) %collective-permute-start.24) | collective-permute-done | bytes 131104 | tf_op jit(solution)/shard_map/ppermute | solution.py:403
  92.1 2.9 %collective-permute-done.20.x_ref = bf16[128,512]{1,0:T(8,128)(2,1)S(1)} collective-permute-done((bf16[128,512]{1,0:T(8,128)(2,1)S(1)}, bf16[128,512]{1,0:T(8,128)(2,1)S(1)}, u32[]{:S(2)}, u32[]{:S(2)}) %collective-permute-start.20) | collective-permute-done | bytes 131104 | tf_op jit(solution)/shard_map/ppermute | solution.py:403
  95.1 1.6 %collective-permute-done.21.y_ref = bf16[128,512]{1,0:T(8,128)(2,1)S(1)} collective-permute-done((bf16[128,512]{1,0:T(8,128)(2,1)S(1)}, bf16[128,512]{1,0:T(8,128)(2,1)S(1)}, u32[]{:S(2)}, u32[]{:S(2)}) %collective-permute-start.21) | collective-permute-done | bytes 131104 | tf_op jit(solution)/shard_map/ppermute | solution.py:403
  96.7 0.1 quarters.3
  96.9 0.4 collective-permute-start.29
  97.3 0.3 collective-permute-start.28
  97.7 0.3 collective-permute-start.25
  98.0 3.9 %collective-permute-start.26 = (bf16[64,512]{1,0:T(8,128)(2,1)S(1)}, bf16[64,512]{1,0:T(8,128)(2,1)S(1)}, u32[]{:S(2)}, u32[]{:S(2)}) collective-permute-start(bf16[64,512]{1,0:T(8,128)(2,1)S(1)} %get-tuple-element.166), channel_id=1, source_target_pairs={{0,16},{8,24},{16,0},{24,8},{1,17},{9,25},{17,1},{25,9},{2,18},{10... | collective-permute-start | bytes 196616 | tf_op jit(solution)/shard_map/ppermute | solution.py:403
  101.8 0.2 collective-permute-start.27
  102.1 5.5 %input_grad.2.refs_2_ = bf16[512,4096]{1,0:T(8,128)(2,1)} custom-call(s32[6]{0:T(128)S(1)} %stack.11.places, bf16[512,512]{1,0:T(8,128)(2,1)S(1)} %copy-done.1, bf16[512,256]{1,0:T(8,128)(2,1)S(1)} %copy-done.2, bf16[512,768]{1,0:T(8,128)(2,1)S(1)} %copy-done.3, bf16[512,768]{1,0:T(8,128)(2,1)S(1)} %copy-done.5, ...), custom_call_target="tpu_custom_call" | custom-call | flops 2415919104 | bytes 11534336 | tf_op jit(solution)/shard_map/input_grad/pallas_call | solution.py:262
  107.6 0.3 collective-permute-done.27.refs_7_
  108.0 0.1 added.1.refs_0_
  108.2 3.3 %collective-permute-start.32 = (bf16[192,512]{1,0:T(8,128)(2,1)S(1)}, bf16[192,512]{1,0:T(8,128)(2,1)S(1)}, u32[]{:S(2)}, u32[]{:S(2)}) collective-permute-start(bf16[192,512]{1,0:T(8,128)(2,1)S(1)} %added.1.refs_0_), channel_id=1, source_target_pairs={{0,24},{8,16},{16,8},{24,0},{1,25},{9,17},{17,9},{25,1},{2,26},{10... | collective-permute-start | bytes 589832 | tf_op jit(solution)/shard_map/ppermute | solution.py:403
  111.5 1.1 collective-permute-start.30
  112.6 2.6 %input_grad.3 = bf16[512,4096]{1,0:T(8,128)(2,1)} custom-call(s32[6]{0:T(128)S(1)} %stack.11.places, bf16[512,512]{1,0:T(8,128)(2,1)S(1)} %copy-done.1, bf16[512,256]{1,0:T(8,128)(2,1)S(1)} %copy-done.2, bf16[512,768]{1,0:T(8,128)(2,1)S(1)} %constant_dynamic-update-slice_fusion.refs_0_, ...), custom_call_target="tpu_custom_call", output_to_operand_aliasing={{}: (5, {})} | custom-call | flops 805306368 | bytes 11534336 | tf_op jit(solution)/shard_map/input_grad/pallas_call | solution.py:262
  115.2 2.6 %collective-permute-done.32.refs_3_ = bf16[192,512]{1,0:T(8,128)(2,1)S(1)} collective-permute-done((bf16[192,512]{1,0:T(8,128)(2,1)S(1)}, bf16[192,512]{1,0:T(8,128)(2,1)S(1)}, u32[]{:S(2)}, u32[]{:S(2)}) %collective-permute-start.32) | collective-permute-done | bytes 196640 | tf_op jit(solution)/shard_map/ppermute | solution.py:403
  117.9 9.8 %collective-permute-done.31.refs_2_ = bf16[192,512]{1,0:T(8,128)(2,1)S(1)} collective-permute-done((bf16[192,512]{1,0:T(8,128)(2,1)S(1)}, bf16[192,512]{1,0:T(8,128)(2,1)S(1)}, u32[]{:S(2)}, u32[]{:S(2)}) %collective-permute-start.31) | collective-permute-done | bytes 196640 | tf_op jit(solution)/shard_map/ppermute | solution.py:403
  127.6 1.5 %joined.1 = bf16[512,768]{1,0:T(8,128)(2,1)} custom-call(s32[1]{0:T(128)} %bitcast.9.z_ref, bf16[192,512]{1,0:T(8,128)(2,1)S(1)} %added.1.refs_0_, bf16[192,512]{1,0:T(8,128)(2,1)S(1)} %collective-permute-done.30.refs_1_, bf16[192,512]{1,0:T(8,128)(2,1)S(1)} %collective-permute-done.31.refs_2_, bf16[192,512]{1,0:T(8,128)(2,1)S(1)} %collective-permute-done.32.refs_3_), custom_call_target="tpu_custom_call" | custom-call | flops 98304 | bytes 2097152 | tf_op jit(solution)/shard_map/joined/pallas_call | solution.py:390
  (58 shorter events, 0.5 us)
Async XLA Ops:
  0.6 14.2 %collective-permute-start.2 = (bf16[512,768]{1,0:T(8,128)(2,1)}, bf16[512,768]{1,0:T(8,128)(2,1)S(1)}, u32[]{:S(2)}, u32[]{:S(2)}) collective-permute-start(bf16[512,768]{1,0:T(8,128)(2,1)} %refs_0_), channel_id=1, source_target_pairs={{0,1},{1,0},{2,3},{3,2},{4,5},{5,4},{6,7},{7,6},{8,9},{9,8},{10,11... | collective-permute-start | bytes 2359304 | tf_op jit(solution)/shard_map/ppermute | solution.py:403
  1.1 7.0 %collective-permute-start.1 = (bf16[512,256]{1,0:T(8,128)(2,1)}, bf16[512,256]{1,0:T(8,128)(2,1)S(1)}, u32[]{:S(2)}, u32[]{:S(2)}) collective-permute-start(bf16[512,256]{1,0:T(8,128)(2,1)} %bitcast.18), channel_id=1, source_target_pairs={{0,1},{2,3},{4,5},{6,7},{1,4},{3,6},{8,9},{10,11},{12,13},{14,15},... | collective-permute-start | bytes 786440 | tf_op jit(solution)/shard_map/ppermute | solution.py:426
  3.1 11.7 %collective-permute-start = (bf16[512,256]{1,0:T(8,128)(2,1)}, bf16[512,256]{1,0:T(8,128)(2,1)S(1)}, u32[]{:S(2)}, u32[]{:S(2)}) collective-permute-start(bf16[512,256]{1,0:T(8,128)(2,1)} %bitcast.19), channel_id=1, source_target_pairs={{0,2},{1,3},{2,4},{3,5},{4,6},{5,7},{8,10},{9,11},{10,12},{11,13},... | collective-permute-start | bytes 786440 | tf_op jit(solution)/shard_map/ppermute | solution.py:425
  14.8 0.9 copy-start.4
  15.7 1.5 %collective-permute-start.3 = (bf16[512,256]{1,0:T(8,128)(2,1)S(1)}, bf16[512,256]{1,0:T(8,128)(2,1)S(1)}, u32[]{:S(2)}, u32[]{:S(2)}) collective-permute-start(bf16[512,256]{1,0:T(8,128)(2,1)S(1)} %collective-permute-done.d2_ref), channel_id=1, source_target_pairs={{0,1},{1,0},{2,3},{3,2},{4,5},{5,4},{6,7},{7,6},{8,9},{9,8},{10,11... | collective-permute-start | bytes 786440 | tf_op jit(solution)/shard_map/ppermute | solution.py:403
  17.2 22.3 %collective-permute-start.6 = (bf16[512,4096]{1,0:T(8,128)(2,1)}, bf16[512,4096]{1,0:T(8,128)(2,1)S(1)}, u32[]{:S(2)}, u32[]{:S(2)}) collective-permute-start(bf16[512,4096]{1,0:T(8,128)(2,1)} %bitcast.11), channel_id=1, source_target_pairs={{0,1},{1,0},{2,3},{3,2},{4,5},{5,4},{6,7},{7,6},{8,9},{9,8},{10,11... | collective-permute-start | bytes 12582920 | tf_op jit(solution)/shard_map/ppermute | solution.py:403
  17.5 20.6 %collective-permute-start.5 = (bf16[512,768]{1,0:T(8,128)(2,1)}, bf16[512,768]{1,0:T(8,128)(2,1)S(1)}, u32[]{:S(2)}, u32[]{:S(2)}) collective-permute-start(bf16[512,768]{1,0:T(8,128)(2,1)} %refs_0_), channel_id=1, source_target_pairs={{0,4},{1,5},{2,6},{3,7},{4,0},{5,1},{6,2},{7,3},{8,12},{9,13},{10,... | collective-permute-start | bytes 2359304 | tf_op jit(solution)/shard_map/ppermute | solution.py:403
  19.8 19.7 %collective-permute-start.4 = (bf16[512,768]{1,0:T(8,128)(2,1)}, bf16[512,768]{1,0:T(8,128)(2,1)S(1)}, u32[]{:S(2)}, u32[]{:S(2)}) collective-permute-start(bf16[512,768]{1,0:T(8,128)(2,1)} %refs_0_), channel_id=1, source_target_pairs={{0,2},{1,3},{2,0},{3,1},{4,6},{5,7},{6,4},{7,5},{8,10},{9,11},{10,... | collective-permute-start | bytes 2359304 | tf_op jit(solution)/shard_map/ppermute | solution.py:403
  19.8 1.0 copy-start.14
  20.9 1.0 copy-start.15
  21.9 0.9 copy-start.16
  22.9 0.7 copy-start.17
  23.5 20.2 %copy-start = (bf16[1,512,4096]{2,1,0:T(8,128)(2,1)S(1)}, bf16[1,512,4096]{2,1,0:T(8,128)(2,1)}, u32[]{:S(2)}) copy-start(bf16[1,512,4096]{2,1,0:T(8,128)(2,1)} %param.6) | copy-start | bytes 12582916
  39.6 1.9 %collective-permute-start.8 = (f32[512,256]{1,0:T(8,128)S(1)}, f32[512,256]{1,0:T(8,128)S(1)}, u32[]{:S(2)}, u32[]{:S(2)}) collective-permute-start(f32[512,256]{1,0:T(8,128)S(1)} %get-tuple-element.110), channel_id=1, source_target_pairs={{0,1},{1,0},{2,3},{3,2},{4,5},{5,4},{6,7},{7,6},{8,9},{9,8},{10,11... | collective-permute-start | bytes 1572872 | tf_op jit(solution)/shard_map/ppermute | solution.py:403
  39.6 2.7 %collective-permute-start.7 = (bf16[512,512]{1,0:T(8,128)(2,1)S(1)}, bf16[512,512]{1,0:T(8,128)(2,1)S(1)}, u32[]{:S(2)}, u32[]{:S(2)}) collective-permute-start(bf16[512,512]{1,0:T(8,128)(2,1)S(1)} %get-tuple-element.108.gt_ref), channel_id=1, source_target_pairs={{0,1},{1,0},{2,3},{3,2},{4,5},{5,4},{6,7},{7,6},{8,9},{9,8},{10,11... | collective-permute-start | bytes 1572872 | tf_op jit(solution)/shard_map/ppermute | solution.py:403
  40.1 7.7 %collective-permute-start.10 = (bf16[512,256]{1,0:T(8,128)(2,1)S(1)}, bf16[512,256]{1,0:T(8,128)(2,1)S(1)}, u32[]{:S(2)}, u32[]{:S(2)}) collective-permute-start(bf16[512,256]{1,0:T(8,128)(2,1)S(1)} %get-tuple-element.112), channel_id=1, source_target_pairs={{1,0},{3,2},{5,4},{7,6},{4,1},{6,3},{9,8},{11,10},{13,12},{15,14},... | collective-permute-start | bytes 786440 | tf_op jit(solution)/shard_map/ppermute | solution.py:443
  42.2 10.5 %collective-permute-start.9 = (bf16[512,256]{1,0:T(8,128)(2,1)S(1)}, bf16[512,256]{1,0:T(8,128)(2,1)S(1)}, u32[]{:S(2)}, u32[]{:S(2)}) collective-permute-start(bf16[512,256]{1,0:T(8,128)(2,1)S(1)} %add_convert_fusion), channel_id=1, source_target_pairs={{2,0},{3,1},{4,2},{5,3},{6,4},{7,5},{10,8},{11,9},{12,10},{13,11},... | collective-permute-start | bytes 786440 | tf_op jit(solution)/shard_map/ppermute | solution.py:452
  52.7 15.6 %collective-permute-start.14 = (bf16[512,768]{1,0:T(8,128)(2,1)S(1)}, bf16[512,768]{1,0:T(8,128)(2,1)S(1)}, u32[]{:S(2)}, u32[]{:S(2)}) collective-permute-start(bf16[512,768]{1,0:T(8,128)(2,1)S(1)} %collective-permute-done.4.refs_2_), channel_id=1, source_target_pairs={{0,1},{1,0},{2,3},{3,2},{4,5},{5,4},{6,7},{7,6},{8,9},{9,8},{10,11... | collective-permute-start | bytes 2359304 | tf_op jit(solution)/shard_map/ppermute | solution.py:403
  52.7 15.6 %collective-permute-start.15 = (bf16[512,768]{1,0:T(8,128)(2,1)S(1)}, bf16[512,768]{1,0:T(8,128)(2,1)S(1)}, u32[]{:S(2)}, u32[]{:S(2)}) collective-permute-start(bf16[512,768]{1,0:T(8,128)(2,1)S(1)} %collective-permute-done.5.refs_4_), channel_id=1, source_target_pairs={{0,1},{1,0},{2,3},{3,2},{4,5},{5,4},{6,7},{7,6},{8,9},{9,8},{10,11... | collective-permute-start | bytes 2359304 | tf_op jit(solution)/shard_map/ppermute | solution.py:403
  53.2 13.8 %collective-permute-start.11 = (bf16[512,512]{1,0:T(8,128)(2,1)S(1)}, bf16[512,512]{1,0:T(8,128)(2,1)S(1)}, u32[]{:S(2)}, u32[]{:S(2)}) collective-permute-start(bf16[512,512]{1,0:T(8,128)(2,1)S(1)} %get-tuple-element.125), channel_id=1, source_target_pairs={{0,2},{1,3},{2,0},{3,1},{4,6},{5,7},{6,4},{7,5},{8,10},{9,11},{10,... | collective-permute-start | bytes 1572872 | tf_op jit(solution)/shard_map/ppermute | solution.py:403
  54.8 13.6 %collective-permute-start.12 = (bf16[512,512]{1,0:T(8,128)(2,1)S(1)}, bf16[512,512]{1,0:T(8,128)(2,1)S(1)}, u32[]{:S(2)}, u32[]{:S(2)}) collective-permute-start(bf16[512,512]{1,0:T(8,128)(2,1)S(1)} %get-tuple-element.126), channel_id=1, source_target_pairs={{0,4},{1,5},{2,6},{3,7},{4,0},{5,1},{6,2},{7,3},{8,12},{9,13},{10,... | collective-permute-start | bytes 1572872 | tf_op jit(solution)/shard_map/ppermute | solution.py:403
  55.8 1.5 %collective-permute-start.13 = (bf16[256,512]{1,0:T(8,128)(2,1)S(1)}, bf16[256,512]{1,0:T(8,128)(2,1)S(1)}, u32[]{:S(2)}, u32[]{:S(2)}) collective-permute-start(bf16[256,512]{1,0:T(8,128)(2,1)S(1)} %get-tuple-element.127.gt_ref), channel_id=1, source_target_pairs={{0,1},{1,0},{2,3},{3,2},{4,5},{5,4},{6,7},{7,6},{8,9},{9,8},{10,11... | collective-permute-start | bytes 786440 | tf_op jit(solution)/shard_map/ppermute | solution.py:403
  61.1 9.1 %copy-start.10 = (f32[256,512]{1,0:T(8,128)}, f32[256,512]{1,0:T(8,128)S(1)}, u32[]{:S(2)}) copy-start(f32[256,512]{1,0:T(8,128)S(1)} %get-tuple-element.145.own_ref) | copy-start | bytes 1572868
  61.1 9.1 %copy-start.12 = (bf16[256,512]{1,0:T(8,128)(2,1)}, bf16[256,512]{1,0:T(8,128)(2,1)S(1)}, u32[]{:S(2)}) copy-start(bf16[256,512]{1,0:T(8,128)(2,1)S(1)} %get-tuple-element.146.keep_ref) | copy-start | bytes 786436
  61.1 41.0 %copy-start.1 = (bf16[512,512]{1,0:T(8,128)(2,1)S(1)}, bf16[512,512]{1,0:T(8,128)(2,1)}, u32[]{:S(2)}) copy-start(bf16[512,512]{1,0:T(8,128)(2,1)} %get-tuple-element.106.gq_ref) | copy-start | bytes 1572868
  61.1 41.0 %copy-start.2 = (bf16[512,256]{1,0:T(8,128)(2,1)S(1)}, bf16[512,256]{1,0:T(8,128)(2,1)}, u32[]{:S(2)}) copy-start(bf16[512,256]{1,0:T(8,128)(2,1)} %get-tuple-element.124.gkv_ref) | copy-start | bytes 786436
  68.3 1.3 copy-start.6
  68.3 1.3 %copy-start.8 = (bf16[512,768]{1,0:T(8,128)(2,1)}, bf16[512,768]{1,0:T(8,128)(2,1)S(1)}, u32[]{:S(2)}) copy-start(bf16[512,768]{1,0:T(8,128)(2,1)S(1)} %collective-permute-done.15.refs_5_) | copy-start | bytes 2359300
  69.7 9.6 %collective-permute-start.16 = (bf16[256,512]{1,0:T(8,128)(2,1)}, bf16[256,512]{1,0:T(8,128)(2,1)}, u32[]{:S(2)}, u32[]{:S(2)}) collective-permute-start(bf16[256,512]{1,0:T(8,128)(2,1)} %get-tuple-element.141), channel_id=1, source_target_pairs={{0,2},{1,3},{2,0},{3,1},{4,6},{5,7},{6,4},{7,5},{8,10},{9,11},{10,... | collective-permute-start | bytes 786440 | tf_op jit(solution)/shard_map/ppermute | solution.py:403
  70.1 9.6 %collective-permute-start.17 = (bf16[256,512]{1,0:T(8,128)(2,1)}, bf16[256,512]{1,0:T(8,128)(2,1)}, u32[]{:S(2)}, u32[]{:S(2)}) collective-permute-start(bf16[256,512]{1,0:T(8,128)(2,1)} %get-tuple-element.142), channel_id=1, source_target_pairs={{0,4},{1,5},{2,6},{3,7},{4,0},{5,1},{6,2},{7,3},{8,12},{9,13},{10,... | collective-permute-start | bytes 786440 | tf_op jit(solution)/shard_map/ppermute | solution.py:403
  70.4 15.1 %collective-permute-start.18 = (bf16[256,512]{1,0:T(8,128)(2,1)}, bf16[256,512]{1,0:T(8,128)(2,1)}, u32[]{:S(2)}, u32[]{:S(2)}) collective-permute-start(bf16[256,512]{1,0:T(8,128)(2,1)} %get-tuple-element.147), channel_id=1, source_target_pairs={{0,2},{1,3},{2,0},{3,1},{4,6},{5,7},{6,4},{7,5},{8,10},{9,11},{10,... | collective-permute-start | bytes 786440 | tf_op jit(solution)/shard_map/ppermute | solution.py:403
  72.0 13.5 %collective-permute-start.19 = (bf16[256,512]{1,0:T(8,128)(2,1)}, bf16[256,512]{1,0:T(8,128)(2,1)}, u32[]{:S(2)}, u32[]{:S(2)}) collective-permute-start(bf16[256,512]{1,0:T(8,128)(2,1)} %get-tuple-element.148), channel_id=1, source_target_pairs={{0,4},{1,5},{2,6},{3,7},{4,0},{5,1},{6,2},{7,3},{8,12},{9,13},{10,... | collective-permute-start | bytes 786440 | tf_op jit(solution)/shard_map/ppermute | solution.py:403
  73.7 28.4 %copy-start.3 = (bf16[512,768]{1,0:T(8,128)(2,1)S(1)}, bf16[512,768]{1,0:T(8,128)(2,1)}, u32[]{:S(2)}) copy-start(bf16[512,768]{1,0:T(8,128)(2,1)} %refs_0_) | copy-start | bytes 2359300
  73.7 28.4 %copy-start.5 = (bf16[512,768]{1,0:T(8,128)(2,1)S(1)}, bf16[512,768]{1,0:T(8,128)(2,1)}, u32[]{:S(2)}) copy-start(bf16[512,768]{1,0:T(8,128)(2,1)} %copy-done.4) | copy-start | bytes 2359300
  73.7 28.4 %copy-start.7 = (bf16[512,768]{1,0:T(8,128)(2,1)S(1)}, bf16[512,768]{1,0:T(8,128)(2,1)}, u32[]{:S(2)}) copy-start(bf16[512,768]{1,0:T(8,128)(2,1)} %copy-done.6) | copy-start | bytes 2359300
  73.7 28.4 %copy-start.9 = (bf16[512,768]{1,0:T(8,128)(2,1)S(1)}, bf16[512,768]{1,0:T(8,128)(2,1)}, u32[]{:S(2)}) copy-start(bf16[512,768]{1,0:T(8,128)(2,1)} %copy-done.8) | copy-start | bytes 2359300
  81.0 9.5 %collective-permute-start.22 = (bf16[128,512]{1,0:T(8,128)(2,1)S(1)}, bf16[128,512]{1,0:T(8,128)(2,1)S(1)}, u32[]{:S(2)}, u32[]{:S(2)}) collective-permute-start(bf16[128,512]{1,0:T(8,128)(2,1)S(1)} %get-tuple-element.151), channel_id=1, source_target_pairs={{0,8},{8,0},{16,24},{24,16},{1,9},{9,1},{17,25},{25,17},{2,10},{10... | collective-permute-start | bytes 393224 | tf_op jit(solution)/shard_map/ppermute | solution.py:403
  82.7 7.9 %collective-permute-start.23 = (bf16[128,512]{1,0:T(8,128)(2,1)S(1)}, bf16[128,512]{1,0:T(8,128)(2,1)S(1)}, u32[]{:S(2)}, u32[]{:S(2)}) collective-permute-start(bf16[128,512]{1,0:T(8,128)(2,1)S(1)} %get-tuple-element.152), channel_id=1, source_target_pairs={{0,16},{8,24},{16,0},{24,8},{1,17},{9,25},{17,1},{25,9},{2,18},{10... | collective-permute-start | bytes 393224 | tf_op jit(solution)/shard_map/ppermute | solution.py:403
  85.3 6.9 %collective-permute-start.24 = (bf16[128,512]{1,0:T(8,128)(2,1)S(1)}, bf16[128,512]{1,0:T(8,128)(2,1)S(1)}, u32[]{:S(2)}, u32[]{:S(2)}) collective-permute-start(bf16[128,512]{1,0:T(8,128)(2,1)S(1)} %get-tuple-element.153), channel_id=1, source_target_pairs={{0,24},{8,16},{16,8},{24,0},{1,25},{9,17},{17,9},{25,1},{2,26},{10... | collective-permute-start | bytes 393224 | tf_op jit(solution)/shard_map/ppermute | solution.py:403
  85.5 1.0 copy-start.11
  86.5 0.9 copy-start.13
  88.6 6.4 %collective-permute-start.20 = (bf16[128,512]{1,0:T(8,128)(2,1)S(1)}, bf16[128,512]{1,0:T(8,128)(2,1)S(1)}, u32[]{:S(2)}, u32[]{:S(2)}) collective-permute-start(bf16[128,512]{1,0:T(8,128)(2,1)S(1)} %get-tuple-element.149), channel_id=1, source_target_pairs={{0,2},{1,3},{2,0},{3,1},{4,6},{5,7},{6,4},{7,5},{8,10},{9,11},{10,... | collective-permute-start | bytes 393224 | tf_op jit(solution)/shard_map/ppermute | solution.py:403
  90.3 6.4 %collective-permute-start.21 = (bf16[128,512]{1,0:T(8,128)(2,1)S(1)}, bf16[128,512]{1,0:T(8,128)(2,1)S(1)}, u32[]{:S(2)}, u32[]{:S(2)}) collective-permute-start(bf16[128,512]{1,0:T(8,128)(2,1)S(1)} %get-tuple-element.150), channel_id=1, source_target_pairs={{0,4},{1,5},{2,6},{3,7},{4,0},{5,1},{6,2},{7,3},{8,12},{9,13},{10,... | collective-permute-start | bytes 393224 | tf_op jit(solution)/shard_map/ppermute | solution.py:403
  96.9 11.0 %collective-permute-start.29 = (bf16[256,768]{1,0:T(8,128)(2,1)S(1)}, bf16[256,768]{1,0:T(8,128)(2,1)S(1)}, u32[]{:S(2)}, u32[]{:S(2)}) collective-permute-start(bf16[256,768]{1,0:T(8,128)(2,1)S(1)} %slice.7), channel_id=1, source_target_pairs={{0,2},{1,3},{2,0},{3,1},{4,6},{5,7},{6,4},{7,5},{8,10},{9,11},{10,... | collective-permute-start | bytes 1179656 | tf_op jit(solution)/shard_map/ppermute | solution.py:403
  97.3 10.6 %collective-permute-start.28 = (bf16[256,768]{1,0:T(8,128)(2,1)S(1)}, bf16[256,768]{1,0:T(8,128)(2,1)S(1)}, u32[]{:S(2)}, u32[]{:S(2)}) collective-permute-start(bf16[256,768]{1,0:T(8,128)(2,1)S(1)} %slice.6), channel_id=1, source_target_pairs={{0,4},{1,5},{2,6},{3,7},{4,0},{5,1},{6,2},{7,3},{8,12},{9,13},{10,... | collective-permute-start | bytes 1179656 | tf_op jit(solution)/shard_map/ppermute | solution.py:403
  97.7 9.9 %collective-permute-start.25 = (bf16[64,512]{1,0:T(8,128)(2,1)S(1)}, bf16[64,512]{1,0:T(8,128)(2,1)S(1)}, u32[]{:S(2)}, u32[]{:S(2)}) collective-permute-start(bf16[64,512]{1,0:T(8,128)(2,1)S(1)} %get-tuple-element.165), channel_id=1, source_target_pairs={{0,8},{8,0},{16,24},{24,16},{1,9},{9,1},{17,25},{25,17},{2,10},{10... | collective-permute-start | bytes 196616 | tf_op jit(solution)/shard_map/ppermute | solution.py:403
  98.0 9.6 %collective-permute-start.26 = (bf16[64,512]{1,0:T(8,128)(2,1)S(1)}, bf16[64,512]{1,0:T(8,128)(2,1)S(1)}, u32[]{:S(2)}, u32[]{:S(2)}) collective-permute-start(bf16[64,512]{1,0:T(8,128)(2,1)S(1)} %get-tuple-element.166), channel_id=1, source_target_pairs={{0,16},{8,24},{16,0},{24,8},{1,17},{9,25},{17,1},{25,9},{2,18},{10... | collective-permute-start | bytes 196616 | tf_op jit(solution)/shard_map/ppermute | solution.py:403
  101.8 6.1 %collective-permute-start.27 = (bf16[64,512]{1,0:T(8,128)(2,1)S(1)}, bf16[64,512]{1,0:T(8,128)(2,1)S(1)}, u32[]{:S(2)}, u32[]{:S(2)}) collective-permute-start(bf16[64,512]{1,0:T(8,128)(2,1)S(1)} %get-tuple-element.167), channel_id=1, source_target_pairs={{0,24},{8,16},{16,8},{24,0},{1,25},{9,17},{17,9},{25,1},{2,26},{10... | collective-permute-start | bytes 196616 | tf_op jit(solution)/shard_map/ppermute | solution.py:403
  108.0 4.7 %collective-permute-start.33 = (bf16[512,768]{1,0:T(8,128)(2,1)S(1)}, bf16[512,768]{1,0:T(8,128)(2,1)S(1)}, u32[]{:S(2)}, u32[]{:S(2)}) collective-permute-start(bf16[512,768]{1,0:T(8,128)(2,1)S(1)} %constant_dynamic-update-slice_fusion.refs_0_), channel_id=1, source_target_pairs={{0,1},{1,0},{2,3},{3,2},{4,5},{5,4},{6,7},{7,6},{8,9},{9,8},{10,11... | collective-permute-start | bytes 2359304 | tf_op jit(solution)/shard_map/ppermute | solution.py:403
  108.2 9.7 %collective-permute-start.32 = (bf16[192,512]{1,0:T(8,128)(2,1)S(1)}, bf16[192,512]{1,0:T(8,128)(2,1)S(1)}, u32[]{:S(2)}, u32[]{:S(2)}) collective-permute-start(bf16[192,512]{1,0:T(8,128)(2,1)S(1)} %added.1.refs_0_), channel_id=1, source_target_pairs={{0,24},{8,16},{16,8},{24,0},{1,25},{9,17},{17,9},{25,1},{2,26},{10... | collective-permute-start | bytes 589832 | tf_op jit(solution)/shard_map/ppermute | solution.py:403
  111.5 16.1 %collective-permute-start.31 = (bf16[192,512]{1,0:T(8,128)(2,1)S(1)}, bf16[192,512]{1,0:T(8,128)(2,1)S(1)}, u32[]{:S(2)}, u32[]{:S(2)}) collective-permute-start(bf16[192,512]{1,0:T(8,128)(2,1)S(1)} %added.1.refs_0_), channel_id=1, source_target_pairs={{0,16},{8,24},{16,0},{24,8},{1,17},{9,25},{17,1},{25,9},{2,18},{10... | collective-permute-start | bytes 589832 | tf_op jit(solution)/shard_map/ppermute | solution.py:403
  111.5 16.1 %collective-permute-start.30 = (bf16[192,512]{1,0:T(8,128)(2,1)S(1)}, bf16[192,512]{1,0:T(8,128)(2,1)S(1)}, u32[]{:S(2)}, u32[]{:S(2)}) collective-permute-start(bf16[192,512]{1,0:T(8,128)(2,1)S(1)} %added.1.refs_0_), channel_id=1, source_target_pairs={{0,8},{8,0},{16,24},{24,16},{1,9},{9,1},{17,25},{25,17},{2,10},{10... | collective-permute-start | bytes 589832 | tf_op jit(solution)/shard_map/ppermute | solution.py:403

commit v6 on v5

--- a/solution.py
+++ b/solution.py
@@ -27,7 +27,7 @@
 
 
 def attention_kernel(
-    idx_ref, len_ref, q_ref, g_ref, own_ref, d2_ref, r_ref, x_ref,
+    info_ref, q_ref, g_ref, own_ref, d2_ref, r_ref, x_ref,
     gq_ref, gqt_ref, own_out, d2_out, r_out, x_out,
     kv_scr, kt_scr, s_scr, dp_scr, acc_scr,
 ):
@@ -36,7 +36,7 @@
     heads = q_ref.shape[1] // hd
     wide = heads * Q_STEP
     scaling = hd ** (-0.5)
-    index = idx_ref[0]
+    index = info_ref[0]
     parity = lax.rem(index, 2)
     base = (index - 3) * rows
     r_off = pl.multiple_of((1 - parity) * 2 * rows, rows)
@@ -51,9 +51,9 @@
     acc_scr[...] = jnp.zeros_like(acc_scr)
     ends = []
     total = -base
-    for j in range(len_ref.shape[1]):
+    for j in range(1, info_ref.shape[0]):
         ends.append(total)
-        total = total + len_ref[0, j]
+        total = total + info_ref[j]
 
     for tile in range(rows // Q_STEP):
         q_rows = slice(tile * Q_STEP, (tile + 1) * Q_STEP)
@@ -121,12 +121,11 @@
     put(own_out, slice(3 * rows, 4 * rows))
 
 
-def attention(index, lengths, q, g, own, d2, r, x):
+def attention(info, q, g, own, d2, r, x):
     rows, width = q.shape
     both = own.shape[1]
     hd = both // 2
     wide = width // hd * Q_STEP
-    whole = lambda shape: pl.BlockSpec(shape, lambda i: (0, 0))
     smem = pl.BlockSpec(memory_space=pltpu.SMEM)
     return pl.pallas_call(
         attention_kernel,
@@ -139,8 +138,7 @@
             jax.ShapeDtypeStruct((rows, both), jnp.float32),
             jax.ShapeDtypeStruct((rows, both), jnp.bfloat16),
         ),
-        grid=(1,),
-        in_specs=[smem, smem] + [whole((rows, width))] * 2 + [whole((rows, both))] + [VMEM] * 3,
+        in_specs=[smem] + [VMEM] * 6,
         out_specs=[VMEM] * 6,
         scratch_shapes=[
             pltpu.VMEM((4 * rows, both), jnp.bfloat16),
@@ -151,7 +149,30 @@
         ],
         compiler_params=pltpu.CompilerParams(vmem_limit_bytes=30 * 2**20),
         cost_estimate=pl.CostEstimate(flops=12 * 10**9, bytes_accessed=6 * 2**20, transcendentals=4 * 2**20),
-    )(index, lengths, q, g, own, d2, r, x)
+    )(info, q, g, own, d2, r, x)
+
+
+def staged_kernel(*refs):
+    count = len(refs) // 2
+    for source, target in zip(refs[:count], refs[count:]):
+        step = 64
+
+        def body(start, source=source, target=target):
+            target[pl.ds(start, step), :] = source[pl.ds(start, step), :]
+
+        row_loop(source.shape[0], step, body)
+
+
+def staged(*arrays):
+    return pl.pallas_call(
+        staged_kernel,
+        name="staged",
+        out_shape=[jax.ShapeDtypeStruct(a.shape, a.dtype) for a in arrays],
+        in_specs=[VMEM] * len(arrays),
+        out_specs=[VMEM] * len(arrays),
+        compiler_params=pltpu.CompilerParams(vmem_limit_bytes=SMALL_VMEM),
+        cost_estimate=pl.CostEstimate(flops=2**20, bytes_accessed=3 * 2**20, transcendentals=0),
+    )(*arrays)
 
 
 def weight_kernel(places, gt_ref, gt_other, x_ref, x_other, own_out, keep_out, to_x, to_y):
@@ -426,7 +447,9 @@
     x = lax.ppermute(own, "ctx", mixed)
     w_swapped = flipped(qkv_weight, 1)
     places = jnp.stack([index // 2, index % 2, *map(jnp.int32, (3, 1, 2, 0))])
-    d2, x, w_swapped, places = together(d2, x, w_swapped, places)
+    info = jnp.concatenate([index.reshape(1), lengths[0]])
+    q, g, near = staged(queries[0], out_grad[0], own)
+    d2, x, w_swapped, places, info, q, g, near = together(d2, x, w_swapped, places, info, q, g, near)
     r = flipped(d2, 1)
     if small:
         w_own, x_in, r = lax.optimization_barrier((qkv_weight, x_local, r))
@@ -435,9 +458,9 @@
     else:
         w_full = lax.all_gather(qkv_weight, "ctx", axis=0, tiled=True)
 
-    grads = attention(index.reshape(1), lengths, queries[0], out_grad[0], own, d2, r, x)
+    grads = attention(info, q, g, near, d2, r, x)
     if small:
-        *grads, w_x, w_y, x_other = lax.optimization_barrier((*grads, w_x, w_y, x_other))
+        *grads, x_other = together(*grads, x_other)
     gq, gqt, kv_own, kv_d2, kv_r, kv_x = grads
     kv_d2 = (kv_d2 + flipped(kv_r, 1)).astype(bf16)
     from_x = lax.ppermute(kv_x, "ctx", back(mixed))
@@ -448,7 +471,7 @@
         def crossed(pieces):
             return [flipped(piece, k + 1, "dp") for k, piece in enumerate(pieces)]
 
-        gqt_other, kv_d2 = together(flipped(gqt, 1), kv_d2)
+        gqt_other, kv_d2, w_x, w_y = together(flipped(gqt, 1), kv_d2, w_x, w_y)
         from_two = lax.ppermute(kv_d2, "ctx", back(by_two))
         q_parts = weight_partials(places, gqt, gqt_other, x_local, x_other, block)
         from_two, from_x, w_x, w_y, *q_parts = together(from_two, from_x, w_x, w_y, *q_parts)

time: 130 us -> 126 us (0.969)
  waiting for transfers between devices: 56.9 us -> 49.2 us
  starting transfers between devices: 35.7 us -> 39.6 us
    ppermute x1, waiting for transfers between devices: 6.7 us -> 2.76 us  [per_device(): d2 = lax.ppermute(own, 'ctx', by_two)]
    ppermute x30, starting transfers between devices: 26.1 us -> 30 us  [flipped(): lax.ppermute(array, axis, [(i, i ^ bits) for i in range(lax.axis_size(axi...]
    ppermute x30, waiting for transfers between devices: 45.3 us -> 42.7 us  [flipped(): lax.ppermute(array, axis, [(i, i ^ bits) for i in range(lax.axis_size(axi...]
    unnamed x37 -> x35, local copies, waits for them, and re-layouts: 6.7 us -> 6.04 us
  transfers between devices with their start and end apart: 34 -> 34, of which waited for: 18 -> 17; matrix products, arithmetic and copies ran while one was open for 0% -> 1% of each run, Pallas kernels for 20% -> 21%
where the time goes in v6:
time: 126 us
  waiting for transfers between devices  49.2 us (39%)
  starting transfers between devices  39.6 us (31%)
  Pallas kernels  28.9 us (23%)
  local copies, waits for them, and re-layouts  6.21 us (5%)
    ppermute x30, waiting for transfers between devices, flipped(): lax.ppermute(array, axis, [(i, i ^ bits) for i in range(lax.axis_size(axi...  42.7 us
    ppermute x30, starting transfers between devices, flipped(): lax.ppermute(array, axis, [(i, i ^ bits) for i in range(lax.axis_size(axi...  30 us
    pallas_call x2, Pallas kernels, input_grad(): pl.pallas_call(functools.partial(input_kernel, count=count), name='input_...  8.06 us
    pallas_call x2, Pallas kernels, weight_partials(): pl.pallas_call(weight_kernel, name='weight_partials', out_shape=[jax.Shap...  7.8 us
    pallas_call x1, Pallas kernels, attention(): pl.pallas_call(attention_kernel, name='attention', out_shape=(jax.ShapeDt...  6.4 us
    unnamed x35, local copies, waits for them, and re-layouts  6.04 us
    ppermute x1, starting transfers between devices, per_device(): d2 = lax.ppermute(own, 'ctx', by_two)  4.86 us
    ppermute x1, waiting for transfers between devices, per_device(): from_two = lax.ppermute(kv_d2, 'ctx', back(by_two))  3.73 us
  transfers between devices with their start and end apart: 34, of which 17 were waited for; matrix products, arithmetic and copies ran while one was open for 1% of the time, Pallas kernels for 21%

profile of v6, /device:TPU:0, one launch (start us, length us, event | category | flops | bytes accessed | tf_op | source)
XLA Modules:
  0.0 125.6 jit_solution(4517921388832572454)
XLA Ops:
  0.6 0.5 collective-permute-start.2
  1.1 2.0 %collective-permute-start.1 = (bf16[512,256]{1,0:T(8,128)(2,1)}, bf16[512,256]{1,0:T(8,128)(2,1)S(1)}, u32[]{:S(2)}, u32[]{:S(2)}) collective-permute-start(bf16[512,256]{1,0:T(8,128)(2,1)} %bitcast.19), channel_id=1, source_target_pairs={{0,1},{2,3},{4,5},{6,7},{1,4},{3,6},{8,9},{10,11},{12,13},{14,15},... | collective-permute-start | bytes 786440 | tf_op jit(solution)/shard_map/ppermute | solution.py:447
  3.1 4.9 %collective-permute-start = (bf16[512,256]{1,0:T(8,128)(2,1)}, bf16[512,256]{1,0:T(8,128)(2,1)S(1)}, u32[]{:S(2)}, u32[]{:S(2)}) collective-permute-start(bf16[512,256]{1,0:T(8,128)(2,1)} %bitcast.20), channel_id=1, source_target_pairs={{0,2},{1,3},{2,4},{3,5},{4,6},{5,7},{8,10},{9,11},{10,12},{11,13},... | collective-permute-start | bytes 786440 | tf_op jit(solution)/shard_map/ppermute | solution.py:446
  8.1 1.0 copy-done.10
  9.1 1.0 copy-done.11
  10.2 0.9 copy-done.14
  11.1 0.2 staged.1
  11.3 0.7 pad_add_fusion.info_ref
  12.0 2.8 %collective-permute-done.d2_ref = bf16[512,256]{1,0:T(8,128)(2,1)S(1)} collective-permute-done((bf16[512,256]{1,0:T(8,128)(2,1)}, bf16[512,256]{1,0:T(8,128)(2,1)S(1)}, u32[]{:S(2)}, u32[]{:S(2)}) %collective-permute-start) | collective-permute-done | bytes 262176 | tf_op jit(solution)/shard_map/ppermute | solution.py:446
  14.8 0.9 copy-done.4
  15.7 0.3 collective-permute-start.3
  16.0 1.2 collective-permute-done.3.r_ref
  17.2 0.3 collective-permute-start.4
  17.5 2.3 %collective-permute-start.8 = (bf16[512,768]{1,0:T(8,128)(2,1)}, bf16[512,768]{1,0:T(8,128)(2,1)S(1)}, u32[]{:S(2)}, u32[]{:S(2)}) collective-permute-start(bf16[512,768]{1,0:T(8,128)(2,1)} %refs_0_), channel_id=1, source_target_pairs={{0,4},{1,5},{2,6},{3,7},{4,0},{5,1},{6,2},{7,3},{8,12},{9,13},{10,... | collective-permute-start | bytes 2359304 | tf_op jit(solution)/shard_map/ppermute | solution.py:424
  19.8 6.4 %attention.1 = (bf16[512,512]{1,0:T(8,128)(2,1)}, bf16[512,512]{1,0:T(8,128)(2,1)S(1)}, f32[512,256]{1,0:T(8,128)S(1)}, f32[512,256]{1,0:T(8,128)S(1)}, f32[512,...) custom-call(s32[17]{0:T(128)S(1)} %pad_add_fusion.info_ref, bf16[512,512]{1,0:T(8,128)(2,1)S(1)} %get-tuple-element.106.q_ref, ...), custom_call_target="tpu_custom_call" | custom-call | flops 12000000000 | bytes 6291456 | tf_op jit(solution)/shard_map/attention/pallas_call | solution.py:130
  26.2 4.1 %collective-permute-start.6 = (f32[512,256]{1,0:T(8,128)S(1)}, f32[512,256]{1,0:T(8,128)S(1)}, u32[]{:S(2)}, u32[]{:S(2)}) collective-permute-start(f32[512,256]{1,0:T(8,128)S(1)} %get-tuple-element.123), channel_id=1, source_target_pairs={{0,1},{1,0},{2,3},{3,2},{4,5},{5,4},{6,7},{7,6},{8,9},{9,8},{10,11... | collective-permute-start | bytes 1572872 | tf_op jit(solution)/shard_map/ppermute | solution.py:424
  30.4 1.3 %collective-permute-start.10 = (bf16[512,256]{1,0:T(8,128)(2,1)S(1)}, bf16[512,256]{1,0:T(8,128)(2,1)S(1)}, u32[]{:S(2)}, u32[]{:S(2)}) collective-permute-start(bf16[512,256]{1,0:T(8,128)(2,1)S(1)} %get-tuple-element.126), channel_id=1, source_target_pairs={{1,0},{3,2},{5,4},{7,6},{4,1},{6,3},{9,8},{11,10},{13,12},{15,14},... | collective-permute-start | bytes 786440 | tf_op jit(solution)/shard_map/ppermute | solution.py:466
  31.7 0.2 collective-permute-done.6
  32.0 6.1 %collective-permute-done.8.refs_4_ = bf16[512,768]{1,0:T(8,128)(2,1)S(1)} collective-permute-done((bf16[512,768]{1,0:T(8,128)(2,1)}, bf16[512,768]{1,0:T(8,128)(2,1)S(1)}, u32[]{:S(2)}, u32[]{:S(2)}) %collective-permute-start.8) | collective-permute-done | bytes 786464 | tf_op jit(solution)/shard_map/ppermute | solution.py:424
  38.1 1.5 %collective-permute-done.7.refs_2_ = bf16[512,768]{1,0:T(8,128)(2,1)S(1)} collective-permute-done((bf16[512,768]{1,0:T(8,128)(2,1)}, bf16[512,768]{1,0:T(8,128)(2,1)S(1)}, u32[]{:S(2)}, u32[]{:S(2)}) %collective-permute-start.7) | collective-permute-done | bytes 786464 | tf_op jit(solution)/shard_map/ppermute | solution.py:424
  39.6 1.5 %collective-permute-start.9 = (bf16[512,256]{1,0:T(8,128)(2,1)S(1)}, bf16[512,256]{1,0:T(8,128)(2,1)S(1)}, u32[]{:S(2)}, u32[]{:S(2)}) collective-permute-start(bf16[512,256]{1,0:T(8,128)(2,1)S(1)} %add_convert_fusion), channel_id=1, source_target_pairs={{2,0},{3,1},{4,2},{5,3},{6,4},{7,5},{10,8},{11,9},{12,10},{13,11},... | collective-permute-start | bytes 786440 | tf_op jit(solution)/shard_map/ppermute | solution.py:475
  41.0 4.1 %weight_partials.2 = (f32[512,512]{1,0:T(8,128)S(1)}, bf16[512,512]{1,0:T(8,128)(2,1)S(1)}, bf16[512,512]{1,0:T(8,128)(2,1)S(1)}, bf16[512,512]{1,0:T(8,128)(2,1)S(1)}) custom-call(s32[6]{0:T(128)S(1)} %stack.11.places, bf16[512,512]{1,0:T(8,128)(2,1)S(1)} %get-tuple-element.121.gt_ref, bf16[512,512]{1,0:T(8,128)(2,1)S(1)} %collective-permute-done.5.gt_other, ...), custom_call_target="tpu_custom_call" | custom-call | flops 2147483648 | bytes 8388608 | tf_op jit(solution)/shard_map/weight_partials/pallas_call | solution.py:209
  45.2 3.7 %collective-permute-done.9.two_ref = bf16[512,256]{1,0:T(8,128)(2,1)S(1)} collective-permute-done((bf16[512,256]{1,0:T(8,128)(2,1)S(1)}, bf16[512,256]{1,0:T(8,128)(2,1)S(1)}, u32[]{:S(2)}, u32[]{:S(2)}) %collective-permute-start.9) | collective-permute-done | bytes 262176 | tf_op jit(solution)/shard_map/ppermute | solution.py:475
  48.9 0.5 collective-permute-start.15
  49.4 1.5 %collective-permute-start.11 = (bf16[512,512]{1,0:T(8,128)(2,1)S(1)}, bf16[512,512]{1,0:T(8,128)(2,1)S(1)}, u32[]{:S(2)}, u32[]{:S(2)}) collective-permute-start(bf16[512,512]{1,0:T(8,128)(2,1)S(1)} %get-tuple-element.139), channel_id=1, source_target_pairs={{0,2},{1,3},{2,0},{3,1},{4,6},{5,7},{6,4},{7,5},{8,10},{9,11},{10,... | collective-permute-start | bytes 1572872 | tf_op jit(solution)/shard_map/ppermute | solution.py:424
  50.9 1.1 finish_kv.1
  52.0 1.5 %collective-permute-done.13.gt_other = bf16[256,512]{1,0:T(8,128)(2,1)S(1)} collective-permute-done((bf16[256,512]{1,0:T(8,128)(2,1)S(1)}, bf16[256,512]{1,0:T(8,128)(2,1)S(1)}, u32[]{:S(2)}, u32[]{:S(2)}) %collective-permute-start.13) | collective-permute-done | bytes 262176 | tf_op jit(solution)/shard_map/ppermute | solution.py:424
  53.5 3.7 %weight_partials.3 = (f32[256,512]{1,0:T(8,128)S(1)}, bf16[256,512]{1,0:T(8,128)(2,1)S(1)}, bf16[256,512]{1,0:T(8,128)(2,1)}, bf16[256,512]{1,0:T(8,128)(2,1)}) custom-call(s32[6]{0:T(128)S(1)} %stack.11.places, bf16[256,512]{1,0:T(8,128)(2,1)S(1)} %get-tuple-element.141.gt_ref, bf16[256,512]{1,0:T(8,128)(2,1)S(1)} %collective-permute-done.13.gt_other, ...), custom_call_target="tpu_custom_call" | custom-call | flops 1073741824 | bytes 8388608 | tf_op jit(solution)/shard_map/weight_partials/pallas_call | solution.py:209
  57.3 6.0 %collective-permute-done.11.from_x = bf16[512,512]{1,0:T(8,128)(2,1)S(1)} collective-permute-done((bf16[512,512]{1,0:T(8,128)(2,1)S(1)}, bf16[512,512]{1,0:T(8,128)(2,1)S(1)}, u32[]{:S(2)}, u32[]{:S(2)}) %collective-permute-start.11) | collective-permute-done | bytes 524320 | tf_op jit(solution)/shard_map/ppermute | solution.py:424
  63.2 1.3 %collective-permute-done.12.from_y = bf16[512,512]{1,0:T(8,128)(2,1)S(1)} collective-permute-done((bf16[512,512]{1,0:T(8,128)(2,1)S(1)}, bf16[512,512]{1,0:T(8,128)(2,1)S(1)}, u32[]{:S(2)}, u32[]{:S(2)}) %collective-permute-start.12) | collective-permute-done | bytes 524320 | tf_op jit(solution)/shard_map/ppermute | solution.py:424
  64.5 1.2 middle.2
  65.8 0.5 collective-permute-start.16
  66.3 0.6 collective-permute-start.17
  66.9 1.2 collective-permute-start.18
  68.2 1.7 %collective-permute-start.19 = (bf16[256,512]{1,0:T(8,128)(2,1)}, bf16[256,512]{1,0:T(8,128)(2,1)}, u32[]{:S(2)}, u32[]{:S(2)}) collective-permute-start(bf16[256,512]{1,0:T(8,128)(2,1)} %get-tuple-element.162), channel_id=1, source_target_pairs={{0,4},{1,5},{2,6},{3,7},{4,0},{5,1},{6,2},{7,3},{8,12},{9,13},{10,... | collective-permute-start | bytes 786440 | tf_op jit(solution)/shard_map/ppermute | solution.py:424
  69.9 5.5 %collective-permute-done.16.x_ref = bf16[256,512]{1,0:T(8,128)(2,1)} collective-permute-done((bf16[256,512]{1,0:T(8,128)(2,1)}, bf16[256,512]{1,0:T(8,128)(2,1)}, u32[]{:S(2)}, u32[]{:S(2)}) %collective-permute-start.16) | collective-permute-done | bytes 262176 | tf_op jit(solution)/shard_map/ppermute | solution.py:424
  75.4 0.5 collective-permute-done.17.y_ref
  75.9 1.3 %quarters.2 = (f32[128,512]{1,0:T(8,128)S(1)}, bf16[128,512]{1,0:T(8,128)(2,1)S(1)}, bf16[128,512]{1,0:T(8,128)(2,1)S(1)}, bf16[128,512]{1,0:T(8,128)(2,1)S(1)}) custom-call(s32[1]{0:T(128)} %bitcast.10.z_ref, f32[512,512]{1,0:T(8,128)S(1)} %get-tuple-element.154.own_ref, bf16[256,512]{1,0:T(8,128)(2,1)} %collective-permute-done.16.x_ref, ...), custom_call_target="tpu_custom_call" | custom-call | flops 1048576 | bytes 2097152 | tf_op jit(solution)/shard_map/quarters/pallas_call | solution.py:350
  77.2 1.6 %collective-permute-start.22 = (bf16[128,512]{1,0:T(8,128)(2,1)S(1)}, bf16[128,512]{1,0:T(8,128)(2,1)S(1)}, u32[]{:S(2)}, u32[]{:S(2)}) collective-permute-start(bf16[128,512]{1,0:T(8,128)(2,1)S(1)} %get-tuple-element.165), channel_id=1, source_target_pairs={{0,8},{8,0},{16,24},{24,16},{1,9},{9,1},{17,25},{25,17},{2,10},{10... | collective-permute-start | bytes 393224 | tf_op jit(solution)/shard_map/ppermute | solution.py:424
  78.9 2.6 %collective-permute-start.23 = (bf16[128,512]{1,0:T(8,128)(2,1)S(1)}, bf16[128,512]{1,0:T(8,128)(2,1)S(1)}, u32[]{:S(2)}, u32[]{:S(2)}) collective-permute-start(bf16[128,512]{1,0:T(8,128)(2,1)S(1)} %get-tuple-element.166), channel_id=1, source_target_pairs={{0,16},{8,24},{16,0},{24,8},{1,17},{9,25},{17,1},{25,9},{2,18},{10... | collective-permute-start | bytes 393224 | tf_op jit(solution)/shard_map/ppermute | solution.py:424
  81.5 0.2 collective-permute-start.24
  81.7 1.0 copy-done.13
  82.7 0.9 copy-done.16
  83.7 1.1 middle.3
  84.8 1.6 %collective-permute-start.20 = (bf16[128,512]{1,0:T(8,128)(2,1)S(1)}, bf16[128,512]{1,0:T(8,128)(2,1)S(1)}, u32[]{:S(2)}, u32[]{:S(2)}) collective-permute-start(bf16[128,512]{1,0:T(8,128)(2,1)S(1)} %get-tuple-element.163), channel_id=1, source_target_pairs={{0,2},{1,3},{2,0},{3,1},{4,6},{5,7},{6,4},{7,5},{8,10},{9,11},{10,... | collective-permute-start | bytes 393224 | tf_op jit(solution)/shard_map/ppermute | solution.py:424
  86.4 0.3 collective-permute-start.21
  86.7 1.6 %collective-permute-done.24.refs_3_ = bf16[128,512]{1,0:T(8,128)(2,1)S(1)} collective-permute-done((bf16[128,512]{1,0:T(8,128)(2,1)S(1)}, bf16[128,512]{1,0:T(8,128)(2,1)S(1)}, u32[]{:S(2)}, u32[]{:S(2)}) %collective-permute-start.24) | collective-permute-done | bytes 131104 | tf_op jit(solution)/shard_map/ppermute | solution.py:424
  88.3 2.9 %collective-permute-done.20.x_ref = bf16[128,512]{1,0:T(8,128)(2,1)S(1)} collective-permute-done((bf16[128,512]{1,0:T(8,128)(2,1)S(1)}, bf16[128,512]{1,0:T(8,128)(2,1)S(1)}, u32[]{:S(2)}, u32[]{:S(2)}) %collective-permute-start.20) | collective-permute-done | bytes 131104 | tf_op jit(solution)/shard_map/ppermute | solution.py:424
  91.3 1.6 %collective-permute-done.21.y_ref = bf16[128,512]{1,0:T(8,128)(2,1)S(1)} collective-permute-done((bf16[128,512]{1,0:T(8,128)(2,1)S(1)}, bf16[128,512]{1,0:T(8,128)(2,1)S(1)}, u32[]{:S(2)}, u32[]{:S(2)}) %collective-permute-start.21) | collective-permute-done | bytes 131104 | tf_op jit(solution)/shard_map/ppermute | solution.py:424
  92.9 0.1 quarters.3
  93.1 0.4 collective-permute-start.29
  93.5 0.7 collective-permute-start.28
  94.2 0.1 collective-permute-start.25
  94.3 4.0 %collective-permute-start.26 = (bf16[64,512]{1,0:T(8,128)(2,1)S(1)}, bf16[64,512]{1,0:T(8,128)(2,1)S(1)}, u32[]{:S(2)}, u32[]{:S(2)}) collective-permute-start(bf16[64,512]{1,0:T(8,128)(2,1)S(1)} %get-tuple-element.180), channel_id=1, source_target_pairs={{0,16},{8,24},{16,0},{24,8},{1,17},{9,25},{17,1},{25,9},{2,18},{10... | collective-permute-start | bytes 196616 | tf_op jit(solution)/shard_map/ppermute | solution.py:424
  98.4 0.2 collective-permute-start.27
  98.6 5.5 %input_grad.2.refs_2_ = bf16[512,4096]{1,0:T(8,128)(2,1)} custom-call(s32[6]{0:T(128)S(1)} %stack.11.places, bf16[512,512]{1,0:T(8,128)(2,1)S(1)} %copy-done.1, bf16[512,256]{1,0:T(8,128)(2,1)S(1)} %copy-done.2, bf16[512,768]{1,0:T(8,128)(2,1)S(1)} %copy-done.3, bf16[512,768]{1,0:T(8,128)(2,1)S(1)} %copy-done.5, ...), custom_call_target="tpu_custom_call" | custom-call | flops 2415919104 | bytes 11534336 | tf_op jit(solution)/shard_map/input_grad/pallas_call | solution.py:283
  104.1 0.3 collective-permute-done.27.refs_7_
  104.6 0.1 added.1.refs_0_
  104.7 3.3 %collective-permute-start.32 = (bf16[192,512]{1,0:T(8,128)(2,1)S(1)}, bf16[192,512]{1,0:T(8,128)(2,1)S(1)}, u32[]{:S(2)}, u32[]{:S(2)}) collective-permute-start(bf16[192,512]{1,0:T(8,128)(2,1)S(1)} %added.1.refs_0_), channel_id=1, source_target_pairs={{0,24},{8,16},{16,8},{24,0},{1,25},{9,17},{17,9},{25,1},{2,26},{10... | collective-permute-start | bytes 589832 | tf_op jit(solution)/shard_map/ppermute | solution.py:424
  108.1 1.1 collective-permute-start.30
  109.2 2.6 %input_grad.3 = bf16[512,4096]{1,0:T(8,128)(2,1)} custom-call(s32[6]{0:T(128)S(1)} %stack.11.places, bf16[512,512]{1,0:T(8,128)(2,1)S(1)} %copy-done.1, bf16[512,256]{1,0:T(8,128)(2,1)S(1)} %copy-done.2, bf16[512,768]{1,0:T(8,128)(2,1)S(1)} %constant_dynamic-update-slice_fusion.refs_0_, ...), custom_call_target="tpu_custom_call", output_to_operand_aliasing={{}: (5, {})} | custom-call | flops 805306368 | bytes 11534336 | tf_op jit(solution)/shard_map/input_grad/pallas_call | solution.py:283
  111.8 2.6 %collective-permute-done.32.refs_3_ = bf16[192,512]{1,0:T(8,128)(2,1)S(1)} collective-permute-done((bf16[192,512]{1,0:T(8,128)(2,1)S(1)}, bf16[192,512]{1,0:T(8,128)(2,1)S(1)}, u32[]{:S(2)}, u32[]{:S(2)}) %collective-permute-start.32) | collective-permute-done | bytes 196640 | tf_op jit(solution)/shard_map/ppermute | solution.py:424
  114.4 9.8 %collective-permute-done.31.refs_2_ = bf16[192,512]{1,0:T(8,128)(2,1)S(1)} collective-permute-done((bf16[192,512]{1,0:T(8,128)(2,1)S(1)}, bf16[192,512]{1,0:T(8,128)(2,1)S(1)}, u32[]{:S(2)}, u32[]{:S(2)}) %collective-permute-start.31) | collective-permute-done | bytes 196640 | tf_op jit(solution)/shard_map/ppermute | solution.py:424
  124.2 1.5 %joined.1 = bf16[512,768]{1,0:T(8,128)(2,1)} custom-call(s32[1]{0:T(128)} %bitcast.10.z_ref, bf16[192,512]{1,0:T(8,128)(2,1)S(1)} %added.1.refs_0_, bf16[192,512]{1,0:T(8,128)(2,1)S(1)} %collective-permute-done.30.refs_1_, bf16[192,512]{1,0:T(8,128)(2,1)S(1)} %collective-permute-done.31.refs_2_, bf16[192,512]{1,0:T(8,128)(2,1)S(1)} %collective-permute-done.32.refs_3_), custom_call_target="tpu_custom_call" | custom-call | flops 98304 | bytes 2097152 | tf_op jit(solution)/shard_map/joined/pallas_call | solution.py:411
  (58 shorter events, 0.5 us)
Async XLA Ops:
  0.6 14.2 %collective-permute-start.2 = (bf16[512,768]{1,0:T(8,128)(2,1)}, bf16[512,768]{1,0:T(8,128)(2,1)S(1)}, u32[]{:S(2)}, u32[]{:S(2)}) collective-permute-start(bf16[512,768]{1,0:T(8,128)(2,1)} %refs_0_), channel_id=1, source_target_pairs={{0,1},{1,0},{2,3},{3,2},{4,5},{5,4},{6,7},{7,6},{8,9},{9,8},{10,11... | collective-permute-start | bytes 2359304 | tf_op jit(solution)/shard_map/ppermute | solution.py:424
  1.1 10.9 %collective-permute-start.1 = (bf16[512,256]{1,0:T(8,128)(2,1)}, bf16[512,256]{1,0:T(8,128)(2,1)S(1)}, u32[]{:S(2)}, u32[]{:S(2)}) collective-permute-start(bf16[512,256]{1,0:T(8,128)(2,1)} %bitcast.19), channel_id=1, source_target_pairs={{0,1},{2,3},{4,5},{6,7},{1,4},{3,6},{8,9},{10,11},{12,13},{14,15},... | collective-permute-start | bytes 786440 | tf_op jit(solution)/shard_map/ppermute | solution.py:447
  3.1 11.7 %collective-permute-start = (bf16[512,256]{1,0:T(8,128)(2,1)}, bf16[512,256]{1,0:T(8,128)(2,1)S(1)}, u32[]{:S(2)}, u32[]{:S(2)}) collective-permute-start(bf16[512,256]{1,0:T(8,128)(2,1)} %bitcast.20), channel_id=1, source_target_pairs={{0,2},{1,3},{2,4},{3,5},{4,6},{5,7},{8,10},{9,11},{10,12},{11,13},... | collective-permute-start | bytes 786440 | tf_op jit(solution)/shard_map/ppermute | solution.py:446
  8.1 1.0 copy-start.10
  9.1 1.0 copy-start.11
  10.2 0.9 copy-start.14
  14.8 0.9 copy-start.4
  15.7 1.5 %collective-permute-start.3 = (bf16[512,256]{1,0:T(8,128)(2,1)S(1)}, bf16[512,256]{1,0:T(8,128)(2,1)S(1)}, u32[]{:S(2)}, u32[]{:S(2)}) collective-permute-start(bf16[512,256]{1,0:T(8,128)(2,1)S(1)} %collective-permute-done.d2_ref), channel_id=1, source_target_pairs={{0,1},{1,0},{2,3},{3,2},{4,5},{5,4},{6,7},{7,6},{8,9},{9,8},{10,11... | collective-permute-start | bytes 786440 | tf_op jit(solution)/shard_map/ppermute | solution.py:424
  17.2 23.8 %copy-start = (bf16[1,512,4096]{2,1,0:T(8,128)(2,1)S(1)}, bf16[1,512,4096]{2,1,0:T(8,128)(2,1)}, u32[]{:S(2)}) copy-start(bf16[1,512,4096]{2,1,0:T(8,128)(2,1)} %param.6) | copy-start | bytes 12582916
  17.2 9.0 %collective-permute-start.4 = (bf16[512,4096]{1,0:T(8,128)(2,1)}, bf16[512,4096]{1,0:T(8,128)(2,1)S(1)}, u32[]{:S(2)}, u32[]{:S(2)}) collective-permute-start(bf16[512,4096]{1,0:T(8,128)(2,1)} %bitcast.12), channel_id=1, source_target_pairs={{0,1},{1,0},{2,3},{3,2},{4,5},{5,4},{6,7},{7,6},{8,9},{9,8},{10,11... | collective-permute-start | bytes 12582920 | tf_op jit(solution)/shard_map/ppermute | solution.py:424
  17.5 20.6 %collective-permute-start.8 = (bf16[512,768]{1,0:T(8,128)(2,1)}, bf16[512,768]{1,0:T(8,128)(2,1)S(1)}, u32[]{:S(2)}, u32[]{:S(2)}) collective-permute-start(bf16[512,768]{1,0:T(8,128)(2,1)} %refs_0_), channel_id=1, source_target_pairs={{0,4},{1,5},{2,6},{3,7},{4,0},{5,1},{6,2},{7,3},{8,12},{9,13},{10,... | collective-permute-start | bytes 2359304 | tf_op jit(solution)/shard_map/ppermute | solution.py:424
  19.8 19.7 %collective-permute-start.7 = (bf16[512,768]{1,0:T(8,128)(2,1)}, bf16[512,768]{1,0:T(8,128)(2,1)S(1)}, u32[]{:S(2)}, u32[]{:S(2)}) collective-permute-start(bf16[512,768]{1,0:T(8,128)(2,1)} %refs_0_), channel_id=1, source_target_pairs={{0,2},{1,3},{2,0},{3,1},{4,6},{5,7},{6,4},{7,5},{8,10},{9,11},{10,... | collective-permute-start | bytes 2359304 | tf_op jit(solution)/shard_map/ppermute | solution.py:424
  26.2 5.7 %collective-permute-start.6 = (f32[512,256]{1,0:T(8,128)S(1)}, f32[512,256]{1,0:T(8,128)S(1)}, u32[]{:S(2)}, u32[]{:S(2)}) collective-permute-start(f32[512,256]{1,0:T(8,128)S(1)} %get-tuple-element.123), channel_id=1, source_target_pairs={{0,1},{1,0},{2,3},{3,2},{4,5},{5,4},{6,7},{7,6},{8,9},{9,8},{10,11... | collective-permute-start | bytes 1572872 | tf_op jit(solution)/shard_map/ppermute | solution.py:424
  30.4 9.2 %collective-permute-start.5 = (bf16[512,512]{1,0:T(8,128)(2,1)S(1)}, bf16[512,512]{1,0:T(8,128)(2,1)S(1)}, u32[]{:S(2)}, u32[]{:S(2)}) collective-permute-start(bf16[512,512]{1,0:T(8,128)(2,1)S(1)} %get-tuple-element.121.gt_ref), channel_id=1, source_target_pairs={{0,1},{1,0},{2,3},{3,2},{4,5},{5,4},{6,7},{7,6},{8,9},{9,8},{10,11... | collective-permute-start | bytes 1572872 | tf_op jit(solution)/shard_map/ppermute | solution.py:424
  30.4 14.8 %collective-permute-start.10 = (bf16[512,256]{1,0:T(8,128)(2,1)S(1)}, bf16[512,256]{1,0:T(8,128)(2,1)S(1)}, u32[]{:S(2)}, u32[]{:S(2)}) collective-permute-start(bf16[512,256]{1,0:T(8,128)(2,1)S(1)} %get-tuple-element.126), channel_id=1, source_target_pairs={{1,0},{3,2},{5,4},{7,6},{4,1},{6,3},{9,8},{11,10},{13,12},{15,14},... | collective-permute-start | bytes 786440 | tf_op jit(solution)/shard_map/ppermute | solution.py:466
  39.6 9.3 %collective-permute-start.9 = (bf16[512,256]{1,0:T(8,128)(2,1)S(1)}, bf16[512,256]{1,0:T(8,128)(2,1)S(1)}, u32[]{:S(2)}, u32[]{:S(2)}) collective-permute-start(bf16[512,256]{1,0:T(8,128)(2,1)S(1)} %add_convert_fusion), channel_id=1, source_target_pairs={{2,0},{3,1},{4,2},{5,3},{6,4},{7,5},{10,8},{11,9},{12,10},{13,11},... | collective-permute-start | bytes 786440 | tf_op jit(solution)/shard_map/ppermute | solution.py:475
  48.9 15.6 %collective-permute-start.14 = (bf16[512,768]{1,0:T(8,128)(2,1)S(1)}, bf16[512,768]{1,0:T(8,128)(2,1)S(1)}, u32[]{:S(2)}, u32[]{:S(2)}) collective-permute-start(bf16[512,768]{1,0:T(8,128)(2,1)S(1)} %collective-permute-done.7.refs_2_), channel_id=1, source_target_pairs={{0,1},{1,0},{2,3},{3,2},{4,5},{5,4},{6,7},{7,6},{8,9},{9,8},{10,11... | collective-permute-start | bytes 2359304 | tf_op jit(solution)/shard_map/ppermute | solution.py:424
  48.9 15.6 %collective-permute-start.15 = (bf16[512,768]{1,0:T(8,128)(2,1)S(1)}, bf16[512,768]{1,0:T(8,128)(2,1)S(1)}, u32[]{:S(2)}, u32[]{:S(2)}) collective-permute-start(bf16[512,768]{1,0:T(8,128)(2,1)S(1)} %collective-permute-done.8.refs_4_), channel_id=1, source_target_pairs={{0,1},{1,0},{2,3},{3,2},{4,5},{5,4},{6,7},{7,6},{8,9},{9,8},{10,11... | collective-permute-start | bytes 2359304 | tf_op jit(solution)/shard_map/ppermute | solution.py:424
  49.4 13.8 %collective-permute-start.11 = (bf16[512,512]{1,0:T(8,128)(2,1)S(1)}, bf16[512,512]{1,0:T(8,128)(2,1)S(1)}, u32[]{:S(2)}, u32[]{:S(2)}) collective-permute-start(bf16[512,512]{1,0:T(8,128)(2,1)S(1)} %get-tuple-element.139), channel_id=1, source_target_pairs={{0,2},{1,3},{2,0},{3,1},{4,6},{5,7},{6,4},{7,5},{8,10},{9,11},{10,... | collective-permute-start | bytes 1572872 | tf_op jit(solution)/shard_map/ppermute | solution.py:424
  50.9 13.6 %collective-permute-start.12 = (bf16[512,512]{1,0:T(8,128)(2,1)S(1)}, bf16[512,512]{1,0:T(8,128)(2,1)S(1)}, u32[]{:S(2)}, u32[]{:S(2)}) collective-permute-start(bf16[512,512]{1,0:T(8,128)(2,1)S(1)} %get-tuple-element.140), channel_id=1, source_target_pairs={{0,4},{1,5},{2,6},{3,7},{4,0},{5,1},{6,2},{7,3},{8,12},{9,13},{10,... | collective-permute-start | bytes 1572872 | tf_op jit(solution)/shard_map/ppermute | solution.py:424
  52.0 1.5 %collective-permute-start.13 = (bf16[256,512]{1,0:T(8,128)(2,1)S(1)}, bf16[256,512]{1,0:T(8,128)(2,1)S(1)}, u32[]{:S(2)}, u32[]{:S(2)}) collective-permute-start(bf16[256,512]{1,0:T(8,128)(2,1)S(1)} %get-tuple-element.141.gt_ref), channel_id=1, source_target_pairs={{0,1},{1,0},{2,3},{3,2},{4,5},{5,4},{6,7},{7,6},{8,9},{9,8},{10,11... | collective-permute-start | bytes 786440 | tf_op jit(solution)/shard_map/ppermute | solution.py:424
  57.2 9.1 %copy-start.12 = (f32[256,512]{1,0:T(8,128)}, f32[256,512]{1,0:T(8,128)S(1)}, u32[]{:S(2)}) copy-start(f32[256,512]{1,0:T(8,128)S(1)} %get-tuple-element.159.own_ref) | copy-start | bytes 1572868
  57.2 9.1 %copy-start.15 = (bf16[256,512]{1,0:T(8,128)(2,1)}, bf16[256,512]{1,0:T(8,128)(2,1)S(1)}, u32[]{:S(2)}) copy-start(bf16[256,512]{1,0:T(8,128)(2,1)S(1)} %get-tuple-element.160.keep_ref) | copy-start | bytes 786436
  57.2 41.3 %copy-start.1 = (bf16[512,512]{1,0:T(8,128)(2,1)S(1)}, bf16[512,512]{1,0:T(8,128)(2,1)}, u32[]{:S(2)}) copy-start(bf16[512,512]{1,0:T(8,128)(2,1)} %get-tuple-element.119.gq_ref) | copy-start | bytes 1572868
  57.2 41.3 %copy-start.2 = (bf16[512,256]{1,0:T(8,128)(2,1)S(1)}, bf16[512,256]{1,0:T(8,128)(2,1)}, u32[]{:S(2)}) copy-start(bf16[512,256]{1,0:T(8,128)(2,1)} %get-tuple-element.138.gkv_ref) | copy-start | bytes 786436
  64.5 1.3 %copy-start.6 = (bf16[512,768]{1,0:T(8,128)(2,1)}, bf16[512,768]{1,0:T(8,128)(2,1)S(1)}, u32[]{:S(2)}) copy-start(bf16[512,768]{1,0:T(8,128)(2,1)S(1)} %collective-permute-done.14.refs_3_) | copy-start | bytes 2359300
  64.5 1.3 %copy-start.8 = (bf16[512,768]{1,0:T(8,128)(2,1)}, bf16[512,768]{1,0:T(8,128)(2,1)S(1)}, u32[]{:S(2)}) copy-start(bf16[512,768]{1,0:T(8,128)(2,1)S(1)} %collective-permute-done.15.refs_5_) | copy-start | bytes 2359300
  65.8 9.6 %collective-permute-start.16 = (bf16[256,512]{1,0:T(8,128)(2,1)}, bf16[256,512]{1,0:T(8,128)(2,1)}, u32[]{:S(2)}, u32[]{:S(2)}) collective-permute-start(bf16[256,512]{1,0:T(8,128)(2,1)} %get-tuple-element.155), channel_id=1, source_target_pairs={{0,2},{1,3},{2,0},{3,1},{4,6},{5,7},{6,4},{7,5},{8,10},{9,11},{10,... | collective-permute-start | bytes 786440 | tf_op jit(solution)/shard_map/ppermute | solution.py:424
  66.3 9.6 %collective-permute-start.17 = (bf16[256,512]{1,0:T(8,128)(2,1)}, bf16[256,512]{1,0:T(8,128)(2,1)}, u32[]{:S(2)}, u32[]{:S(2)}) collective-permute-start(bf16[256,512]{1,0:T(8,128)(2,1)} %get-tuple-element.156), channel_id=1, source_target_pairs={{0,4},{1,5},{2,6},{3,7},{4,0},{5,1},{6,2},{7,3},{8,12},{9,13},{10,... | collective-permute-start | bytes 786440 | tf_op jit(solution)/shard_map/ppermute | solution.py:424
  66.9 14.7 %collective-permute-start.18 = (bf16[256,512]{1,0:T(8,128)(2,1)}, bf16[256,512]{1,0:T(8,128)(2,1)}, u32[]{:S(2)}, u32[]{:S(2)}) collective-permute-start(bf16[256,512]{1,0:T(8,128)(2,1)} %get-tuple-element.161), channel_id=1, source_target_pairs={{0,2},{1,3},{2,0},{3,1},{4,6},{5,7},{6,4},{7,5},{8,10},{9,11},{10,... | collective-permute-start | bytes 786440 | tf_op jit(solution)/shard_map/ppermute | solution.py:424
  68.2 13.5 %collective-permute-start.19 = (bf16[256,512]{1,0:T(8,128)(2,1)}, bf16[256,512]{1,0:T(8,128)(2,1)}, u32[]{:S(2)}, u32[]{:S(2)}) collective-permute-start(bf16[256,512]{1,0:T(8,128)(2,1)} %get-tuple-element.162), channel_id=1, source_target_pairs={{0,4},{1,5},{2,6},{3,7},{4,0},{5,1},{6,2},{7,3},{8,12},{9,13},{10,... | collective-permute-start | bytes 786440 | tf_op jit(solution)/shard_map/ppermute | solution.py:424
  69.9 28.7 %copy-start.3 = (bf16[512,768]{1,0:T(8,128)(2,1)S(1)}, bf16[512,768]{1,0:T(8,128)(2,1)}, u32[]{:S(2)}) copy-start(bf16[512,768]{1,0:T(8,128)(2,1)} %refs_0_) | copy-start | bytes 2359300
  69.9 28.7 %copy-start.5 = (bf16[512,768]{1,0:T(8,128)(2,1)S(1)}, bf16[512,768]{1,0:T(8,128)(2,1)}, u32[]{:S(2)}) copy-start(bf16[512,768]{1,0:T(8,128)(2,1)} %copy-done.4) | copy-start | bytes 2359300
  69.9 28.7 %copy-start.7 = (bf16[512,768]{1,0:T(8,128)(2,1)S(1)}, bf16[512,768]{1,0:T(8,128)(2,1)}, u32[]{:S(2)}) copy-start(bf16[512,768]{1,0:T(8,128)(2,1)} %copy-done.6) | copy-start | bytes 2359300
  69.9 28.7 %copy-start.9 = (bf16[512,768]{1,0:T(8,128)(2,1)S(1)}, bf16[512,768]{1,0:T(8,128)(2,1)}, u32[]{:S(2)}) copy-start(bf16[512,768]{1,0:T(8,128)(2,1)} %copy-done.8) | copy-start | bytes 2359300
  77.2 9.5 %collective-permute-start.22 = (bf16[128,512]{1,0:T(8,128)(2,1)S(1)}, bf16[128,512]{1,0:T(8,128)(2,1)S(1)}, u32[]{:S(2)}, u32[]{:S(2)}) collective-permute-start(bf16[128,512]{1,0:T(8,128)(2,1)S(1)} %get-tuple-element.165), channel_id=1, source_target_pairs={{0,8},{8,0},{16,24},{24,16},{1,9},{9,1},{17,25},{25,17},{2,10},{10... | collective-permute-start | bytes 393224 | tf_op jit(solution)/shard_map/ppermute | solution.py:424
  78.9 7.9 %collective-permute-start.23 = (bf16[128,512]{1,0:T(8,128)(2,1)S(1)}, bf16[128,512]{1,0:T(8,128)(2,1)S(1)}, u32[]{:S(2)}, u32[]{:S(2)}) collective-permute-start(bf16[128,512]{1,0:T(8,128)(2,1)S(1)} %get-tuple-element.166), channel_id=1, source_target_pairs={{0,16},{8,24},{16,0},{24,8},{1,17},{9,25},{17,1},{25,9},{2,18},{10... | collective-permute-start | bytes 393224 | tf_op jit(solution)/shard_map/ppermute | solution.py:424
  81.5 6.9 %collective-permute-start.24 = (bf16[128,512]{1,0:T(8,128)(2,1)S(1)}, bf16[128,512]{1,0:T(8,128)(2,1)S(1)}, u32[]{:S(2)}, u32[]{:S(2)}) collective-permute-start(bf16[128,512]{1,0:T(8,128)(2,1)S(1)} %get-tuple-element.167), channel_id=1, source_target_pairs={{0,24},{8,16},{16,8},{24,0},{1,25},{9,17},{17,9},{25,1},{2,26},{10... | collective-permute-start | bytes 393224 | tf_op jit(solution)/shard_map/ppermute | solution.py:424
  81.7 1.0 copy-start.13
  82.7 0.9 copy-start.16
  84.8 6.4 %collective-permute-start.20 = (bf16[128,512]{1,0:T(8,128)(2,1)S(1)}, bf16[128,512]{1,0:T(8,128)(2,1)S(1)}, u32[]{:S(2)}, u32[]{:S(2)}) collective-permute-start(bf16[128,512]{1,0:T(8,128)(2,1)S(1)} %get-tuple-element.163), channel_id=1, source_target_pairs={{0,2},{1,3},{2,0},{3,1},{4,6},{5,7},{6,4},{7,5},{8,10},{9,11},{10,... | collective-permute-start | bytes 393224 | tf_op jit(solution)/shard_map/ppermute | solution.py:424
  86.4 6.4 %collective-permute-start.21 = (bf16[128,512]{1,0:T(8,128)(2,1)S(1)}, bf16[128,512]{1,0:T(8,128)(2,1)S(1)}, u32[]{:S(2)}, u32[]{:S(2)}) collective-permute-start(bf16[128,512]{1,0:T(8,128)(2,1)S(1)} %get-tuple-element.164), channel_id=1, source_target_pairs={{0,4},{1,5},{2,6},{3,7},{4,0},{5,1},{6,2},{7,3},{8,12},{9,13},{10,... | collective-permute-start | bytes 393224 | tf_op jit(solution)/shard_map/ppermute | solution.py:424
  93.1 11.3 %collective-permute-start.29 = (bf16[256,768]{1,0:T(8,128)(2,1)S(1)}, bf16[256,768]{1,0:T(8,128)(2,1)S(1)}, u32[]{:S(2)}, u32[]{:S(2)}) collective-permute-start(bf16[256,768]{1,0:T(8,128)(2,1)S(1)} %slice.7), channel_id=1, source_target_pairs={{0,2},{1,3},{2,0},{3,1},{4,6},{5,7},{6,4},{7,5},{8,10},{9,11},{10,... | collective-permute-start | bytes 1179656 | tf_op jit(solution)/shard_map/ppermute | solution.py:424
  93.5 10.9 %collective-permute-start.28 = (bf16[256,768]{1,0:T(8,128)(2,1)S(1)}, bf16[256,768]{1,0:T(8,128)(2,1)S(1)}, u32[]{:S(2)}, u32[]{:S(2)}) collective-permute-start(bf16[256,768]{1,0:T(8,128)(2,1)S(1)} %slice.6), channel_id=1, source_target_pairs={{0,4},{1,5},{2,6},{3,7},{4,0},{5,1},{6,2},{7,3},{8,12},{9,13},{10,... | collective-permute-start | bytes 1179656 | tf_op jit(solution)/shard_map/ppermute | solution.py:424
  94.2 9.9 %collective-permute-start.25 = (bf16[64,512]{1,0:T(8,128)(2,1)S(1)}, bf16[64,512]{1,0:T(8,128)(2,1)S(1)}, u32[]{:S(2)}, u32[]{:S(2)}) collective-permute-start(bf16[64,512]{1,0:T(8,128)(2,1)S(1)} %get-tuple-element.179), channel_id=1, source_target_pairs={{0,8},{8,0},{16,24},{24,16},{1,9},{9,1},{17,25},{25,17},{2,10},{10... | collective-permute-start | bytes 196616 | tf_op jit(solution)/shard_map/ppermute | solution.py:424
  94.3 9.7 %collective-permute-start.26 = (bf16[64,512]{1,0:T(8,128)(2,1)S(1)}, bf16[64,512]{1,0:T(8,128)(2,1)S(1)}, u32[]{:S(2)}, u32[]{:S(2)}) collective-permute-start(bf16[64,512]{1,0:T(8,128)(2,1)S(1)} %get-tuple-element.180), channel_id=1, source_target_pairs={{0,16},{8,24},{16,0},{24,8},{1,17},{9,25},{17,1},{25,9},{2,18},{10... | collective-permute-start | bytes 196616 | tf_op jit(solution)/shard_map/ppermute | solution.py:424
  98.4 6.1 %collective-permute-start.27 = (bf16[64,512]{1,0:T(8,128)(2,1)S(1)}, bf16[64,512]{1,0:T(8,128)(2,1)S(1)}, u32[]{:S(2)}, u32[]{:S(2)}) collective-permute-start(bf16[64,512]{1,0:T(8,128)(2,1)S(1)} %get-tuple-element.181), channel_id=1, source_target_pairs={{0,24},{8,16},{16,8},{24,0},{1,25},{9,17},{17,9},{25,1},{2,26},{10... | collective-permute-start | bytes 196616 | tf_op jit(solution)/shard_map/ppermute | solution.py:424
  104.5 4.7 %collective-permute-start.33 = (bf16[512,768]{1,0:T(8,128)(2,1)S(1)}, bf16[512,768]{1,0:T(8,128)(2,1)S(1)}, u32[]{:S(2)}, u32[]{:S(2)}) collective-permute-start(bf16[512,768]{1,0:T(8,128)(2,1)S(1)} %constant_dynamic-update-slice_fusion.refs_0_), channel_id=1, source_target_pairs={{0,1},{1,0},{2,3},{3,2},{4,5},{5,4},{6,7},{7,6},{8,9},{9,8},{10,11... | collective-permute-start | bytes 2359304 | tf_op jit(solution)/shard_map/ppermute | solution.py:424
  104.7 9.7 %collective-permute-start.32 = (bf16[192,512]{1,0:T(8,128)(2,1)S(1)}, bf16[192,512]{1,0:T(8,128)(2,1)S(1)}, u32[]{:S(2)}, u32[]{:S(2)}) collective-permute-start(bf16[192,512]{1,0:T(8,128)(2,1)S(1)} %added.1.refs_0_), channel_id=1, source_target_pairs={{0,24},{8,16},{16,8},{24,0},{1,25},{9,17},{17,9},{25,1},{2,26},{10... | collective-permute-start | bytes 589832 | tf_op jit(solution)/shard_map/ppermute | solution.py:424
  108.0 16.1 %collective-permute-start.31 = (bf16[192,512]{1,0:T(8,128)(2,1)S(1)}, bf16[192,512]{1,0:T(8,128)(2,1)S(1)}, u32[]{:S(2)}, u32[]{:S(2)}) collective-permute-start(bf16[192,512]{1,0:T(8,128)(2,1)S(1)} %added.1.refs_0_), channel_id=1, source_target_pairs={{0,16},{8,24},{16,0},{24,8},{1,17},{9,25},{17,1},{25,9},{2,18},{10... | collective-permute-start | bytes 589832 | tf_op jit(solution)/shard_map/ppermute | solution.py:424
  108.1 16.1 %collective-permute-start.30 = (bf16[192,512]{1,0:T(8,128)(2,1)S(1)}, bf16[192,512]{1,0:T(8,128)(2,1)S(1)}, u32[]{:S(2)}, u32[]{:S(2)}) collective-permute-start(bf16[192,512]{1,0:T(8,128)(2,1)S(1)} %added.1.refs_0_), channel_id=1, source_target_pairs={{0,8},{8,0},{16,24},{24,16},{1,9},{9,1},{17,25},{25,17},{2,10},{10... | collective-permute-start | bytes 589832 | tf_op jit(solution)/shard_map/ppermute | solution.py:424

commit v7 on v6

--- a/solution.py
+++ b/solution.py
@@ -436,8 +436,15 @@
     rows = queries.shape[1]
     assert MOST == 3 * rows
     own = keys_values[0]
-    by_two = [(i, i + 2) for i in range(size - 2)]
-    mixed = [(i, i + 1) for i in range(0, size, 2)] + [(i, i + 3) for i in range(1, size - 3, 2)]
+
+    def needed(source, target):
+        first = target * rows
+        earliest = max(first - (MOST - 1), 1 + MOST if first >= 1 + MOST else 0)
+        return (source + 1) * rows > earliest
+
+    by_two = [(i, i + 2) for i in range(size - 2) if needed(i, i + 2) or needed(i, (i + 2) ^ 1)]
+    mixed = [(i, i + 1) for i in range(0, size, 2)]
+    mixed += [(i, i + 3) for i in range(1, size - 3, 2) if needed(i, i + 3)]
     back = lambda pairs: [(b, a) for a, b in pairs]
     small = size == 8 and planes == 4
     block = qkv_weight.shape[0]

time: 126 us -> 126 us (level)
  starting transfers between devices: 39.6 us -> 41.9 us
  waiting for transfers between devices: 49.2 us -> 47 us
    ppermute x30, waiting for transfers between devices: 42.7 us -> 39.9 us  [flipped(): lax.ppermute(array, axis, [(i, i ^ bits) for i in range(lax.axis_size(axi...]
    ppermute x30, starting transfers between devices: 30 us -> 32.3 us  [flipped(): lax.ppermute(array, axis, [(i, i ^ bits) for i in range(lax.axis_size(axi...]
  transfers between devices with their start and end apart: 34 -> 34, of which waited for: 17 -> 16; matrix products, arithmetic and copies ran while one was open for 1% -> 1% of each run, Pallas kernels for 21% -> 21%
where the time goes in v7:
time: 126 us
  waiting for transfers between devices  47 us (37%)
  starting transfers between devices  41.9 us (33%)
  Pallas kernels  28.9 us (23%)
  local copies, waits for them, and re-layouts  6.21 us (5%)
    ppermute x30, waiting for transfers between devices, flipped(): lax.ppermute(array, axis, [(i, i ^ bits) for i in range(lax.axis_size(axi...  39.9 us
    ppermute x30, starting transfers between devices, flipped(): lax.ppermute(array, axis, [(i, i ^ bits) for i in range(lax.axis_size(axi...  32.3 us
    pallas_call x2, Pallas kernels, input_grad(): pl.pallas_call(functools.partial(input_kernel, count=count), name='input_...  8.05 us
    pallas_call x2, Pallas kernels, weight_partials(): pl.pallas_call(weight_kernel, name='weight_partials', out_shape=[jax.Shap...  7.79 us
    pallas_call x1, Pallas kernels, attention(): pl.pallas_call(attention_kernel, name='attention', out_shape=(jax.ShapeDt...  6.4 us
    unnamed x35, local copies, waits for them, and re-layouts  6.04 us
    ppermute x1, starting transfers between devices, per_device(): d2 = lax.ppermute(own, 'ctx', by_two)  4.86 us
    ppermute x1, waiting for transfers between devices, per_device(): from_two = lax.ppermute(kv_d2, 'ctx', back(by_two))  4.27 us
  transfers between devices with their start and end apart: 34, of which 16 were waited for; matrix products, arithmetic and copies ran while one was open for 1% of the time, Pallas kernels for 21%

profile of v7, /device:TPU:0, one launch (start us, length us, event | category | flops | bytes accessed | tf_op | source)
XLA Modules:
  0.0 125.6 jit_solution(13179342220217517927)
XLA Ops:
  0.6 0.5 collective-permute-start.2
  1.1 2.0 %collective-permute-start.1 = (bf16[512,256]{1,0:T(8,128)(2,1)}, bf16[512,256]{1,0:T(8,128)(2,1)S(1)}, u32[]{:S(2)}, u32[]{:S(2)}) collective-permute-start(bf16[512,256]{1,0:T(8,128)(2,1)} %bitcast.19), channel_id=1, source_target_pairs={{0,1},{2,3},{4,5},{6,7},{3,6},{8,9},{10,11},{12,13},{14,15},{11,14... | collective-permute-start | bytes 786440 | tf_op jit(solution)/shard_map/ppermute | solution.py:454
  3.1 4.9 %collective-permute-start = (bf16[512,256]{1,0:T(8,128)(2,1)}, bf16[512,256]{1,0:T(8,128)(2,1)S(1)}, u32[]{:S(2)}, u32[]{:S(2)}) collective-permute-start(bf16[512,256]{1,0:T(8,128)(2,1)} %bitcast.20), channel_id=1, source_target_pairs={{0,2},{1,3},{3,5},{4,6},{5,7},{8,10},{9,11},{11,13},{12,14},{13,15... | collective-permute-start | bytes 786440 | tf_op jit(solution)/shard_map/ppermute | solution.py:453
  8.0 0.1 stack.11.places
  8.1 1.0 copy-done.10
  9.1 1.0 copy-done.11
  10.2 0.9 copy-done.14
  11.1 0.2 staged.1
  11.3 0.7 pad_add_fusion.info_ref
  12.0 2.8 %collective-permute-done.d2_ref = bf16[512,256]{1,0:T(8,128)(2,1)S(1)} collective-permute-done((bf16[512,256]{1,0:T(8,128)(2,1)}, bf16[512,256]{1,0:T(8,128)(2,1)S(1)}, u32[]{:S(2)}, u32[]{:S(2)}) %collective-permute-start) | collective-permute-done | bytes 262176 | tf_op jit(solution)/shard_map/ppermute | solution.py:453
  14.8 0.9 copy-done.4
  15.7 0.3 collective-permute-start.3
  16.0 1.2 collective-permute-done.3.r_ref
  17.2 0.3 collective-permute-start.4
  17.5 2.3 %collective-permute-start.7 = (bf16[512,768]{1,0:T(8,128)(2,1)}, bf16[512,768]{1,0:T(8,128)(2,1)S(1)}, u32[]{:S(2)}, u32[]{:S(2)}) collective-permute-start(bf16[512,768]{1,0:T(8,128)(2,1)} %refs_0_), channel_id=1, source_target_pairs={{0,2},{1,3},{2,0},{3,1},{4,6},{5,7},{6,4},{7,5},{8,10},{9,11},{10,... | collective-permute-start | bytes 2359304 | tf_op jit(solution)/shard_map/ppermute | solution.py:424
  19.8 6.4 %attention.1 = (bf16[512,512]{1,0:T(8,128)(2,1)}, bf16[512,512]{1,0:T(8,128)(2,1)S(1)}, f32[512,256]{1,0:T(8,128)S(1)}, f32[512,256]{1,0:T(8,128)S(1)}, f32[512,...) custom-call(s32[17]{0:T(128)S(1)} %pad_add_fusion.info_ref, bf16[512,512]{1,0:T(8,128)(2,1)S(1)} %get-tuple-element.106.q_ref, ...), custom_call_target="tpu_custom_call" | custom-call | flops 12000000000 | bytes 6291456 | tf_op jit(solution)/shard_map/attention/pallas_call | solution.py:130
  26.2 4.1 %collective-permute-start.6 = (f32[512,256]{1,0:T(8,128)S(1)}, f32[512,256]{1,0:T(8,128)S(1)}, u32[]{:S(2)}, u32[]{:S(2)}) collective-permute-start(f32[512,256]{1,0:T(8,128)S(1)} %get-tuple-element.123), channel_id=1, source_target_pairs={{0,1},{1,0},{2,3},{3,2},{4,5},{5,4},{6,7},{7,6},{8,9},{9,8},{10,11... | collective-permute-start | bytes 1572872 | tf_op jit(solution)/shard_map/ppermute | solution.py:424
  30.3 1.3 %collective-permute-start.10 = (bf16[512,256]{1,0:T(8,128)(2,1)S(1)}, bf16[512,256]{1,0:T(8,128)(2,1)S(1)}, u32[]{:S(2)}, u32[]{:S(2)}) collective-permute-start(bf16[512,256]{1,0:T(8,128)(2,1)S(1)} %get-tuple-element.126), channel_id=1, source_target_pairs={{1,0},{3,2},{5,4},{7,6},{6,3},{9,8},{11,10},{13,12},{15,14},{14,11... | collective-permute-start | bytes 786440 | tf_op jit(solution)/shard_map/ppermute | solution.py:473
  31.6 0.2 collective-permute-done.6
  31.9 5.5 %collective-permute-done.8.refs_4_ = bf16[512,768]{1,0:T(8,128)(2,1)S(1)} collective-permute-done((bf16[512,768]{1,0:T(8,128)(2,1)}, bf16[512,768]{1,0:T(8,128)(2,1)S(1)}, u32[]{:S(2)}, u32[]{:S(2)}) %collective-permute-start.8) | collective-permute-done | bytes 786464 | tf_op jit(solution)/shard_map/ppermute | solution.py:424
  37.4 0.7 collective-permute-done.7.refs_2_
  38.1 1.5 %collective-permute-start.9 = (bf16[512,256]{1,0:T(8,128)(2,1)S(1)}, bf16[512,256]{1,0:T(8,128)(2,1)S(1)}, u32[]{:S(2)}, u32[]{:S(2)}) collective-permute-start(bf16[512,256]{1,0:T(8,128)(2,1)S(1)} %add_convert_fusion), channel_id=1, source_target_pairs={{2,0},{3,1},{5,3},{6,4},{7,5},{10,8},{11,9},{13,11},{14,12},{15,13... | collective-permute-start | bytes 786440 | tf_op jit(solution)/shard_map/ppermute | solution.py:482
  39.5 4.1 %weight_partials.2 = (f32[512,512]{1,0:T(8,128)S(1)}, bf16[512,512]{1,0:T(8,128)(2,1)S(1)}, bf16[512,512]{1,0:T(8,128)(2,1)S(1)}, bf16[512,512]{1,0:T(8,128)(2,1)S(1)}) custom-call(s32[6]{0:T(128)S(1)} %stack.11.places, bf16[512,512]{1,0:T(8,128)(2,1)S(1)} %get-tuple-element.121.gt_ref, bf16[512,512]{1,0:T(8,128)(2,1)S(1)} %collective-permute-done.5.gt_other, ...), custom_call_target="tpu_custom_call" | custom-call | flops 2147483648 | bytes 8388608 | tf_op jit(solution)/shard_map/weight_partials/pallas_call | solution.py:209
  43.7 4.3 %collective-permute-done.9.two_ref = bf16[512,256]{1,0:T(8,128)(2,1)S(1)} collective-permute-done((bf16[512,256]{1,0:T(8,128)(2,1)S(1)}, bf16[512,256]{1,0:T(8,128)(2,1)S(1)}, u32[]{:S(2)}, u32[]{:S(2)}) %collective-permute-start.9) | collective-permute-done | bytes 262176 | tf_op jit(solution)/shard_map/ppermute | solution.py:482
  47.9 0.5 collective-permute-start.15
  48.4 1.5 %collective-permute-start.12 = (bf16[512,512]{1,0:T(8,128)(2,1)S(1)}, bf16[512,512]{1,0:T(8,128)(2,1)S(1)}, u32[]{:S(2)}, u32[]{:S(2)}) collective-permute-start(bf16[512,512]{1,0:T(8,128)(2,1)S(1)} %get-tuple-element.140), channel_id=1, source_target_pairs={{0,4},{1,5},{2,6},{3,7},{4,0},{5,1},{6,2},{7,3},{8,12},{9,13},{10,... | collective-permute-start | bytes 1572872 | tf_op jit(solution)/shard_map/ppermute | solution.py:424
  50.0 1.1 finish_kv.1
  51.0 1.5 %collective-permute-done.13.gt_other = bf16[256,512]{1,0:T(8,128)(2,1)S(1)} collective-permute-done((bf16[256,512]{1,0:T(8,128)(2,1)S(1)}, bf16[256,512]{1,0:T(8,128)(2,1)S(1)}, u32[]{:S(2)}, u32[]{:S(2)}) %collective-permute-start.13) | collective-permute-done | bytes 262176 | tf_op jit(solution)/shard_map/ppermute | solution.py:424
  52.6 3.7 %weight_partials.3 = (f32[256,512]{1,0:T(8,128)S(1)}, bf16[256,512]{1,0:T(8,128)(2,1)S(1)}, bf16[256,512]{1,0:T(8,128)(2,1)}, bf16[256,512]{1,0:T(8,128)(2,1)}) custom-call(s32[6]{0:T(128)S(1)} %stack.11.places, bf16[256,512]{1,0:T(8,128)(2,1)S(1)} %get-tuple-element.141.gt_ref, bf16[256,512]{1,0:T(8,128)(2,1)S(1)} %collective-permute-done.13.gt_other, ...), custom_call_target="tpu_custom_call" | custom-call | flops 1073741824 | bytes 8388608 | tf_op jit(solution)/shard_map/weight_partials/pallas_call | solution.py:209
  56.3 6.0 %collective-permute-done.11.from_x = bf16[512,512]{1,0:T(8,128)(2,1)S(1)} collective-permute-done((bf16[512,512]{1,0:T(8,128)(2,1)S(1)}, bf16[512,512]{1,0:T(8,128)(2,1)S(1)}, u32[]{:S(2)}, u32[]{:S(2)}) %collective-permute-start.11) | collective-permute-done | bytes 524320 | tf_op jit(solution)/shard_map/ppermute | solution.py:424
  62.3 1.2 middle.2
  63.6 1.7 %collective-permute-start.16 = (bf16[256,512]{1,0:T(8,128)(2,1)}, bf16[256,512]{1,0:T(8,128)(2,1)}, u32[]{:S(2)}, u32[]{:S(2)}) collective-permute-start(bf16[256,512]{1,0:T(8,128)(2,1)} %get-tuple-element.155), channel_id=1, source_target_pairs={{0,2},{1,3},{2,0},{3,1},{4,6},{5,7},{6,4},{7,5},{8,10},{9,11},{10,... | collective-permute-start | bytes 786440 | tf_op jit(solution)/shard_map/ppermute | solution.py:424
  65.4 1.5 %collective-permute-start.17 = (bf16[256,512]{1,0:T(8,128)(2,1)}, bf16[256,512]{1,0:T(8,128)(2,1)}, u32[]{:S(2)}, u32[]{:S(2)}) collective-permute-start(bf16[256,512]{1,0:T(8,128)(2,1)} %get-tuple-element.156), channel_id=1, source_target_pairs={{0,4},{1,5},{2,6},{3,7},{4,0},{5,1},{6,2},{7,3},{8,12},{9,13},{10,... | collective-permute-start | bytes 786440 | tf_op jit(solution)/shard_map/ppermute | solution.py:424
  66.9 0.3 collective-permute-start.18
  67.2 0.5 collective-permute-start.19
  67.7 5.5 %collective-permute-done.16.x_ref = bf16[256,512]{1,0:T(8,128)(2,1)} collective-permute-done((bf16[256,512]{1,0:T(8,128)(2,1)}, bf16[256,512]{1,0:T(8,128)(2,1)}, u32[]{:S(2)}, u32[]{:S(2)}) %collective-permute-start.16) | collective-permute-done | bytes 262176 | tf_op jit(solution)/shard_map/ppermute | solution.py:424
  73.2 1.7 %collective-permute-done.17.y_ref = bf16[256,512]{1,0:T(8,128)(2,1)} collective-permute-done((bf16[256,512]{1,0:T(8,128)(2,1)}, bf16[256,512]{1,0:T(8,128)(2,1)}, u32[]{:S(2)}, u32[]{:S(2)}) %collective-permute-start.17) | collective-permute-done | bytes 262176 | tf_op jit(solution)/shard_map/ppermute | solution.py:424
  74.9 1.3 %quarters.2 = (f32[128,512]{1,0:T(8,128)S(1)}, bf16[128,512]{1,0:T(8,128)(2,1)S(1)}, bf16[128,512]{1,0:T(8,128)(2,1)S(1)}, bf16[128,512]{1,0:T(8,128)(2,1)S(1)}) custom-call(s32[1]{0:T(128)} %bitcast.10.z_ref, f32[512,512]{1,0:T(8,128)S(1)} %get-tuple-element.154.own_ref, bf16[256,512]{1,0:T(8,128)(2,1)} %collective-permute-done.16.x_ref, ...), custom_call_target="tpu_custom_call" | custom-call | flops 1048576 | bytes 2097152 | tf_op jit(solution)/shard_map/quarters/pallas_call | solution.py:350
  76.3 1.6 %collective-permute-start.22 = (bf16[128,512]{1,0:T(8,128)(2,1)S(1)}, bf16[128,512]{1,0:T(8,128)(2,1)S(1)}, u32[]{:S(2)}, u32[]{:S(2)}) collective-permute-start(bf16[128,512]{1,0:T(8,128)(2,1)S(1)} %get-tuple-element.165), channel_id=1, source_target_pairs={{0,8},{8,0},{16,24},{24,16},{1,9},{9,1},{17,25},{25,17},{2,10},{10... | collective-permute-start | bytes 393224 | tf_op jit(solution)/shard_map/ppermute | solution.py:424
  77.9 2.6 %collective-permute-start.23 = (bf16[128,512]{1,0:T(8,128)(2,1)S(1)}, bf16[128,512]{1,0:T(8,128)(2,1)S(1)}, u32[]{:S(2)}, u32[]{:S(2)}) collective-permute-start(bf16[128,512]{1,0:T(8,128)(2,1)S(1)} %get-tuple-element.166), channel_id=1, source_target_pairs={{0,16},{8,24},{16,0},{24,8},{1,17},{9,25},{17,1},{25,9},{2,18},{10... | collective-permute-start | bytes 393224 | tf_op jit(solution)/shard_map/ppermute | solution.py:424
  80.5 0.2 collective-permute-start.24
  80.7 1.0 copy-done.13
  81.8 0.9 copy-done.16
  82.7 1.1 middle.3
  83.9 0.3 collective-permute-start.20
  84.2 1.5 %collective-permute-start.21 = (bf16[128,512]{1,0:T(8,128)(2,1)S(1)}, bf16[128,512]{1,0:T(8,128)(2,1)S(1)}, u32[]{:S(2)}, u32[]{:S(2)}) collective-permute-start(bf16[128,512]{1,0:T(8,128)(2,1)S(1)} %get-tuple-element.164), channel_id=1, source_target_pairs={{0,4},{1,5},{2,6},{3,7},{4,0},{5,1},{6,2},{7,3},{8,12},{9,13},{10,... | collective-permute-start | bytes 393224 | tf_op jit(solution)/shard_map/ppermute | solution.py:424
  85.8 1.6 %collective-permute-done.24.refs_3_ = bf16[128,512]{1,0:T(8,128)(2,1)S(1)} collective-permute-done((bf16[128,512]{1,0:T(8,128)(2,1)S(1)}, bf16[128,512]{1,0:T(8,128)(2,1)S(1)}, u32[]{:S(2)}, u32[]{:S(2)}) %collective-permute-start.24) | collective-permute-done | bytes 131104 | tf_op jit(solution)/shard_map/ppermute | solution.py:424
  87.4 2.9 %collective-permute-done.20.x_ref = bf16[128,512]{1,0:T(8,128)(2,1)S(1)} collective-permute-done((bf16[128,512]{1,0:T(8,128)(2,1)S(1)}, bf16[128,512]{1,0:T(8,128)(2,1)S(1)}, u32[]{:S(2)}, u32[]{:S(2)}) %collective-permute-start.20) | collective-permute-done | bytes 131104 | tf_op jit(solution)/shard_map/ppermute | solution.py:424
  90.3 0.2 collective-permute-done.21.y_ref
  90.5 0.1 quarters.3
  90.7 1.9 %collective-permute-start.29 = (bf16[256,768]{1,0:T(8,128)(2,1)S(1)}, bf16[256,768]{1,0:T(8,128)(2,1)S(1)}, u32[]{:S(2)}, u32[]{:S(2)}) collective-permute-start(bf16[256,768]{1,0:T(8,128)(2,1)S(1)} %slice.7), channel_id=1, source_target_pairs={{0,2},{1,3},{2,0},{3,1},{4,6},{5,7},{6,4},{7,5},{8,10},{9,11},{10,... | collective-permute-start | bytes 1179656 | tf_op jit(solution)/shard_map/ppermute | solution.py:424
  92.7 1.5 %collective-permute-start.28 = (bf16[256,768]{1,0:T(8,128)(2,1)S(1)}, bf16[256,768]{1,0:T(8,128)(2,1)S(1)}, u32[]{:S(2)}, u32[]{:S(2)}) collective-permute-start(bf16[256,768]{1,0:T(8,128)(2,1)S(1)} %slice.6), channel_id=1, source_target_pairs={{0,4},{1,5},{2,6},{3,7},{4,0},{5,1},{6,2},{7,3},{8,12},{9,13},{10,... | collective-permute-start | bytes 1179656 | tf_op jit(solution)/shard_map/ppermute | solution.py:424
  94.2 0.6 collective-permute-start.25
  94.8 3.5 %collective-permute-start.26 = (bf16[64,512]{1,0:T(8,128)(2,1)S(1)}, bf16[64,512]{1,0:T(8,128)(2,1)S(1)}, u32[]{:S(2)}, u32[]{:S(2)}) collective-permute-start(bf16[64,512]{1,0:T(8,128)(2,1)S(1)} %get-tuple-element.180), channel_id=1, source_target_pairs={{0,16},{8,24},{16,0},{24,8},{1,17},{9,25},{17,1},{25,9},{2,18},{10... | collective-permute-start | bytes 196616 | tf_op jit(solution)/shard_map/ppermute | solution.py:424
  98.3 0.2 collective-permute-start.27
  98.6 5.5 %input_grad.2.refs_2_ = bf16[512,4096]{1,0:T(8,128)(2,1)} custom-call(s32[6]{0:T(128)S(1)} %stack.11.places, bf16[512,512]{1,0:T(8,128)(2,1)S(1)} %copy-done.1, bf16[512,256]{1,0:T(8,128)(2,1)S(1)} %copy-done.2, bf16[512,768]{1,0:T(8,128)(2,1)S(1)} %copy-done.3, bf16[512,768]{1,0:T(8,128)(2,1)S(1)} %copy-done.5, ...), custom_call_target="tpu_custom_call" | custom-call | flops 2415919104 | bytes 11534336 | tf_op jit(solution)/shard_map/input_grad/pallas_call | solution.py:283
  104.1 0.3 collective-permute-done.27.refs_7_
  104.6 0.1 added.1.refs_0_
  104.7 3.3 %collective-permute-start.32 = (bf16[192,512]{1,0:T(8,128)(2,1)S(1)}, bf16[192,512]{1,0:T(8,128)(2,1)S(1)}, u32[]{:S(2)}, u32[]{:S(2)}) collective-permute-start(bf16[192,512]{1,0:T(8,128)(2,1)S(1)} %added.1.refs_0_), channel_id=1, source_target_pairs={{0,24},{8,16},{16,8},{24,0},{1,25},{9,17},{17,9},{25,1},{2,26},{10... | collective-permute-start | bytes 589832 | tf_op jit(solution)/shard_map/ppermute | solution.py:424
  108.0 1.1 collective-permute-start.30
  109.2 2.6 %input_grad.3 = bf16[512,4096]{1,0:T(8,128)(2,1)} custom-call(s32[6]{0:T(128)S(1)} %stack.11.places, bf16[512,512]{1,0:T(8,128)(2,1)S(1)} %copy-done.1, bf16[512,256]{1,0:T(8,128)(2,1)S(1)} %copy-done.2, bf16[512,768]{1,0:T(8,128)(2,1)S(1)} %constant_dynamic-update-slice_fusion.refs_0_, ...), custom_call_target="tpu_custom_call", output_to_operand_aliasing={{}: (5, {})} | custom-call | flops 805306368 | bytes 11534336 | tf_op jit(solution)/shard_map/input_grad/pallas_call | solution.py:283
  111.8 2.6 %collective-permute-done.32.refs_3_ = bf16[192,512]{1,0:T(8,128)(2,1)S(1)} collective-permute-done((bf16[192,512]{1,0:T(8,128)(2,1)S(1)}, bf16[192,512]{1,0:T(8,128)(2,1)S(1)}, u32[]{:S(2)}, u32[]{:S(2)}) %collective-permute-start.32) | collective-permute-done | bytes 196640 | tf_op jit(solution)/shard_map/ppermute | solution.py:424
  114.4 9.8 %collective-permute-done.31.refs_2_ = bf16[192,512]{1,0:T(8,128)(2,1)S(1)} collective-permute-done((bf16[192,512]{1,0:T(8,128)(2,1)S(1)}, bf16[192,512]{1,0:T(8,128)(2,1)S(1)}, u32[]{:S(2)}, u32[]{:S(2)}) %collective-permute-start.31) | collective-permute-done | bytes 196640 | tf_op jit(solution)/shard_map/ppermute | solution.py:424
  124.2 1.5 %joined.1 = bf16[512,768]{1,0:T(8,128)(2,1)} custom-call(s32[1]{0:T(128)} %bitcast.10.z_ref, bf16[192,512]{1,0:T(8,128)(2,1)S(1)} %added.1.refs_0_, bf16[192,512]{1,0:T(8,128)(2,1)S(1)} %collective-permute-done.30.refs_1_, bf16[192,512]{1,0:T(8,128)(2,1)S(1)} %collective-permute-done.31.refs_2_, bf16[192,512]{1,0:T(8,128)(2,1)S(1)} %collective-permute-done.32.refs_3_), custom_call_target="tpu_custom_call" | custom-call | flops 98304 | bytes 2097152 | tf_op jit(solution)/shard_map/joined/pallas_call | solution.py:411
  (58 shorter events, 0.4 us)
Async XLA Ops:
  0.6 14.2 %collective-permute-start.2 = (bf16[512,768]{1,0:T(8,128)(2,1)}, bf16[512,768]{1,0:T(8,128)(2,1)S(1)}, u32[]{:S(2)}, u32[]{:S(2)}) collective-permute-start(bf16[512,768]{1,0:T(8,128)(2,1)} %refs_0_), channel_id=1, source_target_pairs={{0,1},{1,0},{2,3},{3,2},{4,5},{5,4},{6,7},{7,6},{8,9},{9,8},{10,11... | collective-permute-start | bytes 2359304 | tf_op jit(solution)/shard_map/ppermute | solution.py:424
  1.1 10.9 %collective-permute-start.1 = (bf16[512,256]{1,0:T(8,128)(2,1)}, bf16[512,256]{1,0:T(8,128)(2,1)S(1)}, u32[]{:S(2)}, u32[]{:S(2)}) collective-permute-start(bf16[512,256]{1,0:T(8,128)(2,1)} %bitcast.19), channel_id=1, source_target_pairs={{0,1},{2,3},{4,5},{6,7},{3,6},{8,9},{10,11},{12,13},{14,15},{11,14... | collective-permute-start | bytes 786440 | tf_op jit(solution)/shard_map/ppermute | solution.py:454
  3.1 11.7 %collective-permute-start = (bf16[512,256]{1,0:T(8,128)(2,1)}, bf16[512,256]{1,0:T(8,128)(2,1)S(1)}, u32[]{:S(2)}, u32[]{:S(2)}) collective-permute-start(bf16[512,256]{1,0:T(8,128)(2,1)} %bitcast.20), channel_id=1, source_target_pairs={{0,2},{1,3},{3,5},{4,6},{5,7},{8,10},{9,11},{11,13},{12,14},{13,15... | collective-permute-start | bytes 786440 | tf_op jit(solution)/shard_map/ppermute | solution.py:453
  8.1 1.0 copy-start.10
  9.1 1.0 copy-start.11
  10.2 0.9 copy-start.14
  14.8 0.9 copy-start.4
  15.7 1.5 %collective-permute-start.3 = (bf16[512,256]{1,0:T(8,128)(2,1)S(1)}, bf16[512,256]{1,0:T(8,128)(2,1)S(1)}, u32[]{:S(2)}, u32[]{:S(2)}) collective-permute-start(bf16[512,256]{1,0:T(8,128)(2,1)S(1)} %collective-permute-done.d2_ref), channel_id=1, source_target_pairs={{0,1},{1,0},{2,3},{3,2},{4,5},{5,4},{6,7},{7,6},{8,9},{9,8},{10,11... | collective-permute-start | bytes 786440 | tf_op jit(solution)/shard_map/ppermute | solution.py:424
  17.2 22.3 %copy-start = (bf16[1,512,4096]{2,1,0:T(8,128)(2,1)S(1)}, bf16[1,512,4096]{2,1,0:T(8,128)(2,1)}, u32[]{:S(2)}) copy-start(bf16[1,512,4096]{2,1,0:T(8,128)(2,1)} %param.6) | copy-start | bytes 12582916
  17.2 9.0 %collective-permute-start.4 = (bf16[512,4096]{1,0:T(8,128)(2,1)}, bf16[512,4096]{1,0:T(8,128)(2,1)S(1)}, u32[]{:S(2)}, u32[]{:S(2)}) collective-permute-start(bf16[512,4096]{1,0:T(8,128)(2,1)} %bitcast.12), channel_id=1, source_target_pairs={{0,1},{1,0},{2,3},{3,2},{4,5},{5,4},{6,7},{7,6},{8,9},{9,8},{10,11... | collective-permute-start | bytes 12582920 | tf_op jit(solution)/shard_map/ppermute | solution.py:424
  17.5 19.9 %collective-permute-start.8 = (bf16[512,768]{1,0:T(8,128)(2,1)}, bf16[512,768]{1,0:T(8,128)(2,1)S(1)}, u32[]{:S(2)}, u32[]{:S(2)}) collective-permute-start(bf16[512,768]{1,0:T(8,128)(2,1)} %refs_0_), channel_id=1, source_target_pairs={{0,4},{1,5},{2,6},{3,7},{4,0},{5,1},{6,2},{7,3},{8,12},{9,13},{10,... | collective-permute-start | bytes 2359304 | tf_op jit(solution)/shard_map/ppermute | solution.py:424
  17.5 20.5 %collective-permute-start.7 = (bf16[512,768]{1,0:T(8,128)(2,1)}, bf16[512,768]{1,0:T(8,128)(2,1)S(1)}, u32[]{:S(2)}, u32[]{:S(2)}) collective-permute-start(bf16[512,768]{1,0:T(8,128)(2,1)} %refs_0_), channel_id=1, source_target_pairs={{0,2},{1,3},{2,0},{3,1},{4,6},{5,7},{6,4},{7,5},{8,10},{9,11},{10,... | collective-permute-start | bytes 2359304 | tf_op jit(solution)/shard_map/ppermute | solution.py:424
  26.2 5.6 %collective-permute-start.6 = (f32[512,256]{1,0:T(8,128)S(1)}, f32[512,256]{1,0:T(8,128)S(1)}, u32[]{:S(2)}, u32[]{:S(2)}) collective-permute-start(f32[512,256]{1,0:T(8,128)S(1)} %get-tuple-element.123), channel_id=1, source_target_pairs={{0,1},{1,0},{2,3},{3,2},{4,5},{5,4},{6,7},{7,6},{8,9},{9,8},{10,11... | collective-permute-start | bytes 1572872 | tf_op jit(solution)/shard_map/ppermute | solution.py:424
  30.3 7.8 %collective-permute-start.5 = (bf16[512,512]{1,0:T(8,128)(2,1)S(1)}, bf16[512,512]{1,0:T(8,128)(2,1)S(1)}, u32[]{:S(2)}, u32[]{:S(2)}) collective-permute-start(bf16[512,512]{1,0:T(8,128)(2,1)S(1)} %get-tuple-element.121.gt_ref), channel_id=1, source_target_pairs={{0,1},{1,0},{2,3},{3,2},{4,5},{5,4},{6,7},{7,6},{8,9},{9,8},{10,11... | collective-permute-start | bytes 1572872 | tf_op jit(solution)/shard_map/ppermute | solution.py:424
  30.3 13.3 %collective-permute-start.10 = (bf16[512,256]{1,0:T(8,128)(2,1)S(1)}, bf16[512,256]{1,0:T(8,128)(2,1)S(1)}, u32[]{:S(2)}, u32[]{:S(2)}) collective-permute-start(bf16[512,256]{1,0:T(8,128)(2,1)S(1)} %get-tuple-element.126), channel_id=1, source_target_pairs={{1,0},{3,2},{5,4},{7,6},{6,3},{9,8},{11,10},{13,12},{15,14},{14,11... | collective-permute-start | bytes 786440 | tf_op jit(solution)/shard_map/ppermute | solution.py:473
  38.1 9.9 %collective-permute-start.9 = (bf16[512,256]{1,0:T(8,128)(2,1)S(1)}, bf16[512,256]{1,0:T(8,128)(2,1)S(1)}, u32[]{:S(2)}, u32[]{:S(2)}) collective-permute-start(bf16[512,256]{1,0:T(8,128)(2,1)S(1)} %add_convert_fusion), channel_id=1, source_target_pairs={{2,0},{3,1},{5,3},{6,4},{7,5},{10,8},{11,9},{13,11},{14,12},{15,13... | collective-permute-start | bytes 786440 | tf_op jit(solution)/shard_map/ppermute | solution.py:482
  47.9 14.3 %collective-permute-start.14 = (bf16[512,768]{1,0:T(8,128)(2,1)S(1)}, bf16[512,768]{1,0:T(8,128)(2,1)S(1)}, u32[]{:S(2)}, u32[]{:S(2)}) collective-permute-start(bf16[512,768]{1,0:T(8,128)(2,1)S(1)} %collective-permute-done.7.refs_2_), channel_id=1, source_target_pairs={{0,1},{1,0},{2,3},{3,2},{4,5},{5,4},{6,7},{7,6},{8,9},{9,8},{10,11... | collective-permute-start | bytes 2359304 | tf_op jit(solution)/shard_map/ppermute | solution.py:424
  47.9 14.4 %collective-permute-start.15 = (bf16[512,768]{1,0:T(8,128)(2,1)S(1)}, bf16[512,768]{1,0:T(8,128)(2,1)S(1)}, u32[]{:S(2)}, u32[]{:S(2)}) collective-permute-start(bf16[512,768]{1,0:T(8,128)(2,1)S(1)} %collective-permute-done.8.refs_4_), channel_id=1, source_target_pairs={{0,1},{1,0},{2,3},{3,2},{4,5},{5,4},{6,7},{7,6},{8,9},{9,8},{10,11... | collective-permute-start | bytes 2359304 | tf_op jit(solution)/shard_map/ppermute | solution.py:424
  48.4 13.8 %collective-permute-start.11 = (bf16[512,512]{1,0:T(8,128)(2,1)S(1)}, bf16[512,512]{1,0:T(8,128)(2,1)S(1)}, u32[]{:S(2)}, u32[]{:S(2)}) collective-permute-start(bf16[512,512]{1,0:T(8,128)(2,1)S(1)} %get-tuple-element.139), channel_id=1, source_target_pairs={{0,2},{1,3},{2,0},{3,1},{4,6},{5,7},{6,4},{7,5},{8,10},{9,11},{10,... | collective-permute-start | bytes 1572872 | tf_op jit(solution)/shard_map/ppermute | solution.py:424
  48.4 13.8 %collective-permute-start.12 = (bf16[512,512]{1,0:T(8,128)(2,1)S(1)}, bf16[512,512]{1,0:T(8,128)(2,1)S(1)}, u32[]{:S(2)}, u32[]{:S(2)}) collective-permute-start(bf16[512,512]{1,0:T(8,128)(2,1)S(1)} %get-tuple-element.140), channel_id=1, source_target_pairs={{0,4},{1,5},{2,6},{3,7},{4,0},{5,1},{6,2},{7,3},{8,12},{9,13},{10,... | collective-permute-start | bytes 1572872 | tf_op jit(solution)/shard_map/ppermute | solution.py:424
  51.0 1.5 %collective-permute-start.13 = (bf16[256,512]{1,0:T(8,128)(2,1)S(1)}, bf16[256,512]{1,0:T(8,128)(2,1)S(1)}, u32[]{:S(2)}, u32[]{:S(2)}) collective-permute-start(bf16[256,512]{1,0:T(8,128)(2,1)S(1)} %get-tuple-element.141.gt_ref), channel_id=1, source_target_pairs={{0,1},{1,0},{2,3},{3,2},{4,5},{5,4},{6,7},{7,6},{8,9},{9,8},{10,11... | collective-permute-start | bytes 786440 | tf_op jit(solution)/shard_map/ppermute | solution.py:424
  56.3 9.1 %copy-start.12 = (f32[256,512]{1,0:T(8,128)}, f32[256,512]{1,0:T(8,128)S(1)}, u32[]{:S(2)}) copy-start(f32[256,512]{1,0:T(8,128)S(1)} %get-tuple-element.159.own_ref) | copy-start | bytes 1572868
  56.3 9.1 %copy-start.15 = (bf16[256,512]{1,0:T(8,128)(2,1)}, bf16[256,512]{1,0:T(8,128)(2,1)S(1)}, u32[]{:S(2)}) copy-start(bf16[256,512]{1,0:T(8,128)(2,1)S(1)} %get-tuple-element.160.keep_ref) | copy-start | bytes 786436
  56.3 42.3 %copy-start.1 = (bf16[512,512]{1,0:T(8,128)(2,1)S(1)}, bf16[512,512]{1,0:T(8,128)(2,1)}, u32[]{:S(2)}) copy-start(bf16[512,512]{1,0:T(8,128)(2,1)} %get-tuple-element.119.gq_ref) | copy-start | bytes 1572868
  56.3 42.3 %copy-start.2 = (bf16[512,256]{1,0:T(8,128)(2,1)S(1)}, bf16[512,256]{1,0:T(8,128)(2,1)}, u32[]{:S(2)}) copy-start(bf16[512,256]{1,0:T(8,128)(2,1)} %get-tuple-element.138.gkv_ref) | copy-start | bytes 786436
  62.3 1.3 %copy-start.6 = (bf16[512,768]{1,0:T(8,128)(2,1)}, bf16[512,768]{1,0:T(8,128)(2,1)S(1)}, u32[]{:S(2)}) copy-start(bf16[512,768]{1,0:T(8,128)(2,1)S(1)} %collective-permute-done.14.refs_3_) | copy-start | bytes 2359300
  62.3 1.3 %copy-start.8 = (bf16[512,768]{1,0:T(8,128)(2,1)}, bf16[512,768]{1,0:T(8,128)(2,1)S(1)}, u32[]{:S(2)}) copy-start(bf16[512,768]{1,0:T(8,128)(2,1)S(1)} %collective-permute-done.15.refs_5_) | copy-start | bytes 2359300
  63.6 9.6 %collective-permute-start.16 = (bf16[256,512]{1,0:T(8,128)(2,1)}, bf16[256,512]{1,0:T(8,128)(2,1)}, u32[]{:S(2)}, u32[]{:S(2)}) collective-permute-start(bf16[256,512]{1,0:T(8,128)(2,1)} %get-tuple-element.155), channel_id=1, source_target_pairs={{0,2},{1,3},{2,0},{3,1},{4,6},{5,7},{6,4},{7,5},{8,10},{9,11},{10,... | collective-permute-start | bytes 786440 | tf_op jit(solution)/shard_map/ppermute | solution.py:424
  65.4 9.6 %collective-permute-start.17 = (bf16[256,512]{1,0:T(8,128)(2,1)}, bf16[256,512]{1,0:T(8,128)(2,1)}, u32[]{:S(2)}, u32[]{:S(2)}) collective-permute-start(bf16[256,512]{1,0:T(8,128)(2,1)} %get-tuple-element.156), channel_id=1, source_target_pairs={{0,4},{1,5},{2,6},{3,7},{4,0},{5,1},{6,2},{7,3},{8,12},{9,13},{10,... | collective-permute-start | bytes 786440 | tf_op jit(solution)/shard_map/ppermute | solution.py:424
  66.9 13.8 %collective-permute-start.18 = (bf16[256,512]{1,0:T(8,128)(2,1)}, bf16[256,512]{1,0:T(8,128)(2,1)}, u32[]{:S(2)}, u32[]{:S(2)}) collective-permute-start(bf16[256,512]{1,0:T(8,128)(2,1)} %get-tuple-element.161), channel_id=1, source_target_pairs={{0,2},{1,3},{2,0},{3,1},{4,6},{5,7},{6,4},{7,5},{8,10},{9,11},{10,... | collective-permute-start | bytes 786440 | tf_op jit(solution)/shard_map/ppermute | solution.py:424
  67.2 13.5 %collective-permute-start.19 = (bf16[256,512]{1,0:T(8,128)(2,1)}, bf16[256,512]{1,0:T(8,128)(2,1)}, u32[]{:S(2)}, u32[]{:S(2)}) collective-permute-start(bf16[256,512]{1,0:T(8,128)(2,1)} %get-tuple-element.162), channel_id=1, source_target_pairs={{0,4},{1,5},{2,6},{3,7},{4,0},{5,1},{6,2},{7,3},{8,12},{9,13},{10,... | collective-permute-start | bytes 786440 | tf_op jit(solution)/shard_map/ppermute | solution.py:424
  67.7 30.9 %copy-start.3 = (bf16[512,768]{1,0:T(8,128)(2,1)S(1)}, bf16[512,768]{1,0:T(8,128)(2,1)}, u32[]{:S(2)}) copy-start(bf16[512,768]{1,0:T(8,128)(2,1)} %refs_0_) | copy-start | bytes 2359300
  67.7 30.9 %copy-start.5 = (bf16[512,768]{1,0:T(8,128)(2,1)S(1)}, bf16[512,768]{1,0:T(8,128)(2,1)}, u32[]{:S(2)}) copy-start(bf16[512,768]{1,0:T(8,128)(2,1)} %copy-done.4) | copy-start | bytes 2359300
  67.7 30.9 %copy-start.7 = (bf16[512,768]{1,0:T(8,128)(2,1)S(1)}, bf16[512,768]{1,0:T(8,128)(2,1)}, u32[]{:S(2)}) copy-start(bf16[512,768]{1,0:T(8,128)(2,1)} %copy-done.6) | copy-start | bytes 2359300
  67.7 30.9 %copy-start.9 = (bf16[512,768]{1,0:T(8,128)(2,1)S(1)}, bf16[512,768]{1,0:T(8,128)(2,1)}, u32[]{:S(2)}) copy-start(bf16[512,768]{1,0:T(8,128)(2,1)} %copy-done.8) | copy-start | bytes 2359300
  76.3 9.5 %collective-permute-start.22 = (bf16[128,512]{1,0:T(8,128)(2,1)S(1)}, bf16[128,512]{1,0:T(8,128)(2,1)S(1)}, u32[]{:S(2)}, u32[]{:S(2)}) collective-permute-start(bf16[128,512]{1,0:T(8,128)(2,1)S(1)} %get-tuple-element.165), channel_id=1, source_target_pairs={{0,8},{8,0},{16,24},{24,16},{1,9},{9,1},{17,25},{25,17},{2,10},{10... | collective-permute-start | bytes 393224 | tf_op jit(solution)/shard_map/ppermute | solution.py:424
  77.9 7.8 %collective-permute-start.23 = (bf16[128,512]{1,0:T(8,128)(2,1)S(1)}, bf16[128,512]{1,0:T(8,128)(2,1)S(1)}, u32[]{:S(2)}, u32[]{:S(2)}) collective-permute-start(bf16[128,512]{1,0:T(8,128)(2,1)S(1)} %get-tuple-element.166), channel_id=1, source_target_pairs={{0,16},{8,24},{16,0},{24,8},{1,17},{9,25},{17,1},{25,9},{2,18},{10... | collective-permute-start | bytes 393224 | tf_op jit(solution)/shard_map/ppermute | solution.py:424
  80.5 6.9 %collective-permute-start.24 = (bf16[128,512]{1,0:T(8,128)(2,1)S(1)}, bf16[128,512]{1,0:T(8,128)(2,1)S(1)}, u32[]{:S(2)}, u32[]{:S(2)}) collective-permute-start(bf16[128,512]{1,0:T(8,128)(2,1)S(1)} %get-tuple-element.167), channel_id=1, source_target_pairs={{0,24},{8,16},{16,8},{24,0},{1,25},{9,17},{17,9},{25,1},{2,26},{10... | collective-permute-start | bytes 393224 | tf_op jit(solution)/shard_map/ppermute | solution.py:424
  80.7 1.0 copy-start.13
  81.8 0.9 copy-start.16
  83.9 6.4 %collective-permute-start.20 = (bf16[128,512]{1,0:T(8,128)(2,1)S(1)}, bf16[128,512]{1,0:T(8,128)(2,1)S(1)}, u32[]{:S(2)}, u32[]{:S(2)}) collective-permute-start(bf16[128,512]{1,0:T(8,128)(2,1)S(1)} %get-tuple-element.163), channel_id=1, source_target_pairs={{0,2},{1,3},{2,0},{3,1},{4,6},{5,7},{6,4},{7,5},{8,10},{9,11},{10,... | collective-permute-start | bytes 393224 | tf_op jit(solution)/shard_map/ppermute | solution.py:424
  84.2 6.3 %collective-permute-start.21 = (bf16[128,512]{1,0:T(8,128)(2,1)S(1)}, bf16[128,512]{1,0:T(8,128)(2,1)S(1)}, u32[]{:S(2)}, u32[]{:S(2)}) collective-permute-start(bf16[128,512]{1,0:T(8,128)(2,1)S(1)} %get-tuple-element.164), channel_id=1, source_target_pairs={{0,4},{1,5},{2,6},{3,7},{4,0},{5,1},{6,2},{7,3},{8,12},{9,13},{10,... | collective-permute-start | bytes 393224 | tf_op jit(solution)/shard_map/ppermute | solution.py:424
  90.7 13.7 %collective-permute-start.29 = (bf16[256,768]{1,0:T(8,128)(2,1)S(1)}, bf16[256,768]{1,0:T(8,128)(2,1)S(1)}, u32[]{:S(2)}, u32[]{:S(2)}) collective-permute-start(bf16[256,768]{1,0:T(8,128)(2,1)S(1)} %slice.7), channel_id=1, source_target_pairs={{0,2},{1,3},{2,0},{3,1},{4,6},{5,7},{6,4},{7,5},{8,10},{9,11},{10,... | collective-permute-start | bytes 1179656 | tf_op jit(solution)/shard_map/ppermute | solution.py:424
  92.7 11.8 %collective-permute-start.28 = (bf16[256,768]{1,0:T(8,128)(2,1)S(1)}, bf16[256,768]{1,0:T(8,128)(2,1)S(1)}, u32[]{:S(2)}, u32[]{:S(2)}) collective-permute-start(bf16[256,768]{1,0:T(8,128)(2,1)S(1)} %slice.6), channel_id=1, source_target_pairs={{0,4},{1,5},{2,6},{3,7},{4,0},{5,1},{6,2},{7,3},{8,12},{9,13},{10,... | collective-permute-start | bytes 1179656 | tf_op jit(solution)/shard_map/ppermute | solution.py:424
  94.2 9.9 %collective-permute-start.25 = (bf16[64,512]{1,0:T(8,128)(2,1)S(1)}, bf16[64,512]{1,0:T(8,128)(2,1)S(1)}, u32[]{:S(2)}, u32[]{:S(2)}) collective-permute-start(bf16[64,512]{1,0:T(8,128)(2,1)S(1)} %get-tuple-element.179), channel_id=1, source_target_pairs={{0,8},{8,0},{16,24},{24,16},{1,9},{9,1},{17,25},{25,17},{2,10},{10... | collective-permute-start | bytes 196616 | tf_op jit(solution)/shard_map/ppermute | solution.py:424
  94.8 9.2 %collective-permute-start.26 = (bf16[64,512]{1,0:T(8,128)(2,1)S(1)}, bf16[64,512]{1,0:T(8,128)(2,1)S(1)}, u32[]{:S(2)}, u32[]{:S(2)}) collective-permute-start(bf16[64,512]{1,0:T(8,128)(2,1)S(1)} %get-tuple-element.180), channel_id=1, source_target_pairs={{0,16},{8,24},{16,0},{24,8},{1,17},{9,25},{17,1},{25,9},{2,18},{10... | collective-permute-start | bytes 196616 | tf_op jit(solution)/shard_map/ppermute | solution.py:424
  98.3 6.1 %collective-permute-start.27 = (bf16[64,512]{1,0:T(8,128)(2,1)S(1)}, bf16[64,512]{1,0:T(8,128)(2,1)S(1)}, u32[]{:S(2)}, u32[]{:S(2)}) collective-permute-start(bf16[64,512]{1,0:T(8,128)(2,1)S(1)} %get-tuple-element.181), channel_id=1, source_target_pairs={{0,24},{8,16},{16,8},{24,0},{1,25},{9,17},{17,9},{25,1},{2,26},{10... | collective-permute-start | bytes 196616 | tf_op jit(solution)/shard_map/ppermute | solution.py:424
  104.5 4.7 %collective-permute-start.33 = (bf16[512,768]{1,0:T(8,128)(2,1)S(1)}, bf16[512,768]{1,0:T(8,128)(2,1)S(1)}, u32[]{:S(2)}, u32[]{:S(2)}) collective-permute-start(bf16[512,768]{1,0:T(8,128)(2,1)S(1)} %constant_dynamic-update-slice_fusion.refs_0_), channel_id=1, source_target_pairs={{0,1},{1,0},{2,3},{3,2},{4,5},{5,4},{6,7},{7,6},{8,9},{9,8},{10,11... | collective-permute-start | bytes 2359304 | tf_op jit(solution)/shard_map/ppermute | solution.py:424
  104.7 9.7 %collective-permute-start.32 = (bf16[192,512]{1,0:T(8,128)(2,1)S(1)}, bf16[192,512]{1,0:T(8,128)(2,1)S(1)}, u32[]{:S(2)}, u32[]{:S(2)}) collective-permute-start(bf16[192,512]{1,0:T(8,128)(2,1)S(1)} %added.1.refs_0_), channel_id=1, source_target_pairs={{0,24},{8,16},{16,8},{24,0},{1,25},{9,17},{17,9},{25,1},{2,26},{10... | collective-permute-start | bytes 589832 | tf_op jit(solution)/shard_map/ppermute | solution.py:424
  108.0 16.1 %collective-permute-start.31 = (bf16[192,512]{1,0:T(8,128)(2,1)S(1)}, bf16[192,512]{1,0:T(8,128)(2,1)S(1)}, u32[]{:S(2)}, u32[]{:S(2)}) collective-permute-start(bf16[192,512]{1,0:T(8,128)(2,1)S(1)} %added.1.refs_0_), channel_id=1, source_target_pairs={{0,16},{8,24},{16,0},{24,8},{1,17},{9,25},{17,1},{25,9},{2,18},{10... | collective-permute-start | bytes 589832 | tf_op jit(solution)/shard_map/ppermute | solution.py:424
  108.0 16.1 %collective-permute-start.30 = (bf16[192,512]{1,0:T(8,128)(2,1)S(1)}, bf16[192,512]{1,0:T(8,128)(2,1)S(1)}, u32[]{:S(2)}, u32[]{:S(2)}) collective-permute-start(bf16[192,512]{1,0:T(8,128)(2,1)S(1)} %added.1.refs_0_), channel_id=1, source_target_pairs={{0,8},{8,0},{16,24},{24,16},{1,9},{9,1},{17,25},{25,17},{2,10},{10... | collective-permute-start | bytes 589832 | tf_op jit(solution)/shard_map/ppermute | solution.py:424

commit v8 on v7

--- a/solution.py
+++ b/solution.py
@@ -14,7 +14,7 @@
 Q_STEP = 256
 
 
-SMALL_VMEM = 4 * 2**20
+SMALL_VMEM = 2 * 2**20
 VMEM = pl.BlockSpec(memory_space=pltpu.VMEM)
 
 
@@ -147,7 +147,7 @@
             pltpu.VMEM((4 * rows, wide), jnp.float32),
             pltpu.VMEM((4 * rows, both), jnp.float32),
         ],
-        compiler_params=pltpu.CompilerParams(vmem_limit_bytes=30 * 2**20),
+        compiler_params=pltpu.CompilerParams(vmem_limit_bytes=28 * 2**20),
         cost_estimate=pl.CostEstimate(flops=12 * 10**9, bytes_accessed=6 * 2**20, transcendentals=4 * 2**20),
     )(info, q, g, own, d2, r, x)
 
@@ -217,7 +217,7 @@
             in_specs=[VMEM] * 2 + [strip] * 2,
             out_specs=[VMEM] * 4,
         ),
-        compiler_params=pltpu.CompilerParams(vmem_limit_bytes=12 * 2**20),
+        compiler_params=pltpu.CompilerParams(vmem_limit_bytes=9 * 2**20),
         cost_estimate=pl.CostEstimate(
             flops=4 * cols * rows * block * chips, bytes_accessed=8 * 2**20, transcendentals=0
         ),

time: 126 us -> 126 us (level)
  no operation moved by 1% of the time
where the time goes in v8:
time: 126 us
  waiting for transfers between devices  47 us (37%)
  starting transfers between devices  41.9 us (33%)
  Pallas kernels  28.9 us (23%)
  local copies, waits for them, and re-layouts  6.21 us (5%)
    ppermute x30, waiting for transfers between devices, flipped(): lax.ppermute(array, axis, [(i, i ^ bits) for i in range(lax.axis_size(axi...  39.9 us
    ppermute x30, starting transfers between devices, flipped(): lax.ppermute(array, axis, [(i, i ^ bits) for i in range(lax.axis_size(axi...  32.3 us
    pallas_call x2, Pallas kernels, input_grad(): pl.pallas_call(functools.partial(input_kernel, count=count), name='input_...  8.05 us
    pallas_call x2, Pallas kernels, weight_partials(): pl.pallas_call(weight_kernel, name='weight_partials', out_shape=[jax.Shap...  7.79 us
    pallas_call x1, Pallas kernels, attention(): pl.pallas_call(attention_kernel, name='attention', out_shape=(jax.ShapeDt...  6.4 us
    unnamed x35, local copies, waits for them, and re-layouts  6.04 us
    ppermute x1, starting transfers between devices, per_device(): d2 = lax.ppermute(own, 'ctx', by_two)  4.86 us
    ppermute x1, waiting for transfers between devices, per_device(): from_two = lax.ppermute(kv_d2, 'ctx', back(by_two))  4.27 us
  transfers between devices with their start and end apart: 34, of which 16 were waited for; matrix products, arithmetic and copies ran while one was open for 1% of the time, Pallas kernels for 21%

profile of v8, /device:TPU:0, one launch (start us, length us, event | category | flops | bytes accessed | tf_op | source)
XLA Modules:
  0.0 125.6 jit_solution(11408845204627606134)
XLA Ops:
  0.6 0.5 collective-permute-start.2
  1.1 2.0 %collective-permute-start.1 = (bf16[512,256]{1,0:T(8,128)(2,1)}, bf16[512,256]{1,0:T(8,128)(2,1)S(1)}, u32[]{:S(2)}, u32[]{:S(2)}) collective-permute-start(bf16[512,256]{1,0:T(8,128)(2,1)} %bitcast.19), channel_id=1, source_target_pairs={{0,1},{2,3},{4,5},{6,7},{3,6},{8,9},{10,11},{12,13},{14,15},{11,14... | collective-permute-start | bytes 786440 | tf_op jit(solution)/shard_map/ppermute | solution.py:454
  3.1 4.9 %collective-permute-start = (bf16[512,256]{1,0:T(8,128)(2,1)}, bf16[512,256]{1,0:T(8,128)(2,1)S(1)}, u32[]{:S(2)}, u32[]{:S(2)}) collective-permute-start(bf16[512,256]{1,0:T(8,128)(2,1)} %bitcast.20), channel_id=1, source_target_pairs={{0,2},{1,3},{3,5},{4,6},{5,7},{8,10},{9,11},{11,13},{12,14},{13,15... | collective-permute-start | bytes 786440 | tf_op jit(solution)/shard_map/ppermute | solution.py:453
  8.0 0.1 stack.11.places
  8.1 1.0 copy-done.10
  9.1 1.0 copy-done.11
  10.2 0.9 copy-done.14
  11.1 0.2 staged.1
  11.3 0.7 pad_add_fusion.info_ref
  12.0 2.8 %collective-permute-done.d2_ref = bf16[512,256]{1,0:T(8,128)(2,1)S(1)} collective-permute-done((bf16[512,256]{1,0:T(8,128)(2,1)}, bf16[512,256]{1,0:T(8,128)(2,1)S(1)}, u32[]{:S(2)}, u32[]{:S(2)}) %collective-permute-start) | collective-permute-done | bytes 262176 | tf_op jit(solution)/shard_map/ppermute | solution.py:453
  14.8 0.9 copy-done.4
  15.7 0.3 collective-permute-start.3
  16.0 1.2 collective-permute-done.3.r_ref
  17.2 0.3 collective-permute-start.4
  17.5 2.3 %collective-permute-start.7 = (bf16[512,768]{1,0:T(8,128)(2,1)}, bf16[512,768]{1,0:T(8,128)(2,1)S(1)}, u32[]{:S(2)}, u32[]{:S(2)}) collective-permute-start(bf16[512,768]{1,0:T(8,128)(2,1)} %refs_0_), channel_id=1, source_target_pairs={{0,2},{1,3},{2,0},{3,1},{4,6},{5,7},{6,4},{7,5},{8,10},{9,11},{10,... | collective-permute-start | bytes 2359304 | tf_op jit(solution)/shard_map/ppermute | solution.py:424
  19.8 6.4 %attention.1 = (bf16[512,512]{1,0:T(8,128)(2,1)}, bf16[512,512]{1,0:T(8,128)(2,1)S(1)}, f32[512,256]{1,0:T(8,128)S(1)}, f32[512,256]{1,0:T(8,128)S(1)}, f32[512,...) custom-call(s32[17]{0:T(128)S(1)} %pad_add_fusion.info_ref, bf16[512,512]{1,0:T(8,128)(2,1)S(1)} %get-tuple-element.106.q_ref, ...), custom_call_target="tpu_custom_call" | custom-call | flops 12000000000 | bytes 6291456 | tf_op jit(solution)/shard_map/attention/pallas_call | solution.py:130
  26.2 4.1 %collective-permute-start.6 = (f32[512,256]{1,0:T(8,128)S(1)}, f32[512,256]{1,0:T(8,128)S(1)}, u32[]{:S(2)}, u32[]{:S(2)}) collective-permute-start(f32[512,256]{1,0:T(8,128)S(1)} %get-tuple-element.123), channel_id=1, source_target_pairs={{0,1},{1,0},{2,3},{3,2},{4,5},{5,4},{6,7},{7,6},{8,9},{9,8},{10,11... | collective-permute-start | bytes 1572872 | tf_op jit(solution)/shard_map/ppermute | solution.py:424
  30.3 1.3 %collective-permute-start.10 = (bf16[512,256]{1,0:T(8,128)(2,1)S(1)}, bf16[512,256]{1,0:T(8,128)(2,1)S(1)}, u32[]{:S(2)}, u32[]{:S(2)}) collective-permute-start(bf16[512,256]{1,0:T(8,128)(2,1)S(1)} %get-tuple-element.126), channel_id=1, source_target_pairs={{1,0},{3,2},{5,4},{7,6},{6,3},{9,8},{11,10},{13,12},{15,14},{14,11... | collective-permute-start | bytes 786440 | tf_op jit(solution)/shard_map/ppermute | solution.py:473
  31.6 0.2 collective-permute-done.6
  31.9 5.5 %collective-permute-done.8.refs_4_ = bf16[512,768]{1,0:T(8,128)(2,1)S(1)} collective-permute-done((bf16[512,768]{1,0:T(8,128)(2,1)}, bf16[512,768]{1,0:T(8,128)(2,1)S(1)}, u32[]{:S(2)}, u32[]{:S(2)}) %collective-permute-start.8) | collective-permute-done | bytes 786464 | tf_op jit(solution)/shard_map/ppermute | solution.py:424
  37.4 0.7 collective-permute-done.7.refs_2_
  38.1 1.5 %collective-permute-start.9 = (bf16[512,256]{1,0:T(8,128)(2,1)S(1)}, bf16[512,256]{1,0:T(8,128)(2,1)S(1)}, u32[]{:S(2)}, u32[]{:S(2)}) collective-permute-start(bf16[512,256]{1,0:T(8,128)(2,1)S(1)} %add_convert_fusion), channel_id=1, source_target_pairs={{2,0},{3,1},{5,3},{6,4},{7,5},{10,8},{11,9},{13,11},{14,12},{15,13... | collective-permute-start | bytes 786440 | tf_op jit(solution)/shard_map/ppermute | solution.py:482
  39.5 4.1 %weight_partials.2 = (f32[512,512]{1,0:T(8,128)S(1)}, bf16[512,512]{1,0:T(8,128)(2,1)S(1)}, bf16[512,512]{1,0:T(8,128)(2,1)S(1)}, bf16[512,512]{1,0:T(8,128)(2,1)S(1)}) custom-call(s32[6]{0:T(128)S(1)} %stack.11.places, bf16[512,512]{1,0:T(8,128)(2,1)S(1)} %get-tuple-element.121.gt_ref, bf16[512,512]{1,0:T(8,128)(2,1)S(1)} %collective-permute-done.5.gt_other, ...), custom_call_target="tpu_custom_call" | custom-call | flops 2147483648 | bytes 8388608 | tf_op jit(solution)/shard_map/weight_partials/pallas_call | solution.py:209
  43.7 4.3 %collective-permute-done.9.two_ref = bf16[512,256]{1,0:T(8,128)(2,1)S(1)} collective-permute-done((bf16[512,256]{1,0:T(8,128)(2,1)S(1)}, bf16[512,256]{1,0:T(8,128)(2,1)S(1)}, u32[]{:S(2)}, u32[]{:S(2)}) %collective-permute-start.9) | collective-permute-done | bytes 262176 | tf_op jit(solution)/shard_map/ppermute | solution.py:482
  47.9 0.5 collective-permute-start.15
  48.4 1.5 %collective-permute-start.12 = (bf16[512,512]{1,0:T(8,128)(2,1)S(1)}, bf16[512,512]{1,0:T(8,128)(2,1)S(1)}, u32[]{:S(2)}, u32[]{:S(2)}) collective-permute-start(bf16[512,512]{1,0:T(8,128)(2,1)S(1)} %get-tuple-element.140), channel_id=1, source_target_pairs={{0,4},{1,5},{2,6},{3,7},{4,0},{5,1},{6,2},{7,3},{8,12},{9,13},{10,... | collective-permute-start | bytes 1572872 | tf_op jit(solution)/shard_map/ppermute | solution.py:424
  50.0 1.1 finish_kv.1
  51.0 1.5 %collective-permute-done.13.gt_other = bf16[256,512]{1,0:T(8,128)(2,1)S(1)} collective-permute-done((bf16[256,512]{1,0:T(8,128)(2,1)S(1)}, bf16[256,512]{1,0:T(8,128)(2,1)S(1)}, u32[]{:S(2)}, u32[]{:S(2)}) %collective-permute-start.13) | collective-permute-done | bytes 262176 | tf_op jit(solution)/shard_map/ppermute | solution.py:424
  52.6 3.7 %weight_partials.3 = (f32[256,512]{1,0:T(8,128)S(1)}, bf16[256,512]{1,0:T(8,128)(2,1)S(1)}, bf16[256,512]{1,0:T(8,128)(2,1)}, bf16[256,512]{1,0:T(8,128)(2,1)}) custom-call(s32[6]{0:T(128)S(1)} %stack.11.places, bf16[256,512]{1,0:T(8,128)(2,1)S(1)} %get-tuple-element.141.gt_ref, bf16[256,512]{1,0:T(8,128)(2,1)S(1)} %collective-permute-done.13.gt_other, ...), custom_call_target="tpu_custom_call" | custom-call | flops 1073741824 | bytes 8388608 | tf_op jit(solution)/shard_map/weight_partials/pallas_call | solution.py:209
  56.3 6.0 %collective-permute-done.11.from_x = bf16[512,512]{1,0:T(8,128)(2,1)S(1)} collective-permute-done((bf16[512,512]{1,0:T(8,128)(2,1)S(1)}, bf16[512,512]{1,0:T(8,128)(2,1)S(1)}, u32[]{:S(2)}, u32[]{:S(2)}) %collective-permute-start.11) | collective-permute-done | bytes 524320 | tf_op jit(solution)/shard_map/ppermute | solution.py:424
  62.3 1.2 middle.2
  63.6 1.7 %collective-permute-start.16 = (bf16[256,512]{1,0:T(8,128)(2,1)}, bf16[256,512]{1,0:T(8,128)(2,1)}, u32[]{:S(2)}, u32[]{:S(2)}) collective-permute-start(bf16[256,512]{1,0:T(8,128)(2,1)} %get-tuple-element.155), channel_id=1, source_target_pairs={{0,2},{1,3},{2,0},{3,1},{4,6},{5,7},{6,4},{7,5},{8,10},{9,11},{10,... | collective-permute-start | bytes 786440 | tf_op jit(solution)/shard_map/ppermute | solution.py:424
  65.4 1.5 %collective-permute-start.17 = (bf16[256,512]{1,0:T(8,128)(2,1)}, bf16[256,512]{1,0:T(8,128)(2,1)}, u32[]{:S(2)}, u32[]{:S(2)}) collective-permute-start(bf16[256,512]{1,0:T(8,128)(2,1)} %get-tuple-element.156), channel_id=1, source_target_pairs={{0,4},{1,5},{2,6},{3,7},{4,0},{5,1},{6,2},{7,3},{8,12},{9,13},{10,... | collective-permute-start | bytes 786440 | tf_op jit(solution)/shard_map/ppermute | solution.py:424
  66.9 0.3 collective-permute-start.18
  67.2 0.5 collective-permute-start.19
  67.7 5.5 %collective-permute-done.16.x_ref = bf16[256,512]{1,0:T(8,128)(2,1)} collective-permute-done((bf16[256,512]{1,0:T(8,128)(2,1)}, bf16[256,512]{1,0:T(8,128)(2,1)}, u32[]{:S(2)}, u32[]{:S(2)}) %collective-permute-start.16) | collective-permute-done | bytes 262176 | tf_op jit(solution)/shard_map/ppermute | solution.py:424
  73.2 1.7 %collective-permute-done.17.y_ref = bf16[256,512]{1,0:T(8,128)(2,1)} collective-permute-done((bf16[256,512]{1,0:T(8,128)(2,1)}, bf16[256,512]{1,0:T(8,128)(2,1)}, u32[]{:S(2)}, u32[]{:S(2)}) %collective-permute-start.17) | collective-permute-done | bytes 262176 | tf_op jit(solution)/shard_map/ppermute | solution.py:424
  74.9 1.3 %quarters.2 = (f32[128,512]{1,0:T(8,128)S(1)}, bf16[128,512]{1,0:T(8,128)(2,1)S(1)}, bf16[128,512]{1,0:T(8,128)(2,1)S(1)}, bf16[128,512]{1,0:T(8,128)(2,1)S(1)}) custom-call(s32[1]{0:T(128)} %bitcast.10.z_ref, f32[512,512]{1,0:T(8,128)S(1)} %get-tuple-element.154.own_ref, bf16[256,512]{1,0:T(8,128)(2,1)} %collective-permute-done.16.x_ref, ...), custom_call_target="tpu_custom_call" | custom-call | flops 1048576 | bytes 2097152 | tf_op jit(solution)/shard_map/quarters/pallas_call | solution.py:350
  76.3 1.6 %collective-permute-start.22 = (bf16[128,512]{1,0:T(8,128)(2,1)S(1)}, bf16[128,512]{1,0:T(8,128)(2,1)S(1)}, u32[]{:S(2)}, u32[]{:S(2)}) collective-permute-start(bf16[128,512]{1,0:T(8,128)(2,1)S(1)} %get-tuple-element.165), channel_id=1, source_target_pairs={{0,8},{8,0},{16,24},{24,16},{1,9},{9,1},{17,25},{25,17},{2,10},{10... | collective-permute-start | bytes 393224 | tf_op jit(solution)/shard_map/ppermute | solution.py:424
  77.9 2.6 %collective-permute-start.23 = (bf16[128,512]{1,0:T(8,128)(2,1)S(1)}, bf16[128,512]{1,0:T(8,128)(2,1)S(1)}, u32[]{:S(2)}, u32[]{:S(2)}) collective-permute-start(bf16[128,512]{1,0:T(8,128)(2,1)S(1)} %get-tuple-element.166), channel_id=1, source_target_pairs={{0,16},{8,24},{16,0},{24,8},{1,17},{9,25},{17,1},{25,9},{2,18},{10... | collective-permute-start | bytes 393224 | tf_op jit(solution)/shard_map/ppermute | solution.py:424
  80.5 0.2 collective-permute-start.24
  80.7 1.0 copy-done.13
  81.8 0.9 copy-done.16
  82.7 1.1 middle.3
  83.9 0.3 collective-permute-start.20
  84.2 1.5 %collective-permute-start.21 = (bf16[128,512]{1,0:T(8,128)(2,1)S(1)}, bf16[128,512]{1,0:T(8,128)(2,1)S(1)}, u32[]{:S(2)}, u32[]{:S(2)}) collective-permute-start(bf16[128,512]{1,0:T(8,128)(2,1)S(1)} %get-tuple-element.164), channel_id=1, source_target_pairs={{0,4},{1,5},{2,6},{3,7},{4,0},{5,1},{6,2},{7,3},{8,12},{9,13},{10,... | collective-permute-start | bytes 393224 | tf_op jit(solution)/shard_map/ppermute | solution.py:424
  85.8 1.6 %collective-permute-done.24.refs_3_ = bf16[128,512]{1,0:T(8,128)(2,1)S(1)} collective-permute-done((bf16[128,512]{1,0:T(8,128)(2,1)S(1)}, bf16[128,512]{1,0:T(8,128)(2,1)S(1)}, u32[]{:S(2)}, u32[]{:S(2)}) %collective-permute-start.24) | collective-permute-done | bytes 131104 | tf_op jit(solution)/shard_map/ppermute | solution.py:424
  87.4 2.9 %collective-permute-done.20.x_ref = bf16[128,512]{1,0:T(8,128)(2,1)S(1)} collective-permute-done((bf16[128,512]{1,0:T(8,128)(2,1)S(1)}, bf16[128,512]{1,0:T(8,128)(2,1)S(1)}, u32[]{:S(2)}, u32[]{:S(2)}) %collective-permute-start.20) | collective-permute-done | bytes 131104 | tf_op jit(solution)/shard_map/ppermute | solution.py:424
  90.3 0.2 collective-permute-done.21.y_ref
  90.5 0.1 quarters.3
  90.7 1.9 %collective-permute-start.29 = (bf16[256,768]{1,0:T(8,128)(2,1)S(1)}, bf16[256,768]{1,0:T(8,128)(2,1)S(1)}, u32[]{:S(2)}, u32[]{:S(2)}) collective-permute-start(bf16[256,768]{1,0:T(8,128)(2,1)S(1)} %slice.7), channel_id=1, source_target_pairs={{0,2},{1,3},{2,0},{3,1},{4,6},{5,7},{6,4},{7,5},{8,10},{9,11},{10,... | collective-permute-start | bytes 1179656 | tf_op jit(solution)/shard_map/ppermute | solution.py:424
  92.7 1.5 %collective-permute-start.28 = (bf16[256,768]{1,0:T(8,128)(2,1)S(1)}, bf16[256,768]{1,0:T(8,128)(2,1)S(1)}, u32[]{:S(2)}, u32[]{:S(2)}) collective-permute-start(bf16[256,768]{1,0:T(8,128)(2,1)S(1)} %slice.6), channel_id=1, source_target_pairs={{0,4},{1,5},{2,6},{3,7},{4,0},{5,1},{6,2},{7,3},{8,12},{9,13},{10,... | collective-permute-start | bytes 1179656 | tf_op jit(solution)/shard_map/ppermute | solution.py:424
  94.2 0.6 collective-permute-start.25
  94.8 3.5 %collective-permute-start.26 = (bf16[64,512]{1,0:T(8,128)(2,1)S(1)}, bf16[64,512]{1,0:T(8,128)(2,1)S(1)}, u32[]{:S(2)}, u32[]{:S(2)}) collective-permute-start(bf16[64,512]{1,0:T(8,128)(2,1)S(1)} %get-tuple-element.180), channel_id=1, source_target_pairs={{0,16},{8,24},{16,0},{24,8},{1,17},{9,25},{17,1},{25,9},{2,18},{10... | collective-permute-start | bytes 196616 | tf_op jit(solution)/shard_map/ppermute | solution.py:424
  98.3 0.2 collective-permute-start.27
  98.6 5.5 %input_grad.2.refs_2_ = bf16[512,4096]{1,0:T(8,128)(2,1)} custom-call(s32[6]{0:T(128)S(1)} %stack.11.places, bf16[512,512]{1,0:T(8,128)(2,1)S(1)} %copy-done.1, bf16[512,256]{1,0:T(8,128)(2,1)S(1)} %copy-done.2, bf16[512,768]{1,0:T(8,128)(2,1)S(1)} %copy-done.3, bf16[512,768]{1,0:T(8,128)(2,1)S(1)} %copy-done.5, ...), custom_call_target="tpu_custom_call" | custom-call | flops 2415919104 | bytes 11534336 | tf_op jit(solution)/shard_map/input_grad/pallas_call | solution.py:283
  104.1 0.3 collective-permute-done.27.refs_7_
  104.6 0.1 added.1.refs_0_
  104.7 3.3 %collective-permute-start.32 = (bf16[192,512]{1,0:T(8,128)(2,1)S(1)}, bf16[192,512]{1,0:T(8,128)(2,1)S(1)}, u32[]{:S(2)}, u32[]{:S(2)}) collective-permute-start(bf16[192,512]{1,0:T(8,128)(2,1)S(1)} %added.1.refs_0_), channel_id=1, source_target_pairs={{0,24},{8,16},{16,8},{24,0},{1,25},{9,17},{17,9},{25,1},{2,26},{10... | collective-permute-start | bytes 589832 | tf_op jit(solution)/shard_map/ppermute | solution.py:424
  108.0 1.1 collective-permute-start.30
  109.2 2.6 %input_grad.3 = bf16[512,4096]{1,0:T(8,128)(2,1)} custom-call(s32[6]{0:T(128)S(1)} %stack.11.places, bf16[512,512]{1,0:T(8,128)(2,1)S(1)} %copy-done.1, bf16[512,256]{1,0:T(8,128)(2,1)S(1)} %copy-done.2, bf16[512,768]{1,0:T(8,128)(2,1)S(1)} %constant_dynamic-update-slice_fusion.refs_0_, ...), custom_call_target="tpu_custom_call", output_to_operand_aliasing={{}: (5, {})} | custom-call | flops 805306368 | bytes 11534336 | tf_op jit(solution)/shard_map/input_grad/pallas_call | solution.py:283
  111.8 2.6 %collective-permute-done.32.refs_3_ = bf16[192,512]{1,0:T(8,128)(2,1)S(1)} collective-permute-done((bf16[192,512]{1,0:T(8,128)(2,1)S(1)}, bf16[192,512]{1,0:T(8,128)(2,1)S(1)}, u32[]{:S(2)}, u32[]{:S(2)}) %collective-permute-start.32) | collective-permute-done | bytes 196640 | tf_op jit(solution)/shard_map/ppermute | solution.py:424
  114.4 9.8 %collective-permute-done.31.refs_2_ = bf16[192,512]{1,0:T(8,128)(2,1)S(1)} collective-permute-done((bf16[192,512]{1,0:T(8,128)(2,1)S(1)}, bf16[192,512]{1,0:T(8,128)(2,1)S(1)}, u32[]{:S(2)}, u32[]{:S(2)}) %collective-permute-start.31) | collective-permute-done | bytes 196640 | tf_op jit(solution)/shard_map/ppermute | solution.py:424
  124.2 1.5 %joined.1 = bf16[512,768]{1,0:T(8,128)(2,1)} custom-call(s32[1]{0:T(128)} %bitcast.10.z_ref, bf16[192,512]{1,0:T(8,128)(2,1)S(1)} %added.1.refs_0_, bf16[192,512]{1,0:T(8,128)(2,1)S(1)} %collective-permute-done.30.refs_1_, bf16[192,512]{1,0:T(8,128)(2,1)S(1)} %collective-permute-done.31.refs_2_, bf16[192,512]{1,0:T(8,128)(2,1)S(1)} %collective-permute-done.32.refs_3_), custom_call_target="tpu_custom_call" | custom-call | flops 98304 | bytes 2097152 | tf_op jit(solution)/shard_map/joined/pallas_call | solution.py:411
  (58 shorter events, 0.4 us)
Async XLA Ops:
  0.6 14.2 %collective-permute-start.2 = (bf16[512,768]{1,0:T(8,128)(2,1)}, bf16[512,768]{1,0:T(8,128)(2,1)S(1)}, u32[]{:S(2)}, u32[]{:S(2)}) collective-permute-start(bf16[512,768]{1,0:T(8,128)(2,1)} %refs_0_), channel_id=1, source_target_pairs={{0,1},{1,0},{2,3},{3,2},{4,5},{5,4},{6,7},{7,6},{8,9},{9,8},{10,11... | collective-permute-start | bytes 2359304 | tf_op jit(solution)/shard_map/ppermute | solution.py:424
  1.1 10.9 %collective-permute-start.1 = (bf16[512,256]{1,0:T(8,128)(2,1)}, bf16[512,256]{1,0:T(8,128)(2,1)S(1)}, u32[]{:S(2)}, u32[]{:S(2)}) collective-permute-start(bf16[512,256]{1,0:T(8,128)(2,1)} %bitcast.19), channel_id=1, source_target_pairs={{0,1},{2,3},{4,5},{6,7},{3,6},{8,9},{10,11},{12,13},{14,15},{11,14... | collective-permute-start | bytes 786440 | tf_op jit(solution)/shard_map/ppermute | solution.py:454
  3.1 11.7 %collective-permute-start = (bf16[512,256]{1,0:T(8,128)(2,1)}, bf16[512,256]{1,0:T(8,128)(2,1)S(1)}, u32[]{:S(2)}, u32[]{:S(2)}) collective-permute-start(bf16[512,256]{1,0:T(8,128)(2,1)} %bitcast.20), channel_id=1, source_target_pairs={{0,2},{1,3},{3,5},{4,6},{5,7},{8,10},{9,11},{11,13},{12,14},{13,15... | collective-permute-start | bytes 786440 | tf_op jit(solution)/shard_map/ppermute | solution.py:453
  8.1 1.0 copy-start.10
  9.1 1.0 copy-start.11
  10.2 0.9 copy-start.14
  14.8 0.9 copy-start.4
  15.7 1.5 %collective-permute-start.3 = (bf16[512,256]{1,0:T(8,128)(2,1)S(1)}, bf16[512,256]{1,0:T(8,128)(2,1)S(1)}, u32[]{:S(2)}, u32[]{:S(2)}) collective-permute-start(bf16[512,256]{1,0:T(8,128)(2,1)S(1)} %collective-permute-done.d2_ref), channel_id=1, source_target_pairs={{0,1},{1,0},{2,3},{3,2},{4,5},{5,4},{6,7},{7,6},{8,9},{9,8},{10,11... | collective-permute-start | bytes 786440 | tf_op jit(solution)/shard_map/ppermute | solution.py:424
  17.2 22.3 %copy-start = (bf16[1,512,4096]{2,1,0:T(8,128)(2,1)S(1)}, bf16[1,512,4096]{2,1,0:T(8,128)(2,1)}, u32[]{:S(2)}) copy-start(bf16[1,512,4096]{2,1,0:T(8,128)(2,1)} %param.6) | copy-start | bytes 12582916
  17.2 9.0 %collective-permute-start.4 = (bf16[512,4096]{1,0:T(8,128)(2,1)}, bf16[512,4096]{1,0:T(8,128)(2,1)S(1)}, u32[]{:S(2)}, u32[]{:S(2)}) collective-permute-start(bf16[512,4096]{1,0:T(8,128)(2,1)} %bitcast.12), channel_id=1, source_target_pairs={{0,1},{1,0},{2,3},{3,2},{4,5},{5,4},{6,7},{7,6},{8,9},{9,8},{10,11... | collective-permute-start | bytes 12582920 | tf_op jit(solution)/shard_map/ppermute | solution.py:424
  17.5 19.9 %collective-permute-start.8 = (bf16[512,768]{1,0:T(8,128)(2,1)}, bf16[512,768]{1,0:T(8,128)(2,1)S(1)}, u32[]{:S(2)}, u32[]{:S(2)}) collective-permute-start(bf16[512,768]{1,0:T(8,128)(2,1)} %refs_0_), channel_id=1, source_target_pairs={{0,4},{1,5},{2,6},{3,7},{4,0},{5,1},{6,2},{7,3},{8,12},{9,13},{10,... | collective-permute-start | bytes 2359304 | tf_op jit(solution)/shard_map/ppermute | solution.py:424
  17.5 20.5 %collective-permute-start.7 = (bf16[512,768]{1,0:T(8,128)(2,1)}, bf16[512,768]{1,0:T(8,128)(2,1)S(1)}, u32[]{:S(2)}, u32[]{:S(2)}) collective-permute-start(bf16[512,768]{1,0:T(8,128)(2,1)} %refs_0_), channel_id=1, source_target_pairs={{0,2},{1,3},{2,0},{3,1},{4,6},{5,7},{6,4},{7,5},{8,10},{9,11},{10,... | collective-permute-start | bytes 2359304 | tf_op jit(solution)/shard_map/ppermute | solution.py:424
  26.2 5.6 %collective-permute-start.6 = (f32[512,256]{1,0:T(8,128)S(1)}, f32[512,256]{1,0:T(8,128)S(1)}, u32[]{:S(2)}, u32[]{:S(2)}) collective-permute-start(f32[512,256]{1,0:T(8,128)S(1)} %get-tuple-element.123), channel_id=1, source_target_pairs={{0,1},{1,0},{2,3},{3,2},{4,5},{5,4},{6,7},{7,6},{8,9},{9,8},{10,11... | collective-permute-start | bytes 1572872 | tf_op jit(solution)/shard_map/ppermute | solution.py:424
  30.3 7.8 %collective-permute-start.5 = (bf16[512,512]{1,0:T(8,128)(2,1)S(1)}, bf16[512,512]{1,0:T(8,128)(2,1)S(1)}, u32[]{:S(2)}, u32[]{:S(2)}) collective-permute-start(bf16[512,512]{1,0:T(8,128)(2,1)S(1)} %get-tuple-element.121.gt_ref), channel_id=1, source_target_pairs={{0,1},{1,0},{2,3},{3,2},{4,5},{5,4},{6,7},{7,6},{8,9},{9,8},{10,11... | collective-permute-start | bytes 1572872 | tf_op jit(solution)/shard_map/ppermute | solution.py:424
  30.3 13.3 %collective-permute-start.10 = (bf16[512,256]{1,0:T(8,128)(2,1)S(1)}, bf16[512,256]{1,0:T(8,128)(2,1)S(1)}, u32[]{:S(2)}, u32[]{:S(2)}) collective-permute-start(bf16[512,256]{1,0:T(8,128)(2,1)S(1)} %get-tuple-element.126), channel_id=1, source_target_pairs={{1,0},{3,2},{5,4},{7,6},{6,3},{9,8},{11,10},{13,12},{15,14},{14,11... | collective-permute-start | bytes 786440 | tf_op jit(solution)/shard_map/ppermute | solution.py:473
  38.1 9.9 %collective-permute-start.9 = (bf16[512,256]{1,0:T(8,128)(2,1)S(1)}, bf16[512,256]{1,0:T(8,128)(2,1)S(1)}, u32[]{:S(2)}, u32[]{:S(2)}) collective-permute-start(bf16[512,256]{1,0:T(8,128)(2,1)S(1)} %add_convert_fusion), channel_id=1, source_target_pairs={{2,0},{3,1},{5,3},{6,4},{7,5},{10,8},{11,9},{13,11},{14,12},{15,13... | collective-permute-start | bytes 786440 | tf_op jit(solution)/shard_map/ppermute | solution.py:482
  47.9 14.3 %collective-permute-start.14 = (bf16[512,768]{1,0:T(8,128)(2,1)S(1)}, bf16[512,768]{1,0:T(8,128)(2,1)S(1)}, u32[]{:S(2)}, u32[]{:S(2)}) collective-permute-start(bf16[512,768]{1,0:T(8,128)(2,1)S(1)} %collective-permute-done.7.refs_2_), channel_id=1, source_target_pairs={{0,1},{1,0},{2,3},{3,2},{4,5},{5,4},{6,7},{7,6},{8,9},{9,8},{10,11... | collective-permute-start | bytes 2359304 | tf_op jit(solution)/shard_map/ppermute | solution.py:424
  47.9 14.4 %collective-permute-start.15 = (bf16[512,768]{1,0:T(8,128)(2,1)S(1)}, bf16[512,768]{1,0:T(8,128)(2,1)S(1)}, u32[]{:S(2)}, u32[]{:S(2)}) collective-permute-start(bf16[512,768]{1,0:T(8,128)(2,1)S(1)} %collective-permute-done.8.refs_4_), channel_id=1, source_target_pairs={{0,1},{1,0},{2,3},{3,2},{4,5},{5,4},{6,7},{7,6},{8,9},{9,8},{10,11... | collective-permute-start | bytes 2359304 | tf_op jit(solution)/shard_map/ppermute | solution.py:424
  48.4 13.8 %collective-permute-start.11 = (bf16[512,512]{1,0:T(8,128)(2,1)S(1)}, bf16[512,512]{1,0:T(8,128)(2,1)S(1)}, u32[]{:S(2)}, u32[]{:S(2)}) collective-permute-start(bf16[512,512]{1,0:T(8,128)(2,1)S(1)} %get-tuple-element.139), channel_id=1, source_target_pairs={{0,2},{1,3},{2,0},{3,1},{4,6},{5,7},{6,4},{7,5},{8,10},{9,11},{10,... | collective-permute-start | bytes 1572872 | tf_op jit(solution)/shard_map/ppermute | solution.py:424
  48.4 13.8 %collective-permute-start.12 = (bf16[512,512]{1,0:T(8,128)(2,1)S(1)}, bf16[512,512]{1,0:T(8,128)(2,1)S(1)}, u32[]{:S(2)}, u32[]{:S(2)}) collective-permute-start(bf16[512,512]{1,0:T(8,128)(2,1)S(1)} %get-tuple-element.140), channel_id=1, source_target_pairs={{0,4},{1,5},{2,6},{3,7},{4,0},{5,1},{6,2},{7,3},{8,12},{9,13},{10,... | collective-permute-start | bytes 1572872 | tf_op jit(solution)/shard_map/ppermute | solution.py:424
  51.0 1.5 %collective-permute-start.13 = (bf16[256,512]{1,0:T(8,128)(2,1)S(1)}, bf16[256,512]{1,0:T(8,128)(2,1)S(1)}, u32[]{:S(2)}, u32[]{:S(2)}) collective-permute-start(bf16[256,512]{1,0:T(8,128)(2,1)S(1)} %get-tuple-element.141.gt_ref), channel_id=1, source_target_pairs={{0,1},{1,0},{2,3},{3,2},{4,5},{5,4},{6,7},{7,6},{8,9},{9,8},{10,11... | collective-permute-start | bytes 786440 | tf_op jit(solution)/shard_map/ppermute | solution.py:424
  56.3 9.1 %copy-start.12 = (f32[256,512]{1,0:T(8,128)}, f32[256,512]{1,0:T(8,128)S(1)}, u32[]{:S(2)}) copy-start(f32[256,512]{1,0:T(8,128)S(1)} %get-tuple-element.159.own_ref) | copy-start | bytes 1572868
  56.3 9.1 %copy-start.15 = (bf16[256,512]{1,0:T(8,128)(2,1)}, bf16[256,512]{1,0:T(8,128)(2,1)S(1)}, u32[]{:S(2)}) copy-start(bf16[256,512]{1,0:T(8,128)(2,1)S(1)} %get-tuple-element.160.keep_ref) | copy-start | bytes 786436
  56.3 42.3 %copy-start.1 = (bf16[512,512]{1,0:T(8,128)(2,1)S(1)}, bf16[512,512]{1,0:T(8,128)(2,1)}, u32[]{:S(2)}) copy-start(bf16[512,512]{1,0:T(8,128)(2,1)} %get-tuple-element.119.gq_ref) | copy-start | bytes 1572868
  56.3 42.3 %copy-start.2 = (bf16[512,256]{1,0:T(8,128)(2,1)S(1)}, bf16[512,256]{1,0:T(8,128)(2,1)}, u32[]{:S(2)}) copy-start(bf16[512,256]{1,0:T(8,128)(2,1)} %get-tuple-element.138.gkv_ref) | copy-start | bytes 786436
  62.3 1.3 %copy-start.6 = (bf16[512,768]{1,0:T(8,128)(2,1)}, bf16[512,768]{1,0:T(8,128)(2,1)S(1)}, u32[]{:S(2)}) copy-start(bf16[512,768]{1,0:T(8,128)(2,1)S(1)} %collective-permute-done.14.refs_3_) | copy-start | bytes 2359300
  62.3 1.3 %copy-start.8 = (bf16[512,768]{1,0:T(8,128)(2,1)}, bf16[512,768]{1,0:T(8,128)(2,1)S(1)}, u32[]{:S(2)}) copy-start(bf16[512,768]{1,0:T(8,128)(2,1)S(1)} %collective-permute-done.15.refs_5_) | copy-start | bytes 2359300
  63.6 9.6 %collective-permute-start.16 = (bf16[256,512]{1,0:T(8,128)(2,1)}, bf16[256,512]{1,0:T(8,128)(2,1)}, u32[]{:S(2)}, u32[]{:S(2)}) collective-permute-start(bf16[256,512]{1,0:T(8,128)(2,1)} %get-tuple-element.155), channel_id=1, source_target_pairs={{0,2},{1,3},{2,0},{3,1},{4,6},{5,7},{6,4},{7,5},{8,10},{9,11},{10,... | collective-permute-start | bytes 786440 | tf_op jit(solution)/shard_map/ppermute | solution.py:424
  65.4 9.6 %collective-permute-start.17 = (bf16[256,512]{1,0:T(8,128)(2,1)}, bf16[256,512]{1,0:T(8,128)(2,1)}, u32[]{:S(2)}, u32[]{:S(2)}) collective-permute-start(bf16[256,512]{1,0:T(8,128)(2,1)} %get-tuple-element.156), channel_id=1, source_target_pairs={{0,4},{1,5},{2,6},{3,7},{4,0},{5,1},{6,2},{7,3},{8,12},{9,13},{10,... | collective-permute-start | bytes 786440 | tf_op jit(solution)/shard_map/ppermute | solution.py:424
  66.9 13.8 %collective-permute-start.18 = (bf16[256,512]{1,0:T(8,128)(2,1)}, bf16[256,512]{1,0:T(8,128)(2,1)}, u32[]{:S(2)}, u32[]{:S(2)}) collective-permute-start(bf16[256,512]{1,0:T(8,128)(2,1)} %get-tuple-element.161), channel_id=1, source_target_pairs={{0,2},{1,3},{2,0},{3,1},{4,6},{5,7},{6,4},{7,5},{8,10},{9,11},{10,... | collective-permute-start | bytes 786440 | tf_op jit(solution)/shard_map/ppermute | solution.py:424
  67.2 13.5 %collective-permute-start.19 = (bf16[256,512]{1,0:T(8,128)(2,1)}, bf16[256,512]{1,0:T(8,128)(2,1)}, u32[]{:S(2)}, u32[]{:S(2)}) collective-permute-start(bf16[256,512]{1,0:T(8,128)(2,1)} %get-tuple-element.162), channel_id=1, source_target_pairs={{0,4},{1,5},{2,6},{3,7},{4,0},{5,1},{6,2},{7,3},{8,12},{9,13},{10,... | collective-permute-start | bytes 786440 | tf_op jit(solution)/shard_map/ppermute | solution.py:424
  67.7 30.9 %copy-start.3 = (bf16[512,768]{1,0:T(8,128)(2,1)S(1)}, bf16[512,768]{1,0:T(8,128)(2,1)}, u32[]{:S(2)}) copy-start(bf16[512,768]{1,0:T(8,128)(2,1)} %refs_0_) | copy-start | bytes 2359300
  67.7 30.9 %copy-start.5 = (bf16[512,768]{1,0:T(8,128)(2,1)S(1)}, bf16[512,768]{1,0:T(8,128)(2,1)}, u32[]{:S(2)}) copy-start(bf16[512,768]{1,0:T(8,128)(2,1)} %copy-done.4) | copy-start | bytes 2359300
  67.7 30.9 %copy-start.7 = (bf16[512,768]{1,0:T(8,128)(2,1)S(1)}, bf16[512,768]{1,0:T(8,128)(2,1)}, u32[]{:S(2)}) copy-start(bf16[512,768]{1,0:T(8,128)(2,1)} %copy-done.6) | copy-start | bytes 2359300
  67.7 30.9 %copy-start.9 = (bf16[512,768]{1,0:T(8,128)(2,1)S(1)}, bf16[512,768]{1,0:T(8,128)(2,1)}, u32[]{:S(2)}) copy-start(bf16[512,768]{1,0:T(8,128)(2,1)} %copy-done.8) | copy-start | bytes 2359300
  76.3 9.5 %collective-permute-start.22 = (bf16[128,512]{1,0:T(8,128)(2,1)S(1)}, bf16[128,512]{1,0:T(8,128)(2,1)S(1)}, u32[]{:S(2)}, u32[]{:S(2)}) collective-permute-start(bf16[128,512]{1,0:T(8,128)(2,1)S(1)} %get-tuple-element.165), channel_id=1, source_target_pairs={{0,8},{8,0},{16,24},{24,16},{1,9},{9,1},{17,25},{25,17},{2,10},{10... | collective-permute-start | bytes 393224 | tf_op jit(solution)/shard_map/ppermute | solution.py:424
  77.9 7.8 %collective-permute-start.23 = (bf16[128,512]{1,0:T(8,128)(2,1)S(1)}, bf16[128,512]{1,0:T(8,128)(2,1)S(1)}, u32[]{:S(2)}, u32[]{:S(2)}) collective-permute-start(bf16[128,512]{1,0:T(8,128)(2,1)S(1)} %get-tuple-element.166), channel_id=1, source_target_pairs={{0,16},{8,24},{16,0},{24,8},{1,17},{9,25},{17,1},{25,9},{2,18},{10... | collective-permute-start | bytes 393224 | tf_op jit(solution)/shard_map/ppermute | solution.py:424
  80.5 6.9 %collective-permute-start.24 = (bf16[128,512]{1,0:T(8,128)(2,1)S(1)}, bf16[128,512]{1,0:T(8,128)(2,1)S(1)}, u32[]{:S(2)}, u32[]{:S(2)}) collective-permute-start(bf16[128,512]{1,0:T(8,128)(2,1)S(1)} %get-tuple-element.167), channel_id=1, source_target_pairs={{0,24},{8,16},{16,8},{24,0},{1,25},{9,17},{17,9},{25,1},{2,26},{10... | collective-permute-start | bytes 393224 | tf_op jit(solution)/shard_map/ppermute | solution.py:424
  80.7 1.0 copy-start.13
  81.8 0.9 copy-start.16
  83.9 6.4 %collective-permute-start.20 = (bf16[128,512]{1,0:T(8,128)(2,1)S(1)}, bf16[128,512]{1,0:T(8,128)(2,1)S(1)}, u32[]{:S(2)}, u32[]{:S(2)}) collective-permute-start(bf16[128,512]{1,0:T(8,128)(2,1)S(1)} %get-tuple-element.163), channel_id=1, source_target_pairs={{0,2},{1,3},{2,0},{3,1},{4,6},{5,7},{6,4},{7,5},{8,10},{9,11},{10,... | collective-permute-start | bytes 393224 | tf_op jit(solution)/shard_map/ppermute | solution.py:424
  84.2 6.3 %collective-permute-start.21 = (bf16[128,512]{1,0:T(8,128)(2,1)S(1)}, bf16[128,512]{1,0:T(8,128)(2,1)S(1)}, u32[]{:S(2)}, u32[]{:S(2)}) collective-permute-start(bf16[128,512]{1,0:T(8,128)(2,1)S(1)} %get-tuple-element.164), channel_id=1, source_target_pairs={{0,4},{1,5},{2,6},{3,7},{4,0},{5,1},{6,2},{7,3},{8,12},{9,13},{10,... | collective-permute-start | bytes 393224 | tf_op jit(solution)/shard_map/ppermute | solution.py:424
  90.7 13.7 %collective-permute-start.29 = (bf16[256,768]{1,0:T(8,128)(2,1)S(1)}, bf16[256,768]{1,0:T(8,128)(2,1)S(1)}, u32[]{:S(2)}, u32[]{:S(2)}) collective-permute-start(bf16[256,768]{1,0:T(8,128)(2,1)S(1)} %slice.7), channel_id=1, source_target_pairs={{0,2},{1,3},{2,0},{3,1},{4,6},{5,7},{6,4},{7,5},{8,10},{9,11},{10,... | collective-permute-start | bytes 1179656 | tf_op jit(solution)/shard_map/ppermute | solution.py:424
  92.7 11.8 %collective-permute-start.28 = (bf16[256,768]{1,0:T(8,128)(2,1)S(1)}, bf16[256,768]{1,0:T(8,128)(2,1)S(1)}, u32[]{:S(2)}, u32[]{:S(2)}) collective-permute-start(bf16[256,768]{1,0:T(8,128)(2,1)S(1)} %slice.6), channel_id=1, source_target_pairs={{0,4},{1,5},{2,6},{3,7},{4,0},{5,1},{6,2},{7,3},{8,12},{9,13},{10,... | collective-permute-start | bytes 1179656 | tf_op jit(solution)/shard_map/ppermute | solution.py:424
  94.2 9.9 %collective-permute-start.25 = (bf16[64,512]{1,0:T(8,128)(2,1)S(1)}, bf16[64,512]{1,0:T(8,128)(2,1)S(1)}, u32[]{:S(2)}, u32[]{:S(2)}) collective-permute-start(bf16[64,512]{1,0:T(8,128)(2,1)S(1)} %get-tuple-element.179), channel_id=1, source_target_pairs={{0,8},{8,0},{16,24},{24,16},{1,9},{9,1},{17,25},{25,17},{2,10},{10... | collective-permute-start | bytes 196616 | tf_op jit(solution)/shard_map/ppermute | solution.py:424
  94.8 9.2 %collective-permute-start.26 = (bf16[64,512]{1,0:T(8,128)(2,1)S(1)}, bf16[64,512]{1,0:T(8,128)(2,1)S(1)}, u32[]{:S(2)}, u32[]{:S(2)}) collective-permute-start(bf16[64,512]{1,0:T(8,128)(2,1)S(1)} %get-tuple-element.180), channel_id=1, source_target_pairs={{0,16},{8,24},{16,0},{24,8},{1,17},{9,25},{17,1},{25,9},{2,18},{10... | collective-permute-start | bytes 196616 | tf_op jit(solution)/shard_map/ppermute | solution.py:424
  98.3 6.1 %collective-permute-start.27 = (bf16[64,512]{1,0:T(8,128)(2,1)S(1)}, bf16[64,512]{1,0:T(8,128)(2,1)S(1)}, u32[]{:S(2)}, u32[]{:S(2)}) collective-permute-start(bf16[64,512]{1,0:T(8,128)(2,1)S(1)} %get-tuple-element.181), channel_id=1, source_target_pairs={{0,24},{8,16},{16,8},{24,0},{1,25},{9,17},{17,9},{25,1},{2,26},{10... | collective-permute-start | bytes 196616 | tf_op jit(solution)/shard_map/ppermute | solution.py:424
  104.5 4.7 %collective-permute-start.33 = (bf16[512,768]{1,0:T(8,128)(2,1)S(1)}, bf16[512,768]{1,0:T(8,128)(2,1)S(1)}, u32[]{:S(2)}, u32[]{:S(2)}) collective-permute-start(bf16[512,768]{1,0:T(8,128)(2,1)S(1)} %constant_dynamic-update-slice_fusion.refs_0_), channel_id=1, source_target_pairs={{0,1},{1,0},{2,3},{3,2},{4,5},{5,4},{6,7},{7,6},{8,9},{9,8},{10,11... | collective-permute-start | bytes 2359304 | tf_op jit(solution)/shard_map/ppermute | solution.py:424
  104.7 9.7 %collective-permute-start.32 = (bf16[192,512]{1,0:T(8,128)(2,1)S(1)}, bf16[192,512]{1,0:T(8,128)(2,1)S(1)}, u32[]{:S(2)}, u32[]{:S(2)}) collective-permute-start(bf16[192,512]{1,0:T(8,128)(2,1)S(1)} %added.1.refs_0_), channel_id=1, source_target_pairs={{0,24},{8,16},{16,8},{24,0},{1,25},{9,17},{17,9},{25,1},{2,26},{10... | collective-permute-start | bytes 589832 | tf_op jit(solution)/shard_map/ppermute | solution.py:424
  108.0 16.1 %collective-permute-start.31 = (bf16[192,512]{1,0:T(8,128)(2,1)S(1)}, bf16[192,512]{1,0:T(8,128)(2,1)S(1)}, u32[]{:S(2)}, u32[]{:S(2)}) collective-permute-start(bf16[192,512]{1,0:T(8,128)(2,1)S(1)} %added.1.refs_0_), channel_id=1, source_target_pairs={{0,16},{8,24},{16,0},{24,8},{1,17},{9,25},{17,1},{25,9},{2,18},{10... | collective-permute-start | bytes 589832 | tf_op jit(solution)/shard_map/ppermute | solution.py:424
  108.0 16.1 %collective-permute-start.30 = (bf16[192,512]{1,0:T(8,128)(2,1)S(1)}, bf16[192,512]{1,0:T(8,128)(2,1)S(1)}, u32[]{:S(2)}, u32[]{:S(2)}) collective-permute-start(bf16[192,512]{1,0:T(8,128)(2,1)S(1)} %added.1.refs_0_), channel_id=1, source_target_pairs={{0,8},{8,0},{16,24},{24,16},{1,9},{9,1},{17,25},{25,17},{2,10},{10... | collective-permute-start | bytes 589832 | tf_op jit(solution)/shard_map/ppermute | solution.py:424
